TPU v7x, 32 devices: a whole 2x2x4 slice. The times are simulated.
32 devices in a mesh: grp: 2 (over y), tm: 8 (over z, x), head: 2 (over core).
Axes of the slice: x: 2, y: 2, z: 4, core: 2. Of those that a mesh axis runs over, the one named last changes fastest.
Arguments:
- frames: bfloat16 [8192, 1024], P(('grp', 'tm'), 'head'), parts along dimension 0
- segment_ids: int32 [8192], P(('grp', 'tm')), parts along dimension 0, may hold values from 0 to 15, never falling along the last dimension, each value on 1 to 2048 neighbouring positions
- utt_valid: int32 [32], P('grp'), parts along dimension 0, may hold values from 64 to 2047
- attn_gain: float32 [1024], replicated, may hold values from 0.1 to 1.9
- qkv_weight: bfloat16 [1024, 3, 512], P(None, None, 'head')
- out_weight: bfloat16 [512, 1024], P('head'), may hold values from -0.25 to 0.25
- conv_gain: float32 [1024], replicated, may hold values from 0.1 to 1.9
- pointwise_in: bfloat16 [1024, 2, 512], P(None, None, 'head'), may hold values from -0.1875 to 0.1875
- depthwise: float32 [31, 512], P(None, 'head')
- mid_gain: float32 [512], P('head'), may hold values from 0.1 to 1.9
- pointwise_out: bfloat16 [512, 1024], P('head'), may hold values from -0.25 to 0.25
Outputs:
- block_out: bfloat16 [8192, 1024], P(('grp', 'tm'), 'head'), parts along dimension 0
There are 2 independent parts, one for each index of `grp`. A program takes and returns all parts, laid end to end along the dimension named above; an argument that names none is the same for every part. Nothing has to cross between parts.
Inputs may be any that keep to these rules, and one draw needn't show every extreme that they name: `segment_ids`: segment ids never fall along the frames; each utterance holds 1 to 2048 frames, one exactly 2048.
All inputs are finite; a program needn't handle non-finite values.
Results may differ from a plain program's by a relative error of at most 0.015.
Values may be sent and summed in bfloat16 or wider, within the bound.
No kernel may reach another device: no remote copies, remote signals or barrier semaphores. Data moves between devices by JAX's collectives and lax.ppermute only.
A program may use at most 64 MiB of HBM per device.

v0:
```python
import jax
import jax.numpy as jnp
from jax import lax
from jax.sharding import PartitionSpec as P

HEAD_DIM = 64
CONV_CH = 512
KERNEL = 31
WIN = 512


def with_halo(block, sides, width):
    for axis, dim in sides:
        count = lax.axis_size(axis)
        forward = [(i, i + 1) for i in range(count - 1)]
        backward = [(target, source) for source, target in forward]
        low = lax.ppermute(
            lax.slice_in_dim(block, block.shape[dim] - width, None, axis=dim), axis, forward
        )
        high = lax.ppermute(lax.slice_in_dim(block, 0, width, axis=dim), axis, backward)
        block = jnp.concatenate([low, block, high], axis=dim)
    return block


def normalize(values, gain):
    mean = jnp.mean(values, axis=-1, keepdims=True)
    centred = values - mean
    spread = jnp.mean(centred * centred, axis=-1, keepdims=True)
    return centred * lax.rsqrt(spread + 1e-05) * gain


def attend(query, keys, values, allowed):
    scores = jnp.einsum(
        "qhe,khe->hqk", query, keys, preferred_element_type=jnp.float32
    ) * HEAD_DIM ** (-0.5)
    masked = jnp.where(allowed[None], scores, -jnp.inf)
    peak = jnp.max(masked, axis=-1, keepdims=True)
    peak = jnp.where(jnp.isfinite(peak), peak, 0.0)
    expw = jnp.where(allowed[None], jnp.exp(scores - peak), 0.0)
    total = jnp.sum(expw, axis=-1)
    weights = expw.astype(jnp.bfloat16)
    context = jnp.einsum("hqk,khe->qhe", weights, values, preferred_element_type=jnp.float32)
    return context / jnp.maximum(total, 1.0).T[:, :, None]


def local(
    frames,
    segment_ids,
    utt_valid,
    attn_gain,
    qkv_weight,
    out_weight,
    conv_gain,
    pointwise_in,
    depthwise,
    mid_gain,
    pointwise_out,
):
    rows, own_width = frames.shape
    width = qkv_weight.shape[2]
    chan = pointwise_in.shape[2]
    whole = lax.all_gather(frames, "head", axis=1, tiled=True)
    x_full = whole.astype(jnp.float32)
    normed = normalize(x_full, attn_gain).astype(jnp.bfloat16)
    ids = jnp.arange(utt_valid.shape[0], dtype=jnp.int32)
    onehot = segment_ids[:, None] == ids[None, :]
    local_counts = jnp.sum(onehot.astype(jnp.int32), axis=0)
    counts = lax.psum(local_counts, "tm")
    starts = jnp.cumsum(counts) - counts
    ends = starts + counts
    total_frames = rows * lax.axis_size("tm")
    position = lax.axis_index("tm") * rows + jnp.arange(rows, dtype=jnp.int32)
    start_of = jnp.sum(jnp.where(onehot, starts[None, :], 0), axis=1)
    limit = jnp.sum(jnp.where(onehot, utt_valid[None, :], 0), axis=1)
    mark = jnp.where(position - start_of < limit, segment_ids + 1, 0)
    wide_pos = lax.axis_index("tm") * rows - WIN + jnp.arange(rows + 2 * WIN, dtype=jnp.int32)
    wide_seg = jnp.sum((wide_pos[:, None] >= ends[None, :]).astype(jnp.int32), axis=1)
    wide_hot = wide_seg[:, None] == ids[None, :]
    wide_start = jnp.sum(jnp.where(wide_hot, starts[None, :], 0), axis=1)
    wide_limit = jnp.sum(jnp.where(wide_hot, utt_valid[None, :], 0), axis=1)
    inside = (wide_pos >= 0) & (wide_pos < total_frames)
    mark_ext = jnp.where(inside & (wide_pos - wide_start < wide_limit), wide_seg + 1, 0)
    projected = jnp.dot(
        normed, qkv_weight.reshape(normed.shape[1], 3 * width), preferred_element_type=jnp.float32
    )
    projected = projected.reshape(rows, 3, width).astype(jnp.bfloat16)
    query = projected[:, 0].reshape(rows, -1, HEAD_DIM)
    paired = projected[:, 1:].reshape(rows, 2 * width)
    paired_ext = with_halo(paired, (("tm", 0),), WIN)
    span = paired_ext.shape[0]
    keys = paired_ext[:, :width].reshape(span, -1, HEAD_DIM)
    values = paired_ext[:, width:].reshape(span, -1, HEAD_DIM)
    offsets = (
        jnp.arange(span, dtype=jnp.int32)[None, :] - jnp.arange(rows, dtype=jnp.int32)[:, None]
    )
    near = (offsets >= 0) & (offsets <= 2 * WIN)
    allowed = near & (mark[:, None] == mark_ext[None, :]) & (mark[:, None] > 0)
    context = attend(query, keys, values, allowed)
    context = context.reshape(rows, width).astype(jnp.bfloat16)
    partial_attn = jnp.dot(context, out_weight, preferred_element_type=jnp.float32)
    attn_sum = lax.psum(partial_attn.astype(jnp.bfloat16), "head").astype(jnp.float32)
    mid_full = (x_full + attn_sum).astype(jnp.bfloat16)
    mid_own = lax.dynamic_slice_in_dim(mid_full, lax.axis_index("head") * own_width, own_width, 1)
    normed2 = normalize(mid_full.astype(jnp.float32), conv_gain).astype(jnp.bfloat16)
    pre = jnp.dot(
        normed2,
        pointwise_in.reshape(normed2.shape[1], 2 * chan),
        preferred_element_type=jnp.float32,
    ).reshape(rows, 2, chan)
    glu = pre[:, 0] * jax.nn.sigmoid(pre[:, 1])
    glu = jnp.where((mark > 0)[:, None], glu, 0.0).astype(jnp.bfloat16)
    reach = KERNEL // 2
    glu_ext = with_halo(glu, (("tm", 0),), reach)
    mark_conv = mark_ext[WIN - reach : WIN + rows + reach]
    convolved = jnp.zeros((rows, chan), jnp.float32)
    for tap in range(KERNEL):
        same = (mark_conv[tap : tap + rows] == mark)[:, None]
        convolved = (
            convolved
            + jnp.where(same, glu_ext[tap : tap + rows].astype(jnp.float32), 0.0) * depthwise[tap]
        )
    sum_first, sum_second = lax.psum(
        (jnp.sum(convolved, axis=-1), jnp.sum(convolved * convolved, axis=-1)), "head"
    )
    mean = (sum_first / CONV_CH)[:, None]
    square = (sum_second / CONV_CH)[:, None]
    scaled = (convolved - mean) * lax.rsqrt(square - mean * mean + 1e-05) * mid_gain
    act = (scaled * jax.nn.sigmoid(scaled)).astype(jnp.bfloat16)
    partial_conv = jnp.dot(act, pointwise_out, preferred_element_type=jnp.float32)
    conv_own = lax.psum_scatter(
        partial_conv.astype(jnp.bfloat16), "head", scatter_dimension=1, tiled=True
    ).astype(jnp.float32)
    return (mid_own.astype(jnp.float32) + conv_own).astype(jnp.bfloat16)


def solution(mesh):
    in_specs = (
        P(("grp", "tm"), "head"),
        P(("grp", "tm")),
        P("grp"),
        P(),
        P(None, None, "head"),
        P("head", None),
        P(),
        P(None, None, "head"),
        P(None, "head"),
        P("head"),
        P("head", None),
    )
    out_specs = P(("grp", "tm"), "head")
    return jax.shard_map(local, mesh=mesh, in_specs=in_specs, out_specs=out_specs, check_vma=False)
```

profile of v0, /device:TPU:0, one launch (start us, length us, event | category | flops | bytes accessed | tf_op | source)
XLA Modules:
  0.0 125.3 jit_solution(2234566133149236479)
XLA Ops:
  8.1 13.1 %psum.28 = s32[16]{0:T(128)S(1)} all-reduce(s32[16]{0:T(128)S(1)} %convert_reduce_fusion.3), channel_id=1, replica_groups=mesh['grp'=2,'tm'=8,'head'=2] {'tm'}, use_global_device_ids=true, to_apply=%region_3.0 | all-reduce | flops 16 | bytes 128 | tf_op jit(solution)/shard_map/psum | solution.py:68
  21.4 1.7 %copy.17 = bf16[1024,3,256]{0,2,1:T(8,128)(2,1)S(1)} copy(bf16[1024,3,256]{2,0,1:T(8,128)(2,1)} %param.15) | data formatting | bytes 3145728 | tf_op args[4]
  23.6 1.5 %convert_reduce_fusion = f32[512]{0:T(512)S(1)} fusion(bf16[512,1024]{1,0:T(8,128)(2,1)} %all-gather.2.cloned.1.call-done), kind=kLoop, calls=%fused_computation.11 | loop fusion | flops 1048064 | bytes 1050624 | tf_op jit(solution)/shard_map/reduce_sum | solution.py:26
  25.1 1.6 %fusion.14 = f32[512]{0:T(512)S(1)} fusion(bf16[512,1024]{1,0:T(8,128)(2,1)} %all-gather.2.cloned.1.call-done, f32[512]{0:T(512)S(1)} %broadcast_multiply_fusion.2), kind=kLoop, calls=%fused_computation.21 | loop fusion | flops 2096640 | bytes 1052672 | tf_op jit(solution)/shard_map/reduce_sum | solution.py:28
  26.8 1.2 fusion.23
  28.0 3.4 %collective-permute-start = (bf16[512,512]{0,1:T(8,128)(2,1)S(1)}, bf16[512,512]{0,1:T(8,128)(2,1)S(1)}, u32[]{:S(2)}, u32[]{:S(2)}) collective-permute-start(bf16[512,512]{0,1:T(8,128)(2,1)S(1)} %bitcast.80), channel_id=1, source_target_pairs={{0,2},{2,4},{4,6},{6,8},{8,10},{10,12},{12,14},{1,3},{3,5},{5,7},{... | collective-permute-start | bytes 1572872 | tf_op jit(solution)/shard_map/ppermute | solution.py:17
  31.4 1.3 %collective-permute-start.1 = (bf16[512,512]{0,1:T(8,128)(2,1)S(1)}, bf16[512,512]{0,1:T(8,128)(2,1)S(1)}, u32[]{:S(2)}, u32[]{:S(2)}) collective-permute-start(bf16[512,512]{0,1:T(8,128)(2,1)S(1)} %bitcast.81), channel_id=1, source_target_pairs={{2,0},{4,2},{6,4},{8,6},{10,8},{12,10},{14,12},{3,1},{5,3},{7,5},{... | collective-permute-start | bytes 1572872 | tf_op jit(solution)/shard_map/ppermute | solution.py:20
  33.5 18.1 %collective-permute-done = bf16[512,512]{0,1:T(8,128)(2,1)S(1)} collective-permute-done((bf16[512,512]{0,1:T(8,128)(2,1)S(1)}, bf16[512,512]{0,1:T(8,128)(2,1)S(1)}, u32[]{:S(2)}, u32[]{:S(2)}) %collective-permute-start) | collective-permute-done | bytes 524320 | tf_op jit(solution)/shard_map/ppermute | solution.py:17
  51.8 2.4 %select_reduce_fusion = (f32[4,512]{1,0:T(4,128)S(1)}, f32[4,512,1536]{2,1,0:T(8,128)S(1)}) fusion(pred[512,1536]{1,0:T(8,128)(4,1)S(1)} %fusion.9, bf16[512,4,64]{0,2,1:T(8,128)(2,1)S(1)} %bitcast.83, bf16[1536,4,64]{0,2,1:T(8,128)(2,1)S(1)} %bitcast.79), kind=kOutput, calls=%fused_computation.1 | convolution fusion | flops 412088320 | bytes 14426112 | tf_op jit(solution)/shard_map/qhe,khe->hqk/dot_general | solution.py:33
  54.2 4.1 %fusion = f32[4,512]{1,0:T(4,128)S(1)} fusion(f32[4,512,1536]{2,1,0:T(8,128)S(1)} %get-tuple-element.87, f32[4,512]{1,0:T(4,128)S(1)} %is-finite_select_fusion, pred[512,1536]{1,0:T(8,128)(4,1)S(1)} %fusion.9), kind=kLoop, calls=%fused_computation.2 | loop fusion | flops 12580864 | bytes 13385728 | tf_op jit(solution)/shard_map/reduce_sum | solution.py:40
  58.4 2.9 %fusion.43 = bf16[512,4,64]{0,2,1:T(8,128)(2,1)S(1)} fusion(bf16[1536,4,64]{0,2,1:T(8,128)(2,1)S(1)} %bitcast.86, f32[4,512,1536]{2,1,0:T(8,128)S(1)} %get-tuple-element.87, f32[4,512]{1,0:T(4,128)S(1)} %is-finite_select_fusion, pred[512,1536]{1,0:T(8,128)(4,1)S(1)} %fusion.9, f32[512,4]{0,1:T(4,128)S(1)} %maximum_bitcast_fusion), kind=kOutput, calls=%fused_computation.74 | convolution fusion | flops 415498240 | bytes 14434304 | tf_op jit(solution)/shard_map/hqk,khe->qhe/dot_general | solution.py:42
  61.3 1.4 %convolution_convert_fusion.1 = bf16[512,1024]{1,0:T(8,128)(2,1)} fusion(bf16[512,256]{0,1:T(8,128)(2,1)S(1)} %bitcast.87, bf16[256,1024]{1,0:T(8,128)(2,1)S(1)} %copy-done), kind=kOutput, calls=%fused_computation.60 | convolution fusion | flops 268959744 | bytes 1835008 | tf_op jit(solution)/shard_map/dot_general | solution.py:100
  62.8 1.5 %copy.20 = bf16[128,8,2,256]{3,1,2,0:T(8,128)(2,1)S(1)} copy(bf16[128,8,2,256]{3,2,1,0:T(2,128)(2,1)} %bitcast.84) | data formatting | bytes 2097152
  64.3 1.3 %copy.19 = bf16[512,1024]{1,0:T(8,128)(2,1)} copy(bf16[512,1024]{0,1:T(8,128)(2,1)S(1)} %bitcast.78) | data formatting | bytes 2097152 | tf_op jit(solution)/shard_map/dot_general | solution.py:105
  65.7 18.8 %all-reduce.3.cloned.1.call-done = bf16[512,1024]{1,0:T(8,128)(2,1)} async-done(((bf16[512,1024]{1,0:T(8,128)(2,1)}), bf16[512,1024]{1,0:T(8,128)(2,1)}) %all-reduce.3.cloned.1.call-update) | async-done | bytes 1048592 | tf_op jit(solution)/shard_map/psum | solution.py:101
  84.4 1.7 %convert_reduce_fusion.1 = (f32[512]{0:T(512)S(1)}, bf16[512,1024]{1,0:T(8,128)(2,1)S(1)}) fusion(bf16[512,1024]{1,0:T(8,128)(2,1)} %all-reduce.3.cloned.1.call-done, bf16[512,1024]{1,0:T(8,128)(2,1)S(1)} %copy-done.1), kind=kLoop, calls=%fused_computation.16 | loop fusion | flops 3145216 | bytes 3147776 | tf_op jit(solution)/shard_map/reduce_sum | solution.py:26
  87.6 3.6 %collective-permute-start.2 = (bf16[15,256]{1,0:T(8,128)(2,1)S(1)}, bf16[15,256]{1,0:T(8,128)(2,1)S(1)}, u32[]{:S(2)}, u32[]{:S(2)}) collective-permute-start(bf16[15,256]{1,0:T(8,128)(2,1)S(1)} %get-tuple-element.20), channel_id=1, source_target_pairs={{0,2},{2,4},{4,6},{6,8},{8,10},{10,12},{12,14},{1,3},{3,5},{5,7},{... | collective-permute-start | bytes 23048 | tf_op jit(solution)/shard_map/ppermute | solution.py:17
  91.2 1.5 %collective-permute-start.3 = (bf16[15,256]{1,0:T(8,128)(2,1)S(1)}, bf16[15,256]{1,0:T(8,128)(2,1)S(1)}, u32[]{:S(2)}, u32[]{:S(2)}) collective-permute-start(bf16[15,256]{1,0:T(8,128)(2,1)S(1)} %get-tuple-element.21), channel_id=1, source_target_pairs={{2,0},{4,2},{6,4},{8,6},{10,8},{12,10},{14,12},{3,1},{5,3},{7,5},{... | collective-permute-start | bytes 23048 | tf_op jit(solution)/shard_map/ppermute | solution.py:20
  92.8 4.0 %collective-permute-done.3 = bf16[15,256]{1,0:T(8,128)(2,1)S(1)} collective-permute-done((bf16[15,256]{1,0:T(8,128)(2,1)S(1)}, bf16[15,256]{1,0:T(8,128)(2,1)S(1)}, u32[]{:S(2)}, u32[]{:S(2)}) %collective-permute-start.3) | collective-permute-done | bytes 7712 | tf_op jit(solution)/shard_map/ppermute | solution.py:20
  96.8 5.3 %fusion.92 = (f32[512]{0:T(512)S(1)}, f32[512]{0:T(512)S(1)}, f32[512,256]{1,0:T(8,128)S(1)}) fusion(f32[256]{0:T(256)S(1)} %bitcast.98, bf16[15,256]{1,0:T(8,128)(2,1)S(1)} %collective-permute-done.3, bf16[512,256]{1,0:T(8,128)(2,1)S(1)} %fusion.52, pred[512]{0:T(512)(128)(4,1)S(1)} %get-tuple-element.82, f32[256]{0:T(256)S(1)} %bitcast.99, ...), kind=kLoop, calls=%fused_computation.196 | loop fusion | flops 28310528 | bytes 853504 | tf_op jit(solution)/shard_map/reduce_sum | solution.py:123
  102.1 2.5 %all-reduce = (f32[512]{0:T(512)S(1)}, f32[512]{0:T(512)S(1)}) all-reduce(f32[512]{0:T(512)S(1)} %get-tuple-element.6, f32[512]{0:T(512)S(1)} %get-tuple-element.5), channel_id=1, replica_groups=mesh['grp'=2,'tm'=8,'head'=2] {'head'}, use_global_device_ids=true, to_apply=%region_18.19 | all-reduce | flops 1024 | bytes 8192 | tf_op jit(solution)/shard_map/psum | solution.py:122
  104.6 2.6 %convolution_convert_fusion = bf16[512,1024]{1,0:T(8,128)(2,1)} fusion(bf16[256,1024]{1,0:T(8,128)(2,1)} %param.21, f32[512,256]{1,0:T(8,128)S(1)} %get-tuple-element.13, f32[256]{0:T(256)S(1)} %copy-done.8, f32[512]{0:T(512)S(1)} %get-tuple-element.84, f32[512]{0:T(512)S(1)} %get-tuple-element.83), kind=kOutput, calls=%fused_computation.59 | convolution fusion | flops 270008320 | bytes 2102272 | tf_op jit(solution)/shard_map/dot_general | solution.py:129
  107.2 9.6 %reduce-scatter.2.cloned.1.call-done = bf16[512,512]{1,0:T(8,128)(2,1)} async-done(((bf16[512,1024]{1,0:T(8,128)(2,1)}), bf16[512,512]{1,0:T(8,128)(2,1)}) %reduce-scatter.2.cloned.1.call-update) | async-done | bytes 524304 | tf_op jit(solution)/shard_map/reduce_scatter | solution.py:130
  116.8 2.0 %add_convert_fusion = bf16[512,512]{1,0:T(8,128)(2,1)} fusion(bf16[512,512]{1,0:T(8,128)(2,1)} %reduce-scatter.2.cloned.1.call-done, bf16[512,1024]{1,0:T(8,128)(2,1)S(1)} %get-tuple-element.17, s32[]{:T(128)S(6)} %select_n.151), kind=kLoop, calls=%fused_computation.66 | loop fusion | flops 1048576 | bytes 1572868 | tf_op jit(solution)/shard_map/convert_element_type | solution.py:133
  (58 shorter events, 4.9 us)
Async XLA Ops:
  6.5 54.8 %copy-start = (bf16[256,1024]{1,0:T(8,128)(2,1)S(1)}, bf16[256,1024]{1,0:T(8,128)(2,1)}, u32[]{:S(2)}) copy-start(bf16[256,1024]{1,0:T(8,128)(2,1)} %param.16) | copy-start | bytes 1572868
  6.5 16.7 %copy-start.4 = (s32[512]{0:T(512)S(1)}, s32[512]{0:T(512)}, u32[]{:S(2)}) copy-start(s32[512]{0:T(512)} %param.12) | copy-start | bytes 6148
  6.5 16.8 %copy-start.5 = (s32[16]{0:T(128)S(1)}, s32[16]{0:T(128)}, u32[]{:S(2)}) copy-start(s32[16]{0:T(128)} %param.13) | copy-start | bytes 196
  6.5 17.1 %all-gather.2.cloned.1.call-start = ((), (), s32[]{:S(2)}) async-start(), calls=%async_computation.1 | async-start | bytes 1572864 | tf_op jit(solution)/shard_map/all_gather | solution.py:62
  7.3 77.2 %all-reduce.3.cloned.1.call-start = ((), (), s32[]{:S(2)}) async-start(), calls=%async_computation.2 | async-start | bytes 2097152 | tf_op jit(solution)/shard_map/psum | solution.py:101
  21.4 5.4 %copy-start.6 = (f32[1024]{0:T(1024)S(1)}, f32[1024]{0:T(1024)}, u32[]{:S(2)}) copy-start(f32[1024]{0:T(1024)} %param.14) | copy-start | bytes 12292
  23.6 3.2 %copy-start.1 = (bf16[512,1024]{1,0:T(8,128)(2,1)S(1)}, bf16[512,1024]{1,0:T(8,128)(2,1)}, u32[]{:S(2)}) copy-start(bf16[512,1024]{1,0:T(8,128)(2,1)} %all-gather.2.cloned.1.call-done) | copy-start | bytes 3145732
  28.0 23.6 %collective-permute-start = (bf16[512,512]{0,1:T(8,128)(2,1)S(1)}, bf16[512,512]{0,1:T(8,128)(2,1)S(1)}, u32[]{:S(2)}, u32[]{:S(2)}) collective-permute-start(bf16[512,512]{0,1:T(8,128)(2,1)S(1)} %bitcast.80), channel_id=1, source_target_pairs={{0,2},{2,4},{4,6},{6,8},{8,10},{10,12},{12,14},{1,3},{3,5},{5,7},{... | collective-permute-start | bytes 1572872 | tf_op jit(solution)/shard_map/ppermute | solution.py:17
  31.4 20.1 %collective-permute-start.1 = (bf16[512,512]{0,1:T(8,128)(2,1)S(1)}, bf16[512,512]{0,1:T(8,128)(2,1)S(1)}, u32[]{:S(2)}, u32[]{:S(2)}) collective-permute-start(bf16[512,512]{0,1:T(8,128)(2,1)S(1)} %bitcast.81), channel_id=1, source_target_pairs={{2,0},{4,2},{6,4},{8,6},{10,8},{12,10},{14,12},{3,1},{5,3},{7,5},{... | collective-permute-start | bytes 1572872 | tf_op jit(solution)/shard_map/ppermute | solution.py:20
  62.8 54.0 %reduce-scatter.2.cloned.1.call-start = ((), (), s32[]{:S(2)}) async-start(), calls=%async_computation.3 | async-start | bytes 1572864 | tf_op jit(solution)/shard_map/reduce_scatter | solution.py:130
  62.8 2.8 %copy-start.3 = (f32[31,256]{1,0:T(8,128)S(1)}, f32[31,256]{1,0:T(8,128)}, u32[]{:S(2)}) copy-start(f32[31,256]{1,0:T(8,128)} %param.19) | copy-start | bytes 95236
  65.7 20.9 %copy-start.7 = (f32[1024]{0:T(1024)S(1)}, f32[1024]{0:T(1024)}, u32[]{:S(2)}) copy-start(f32[1024]{0:T(1024)} %param.17) | copy-start | bytes 12292
  84.4 2.1 %copy-start.2 = (bf16[512,1024]{1,0:T(8,128)(2,1)S(1)}, bf16[512,1024]{1,0:T(8,128)(2,1)}, u32[]{:S(2)}) copy-start(bf16[512,1024]{1,0:T(8,128)(2,1)} %copy.19) | copy-start | bytes 3145732
  87.4 17.2 %copy-start.8 = (f32[256]{0:T(256)S(1)}, f32[256]{0:T(256)}, u32[]{:S(2)}) copy-start(f32[256]{0:T(256)} %param.20) | copy-start | bytes 3076
  87.6 5.2 %collective-permute-start.2 = (bf16[15,256]{1,0:T(8,128)(2,1)S(1)}, bf16[15,256]{1,0:T(8,128)(2,1)S(1)}, u32[]{:S(2)}, u32[]{:S(2)}) collective-permute-start(bf16[15,256]{1,0:T(8,128)(2,1)S(1)} %get-tuple-element.20), channel_id=1, source_target_pairs={{0,2},{2,4},{4,6},{6,8},{8,10},{10,12},{12,14},{1,3},{3,5},{5,7},{... | collective-permute-start | bytes 23048 | tf_op jit(solution)/shard_map/ppermute | solution.py:17
  91.2 5.5 %collective-permute-start.3 = (bf16[15,256]{1,0:T(8,128)(2,1)S(1)}, bf16[15,256]{1,0:T(8,128)(2,1)S(1)}, u32[]{:S(2)}, u32[]{:S(2)}) collective-permute-start(bf16[15,256]{1,0:T(8,128)(2,1)S(1)} %get-tuple-element.21), channel_id=1, source_target_pairs={{2,0},{4,2},{6,4},{8,6},{10,8},{12,10},{14,12},{3,1},{5,3},{7,5},{... | collective-permute-start | bytes 23048 | tf_op jit(solution)/shard_map/ppermute | solution.py:20
Sparse Core Ops, SparseCore 0:
  8.9 11.7 all-gather.1
  62.9 21.4 all-reduce.2
  107.3 9.4 reduce-scatter.1
where the time goes:
time: 126 us; the launch traced here: 125 us
  waiting for transfers between devices  51.1 us (41%)
  other arithmetic  19.2 us (15%)
  blocking collectives  15.5 us (12%)
  between operations  13.4 us (11%)
  matrix products  11.3 us (9%)
  starting transfers between devices  9.93 us (8%)
  local copies, waits for them, and re-layouts  4.83 us (4%)
    psum x1, waiting for transfers between devices, local(): lax.psum(partial_attn.astype(jnp.bfloat16), 'head').astype(jnp.float32)  18.8 us
    ppermute x2, waiting for transfers between devices, with_halo(): lax.ppermute(lax.slice_in_dim(block, block.shape[dim] - width, None, axis...  18.1 us
    psum x1, blocking collectives, local(): counts = lax.psum(local_counts, 'tm')  13.1 us
    reduce_scatter x1, waiting for transfers between devices, local(): lax.psum_scatter(partial_conv.astype(jnp.bfloat16), 'head', scatter_dimen...  9.6 us
    ppermute x2, starting transfers between devices, with_halo(): lax.ppermute(lax.slice_in_dim(block, block.shape[dim] - width, None, axis...  7.08 us
    reduce_sum x1, other arithmetic, local(): jnp.sum(convolved, axis=-1)  5.33 us
    reduce_sum x1, other arithmetic, attend(): total = jnp.sum(expw, axis=-1)  4.12 us
    ppermute x2, waiting for transfers between devices, with_halo(): lax.ppermute(lax.slice_in_dim(block, 0, width, axis=dim), axis, backward)  3.96 us
  transfers between devices with their start and end apart: 7, of which 4 were waited for; matrix products, arithmetic and copies ran while one was open for 5% of the time, Pallas kernels for 0%

commit v1 on v0

--- a/solution.py
+++ b/solution.py
@@ -59,7 +59,14 @@
     rows, own_width = frames.shape
     width = qkv_weight.shape[2]
     chan = pointwise_in.shape[2]
-    whole = lax.all_gather(frames, "head", axis=1, tiled=True)
+    swap = [(0, 1), (1, 0)]
+    other = lax.ppermute(frames, "head", swap)
+    me = lax.axis_index("head")
+    whole = jnp.where(
+        me == 0,
+        jnp.concatenate([frames, other], axis=1),
+        jnp.concatenate([other, frames], axis=1),
+    )
     x_full = whole.astype(jnp.float32)
     normed = normalize(x_full, attn_gain).astype(jnp.bfloat16)
     ids = jnp.arange(utt_valid.shape[0], dtype=jnp.int32)
@@ -98,7 +105,10 @@
     context = attend(query, keys, values, allowed)
     context = context.reshape(rows, width).astype(jnp.bfloat16)
     partial_attn = jnp.dot(context, out_weight, preferred_element_type=jnp.float32)
-    attn_sum = lax.psum(partial_attn.astype(jnp.bfloat16), "head").astype(jnp.float32)
+    partial_attn = partial_attn.astype(jnp.bfloat16)
+    attn_sum = partial_attn.astype(jnp.float32) + lax.ppermute(
+        partial_attn, "head", swap
+    ).astype(jnp.float32)
     mid_full = (x_full + attn_sum).astype(jnp.bfloat16)
     mid_own = lax.dynamic_slice_in_dim(mid_full, lax.axis_index("head") * own_width, own_width, 1)
     normed2 = normalize(mid_full.astype(jnp.float32), conv_gain).astype(jnp.bfloat16)
@@ -127,9 +137,12 @@
     scaled = (convolved - mean) * lax.rsqrt(square - mean * mean + 1e-05) * mid_gain
     act = (scaled * jax.nn.sigmoid(scaled)).astype(jnp.bfloat16)
     partial_conv = jnp.dot(act, pointwise_out, preferred_element_type=jnp.float32)
-    conv_own = lax.psum_scatter(
-        partial_conv.astype(jnp.bfloat16), "head", scatter_dimension=1, tiled=True
-    ).astype(jnp.float32)
+    partial_conv = partial_conv.astype(jnp.bfloat16)
+    conv_keep = lax.dynamic_slice_in_dim(partial_conv, me * own_width, own_width, 1)
+    conv_send = lax.dynamic_slice_in_dim(partial_conv, (1 - me) * own_width, own_width, 1)
+    conv_own = conv_keep.astype(jnp.float32) + lax.ppermute(conv_send, "head", swap).astype(
+        jnp.float32
+    )
     return (mid_own.astype(jnp.float32) + conv_own).astype(jnp.bfloat16)
 
 

time: 126 us -> 84.7 us (0.67)
  waiting for transfers between devices: 51.1 us -> 25.3 us
  between operations: 13.4 us -> 0.3 us
  other arithmetic: 19.2 us -> 16.3 us
  starting transfers between devices: 9.93 us -> 11.3 us
    psum x1 -> x0, waiting for transfers between devices: 18.8 us -> none  [local(): lax.psum(partial_attn.astype(jnp.bfloat16), 'head').astype(jnp.float32)]
    reduce_scatter x1 -> x0, waiting for transfers between devices: 9.6 us -> none  [local(): lax.psum_scatter(partial_conv.astype(jnp.bfloat16), 'head', scatter_dimen...]
    ppermute x0 -> x3, waiting for transfers between devices: none -> 3.32 us  [the longest x1 1.96 us: local(): lax.ppermute(conv_send, 'head', swap).astype(jnp.float32)]
    unnamed x20 -> x24, local copies, waits for them, and re-layouts: 3.21 us -> 3.22 us
  transfers between devices with their start and end apart: 7 -> 7, of which waited for: 4 -> 4; matrix products, arithmetic and copies ran while one was open for 5% -> 8% of each run, Pallas kernels for 0% -> 0%
where the time goes in v1:
time: 84.7 us; the launch traced here: 84.4 us
  waiting for transfers between devices  25.3 us (30%)
  other arithmetic  16.3 us (19%)
  blocking collectives  15.2 us (18%)
  starting transfers between devices  11.3 us (13%)
  matrix products  10.4 us (12%)
  local copies, waits for them, and re-layouts  5.67 us (7%)
    ppermute x2, waiting for transfers between devices, with_halo(): lax.ppermute(lax.slice_in_dim(block, block.shape[dim] - width, None, axis...  18 us
    psum x1, blocking collectives, local(): counts = lax.psum(local_counts, 'tm')  12.7 us
    ppermute x2, starting transfers between devices, with_halo(): lax.ppermute(lax.slice_in_dim(block, block.shape[dim] - width, None, axis...  7.83 us
    reduce_sum x1, other arithmetic, local(): jnp.sum(convolved, axis=-1)  5.34 us
    reduce_sum x1, other arithmetic, attend(): total = jnp.sum(expw, axis=-1)  4.12 us
    ppermute x2, waiting for transfers between devices, with_halo(): lax.ppermute(lax.slice_in_dim(block, 0, width, axis=dim), axis, backward)  3.96 us
    unnamed x24, local copies, waits for them, and re-layouts  3.22 us
    dot_general x1, matrix products, attend(): jnp.einsum('hqk,khe->qhe', weights, values, preferred_element_type=jnp.fl...  2.93 us
  transfers between devices with their start and end apart: 7, of which 4 were waited for; matrix products, arithmetic and copies ran while one was open for 8% of the time, Pallas kernels for 0%

profile of v1, /device:TPU:0, one launch (start us, length us, event | category | flops | bytes accessed | tf_op | source)
XLA Modules:
  0.0 84.4 jit_solution(6287025756378135902)
XLA Ops:
  0.5 0.8 convert_reduce_fusion.3
  1.3 12.7 %psum.21 = s32[16]{0:T(128)S(1)} all-reduce(s32[16]{0:T(128)S(1)} %convert_reduce_fusion.3), channel_id=1, replica_groups=mesh['grp'=2,'tm'=8,'head'=2] {'tm'}, use_global_device_ids=true, to_apply=%region_3.4 | all-reduce | flops 16 | bytes 128 | tf_op jit(solution)/shard_map/psum | solution.py:75
  14.4 2.6 %copy.17 = bf16[1024,3,256]{0,2,1:T(8,128)(2,1)} copy(bf16[1024,3,256]{2,0,1:T(8,128)(2,1)} %param.15) | data formatting | bytes 3145728 | tf_op args[4]
  18.4 1.2 %fusion.23 = bf16[512,3,256]{0,2,1:T(8,128)(2,1)S(1)} fusion(bf16[1024,3,256]{0,2,1:T(8,128)(2,1)S(1)} %copy-done.2, f32[1024]{0:T(1024)S(1)} %copy-done.8, f32[512]{0:T(512)S(1)} %add_rsqrt_fusion.2, f32[512]{0:T(512)S(1)} %broadcast_multiply_fusion.2, bf16[512,512]{1,0:T(8,128)(2,1)S(1)} %collective-permute-done, bf16[512,512]{1,0:T(8,128)(2,1)S(1)} %copy-done.1, ...), kind=kOutput, calls=%fused_computation.61 | convolution fusion | flops 813039616 | bytes 3416065 | tf_op jit(solution)/shard_map/dot_general | solution.py:90
  19.7 3.4 %collective-permute-start.1 = (bf16[512,512]{0,1:T(8,128)(2,1)S(1)}, bf16[512,512]{0,1:T(8,128)(2,1)S(1)}, u32[]{:S(2)}, u32[]{:S(2)}) collective-permute-start(bf16[512,512]{0,1:T(8,128)(2,1)S(1)} %bitcast.80), channel_id=1, source_target_pairs={{0,2},{2,4},{4,6},{6,8},{8,10},{10,12},{12,14},{1,3},{3,5},{5,7},{... | collective-permute-start | bytes 1572872 | tf_op jit(solution)/shard_map/ppermute | solution.py:17
  23.1 1.3 %collective-permute-start.2 = (bf16[512,512]{0,1:T(8,128)(2,1)S(1)}, bf16[512,512]{0,1:T(8,128)(2,1)S(1)}, u32[]{:S(2)}, u32[]{:S(2)}) collective-permute-start(bf16[512,512]{0,1:T(8,128)(2,1)S(1)} %bitcast.81), channel_id=1, source_target_pairs={{2,0},{4,2},{6,4},{8,6},{10,8},{12,10},{14,12},{3,1},{5,3},{7,5},{... | collective-permute-start | bytes 1572872 | tf_op jit(solution)/shard_map/ppermute | solution.py:20
  25.2 18.0 %collective-permute-done.1 = bf16[512,512]{0,1:T(8,128)(2,1)S(1)} collective-permute-done((bf16[512,512]{0,1:T(8,128)(2,1)S(1)}, bf16[512,512]{0,1:T(8,128)(2,1)S(1)}, u32[]{:S(2)}, u32[]{:S(2)}) %collective-permute-start.1) | collective-permute-done | bytes 524320 | tf_op jit(solution)/shard_map/ppermute | solution.py:17
  43.4 2.4 %select_reduce_fusion = (f32[4,512]{1,0:T(4,128)S(1)}, f32[4,512,1536]{2,1,0:T(8,128)S(1)}) fusion(pred[512,1536]{1,0:T(8,128)(4,1)S(1)} %fusion.9, bf16[512,4,64]{0,2,1:T(8,128)(2,1)S(1)} %bitcast.83, bf16[1536,4,64]{0,2,1:T(8,128)(2,1)S(1)} %bitcast.79), kind=kOutput, calls=%fused_computation.1 | convolution fusion | flops 412088320 | bytes 14426112 | tf_op jit(solution)/shard_map/qhe,khe->hqk/dot_general | solution.py:33
  45.8 4.1 %fusion = f32[4,512]{1,0:T(4,128)S(1)} fusion(f32[4,512,1536]{2,1,0:T(8,128)S(1)} %get-tuple-element.87, f32[4,512]{1,0:T(4,128)S(1)} %is-finite_select_fusion, pred[512,1536]{1,0:T(8,128)(4,1)S(1)} %fusion.9), kind=kLoop, calls=%fused_computation.2 | loop fusion | flops 12580864 | bytes 13385728 | tf_op jit(solution)/shard_map/reduce_sum | solution.py:40
  50.0 2.9 %fusion.43 = bf16[512,4,64]{0,2,1:T(8,128)(2,1)S(1)} fusion(bf16[1536,4,64]{0,2,1:T(8,128)(2,1)S(1)} %bitcast.86, f32[4,512,1536]{2,1,0:T(8,128)S(1)} %get-tuple-element.87, f32[4,512]{1,0:T(4,128)S(1)} %is-finite_select_fusion, pred[512,1536]{1,0:T(8,128)(4,1)S(1)} %fusion.9, f32[512,4]{0,1:T(4,128)S(1)} %maximum_bitcast_fusion), kind=kOutput, calls=%fused_computation.75 | convolution fusion | flops 415498240 | bytes 14434304 | tf_op jit(solution)/shard_map/hqk,khe->qhe/dot_general | solution.py:42
  52.9 1.5 %convolution_convert_fusion.1 = bf16[512,1024]{1,0:T(8,128)(2,1)} fusion(bf16[512,256]{0,1:T(8,128)(2,1)S(1)} %bitcast.87, bf16[256,1024]{1,0:T(8,128)(2,1)S(1)} %copy-done), kind=kOutput, calls=%fused_computation.60 | convolution fusion | flops 268959744 | bytes 1835008 | tf_op jit(solution)/shard_map/dot_general | solution.py:107
  54.7 1.3 %copy.19 = bf16[512,1024]{1,0:T(8,128)(2,1)} copy(bf16[512,1024]{0,1:T(8,128)(2,1)S(1)} %bitcast.78) | data formatting | bytes 2097152 | tf_op jit(solution)/shard_map/dot_general | solution.py:115
  56.1 1.4 %collective-permute-done.3 = bf16[512,1024]{1,0:T(8,128)(2,1)} collective-permute-done((bf16[512,1024]{1,0:T(8,128)(2,1)}, bf16[512,1024]{1,0:T(8,128)(2,1)}, u32[]{:S(2)}, u32[]{:S(2)}) %collective-permute-start.3) | collective-permute-done | bytes 1048608 | tf_op jit(solution)/shard_map/ppermute | solution.py:109
  57.4 2.1 %convert_reduce_fusion.1 = (f32[512]{0:T(512)S(1)}, bf16[512,1024]{1,0:T(8,128)(2,1)S(1)}) fusion(bf16[512,1024]{1,0:T(8,128)(2,1)} %collective-permute-done.3, bf16[512,1024]{1,0:T(8,128)(2,1)} %convolution_convert_fusion.1, bf16[512,512]{1,0:T(8,128)(2,1)S(1)} %copy-done.1, bf16[512,512]{1,0:T(8,128)(2,1)S(1)} %collective-permute-done, pred[]{:T(512)S(6)} %eq.139), kind=kLoop, calls=%fused_computation.16 | loop fusion | flops 8912384 | bytes 4196353 | tf_op jit(solution)/shard_map/reduce_sum | solution.py:26
  60.0 0.8 fusion.30
  61.0 4.4 %collective-permute-start.4 = (bf16[15,256]{1,0:T(8,128)(2,1)S(1)}, bf16[15,256]{1,0:T(8,128)(2,1)S(1)}, u32[]{:S(2)}, u32[]{:S(2)}) collective-permute-start(bf16[15,256]{1,0:T(8,128)(2,1)S(1)} %get-tuple-element.20), channel_id=1, source_target_pairs={{0,2},{2,4},{4,6},{6,8},{8,10},{10,12},{12,14},{1,3},{3,5},{5,7},{... | collective-permute-start | bytes 23048 | tf_op jit(solution)/shard_map/ppermute | solution.py:17
  65.4 1.5 %collective-permute-start.5 = (bf16[15,256]{1,0:T(8,128)(2,1)S(1)}, bf16[15,256]{1,0:T(8,128)(2,1)S(1)}, u32[]{:S(2)}, u32[]{:S(2)}) collective-permute-start(bf16[15,256]{1,0:T(8,128)(2,1)S(1)} %get-tuple-element.21), channel_id=1, source_target_pairs={{2,0},{4,2},{6,4},{8,6},{10,8},{12,10},{14,12},{3,1},{5,3},{7,5},{... | collective-permute-start | bytes 23048 | tf_op jit(solution)/shard_map/ppermute | solution.py:20
  67.0 4.0 %collective-permute-done.5 = bf16[15,256]{1,0:T(8,128)(2,1)S(1)} collective-permute-done((bf16[15,256]{1,0:T(8,128)(2,1)S(1)}, bf16[15,256]{1,0:T(8,128)(2,1)S(1)}, u32[]{:S(2)}, u32[]{:S(2)}) %collective-permute-start.5) | collective-permute-done | bytes 7712 | tf_op jit(solution)/shard_map/ppermute | solution.py:20
  70.9 5.3 %fusion.92 = (f32[512]{0:T(512)S(1)}, f32[512]{0:T(512)S(1)}, f32[512,256]{1,0:T(8,128)S(1)}) fusion(f32[256]{0:T(256)S(1)} %bitcast.98, bf16[15,256]{1,0:T(8,128)(2,1)S(1)} %collective-permute-done.5, bf16[512,256]{1,0:T(8,128)(2,1)S(1)} %fusion.52, pred[512]{0:T(512)(128)(4,1)S(1)} %get-tuple-element.82, f32[256]{0:T(256)S(1)} %bitcast.99, ...), kind=kLoop, calls=%fused_computation.198 | loop fusion | flops 28310528 | bytes 853504 | tf_op jit(solution)/shard_map/reduce_sum | solution.py:133
  76.3 2.5 %all-reduce = (f32[512]{0:T(512)S(1)}, f32[512]{0:T(512)S(1)}) all-reduce(f32[512]{0:T(512)S(1)} %get-tuple-element.6, f32[512]{0:T(512)S(1)} %get-tuple-element.5), channel_id=1, replica_groups=mesh['grp'=2,'tm'=8,'head'=2] {'head'}, use_global_device_ids=true, to_apply=%region_17.18 | all-reduce | flops 1024 | bytes 8192 | tf_op jit(solution)/shard_map/psum | solution.py:132
  78.8 1.6 %convolution_convert_fusion = bf16[512,1024]{1,0:T(8,128)(2,1)S(1)} fusion(bf16[256,1024]{1,0:T(8,128)(2,1)} %param.21, f32[512,256]{1,0:T(8,128)S(1)} %get-tuple-element.13, f32[256]{0:T(256)S(1)} %copy-done.10, f32[512]{0:T(512)S(1)} %get-tuple-element.84, f32[512]{0:T(512)S(1)} %get-tuple-element.83), kind=kOutput, calls=%fused_computation.59 | convolution fusion | flops 270008320 | bytes 2102272 | tf_op jit(solution)/shard_map/dot_general | solution.py:139
  80.3 0.8 constant_dynamic-slice_fusion
  81.3 2.0 %collective-permute-done.6 = bf16[512,512]{1,0:T(8,128)(2,1)S(1)} collective-permute-done((bf16[512,512]{1,0:T(8,128)(2,1)}, bf16[512,512]{1,0:T(8,128)(2,1)S(1)}, u32[]{:S(2)}, u32[]{:S(2)}) %collective-permute-start.6) | collective-permute-done | bytes 524320 | tf_op jit(solution)/shard_map/ppermute | solution.py:143
  83.3 1.1 %add_convert_fusion = bf16[512,512]{1,0:T(8,128)(2,1)} fusion(bf16[512,512]{1,0:T(8,128)(2,1)S(1)} %collective-permute-done.6, bf16[512,1024]{1,0:T(8,128)(2,1)S(1)} %convolution_convert_fusion, s32[]{:T(128)S(6)} %select_n.165, bf16[512,1024]{1,0:T(8,128)(2,1)S(1)} %get-tuple-element.17), kind=kLoop, calls=%fused_computation.67 | loop fusion | flops 1572864 | bytes 2097156 | tf_op jit(solution)/shard_map/convert_element_type | solution.py:146
  (60 shorter events, 4.4 us)
Async XLA Ops:
  0.0 52.9 %copy-start = (bf16[256,1024]{1,0:T(8,128)(2,1)S(1)}, bf16[256,1024]{1,0:T(8,128)(2,1)}, u32[]{:S(2)}) copy-start(bf16[256,1024]{1,0:T(8,128)(2,1)} %param.16) | copy-start | bytes 1572868
  0.0 17.3 %copy-start.1 = (bf16[512,512]{1,0:T(8,128)(2,1)S(1)}, bf16[512,512]{1,0:T(8,128)(2,1)}, u32[]{:S(2)}) copy-start(bf16[512,512]{1,0:T(8,128)(2,1)} %param.11) | copy-start | bytes 1572868
  0.0 17.1 %copy-start.6 = (s32[512]{0:T(512)S(1)}, s32[512]{0:T(512)}, u32[]{:S(2)}) copy-start(s32[512]{0:T(512)} %param.12) | copy-start | bytes 6148
  0.0 17.0 %copy-start.7 = (s32[16]{0:T(128)S(1)}, s32[16]{0:T(128)}, u32[]{:S(2)}) copy-start(s32[16]{0:T(128)} %param.13) | copy-start | bytes 196
  0.0 17.3 %collective-permute-start = (bf16[512,512]{1,0:T(8,128)(2,1)}, bf16[512,512]{1,0:T(8,128)(2,1)S(1)}, u32[]{:S(2)}, u32[]{:S(2)}) collective-permute-start(bf16[512,512]{1,0:T(8,128)(2,1)} %param.11), channel_id=1, source_target_pairs={{0,1},{1,0},{2,3},{3,2},{4,5},{5,4},{6,7},{7,6},{8,9},{9,8},{10,11... | collective-permute-start | bytes 1572872 | tf_op jit(solution)/shard_map/ppermute | solution.py:63
  14.4 3.7 %copy-start.8 = (f32[1024]{0:T(1024)S(1)}, f32[1024]{0:T(1024)}, u32[]{:S(2)}) copy-start(f32[1024]{0:T(1024)} %param.14) | copy-start | bytes 12292
  17.0 1.4 %copy-start.2 = (bf16[1024,3,256]{0,2,1:T(8,128)(2,1)S(1)}, bf16[1024,3,256]{0,2,1:T(8,128)(2,1)}, u32[]{:S(2)}) copy-start(bf16[1024,3,256]{0,2,1:T(8,128)(2,1)} %copy.17) | copy-start | bytes 4718596
  19.7 23.5 %collective-permute-start.1 = (bf16[512,512]{0,1:T(8,128)(2,1)S(1)}, bf16[512,512]{0,1:T(8,128)(2,1)S(1)}, u32[]{:S(2)}, u32[]{:S(2)}) collective-permute-start(bf16[512,512]{0,1:T(8,128)(2,1)S(1)} %bitcast.80), channel_id=1, source_target_pairs={{0,2},{2,4},{4,6},{6,8},{8,10},{10,12},{12,14},{1,3},{3,5},{5,7},{... | collective-permute-start | bytes 1572872 | tf_op jit(solution)/shard_map/ppermute | solution.py:17
  23.1 20.1 %collective-permute-start.2 = (bf16[512,512]{0,1:T(8,128)(2,1)S(1)}, bf16[512,512]{0,1:T(8,128)(2,1)S(1)}, u32[]{:S(2)}, u32[]{:S(2)}) collective-permute-start(bf16[512,512]{0,1:T(8,128)(2,1)S(1)} %bitcast.81), channel_id=1, source_target_pairs={{2,0},{4,2},{6,4},{8,6},{10,8},{12,10},{14,12},{3,1},{5,3},{7,5},{... | collective-permute-start | bytes 1572872 | tf_op jit(solution)/shard_map/ppermute | solution.py:20
  52.9 1.5 %copy-start.3 = (bf16[1024,2,256]{2,1,0:T(2,128)(2,1)S(1)}, bf16[1024,2,256]{2,1,0:T(2,128)(2,1)}, u32[]{:S(2)}) copy-start(bf16[1024,2,256]{2,1,0:T(2,128)(2,1)} %param.18) | copy-start | bytes 3145732
  54.4 3.0 %collective-permute-start.3 = (bf16[512,1024]{1,0:T(8,128)(2,1)}, bf16[512,1024]{1,0:T(8,128)(2,1)}, u32[]{:S(2)}, u32[]{:S(2)}) collective-permute-start(bf16[512,1024]{1,0:T(8,128)(2,1)} %convolution_convert_fusion.1), channel_id=1, source_target_pairs={{0,1},{1,0},{2,3},{3,2},{4,5},{5,4},{6,7},{7,6},{8,9},{9,8},{10,11... | collective-permute-start | bytes 3145736 | tf_op jit(solution)/shard_map/ppermute | solution.py:109
  54.4 1.6 %copy-start.5 = (f32[31,256]{1,0:T(8,128)S(1)}, f32[31,256]{1,0:T(8,128)}, u32[]{:S(2)}) copy-start(f32[31,256]{1,0:T(8,128)} %param.19) | copy-start | bytes 95236
  56.0 3.9 %copy-start.4 = (bf16[512,1024]{1,0:T(8,128)(2,1)S(1)}, bf16[512,1024]{1,0:T(8,128)(2,1)}, u32[]{:S(2)}) copy-start(bf16[512,1024]{1,0:T(8,128)(2,1)} %copy.19) | copy-start | bytes 3145732
  56.0 3.9 %copy-start.9 = (f32[1024]{0:T(1024)S(1)}, f32[1024]{0:T(1024)}, u32[]{:S(2)}) copy-start(f32[1024]{0:T(1024)} %param.17) | copy-start | bytes 12292
  60.8 18.0 %copy-start.10 = (f32[256]{0:T(256)S(1)}, f32[256]{0:T(256)}, u32[]{:S(2)}) copy-start(f32[256]{0:T(256)} %param.20) | copy-start | bytes 3076
  61.0 6.0 %collective-permute-start.4 = (bf16[15,256]{1,0:T(8,128)(2,1)S(1)}, bf16[15,256]{1,0:T(8,128)(2,1)S(1)}, u32[]{:S(2)}, u32[]{:S(2)}) collective-permute-start(bf16[15,256]{1,0:T(8,128)(2,1)S(1)} %get-tuple-element.20), channel_id=1, source_target_pairs={{0,2},{2,4},{4,6},{6,8},{8,10},{10,12},{12,14},{1,3},{3,5},{5,7},{... | collective-permute-start | bytes 23048 | tf_op jit(solution)/shard_map/ppermute | solution.py:17
  65.4 5.5 %collective-permute-start.5 = (bf16[15,256]{1,0:T(8,128)(2,1)S(1)}, bf16[15,256]{1,0:T(8,128)(2,1)S(1)}, u32[]{:S(2)}, u32[]{:S(2)}) collective-permute-start(bf16[15,256]{1,0:T(8,128)(2,1)S(1)} %get-tuple-element.21), channel_id=1, source_target_pairs={{2,0},{4,2},{6,4},{8,6},{10,8},{12,10},{14,12},{3,1},{5,3},{7,5},{... | collective-permute-start | bytes 23048 | tf_op jit(solution)/shard_map/ppermute | solution.py:20
  81.2 2.1 %collective-permute-start.6 = (bf16[512,512]{1,0:T(8,128)(2,1)}, bf16[512,512]{1,0:T(8,128)(2,1)S(1)}, u32[]{:S(2)}, u32[]{:S(2)}) collective-permute-start(bf16[512,512]{1,0:T(8,128)(2,1)} %constant_dynamic-slice_fusion), channel_id=1, source_target_pairs={{0,1},{1,0},{2,3},{3,2},{4,5},{5,4},{6,7},{7,6},{8,9},{9,8},{10,11... | collective-permute-start | bytes 1572872 | tf_op jit(solution)/shard_map/ppermute | solution.py:143

commit v2 on v0

v2 whole, which is shorter than its diff:
```python
import functools
import math

import jax
import jax.numpy as jnp
from jax import lax
from jax.experimental import pallas as pl
from jax.experimental.pallas import tpu as pltpu
from jax.sharding import PartitionSpec as P

HEAD_DIM = 64
CONV_CH = 512
KERNEL = 31
WIN = 512
EDGE = 16
NEG = -1e30
EXP_SCALE = HEAD_DIM ** (-0.5) * math.log2(math.e)
F32 = jnp.float32
BF16 = jnp.bfloat16
VMEM_LIMIT = 28 * 1024 * 1024


def dot(a, b):
    return jnp.dot(a, b, preferred_element_type=F32)


def normalize_halves(own, other, gain_own, gain_other):
    width = own.shape[1] + other.shape[1]
    mean = (
        jnp.sum(own, axis=1, keepdims=True) + jnp.sum(other, axis=1, keepdims=True)
    ) / width
    own = own - mean
    other = other - mean
    spread = (
        jnp.sum(own * own, axis=1, keepdims=True) + jnp.sum(other * other, axis=1, keepdims=True)
    ) / width
    scale = lax.rsqrt(spread + 1e-05)
    return (own * scale * gain_own).astype(BF16), (other * scale * gain_other).astype(BF16)


def qkv_kernel(head, own_ref, other_ref, gain_own, gain_other, w_own, w_other, q_ref, kv_ref):
    n_own, n_other = normalize_halves(
        own_ref[...].astype(F32), other_ref[...].astype(F32), gain_own[0], gain_other[0]
    )
    width = q_ref.shape[1]
    for part in range(3):
        value = (dot(n_own, w_own[part, 0]) + dot(n_other, w_other[part, 0])).astype(BF16)
        if part == 0:
            q_ref[...] = value
        else:
            kv_ref[:, (part - 1) * width : part * width] = value


def project(head, frames, other, gain, weight):
    rows, half = frames.shape
    width = weight.shape[2]
    tile = 256
    w = weight.transpose(1, 0, 2).reshape(3, 2, half, width)
    g = gain.reshape(2, 1, half)
    grid_spec = pltpu.PrefetchScalarGridSpec(
        num_scalar_prefetch=1,
        grid=(rows // tile,),
        in_specs=[
            pl.BlockSpec((tile, half), lambda i, s: (i, 0)),
            pl.BlockSpec((tile, half), lambda i, s: (i, 0)),
            pl.BlockSpec((1, 1, half), lambda i, s: (s[0], 0, 0)),
            pl.BlockSpec((1, 1, half), lambda i, s: (1 - s[0], 0, 0)),
            pl.BlockSpec((3, 1, half, width), lambda i, s: (0, s[0], 0, 0)),
            pl.BlockSpec((3, 1, half, width), lambda i, s: (0, 1 - s[0], 0, 0)),
        ],
        out_specs=[
            pl.BlockSpec((tile, width), lambda i, s: (i, 0)),
            pl.BlockSpec((tile, 2 * width), lambda i, s: (i, 0)),
        ],
    )
    return pl.pallas_call(
        qkv_kernel,
        grid_spec=grid_spec,
        out_shape=[
            jax.ShapeDtypeStruct((rows, width), BF16),
            jax.ShapeDtypeStruct((rows, 2 * width), BF16),
        ],
        compiler_params=pltpu.CompilerParams(vmem_limit_bytes=VMEM_LIMIT),
        name="project",
    )(head, frames, other, g, g, w, w)


def attend_kernel(q_ref, own_ref, low_ref, high_ref, lo_ref, hi_ref, out_ref):
    rows, width = q_ref.shape
    tile = rows // 2
    half = WIN // 2
    lane = lax.broadcasted_iota(jnp.int32, (tile, 128), 1)
    for block in range(2):
        at = block * tile
        pieces = (
            ((low_ref, 0, WIN, -WIN), (own_ref, 0, rows, 0), (high_ref, 0, half, rows))
            if block == 0
            else ((low_ref, half, half, -WIN), (own_ref, 0, rows, 0), (high_ref, 0, WIN, rows))
        )
        lo = lo_ref[at : at + tile, :]
        hi = hi_ref[at : at + tile, :]
        biases = []
        for _, first, size, origin in pieces:
            u = lax.broadcasted_iota(jnp.int32, (tile, size), 1) + (origin + first)
            biases.append(jnp.where((u >= lo) & (u < hi), 0.0, NEG))
        for pair in range(width // 128):
            cols = slice(pair * 128, pair * 128 + 128)
            vcols = slice(width + pair * 128, width + pair * 128 + 128)
            q = q_ref[at : at + tile, cols]
            outs = []
            for sub in range(2):
                q_sub = jnp.where((lane >= 64) == (sub == 1), q, jnp.zeros_like(q))
                scores = []
                for (ref, first, size, _), bias in zip(pieces, biases):
                    k = ref[first : first + size, cols]
                    s = lax.dot_general(
                        q_sub, k, (((1,), (1,)), ((), ())), preferred_element_type=F32
                    )
                    scores.append(s + bias)
                peak = functools.reduce(
                    jnp.maximum, [jnp.max(s, axis=1, keepdims=True) for s in scores]
                )
                total = jnp.zeros((tile, 1), F32)
                context = jnp.zeros((tile, 128), F32)
                for (ref, first, size, _), s in zip(pieces, scores):
                    expw = jnp.exp2((s - peak) * EXP_SCALE)
                    total = total + jnp.sum(expw, axis=1, keepdims=True)
                    context = context + dot(
                        expw.astype(BF16), ref[first : first + size, vcols]
                    )
                outs.append(context / jnp.maximum(total, 1.0))
            joined = jnp.where(lane >= 64, outs[1], outs[0])
            out_ref[at : at + tile, cols] = jnp.where(hi > lo, joined, 0.0).astype(BF16)


def attend(q, own, low, high, lo, hi):
    return pl.pallas_call(
        attend_kernel,
        out_shape=jax.ShapeDtypeStruct(q.shape, BF16),
        compiler_params=pltpu.CompilerParams(vmem_limit_bytes=VMEM_LIMIT),
        name="attend",
    )(q, own, low, high, lo, hi)


def gate_kernel(
    head,
    ctx_own, ctx_other,
    x_own, x_other,
    out_own, out_other,
    gain_ref,
    in_own, in_other,
    valid_ref,
    glu_ref, edge_ref, mid_keep, mid_send,
):
    h = head[0]
    half = x_own.shape[1]
    rows = glu_ref.shape[0]
    here = pl.ds(pl.multiple_of(h * (rows - 2 * EDGE), EDGE), rows)
    c_own = ctx_own[here, :]
    c_other = ctx_other[here, :]
    own_cols = pl.ds(pl.multiple_of(h * half, half), half)
    other_cols = pl.ds(pl.multiple_of((1 - h) * half, half), half)

    def mid(cols, x_ref):
        first = dot(c_own, out_own[:, cols]).astype(BF16).astype(F32)
        second = dot(c_other, out_other[:, cols]).astype(BF16).astype(F32)
        return (x_ref[here, :].astype(F32) + (first + second)).astype(BF16)

    m_own = mid(own_cols, x_own)
    m_other = mid(other_cols, x_other)
    keep = rows - EDGE

    @pl.when(h == 0)
    def _():
        mid_keep[...] = m_own[:keep]
        mid_send[...] = m_other[:keep]

    @pl.when(h == 1)
    def _():
        mid_keep[...] = m_own[EDGE:]
        mid_send[...] = m_other[EDGE:]

    n_own, n_other = normalize_halves(
        m_own.astype(F32), m_other.astype(F32), gain_ref[h], gain_ref[1 - h]
    )
    valid = valid_ref[here, :] > 0
    glus = []
    for w_ref in (in_own, in_other):
        value = dot(n_own, w_ref[0, own_cols, :]) + dot(n_other, w_ref[0, other_cols, :])
        gate = dot(n_own, w_ref[1, own_cols, :]) + dot(n_other, w_ref[1, other_cols, :])
        glu = value / (1.0 + jnp.exp(-gate))
        glus.append(jnp.where(valid, glu, 0.0).astype(BF16))
    chan = glus[0].shape[1]
    glu_ref[:, :chan] = glus[0]
    glu_ref[:, chan:] = glus[1]

    @pl.when(h == 0)
    def _():
        edge_ref[:, :chan] = glus[1][:EDGE]
        edge_ref[:, chan:] = glus[0][:EDGE]

    @pl.when(h == 1)
    def _():
        edge_ref[:, :chan] = glus[1][rows - EDGE :]
        edge_ref[:, chan:] = glus[0][rows - EDGE :]


def gated(head, ctx_own, ctx_other, x_own, x_other, out_own, out_other, gain, in_own, in_other, valid):
    rows = x_own.shape[0] // 2 + EDGE
    half = x_own.shape[1]
    chan = in_own.shape[2]
    vmem = pl.BlockSpec(memory_space=pltpu.VMEM)
    return pl.pallas_call(
        gate_kernel,
        in_specs=[pl.BlockSpec(memory_space=pltpu.SMEM)] + [vmem] * 10,
        out_specs=[vmem] * 4,
        out_shape=[
            jax.ShapeDtypeStruct((rows, 2 * chan), BF16),
            jax.ShapeDtypeStruct((EDGE, 2 * chan), BF16),
            jax.ShapeDtypeStruct((rows - EDGE, half), BF16),
            jax.ShapeDtypeStruct((rows - EDGE, half), BF16),
        ],
        compiler_params=pltpu.CompilerParams(vmem_limit_bytes=VMEM_LIMIT),
        name="gated",
    )(head, ctx_own, ctx_other, x_own, x_other, out_own, out_other,
      gain.reshape(2, 1, half), in_own, in_other, valid)


def conv_kernel(head, glu_ref, edge_ref, lo_ref, hi_ref, dw_own, dw_other, g_own, g_other,
                act_ref, ext):
    h = head[0]
    rows, width = act_ref.shape
    chan = width // 2
    got = glu_ref.shape[0]
    ext[pl.ds(pl.multiple_of((1 - h) * EDGE, EDGE), got), :] = glu_ref[...].astype(F32)
    ext[pl.ds(pl.multiple_of(h * got, EDGE), EDGE), :] = edge_ref[...].astype(F32)
    first = pl.multiple_of(h * rows, rows)
    at = lax.broadcasted_iota(jnp.int32, (rows, 1), 0) + first
    low = lo_ref[pl.ds(first, rows), :] - at
    high = hi_ref[pl.ds(first, rows), :] - at
    reach = KERNEL // 2
    step = 64
    for base in range(0, rows, step):
        low_b = jnp.broadcast_to(low[base : base + step], (step, 128))
        high_b = jnp.broadcast_to(high[base : base + step], (step, 128))
        sums = jnp.zeros((step, 128), F32)
        squares = jnp.zeros((step, 128), F32)
        results = []
        for col in range(0, width, 128):
            dw_ref, c = (dw_own, col) if col < chan else (dw_other, col - chan)
            total = jnp.zeros((step, 128), F32)
            for tap in range(KERNEL):
                shift = tap - reach
                row = base + EDGE + shift
                piece = ext[row : row + step, col : col + 128]
                same = (low_b <= shift) & (high_b > shift)
                total = total + jnp.where(same, piece, 0.0) * dw_ref[tap : tap + 1, c : c + 128]
            sums = sums + total
            squares = squares + total * total
            results.append(total)
        mean = jnp.sum(sums, axis=1, keepdims=True) / CONV_CH
        square = jnp.sum(squares, axis=1, keepdims=True) / CONV_CH
        scale = lax.rsqrt(square - mean * mean + 1e-05)
        for col, total in zip(range(0, width, 128), results):
            g_ref, c = (g_own, col) if col < chan else (g_other, col - chan)
            y = (total - mean) * scale * g_ref[:, c : c + 128]
            act_ref[base : base + step, col : col + 128] = (y / (1.0 + jnp.exp(-y))).astype(BF16)


def convolve(head, glu, edge, lo, hi, dw_own, dw_other, g_own, g_other):
    rows = glu.shape[0] - EDGE
    width = glu.shape[1]
    vmem = pl.BlockSpec(memory_space=pltpu.VMEM)
    return pl.pallas_call(
        conv_kernel,
        in_specs=[pl.BlockSpec(memory_space=pltpu.SMEM)] + [vmem] * 8,
        out_specs=vmem,
        out_shape=jax.ShapeDtypeStruct((rows, width), BF16),
        scratch_shapes=[pltpu.VMEM((rows + 2 * EDGE, width), F32)],
        compiler_params=pltpu.CompilerParams(vmem_limit_bytes=VMEM_LIMIT),
        name="convolve",
    )(head, glu, edge, lo, hi, dw_own, dw_other, g_own.reshape(1, -1), g_other.reshape(1, -1))


def finish_kernel(head, act_own, act_other, mid_own, mid_other, w_own, w_other, out_ref):
    h = head[0]
    rows, chan2 = act_own.shape
    chan = chan2 // 2
    half = out_ref.shape[1]
    cols = pl.ds(pl.multiple_of(h * half, half), half)
    w_a = w_own[:, cols]
    w_b = w_other[:, cols]

    def rows_of(act, mid, flip):
        first = dot(act[:, :chan], w_b if flip else w_a).astype(BF16).astype(F32)
        second = dot(act[:, chan:], w_a if flip else w_b).astype(BF16).astype(F32)
        return (mid[...].astype(F32) + (first + second)).astype(BF16)

    out_ref[pl.ds(pl.multiple_of(h * rows, rows), rows), :] = rows_of(act_own, mid_own, False)
    out_ref[pl.ds(pl.multiple_of((1 - h) * rows, rows), rows), :] = rows_of(
        act_other, mid_other, True
    )


def finish(head, act_own, act_other, mid_own, mid_other, w_own, w_other):
    rows, half = mid_own.shape
    vmem = pl.BlockSpec(memory_space=pltpu.VMEM)
    return pl.pallas_call(
        finish_kernel,
        in_specs=[pl.BlockSpec(memory_space=pltpu.SMEM)] + [vmem] * 6,
        out_specs=vmem,
        out_shape=jax.ShapeDtypeStruct((2 * rows, half), BF16),
        compiler_params=pltpu.CompilerParams(vmem_limit_bytes=VMEM_LIMIT),
        name="finish",
    )(head, act_own, act_other, mid_own, mid_other, w_own, w_other)


def local(
    blocks,
    frames,
    segment_ids,
    utt_valid,
    attn_gain,
    qkv_weight,
    out_weight,
    conv_gain,
    pointwise_in,
    depthwise,
    mid_gain,
    pointwise_out,
):
    rows = frames.shape[0]

    def swap(value):
        return lax.ppermute(value, "head", [(0, 1), (1, 0)])

    head = lax.axis_index("head").astype(jnp.int32).reshape(1)
    block = lax.axis_index("tm")
    other = swap(frames)
    q, kv = project(head, frames, other, attn_gain, qkv_weight)
    low = lax.ppermute(kv, "tm", [(i, i + 1) for i in range(blocks - 1)])
    high = lax.ppermute(kv, "tm", [(i + 1, i) for i in range(blocks - 1)])

    pointwise = pointwise_in.transpose(1, 0, 2)
    mine, segment_ids = lax.optimization_barrier(
        ((out_weight, pointwise, depthwise, mid_gain, pointwise_out, kv), segment_ids)
    )
    out_weight, pointwise, depthwise, mid_gain, pointwise_out, _ = mine
    out_other = swap(out_weight)
    pointwise_other = swap(pointwise)
    depthwise_other = swap(depthwise)
    mid_gain_other = swap(mid_gain)
    pointwise_out_other = swap(pointwise_out)

    ids = jnp.arange(utt_valid.shape[0], dtype=jnp.int32)
    onehot = segment_ids[:, None] == ids[None, :]
    counts = lax.psum(jnp.sum(onehot.astype(jnp.int32), axis=0), "tm")
    starts = jnp.cumsum(counts) - counts
    stops = starts + jnp.minimum(counts, utt_valid)
    origin = block * rows
    position = jnp.arange(rows, dtype=jnp.int32)
    lo = jnp.sum(jnp.where(onehot, starts[None, :] - origin, 0), axis=1)
    hi = jnp.sum(jnp.where(onehot, stops[None, :] - origin, 0), axis=1)
    valid = position < hi
    lo = jnp.where(valid, lo, 0)
    hi = jnp.where(valid, hi, 0)
    near_lo = jnp.where(valid, jnp.maximum(lo, position - WIN), 0)
    near_hi = jnp.where(valid, jnp.minimum(hi, position + (WIN + 1)), 0)

    context = attend(q, kv, low, high, near_lo[:, None], near_hi[:, None])
    context_other = swap(context)
    glu, edge, mid_keep, mid_send = gated(
        head, context, context_other, frames, other, out_weight, out_other, conv_gain,
        pointwise, pointwise_other, valid.astype(jnp.int32)[:, None],
    )
    edges = [(2 * i, 2 * (i - 1) + 1) for i in range(1, blocks)]
    edges += [(2 * i + 1, 2 * (i + 1)) for i in range(blocks - 1)]
    edge = lax.ppermute(edge, ("tm", "head"), edges)
    mid_other = swap(mid_send)
    act = convolve(
        head, glu, edge, lo[:, None], hi[:, None], depthwise, depthwise_other, mid_gain,
        mid_gain_other,
    )
    act_other = swap(act)
    return finish(
        head, act, act_other, mid_keep, mid_other, pointwise_out, pointwise_out_other
    )


def solution(mesh):
    in_specs = (
        P(("grp", "tm"), "head"),
        P(("grp", "tm")),
        P("grp"),
        P(),
        P(None, None, "head"),
        P("head", None),
        P(),
        P(None, None, "head"),
        P(None, "head"),
        P("head"),
        P("head", None),
    )
    out_specs = P(("grp", "tm"), "head")
    return jax.shard_map(
        functools.partial(local, mesh.shape["tm"]),
        mesh=mesh,
        in_specs=in_specs,
        out_specs=out_specs,
        check_vma=False,
    )
```

time: 126 us -> 71.4 us (0.57)
  waiting for transfers between devices: 51.1 us -> 3.21 us
  Pallas kernels: 0 us -> 16.9 us
  other arithmetic: 19.2 us -> 2.54 us
  blocking collectives: 15.5 us -> 30.8 us
  between operations: 13.4 us -> 0.2 us
  matrix products: 11.3 us -> 0 us
  starting transfers between devices: 9.93 us -> 12.3 us
    ppermute x4 -> x12, waiting for transfers between devices: 22 us -> 3.21 us  [the longest x9 3.2 us: swap(): return lax.ppermute(value, 'head', [(0, 1), (1, 0)])]
    psum x1 -> x0, waiting for transfers between devices: 18.8 us -> none  [local(): lax.psum(partial_attn.astype(jnp.bfloat16), 'head').astype(jnp.float32)]
    pallas_call x0 -> x5, Pallas kernels: none -> 16.9 us  [the longest x1 5.99 us: attend(): pl.pallas_call(attend_kernel, out_shape=jax.ShapeDtypeStruct(q.shape, BF1...]
    reduce_sum x10 -> x2, other arithmetic: 15.8 us -> 0.21 us  [the longest x1 0.12 us: local(): counts = lax.psum(jnp.sum(onehot.astype(jnp.int32), axis=0), 'tm')]
    psum x2 -> x1, blocking collectives: 15.5 us -> 30.8 us  [local(): counts = lax.psum(jnp.sum(onehot.astype(jnp.int32), axis=0), 'tm')]
    dot_general x6 -> x0, matrix products: 11.3 us -> none  [the longest x1 2.92 us: attend(): jnp.einsum('hqk,khe->qhe', weights, values, preferred_element_type=jnp.fl...]
    reduce_scatter x1 -> x0, waiting for transfers between devices: 9.6 us -> none  [local(): lax.psum_scatter(partial_conv.astype(jnp.bfloat16), 'head', scatter_dimen...]
    ppermute x4 -> x12, starting transfers between devices: 9.84 us -> 12.3 us  [the longest x9 5.35 us: swap(): return lax.ppermute(value, 'head', [(0, 1), (1, 0)])]
  transfers between devices with their start and end apart: 7 -> 12, of which waited for: 4 -> 4; matrix products, arithmetic and copies ran while one was open for 5% -> 8% of each run, Pallas kernels for 0% -> 17%
where the time goes in v2:
time: 71.4 us; the launch traced here: 71.1 us
  blocking collectives  30.8 us (43%)
  Pallas kernels  16.9 us (24%)
  starting transfers between devices  12.3 us (17%)
  local copies, waits for them, and re-layouts  5.09 us (7%)
  waiting for transfers between devices  3.21 us (4%)
  other arithmetic  2.54 us (4%)
    psum x1, blocking collectives, local(): counts = lax.psum(jnp.sum(onehot.astype(jnp.int32), axis=0), 'tm')  30.8 us
    pallas_call x1, Pallas kernels, attend(): pl.pallas_call(attend_kernel, out_shape=jax.ShapeDtypeStruct(q.shape, BF1...  5.99 us
    ppermute x9, starting transfers between devices, swap(): return lax.ppermute(value, 'head', [(0, 1), (1, 0)])  5.35 us
    ppermute x1, starting transfers between devices, local(): low = lax.ppermute(kv, 'tm', [(i, i + 1) for i in range(blocks - 1)])  4.79 us
    pallas_call x1, Pallas kernels, convolve(): pl.pallas_call(conv_kernel, in_specs=[pl.BlockSpec(memory_space=pltpu.SME...  3.45 us
    pallas_call x1, Pallas kernels, project(): pl.pallas_call(qkv_kernel, grid_spec=grid_spec, out_shape=[jax.ShapeDtype...  3.34 us
    unnamed x25, local copies, waits for them, and re-layouts  3.26 us
    ppermute x9, waiting for transfers between devices, swap(): return lax.ppermute(value, 'head', [(0, 1), (1, 0)])  3.2 us
  transfers between devices with their start and end apart: 12, of which 4 were waited for; matrix products, arithmetic and copies ran while one was open for 8% of the time, Pallas kernels for 17%

profile of v2, /device:TPU:0, one launch (start us, length us, event | category | flops | bytes accessed | tf_op | source)
XLA Modules:
  0.0 71.1 jit_solution(9848215979645058943)
XLA Ops:
  0.0 0.5 collective-permute-start
  0.5 1.5 %copy.25 = bf16[1024,2,256]{2,0,1:T(8,128)(2,1)S(1)} copy(bf16[1024,2,256]{2,1,0:T(2,128)(2,1)} %param.18) | data formatting | bytes 2097152 | tf_op args[7]
  2.4 3.3 %project.1 = (bf16[512,256]{1,0:T(8,128)(2,1)S(1)}, bf16[512,512]{1,0:T(8,128)(2,1)}) custom-call(s32[1]{0:T(128)} %bitcast.head, bf16[512,512]{1,0:T(8,128)(2,1)S(1)} %copy-done.1, bf16[512,512]{1,0:T(8,128)(2,1)} %collective-permute-done.other_ref.x_other, f32[2,1,512]{2,1,0:T(1,128)S(1)} %bitcast.18, f32[2,1,512]{2,1,0:T(1,128)S(1)} %bitcast.19, ...), custom_call_target="tpu_custom_call" | custom-call | tf_op jit(solution)/shard_map/project/pallas_call | solution.py:76
  5.8 0.7 copy-done.4
  6.5 4.8 %collective-permute-start.1 = (bf16[512,512]{1,0:T(8,128)(2,1)}, bf16[512,512]{1,0:T(8,128)(2,1)S(1)}, u32[]{:S(2)}, u32[]{:S(2)}) collective-permute-start(bf16[512,512]{1,0:T(8,128)(2,1)} %get-tuple-element.18.own_ref), channel_id=1, source_target_pairs={{0,2},{2,4},{4,6},{6,8},{8,10},{10,12},{12,14},{1,3},{3,5},{5,7},{... | collective-permute-start | bytes 1572872 | tf_op jit(solution)/shard_map/ppermute | solution.py:341
  11.4 1.3 %collective-permute-start.2 = (bf16[512,512]{1,0:T(8,128)(2,1)}, bf16[512,512]{1,0:T(8,128)(2,1)}, u32[]{:S(2)}, u32[]{:S(2)}) collective-permute-start(bf16[512,512]{1,0:T(8,128)(2,1)} %get-tuple-element.18.own_ref), channel_id=1, source_target_pairs={{2,0},{4,2},{6,4},{8,6},{10,8},{12,10},{14,12},{3,1},{5,3},{7,5},{... | collective-permute-start | bytes 1572872 | tf_op jit(solution)/shard_map/ppermute | solution.py:342
  12.7 30.8 %psum.7 = s32[16]{0:T(128)S(1)} all-reduce(s32[16]{0:T(128)S(1)} %convert_reduce_fusion), channel_id=1, replica_groups=mesh['grp'=2,'tm'=8,'head'=2] {'tm'}, use_global_device_ids=true, to_apply=%region_1.0 | all-reduce | flops 16 | bytes 128 | tf_op jit(solution)/shard_map/psum | solution.py:357
  44.0 0.9 %copy.21 = s32[512,1]{1,0:T(8,128)} copy(s32[512,1]{0,1:T(1,128)S(1)} %bitcast.24) | data formatting | bytes 4096 | tf_op jit(solution)/shard_map/reduce_sum | solution.py:363
  44.9 0.5 collective-permute-start.4
  45.4 1.0 %broadcast_select_fusion = (s32[512,1]{1,0:T(8,128)S(1)}, pred[512,1]{1,0:T(8,128)(4,1)S(1)}) fusion(s32[512,1]{1,0:T(8,128)} %copy.21), kind=kLoop, calls=%fused_computation.4 | loop fusion | flops 1024 | bytes 4608 | tf_op jit(solution)/shard_map/jit(_where)/select_n | solution.py:366
  46.4 0.8 %copy.22 = s32[512,1]{1,0:T(8,128)} copy(s32[512,1]{0,1:T(1,128)S(1)} %bitcast.23) | data formatting | bytes 4096 | tf_op jit(solution)/shard_map/reduce_sum | solution.py:362
  47.2 1.1 %broadcast_select_fusion.1 = (s32[512,1]{1,0:T(8,128)S(1)}, s32[512,1]{1,0:T(8,128)S(1)}, s32[512,1]{1,0:T(8,128)S(1)}) fusion(pred[512,1]{1,0:T(8,128)(4,1)S(1)} %get-tuple-element.32, s32[512,1]{1,0:T(8,128)} %copy.22, s32[512,1]{1,0:T(8,128)} %copy.21), kind=kLoop, calls=%fused_computation.5 | loop fusion | flops 4096 | bytes 10752 | tf_op jit(solution)/shard_map/jit(_where)/select_n | solution.py:365
  48.4 1.0 %copy-done.5 = bf16[512,256]{1,0:T(8,128)(2,1)S(1)} copy-done((bf16[512,256]{1,0:T(8,128)(2,1)S(1)}, bf16[512,256]{1,0:T(8,128)(2,1)}, u32[]{:S(2)}) %copy-start.5) | copy-done | bytes 262168
  49.4 6.0 %attend.1.ctx_own = bf16[512,256]{1,0:T(8,128)(2,1)S(1)} custom-call(bf16[512,256]{1,0:T(8,128)(2,1)S(1)} %copy-done.5, bf16[512,512]{1,0:T(8,128)(2,1)} %get-tuple-element.18.own_ref, bf16[512,512]{1,0:T(8,128)(2,1)S(1)} %collective-permute-done.1.low_ref, bf16[512,512]{1,0:T(8,128)(2,1)} %collective-permute-done.2.high_ref, ...), custom_call_target="tpu_custom_call" | custom-call | tf_op jit(solution)/shard_map/attend/pallas_call | solution.py:137
  55.5 0.5 collective-permute-start.11
  56.1 0.9 %collective-permute-done.3.ctx_other = bf16[512,256]{1,0:T(8,128)(2,1)S(1)} collective-permute-done((bf16[512,256]{1,0:T(8,128)(2,1)S(1)}, bf16[512,256]{1,0:T(8,128)(2,1)S(1)}, u32[]{:S(2)}, u32[]{:S(2)}) %collective-permute-start.3) | collective-permute-done | bytes 262176 | tf_op jit(solution)/shard_map/ppermute | solution.py:335
  57.1 2.9 %gated.1 = (bf16[272,512]{1,0:T(8,128)(2,1)S(1)}, bf16[16,512]{1,0:T(8,128)(2,1)S(1)}, bf16[256,512]{1,0:T(8,128)(2,1)S(1)}, bf16[256,512]{1,0:T(8,128)(2,1)S(1)}) custom-call(s32[1]{0:T(128)} %bitcast.head, bf16[512,256]{1,0:T(8,128)(2,1)S(1)} %attend.1.ctx_own, bf16[512,256]{1,0:T(8,128)(2,1)S(1)} %collective-permute-done.3.ctx_other, ...), custom_call_target="tpu_custom_call" | custom-call | tf_op jit(solution)/shard_map/gated/pallas_call | solution.py:213
  59.9 0.8 %collective-permute-start.6 = (bf16[16,512]{1,0:T(8,128)(2,1)S(1)}, bf16[16,512]{1,0:T(8,128)(2,1)S(1)}, u32[]{:S(2)}, u32[]{:S(2)}) collective-permute-start(bf16[16,512]{1,0:T(8,128)(2,1)S(1)} %get-tuple-element.23), channel_id=1, source_target_pairs={{2,1},{4,3},{6,5},{8,7},{10,9},{12,11},{14,13},{1,2},{3,4},{5,6},{... | collective-permute-start | bytes 49160 | tf_op jit(solution)/shard_map/ppermute | solution.py:378
  60.8 1.4 %collective-permute-start.8 = (f32[256]{0:T(256)S(1)}, f32[256]{0:T(256)S(1)}, u32[]{:S(2)}, u32[]{:S(2)}) collective-permute-start(f32[256]{0:T(256)S(1)} %copy-done.9), channel_id=1, source_target_pairs={{0,1},{1,0},{2,3},{3,2},{4,5},{5,4},{6,7},{7,6},{8,9},{9,8},{10,11... | collective-permute-start | bytes 3080 | tf_op jit(solution)/shard_map/ppermute | solution.py:335
  62.3 0.7 %collective-permute-done.8 = f32[256]{0:T(256)S(1)} collective-permute-done((f32[256]{0:T(256)S(1)}, f32[256]{0:T(256)S(1)}, u32[]{:S(2)}, u32[]{:S(2)}) %collective-permute-start.8) | collective-permute-done | bytes 1056 | tf_op jit(solution)/shard_map/ppermute | solution.py:335
  63.1 3.5 %convolve.1.act_own = bf16[256,512]{1,0:T(8,128)(2,1)S(1)} custom-call(s32[1]{0:T(128)} %bitcast.head, bf16[272,512]{1,0:T(8,128)(2,1)S(1)} %get-tuple-element.22.glu_ref, bf16[16,512]{1,0:T(8,128)(2,1)S(1)} %collective-permute-done.6.edge_ref, s32[512,1]{1,0:T(8,128)S(1)} %get-tuple-element.33.lo_ref, s32[512,1]{1,0:T(8,128)S(1)} %get-tuple-element.31.hi_ref, ...), custom_call_target="tpu_custom_call" | custom-call | tf_op jit(solution)/shard_map/convolve/pallas_call | solution.py:274
  66.5 2.1 %collective-permute-start.9 = (bf16[256,512]{1,0:T(8,128)(2,1)S(1)}, bf16[256,512]{1,0:T(8,128)(2,1)S(1)}, u32[]{:S(2)}, u32[]{:S(2)}) collective-permute-start(bf16[256,512]{1,0:T(8,128)(2,1)S(1)} %convolve.1.act_own), channel_id=1, source_target_pairs={{0,1},{1,0},{2,3},{3,2},{4,5},{5,4},{6,7},{7,6},{8,9},{9,8},{10,11... | collective-permute-start | bytes 786440 | tf_op jit(solution)/shard_map/ppermute | solution.py:335
  68.6 1.2 %collective-permute-done.9.act_other = bf16[256,512]{1,0:T(8,128)(2,1)S(1)} collective-permute-done((bf16[256,512]{1,0:T(8,128)(2,1)S(1)}, bf16[256,512]{1,0:T(8,128)(2,1)S(1)}, u32[]{:S(2)}, u32[]{:S(2)}) %collective-permute-start.9) | collective-permute-done | bytes 262176 | tf_op jit(solution)/shard_map/ppermute | solution.py:335
  69.8 1.3 %finish.1 = bf16[512,512]{1,0:T(8,128)(2,1)} custom-call(s32[1]{0:T(128)} %bitcast.head, bf16[256,512]{1,0:T(8,128)(2,1)S(1)} %convolve.1.act_own, bf16[256,512]{1,0:T(8,128)(2,1)S(1)} %collective-permute-done.9.act_other, bf16[256,512]{1,0:T(8,128)(2,1)S(1)} %get-tuple-element.26.mid_own, bf16[256,512]{1,0:T(8,128)(2,1)S(1)} %collective-permute-done.10.mid_other, ...), custom_call_target="tpu_custom_call" | custom-call | tf_op jit(solution)/shard_map/finish/pallas_call | solution.py:308
  (42 shorter events, 1.3 us)
Async XLA Ops:
  0.0 2.4 %copy-start.1 = (bf16[512,512]{1,0:T(8,128)(2,1)S(1)}, bf16[512,512]{1,0:T(8,128)(2,1)}, u32[]{:S(2)}) copy-start(bf16[512,512]{1,0:T(8,128)(2,1)} %x_own.1) | copy-start | bytes 1572868
  0.0 2.4 %copy-start.7 = (f32[1024]{0:T(1024)S(1)}, f32[1024]{0:T(1024)}, u32[]{:S(2)}) copy-start(f32[1024]{0:T(1024)} %param.14) | copy-start | bytes 12292
  0.0 2.4 %copy-start = (bf16[1024,3,256]{2,0,1:T(8,128)(2,1)S(1)}, bf16[1024,3,256]{2,0,1:T(8,128)(2,1)}, u32[]{:S(2)}) copy-start(bf16[1024,3,256]{2,0,1:T(8,128)(2,1)} %param.15) | copy-start | bytes 4718596
  0.0 2.4 %collective-permute-start = (bf16[512,512]{1,0:T(8,128)(2,1)}, bf16[512,512]{1,0:T(8,128)(2,1)}, u32[]{:S(2)}, u32[]{:S(2)}) collective-permute-start(bf16[512,512]{1,0:T(8,128)(2,1)} %x_own.1), channel_id=1, source_target_pairs={{0,1},{1,0},{2,3},{3,2},{4,5},{5,4},{6,7},{7,6},{8,9},{9,8},{10,11... | collective-permute-start | bytes 1572872 | tf_op jit(solution)/shard_map/ppermute | solution.py:335
  2.4 8.9 %copy-start.10 = (s32[512]{0:T(512)S(1)}, s32[512]{0:T(512)}, u32[]{:S(2)}) copy-start(s32[512]{0:T(512)} %param.12) | copy-start | bytes 6148
  2.4 41.4 %copy-start.11 = (s32[16]{0:T(128)S(1)}, s32[16]{0:T(128)}, u32[]{:S(2)}) copy-start(s32[16]{0:T(128)} %param.13) | copy-start | bytes 196
  5.8 0.7 %copy-start.4 = (bf16[512,256]{1,0:T(8,128)(2,1)}, bf16[512,256]{1,0:T(8,128)(2,1)S(1)}, u32[]{:S(2)}) copy-start(bf16[512,256]{1,0:T(8,128)(2,1)S(1)} %get-tuple-element.17.q_ref) | copy-start | bytes 786436
  6.5 41.9 %collective-permute-start.1 = (bf16[512,512]{1,0:T(8,128)(2,1)}, bf16[512,512]{1,0:T(8,128)(2,1)S(1)}, u32[]{:S(2)}, u32[]{:S(2)}) collective-permute-start(bf16[512,512]{1,0:T(8,128)(2,1)} %get-tuple-element.18.own_ref), channel_id=1, source_target_pairs={{0,2},{2,4},{4,6},{6,8},{8,10},{10,12},{12,14},{1,3},{3,5},{5,7},{... | collective-permute-start | bytes 1572872 | tf_op jit(solution)/shard_map/ppermute | solution.py:341
  11.4 37.0 %collective-permute-start.2 = (bf16[512,512]{1,0:T(8,128)(2,1)}, bf16[512,512]{1,0:T(8,128)(2,1)}, u32[]{:S(2)}, u32[]{:S(2)}) collective-permute-start(bf16[512,512]{1,0:T(8,128)(2,1)} %get-tuple-element.18.own_ref), channel_id=1, source_target_pairs={{2,0},{4,2},{6,4},{8,6},{10,8},{12,10},{14,12},{3,1},{5,3},{7,5},{... | collective-permute-start | bytes 1572872 | tf_op jit(solution)/shard_map/ppermute | solution.py:342
  43.8 13.3 %collective-permute-start.5 = (bf16[2,1024,256]{2,1,0:T(8,128)(2,1)S(1)}, bf16[2,1024,256]{2,1,0:T(8,128)(2,1)S(1)}, u32[]{:S(2)}, u32[]{:S(2)}) collective-permute-start(bf16[2,1024,256]{2,1,0:T(8,128)(2,1)S(1)} %bitcast.16), channel_id=1, source_target_pairs={{0,1},{1,0},{2,3},{3,2},{4,5},{5,4},{6,7},{7,6},{8,9},{9,8},{10,11... | collective-permute-start | bytes 3145736 | tf_op jit(solution)/shard_map/ppermute | solution.py:335
  44.9 11.3 %collective-permute-start.4 = (bf16[256,1024]{1,0:T(8,128)(2,1)}, bf16[256,1024]{1,0:T(8,128)(2,1)}, u32[]{:S(2)}, u32[]{:S(2)}) collective-permute-start(bf16[256,1024]{1,0:T(8,128)(2,1)} %out_own), channel_id=1, source_target_pairs={{0,1},{1,0},{2,3},{3,2},{4,5},{5,4},{6,7},{7,6},{8,9},{9,8},{10,11... | collective-permute-start | bytes 1572872 | tf_op jit(solution)/shard_map/ppermute | solution.py:335
  47.2 8.8 %copy-start.6 = (f32[31,256]{1,0:T(8,128)S(1)}, f32[31,256]{1,0:T(8,128)}, u32[]{:S(2)}) copy-start(f32[31,256]{1,0:T(8,128)} %dw_own) | copy-start | bytes 95236
  47.2 9.8 %copy-start.8 = (f32[1024]{0:T(1024)S(1)}, f32[1024]{0:T(1024)}, u32[]{:S(2)}) copy-start(f32[1024]{0:T(1024)} %param.17) | copy-start | bytes 12292
  48.4 7.2 %copy-start.3 = (bf16[256,1024]{1,0:T(8,128)(2,1)S(1)}, bf16[256,1024]{1,0:T(8,128)(2,1)}, u32[]{:S(2)}) copy-start(bf16[256,1024]{1,0:T(8,128)(2,1)} %w_own) | copy-start | bytes 1572868
  48.4 8.7 %copy-start.2 = (bf16[256,1024]{1,0:T(8,128)(2,1)S(1)}, bf16[256,1024]{1,0:T(8,128)(2,1)}, u32[]{:S(2)}) copy-start(bf16[256,1024]{1,0:T(8,128)(2,1)} %out_own) | copy-start | bytes 1572868
  48.4 1.0 %copy-start.5 = (bf16[512,256]{1,0:T(8,128)(2,1)S(1)}, bf16[512,256]{1,0:T(8,128)(2,1)}, u32[]{:S(2)}) copy-start(bf16[512,256]{1,0:T(8,128)(2,1)} %copy-done.4) | copy-start | bytes 786436
  55.4 1.6 %collective-permute-start.3 = (bf16[512,256]{1,0:T(8,128)(2,1)S(1)}, bf16[512,256]{1,0:T(8,128)(2,1)S(1)}, u32[]{:S(2)}, u32[]{:S(2)}) collective-permute-start(bf16[512,256]{1,0:T(8,128)(2,1)S(1)} %attend.1.ctx_own), channel_id=1, source_target_pairs={{0,1},{1,0},{2,3},{3,2},{4,5},{5,4},{6,7},{7,6},{8,9},{9,8},{10,11... | collective-permute-start | bytes 786440 | tf_op jit(solution)/shard_map/ppermute | solution.py:335
  55.5 13.1 %collective-permute-start.11 = (bf16[256,1024]{1,0:T(8,128)(2,1)S(1)}, bf16[256,1024]{1,0:T(8,128)(2,1)S(1)}, u32[]{:S(2)}, u32[]{:S(2)}) collective-permute-start(bf16[256,1024]{1,0:T(8,128)(2,1)S(1)} %copy-done.3), channel_id=1, source_target_pairs={{0,1},{1,0},{2,3},{3,2},{4,5},{5,4},{6,7},{7,6},{8,9},{9,8},{10,11... | collective-permute-start | bytes 1572872 | tf_op jit(solution)/shard_map/ppermute | solution.py:335
  56.0 7.0 %collective-permute-start.7 = (f32[31,256]{1,0:T(8,128)S(1)}, f32[31,256]{1,0:T(8,128)S(1)}, u32[]{:S(2)}, u32[]{:S(2)}) collective-permute-start(f32[31,256]{1,0:T(8,128)S(1)} %copy-done.6), channel_id=1, source_target_pairs={{0,1},{1,0},{2,3},{3,2},{4,5},{5,4},{6,7},{7,6},{8,9},{9,8},{10,11... | collective-permute-start | bytes 95240 | tf_op jit(solution)/shard_map/ppermute | solution.py:335
  57.1 3.7 %copy-start.9 = (f32[256]{0:T(256)S(1)}, f32[256]{0:T(256)}, u32[]{:S(2)}) copy-start(f32[256]{0:T(256)} %param.20) | copy-start | bytes 3076
  59.9 3.1 %collective-permute-start.6 = (bf16[16,512]{1,0:T(8,128)(2,1)S(1)}, bf16[16,512]{1,0:T(8,128)(2,1)S(1)}, u32[]{:S(2)}, u32[]{:S(2)}) collective-permute-start(bf16[16,512]{1,0:T(8,128)(2,1)S(1)} %get-tuple-element.23), channel_id=1, source_target_pairs={{2,1},{4,3},{6,5},{8,7},{10,9},{12,11},{14,13},{1,2},{3,4},{5,6},{... | collective-permute-start | bytes 49160 | tf_op jit(solution)/shard_map/ppermute | solution.py:378
  60.8 2.3 %collective-permute-start.8 = (f32[256]{0:T(256)S(1)}, f32[256]{0:T(256)S(1)}, u32[]{:S(2)}, u32[]{:S(2)}) collective-permute-start(f32[256]{0:T(256)S(1)} %copy-done.9), channel_id=1, source_target_pairs={{0,1},{1,0},{2,3},{3,2},{4,5},{5,4},{6,7},{7,6},{8,9},{9,8},{10,11... | collective-permute-start | bytes 3080 | tf_op jit(solution)/shard_map/ppermute | solution.py:335
  62.2 6.4 %collective-permute-start.10 = (bf16[256,512]{1,0:T(8,128)(2,1)S(1)}, bf16[256,512]{1,0:T(8,128)(2,1)S(1)}, u32[]{:S(2)}, u32[]{:S(2)}) collective-permute-start(bf16[256,512]{1,0:T(8,128)(2,1)S(1)} %get-tuple-element.27), channel_id=1, source_target_pairs={{0,1},{1,0},{2,3},{3,2},{4,5},{5,4},{6,7},{7,6},{8,9},{9,8},{10,11... | collective-permute-start | bytes 786440 | tf_op jit(solution)/shard_map/ppermute | solution.py:335
  66.5 3.3 %collective-permute-start.9 = (bf16[256,512]{1,0:T(8,128)(2,1)S(1)}, bf16[256,512]{1,0:T(8,128)(2,1)S(1)}, u32[]{:S(2)}, u32[]{:S(2)}) collective-permute-start(bf16[256,512]{1,0:T(8,128)(2,1)S(1)} %convolve.1.act_own), channel_id=1, source_target_pairs={{0,1},{1,0},{2,3},{3,2},{4,5},{5,4},{6,7},{7,6},{8,9},{9,8},{10,11... | collective-permute-start | bytes 786440 | tf_op jit(solution)/shard_map/ppermute | solution.py:335

commit v3 on v2

v3 whole, which is shorter than its diff:
```python
import functools
import math

import jax
import jax.numpy as jnp
from jax import lax
from jax.experimental import pallas as pl
from jax.experimental.pallas import tpu as pltpu
from jax.sharding import PartitionSpec as P

HEAD_DIM = 64
CONV_CH = 512
KERNEL = 31
WIN = 512
EDGE = 16
NEG = -1e30
EXP_SCALE = HEAD_DIM ** (-0.5) * math.log2(math.e)
F32 = jnp.float32
BF16 = jnp.bfloat16
VMEM_LIMIT = 28 * 1024 * 1024


def dot(a, b):
    return jnp.dot(a, b, preferred_element_type=F32)


def normalize_halves(own, other, gain_own, gain_other):
    width = own.shape[1] + other.shape[1]
    mean = (
        jnp.sum(own, axis=1, keepdims=True) + jnp.sum(other, axis=1, keepdims=True)
    ) / width
    own = own - mean
    other = other - mean
    spread = (
        jnp.sum(own * own, axis=1, keepdims=True) + jnp.sum(other * other, axis=1, keepdims=True)
    ) / width
    scale = lax.rsqrt(spread + 1e-05)
    return (own * scale * gain_own).astype(BF16), (other * scale * gain_other).astype(BF16)


def qkv_kernel(
    meta, own_ref, other_ref, gain_own, gain_other, w_own, w_other,
    keep_ref, query_ref, send_ref, pass_ref,
):
    first = meta[1] == 0
    n_own, n_other = normalize_halves(
        own_ref[...].astype(F32), other_ref[...].astype(F32), gain_own[0], gain_other[0]
    )
    for slot, part in enumerate((1, 2, 0)):
        value = (dot(n_own, w_own[part, 0]) + dot(n_other, w_other[part, 0])).astype(BF16)
        sub = value.shape[1] // 2
        cols = slice(slot * sub, slot * sub + sub)
        keep = jnp.where(first, value[:, :sub], value[:, sub:])
        send = jnp.where(first, value[:, sub:], value[:, :sub])
        send_ref[:, cols] = send
        if slot < 2:
            keep_ref[:, cols] = keep
            pass_ref[:, cols] = send
        else:
            query_ref[...] = keep


def project(meta, frames, other, gain, weight):
    rows, half = frames.shape
    width = weight.shape[2]
    tile = 256
    w = weight.transpose(1, 0, 2).reshape(3, 2, half, width)
    g = gain.reshape(2, 1, half)
    grid_spec = pltpu.PrefetchScalarGridSpec(
        num_scalar_prefetch=1,
        grid=(rows // tile,),
        in_specs=[
            pl.BlockSpec((tile, half), lambda i, s: (i, 0)),
            pl.BlockSpec((tile, half), lambda i, s: (i, 0)),
            pl.BlockSpec((1, 1, half), lambda i, s: (s[0], 0, 0)),
            pl.BlockSpec((1, 1, half), lambda i, s: (1 - s[0], 0, 0)),
            pl.BlockSpec((3, 1, half, width), lambda i, s: (0, s[0], 0, 0)),
            pl.BlockSpec((3, 1, half, width), lambda i, s: (0, 1 - s[0], 0, 0)),
        ],
        out_specs=[
            pl.BlockSpec((tile, width), lambda i, s: (i, 0)),
            pl.BlockSpec((tile, width // 2), lambda i, s: (i, 0)),
            pl.BlockSpec((tile, 3 * width // 2), lambda i, s: (i, 0)),
            pl.BlockSpec((tile, width), lambda i, s: (i, 0)),
        ],
    )
    return pl.pallas_call(
        qkv_kernel,
        grid_spec=grid_spec,
        out_shape=[
            jax.ShapeDtypeStruct((rows, width), BF16),
            jax.ShapeDtypeStruct((rows, width // 2), BF16),
            jax.ShapeDtypeStruct((rows, 3 * width // 2), BF16),
            jax.ShapeDtypeStruct((rows, width), BF16),
        ],
        compiler_params=pltpu.CompilerParams(vmem_limit_bytes=VMEM_LIMIT),
        name="project",
    )(meta, frames, other, g, g, w, w)


def bounds_kernel(meta, counts, valid, lo_own, hi_own, lo_pair, hi_pair):
    utts = valid.shape[0]
    spans = []
    start = jnp.int32(0)
    for s in range(utts):
        count = lax.fori_loop(
            0, counts.shape[0], lambda b, acc, s=s: acc + counts[b, s], jnp.int32(0)
        )
        spans.append((start, start + jnp.minimum(count, valid[s])))
        start = start + count
    for slot, (lo_ref, hi_ref) in enumerate(((lo_own, hi_own), (lo_pair, hi_pair))):
        origin = meta[2 + slot]
        at = lax.broadcasted_iota(jnp.int32, lo_ref.shape, 0)
        lo = jnp.zeros(lo_ref.shape, jnp.int32)
        hi = jnp.zeros(lo_ref.shape, jnp.int32)
        for begin, end in spans:
            inside = (at >= begin - origin) & (at < end - origin)
            lo = jnp.where(inside, begin - origin, lo)
            hi = jnp.where(inside, end - origin, hi)
        lo_ref[...] = lo
        hi_ref[...] = hi


def bounds(meta, counts, valid, rows):
    smem = pl.BlockSpec(memory_space=pltpu.SMEM)
    vmem = pl.BlockSpec(memory_space=pltpu.VMEM)
    return pl.pallas_call(
        bounds_kernel,
        in_specs=[smem] * 3,
        out_specs=[vmem] * 4,
        out_shape=[jax.ShapeDtypeStruct((rows, 128), jnp.int32)] * 4,
        compiler_params=pltpu.CompilerParams(vmem_limit_bytes=VMEM_LIMIT),
        name="bounds",
    )(meta, counts, valid)


def attend_kernel(a_high, query, center, side_a, side_b, lo_ref, hi_ref, out_ref, ext, q_ref, sems):
    rows, width = q_ref.shape
    flip = a_high[0]
    at_a = pl.multiple_of(flip * 2 * rows, rows)
    at_b = pl.multiple_of((1 - flip) * 2 * rows, rows)
    both = pl.ds(0, 2 * width)
    copies = [
        pltpu.make_async_copy(center.at[:, both], ext.at[pl.ds(rows, rows)], sems.at[0]),
        pltpu.make_async_copy(query.at[:, pl.ds(query.shape[1] - width, width)], q_ref, sems.at[1]),
        pltpu.make_async_copy(side_a.at[:, both], ext.at[pl.ds(at_a, rows)], sems.at[2]),
        pltpu.make_async_copy(side_b.at[:, both], ext.at[pl.ds(at_b, rows)], sems.at[3]),
    ]
    for copy in copies:
        copy.start()
    for copy in copies:
        copy.wait()
    tile = rows // 2
    span = tile + 2 * WIN
    lane = lax.broadcasted_iota(jnp.int32, (tile, width), 1)
    for block in range(2):
        at = block * tile
        position = lax.broadcasted_iota(jnp.int32, (tile, 1), 0) + at
        lo = lo_ref[at : at + tile, :1]
        hi = hi_ref[at : at + tile, :1]
        near_lo = jnp.maximum(lo, position - WIN)
        near_hi = jnp.minimum(hi, position + (WIN + 1))
        u = lax.broadcasted_iota(jnp.int32, (tile, span), 1) + (at - WIN)
        bias = jnp.where((u >= near_lo) & (u < near_hi), 0.0, NEG)
        first = at + rows - WIN
        k = ext[first : first + span, :width]
        v = ext[first : first + span, width:]
        q = q_ref[at : at + tile, :]
        outs = []
        for sub in range(2):
            q_sub = jnp.where((lane >= HEAD_DIM) == (sub == 1), q, jnp.zeros_like(q))
            scores = (
                lax.dot_general(q_sub, k, (((1,), (1,)), ((), ())), preferred_element_type=F32)
                + bias
            )
            peak = jnp.max(scores, axis=1, keepdims=True)
            expw = jnp.exp2((scores - peak) * EXP_SCALE)
            total = jnp.sum(expw, axis=1, keepdims=True)
            outs.append(dot(expw.astype(BF16), v) / jnp.maximum(total, 1.0))
        joined = jnp.where(lane >= HEAD_DIM, outs[1], outs[0])
        out_ref[at : at + tile, :] = jnp.where(hi > lo, joined, 0.0).astype(BF16)


def attend(a_high, query, center, side_a, side_b, lo, hi):
    rows, width = side_b.shape[0], side_b.shape[1] // 2
    vmem = pl.BlockSpec(memory_space=pltpu.VMEM)
    anywhere = pl.BlockSpec(memory_space=pl.ANY)
    return pl.pallas_call(
        attend_kernel,
        in_specs=[pl.BlockSpec(memory_space=pltpu.SMEM)] + [anywhere] * 4 + [vmem] * 2,
        out_specs=vmem,
        out_shape=jax.ShapeDtypeStruct((rows, width), BF16),
        scratch_shapes=[
            pltpu.VMEM((3 * rows, 2 * width), BF16),
            pltpu.VMEM((rows, width), BF16),
            pltpu.SemaphoreType.DMA((4,)),
        ],
        compiler_params=pltpu.CompilerParams(vmem_limit_bytes=VMEM_LIMIT),
        name="attend",
    )(a_high, query, center, side_a, side_b, lo, hi)


def gate_kernel(
    meta,
    mine_own, pair_own, mine_other, pair_other,
    x_own, x_other,
    out_own, out_other,
    gain_ref,
    in_own, in_other,
    lo_ref, hi_ref,
    glu_ref, edge_ref, mid_keep, mid_send,
):
    h = meta[0]
    first = meta[1] == 0
    half = x_own.shape[1]
    rows = glu_ref.shape[0]
    here = pl.ds(pl.multiple_of(h * (rows - 2 * EDGE), EDGE), rows)

    def joined(mine, pair):
        mine = mine[here, :]
        pair = pair[here, :]
        return jnp.concatenate(
            [jnp.where(first, mine, pair), jnp.where(first, pair, mine)], axis=1
        )

    c_own = joined(mine_own, pair_own)
    c_other = joined(mine_other, pair_other)
    own_cols = pl.ds(pl.multiple_of(h * half, half), half)
    other_cols = pl.ds(pl.multiple_of((1 - h) * half, half), half)

    def mid(cols, x_ref):
        first = dot(c_own, out_own[:, cols]).astype(BF16).astype(F32)
        second = dot(c_other, out_other[:, cols]).astype(BF16).astype(F32)
        return (x_ref[here, :].astype(F32) + (first + second)).astype(BF16)

    m_own = mid(own_cols, x_own)
    m_other = mid(other_cols, x_other)
    keep = rows - EDGE

    @pl.when(h == 0)
    def _():
        mid_keep[...] = m_own[:keep]
        mid_send[...] = m_other[:keep]

    @pl.when(h == 1)
    def _():
        mid_keep[...] = m_own[EDGE:]
        mid_send[...] = m_other[EDGE:]

    n_own, n_other = normalize_halves(
        m_own.astype(F32), m_other.astype(F32), gain_ref[h], gain_ref[1 - h]
    )
    valid = (hi_ref[here, :] > lo_ref[here, :])[:, :1]
    glus = []
    for w_ref in (in_own, in_other):
        value = dot(n_own, w_ref[0, own_cols, :]) + dot(n_other, w_ref[0, other_cols, :])
        gate = dot(n_own, w_ref[1, own_cols, :]) + dot(n_other, w_ref[1, other_cols, :])
        glu = value / (1.0 + jnp.exp(-gate))
        glus.append(jnp.where(valid, glu, 0.0).astype(BF16))
    chan = glus[0].shape[1]
    glu_ref[:, :chan] = glus[0]
    glu_ref[:, chan:] = glus[1]

    @pl.when(h == 0)
    def _():
        edge_ref[:, :chan] = glus[1][:EDGE]
        edge_ref[:, chan:] = glus[0][:EDGE]

    @pl.when(h == 1)
    def _():
        edge_ref[:, :chan] = glus[1][rows - EDGE :]
        edge_ref[:, chan:] = glus[0][rows - EDGE :]


def gated(meta, contexts, x_own, x_other, out_own, out_other, gain, in_own, in_other, lo, hi):
    rows = x_own.shape[0] // 2 + EDGE
    half = x_own.shape[1]
    chan = in_own.shape[2]
    vmem = pl.BlockSpec(memory_space=pltpu.VMEM)
    return pl.pallas_call(
        gate_kernel,
        in_specs=[pl.BlockSpec(memory_space=pltpu.SMEM)] + [vmem] * 13,
        out_specs=[vmem] * 4,
        out_shape=[
            jax.ShapeDtypeStruct((rows, 2 * chan), BF16),
            jax.ShapeDtypeStruct((EDGE, 2 * chan), BF16),
            jax.ShapeDtypeStruct((rows - EDGE, half), BF16),
            jax.ShapeDtypeStruct((rows - EDGE, half), BF16),
        ],
        compiler_params=pltpu.CompilerParams(vmem_limit_bytes=VMEM_LIMIT),
        name="gated",
    )(meta, *contexts, x_own, x_other, out_own, out_other,
      gain.reshape(2, 1, half), in_own, in_other, lo, hi)


def conv_kernel(meta, glu_ref, edge_ref, lo_ref, hi_ref, dw_own, dw_other, g_own, g_other,
                act_ref, ext):
    h = meta[0]
    rows, width = act_ref.shape
    chan = width // 2
    got = glu_ref.shape[0]
    ext[pl.ds(pl.multiple_of((1 - h) * EDGE, EDGE), got), :] = glu_ref[...].astype(F32)
    ext[pl.ds(pl.multiple_of(h * got, EDGE), EDGE), :] = edge_ref[...].astype(F32)
    first = pl.multiple_of(h * rows, rows)
    at = lax.broadcasted_iota(jnp.int32, (rows, 128), 0) + first
    low = lo_ref[pl.ds(first, rows), :] - at
    high = hi_ref[pl.ds(first, rows), :] - at
    reach = KERNEL // 2
    step = 64
    for base in range(0, rows, step):
        low_b = low[base : base + step]
        high_b = high[base : base + step]
        sums = jnp.zeros((step, 128), F32)
        squares = jnp.zeros((step, 128), F32)
        results = []
        for col in range(0, width, 128):
            dw_ref, c = (dw_own, col) if col < chan else (dw_other, col - chan)
            total = jnp.zeros((step, 128), F32)
            for tap in range(KERNEL):
                shift = tap - reach
                row = base + EDGE + shift
                piece = ext[row : row + step, col : col + 128]
                same = (low_b <= shift) & (high_b > shift)
                total = total + jnp.where(same, piece, 0.0) * dw_ref[tap : tap + 1, c : c + 128]
            sums = sums + total
            squares = squares + total * total
            results.append(total)
        mean = jnp.sum(sums, axis=1, keepdims=True) / CONV_CH
        square = jnp.sum(squares, axis=1, keepdims=True) / CONV_CH
        scale = lax.rsqrt(square - mean * mean + 1e-05)
        for col, total in zip(range(0, width, 128), results):
            g_ref, c = (g_own, col) if col < chan else (g_other, col - chan)
            y = (total - mean) * scale * g_ref[:, c : c + 128]
            act_ref[base : base + step, col : col + 128] = (y / (1.0 + jnp.exp(-y))).astype(BF16)


def convolve(meta, glu, edge, lo, hi, dw_own, dw_other, g_own, g_other):
    rows = glu.shape[0] - EDGE
    width = glu.shape[1]
    vmem = pl.BlockSpec(memory_space=pltpu.VMEM)
    return pl.pallas_call(
        conv_kernel,
        in_specs=[pl.BlockSpec(memory_space=pltpu.SMEM)] + [vmem] * 8,
        out_specs=vmem,
        out_shape=jax.ShapeDtypeStruct((rows, width), BF16),
        scratch_shapes=[pltpu.VMEM((rows + 2 * EDGE, width), F32)],
        compiler_params=pltpu.CompilerParams(vmem_limit_bytes=VMEM_LIMIT),
        name="convolve",
    )(meta, glu, edge, lo, hi, dw_own, dw_other, g_own.reshape(1, -1), g_other.reshape(1, -1))


def finish_kernel(meta, act_own, act_other, mid_own, mid_other, w_own, w_other, out_ref):
    h = meta[0]
    rows, chan2 = act_own.shape
    chan = chan2 // 2
    half = out_ref.shape[1]
    cols = pl.ds(pl.multiple_of(h * half, half), half)
    w_a = w_own[:, cols]
    w_b = w_other[:, cols]

    def rows_of(act, mid, flip):
        first = dot(act[:, :chan], w_b if flip else w_a).astype(BF16).astype(F32)
        second = dot(act[:, chan:], w_a if flip else w_b).astype(BF16).astype(F32)
        return (mid[...].astype(F32) + (first + second)).astype(BF16)

    out_ref[pl.ds(pl.multiple_of(h * rows, rows), rows), :] = rows_of(act_own, mid_own, False)
    out_ref[pl.ds(pl.multiple_of((1 - h) * rows, rows), rows), :] = rows_of(
        act_other, mid_other, True
    )


def finish(meta, act_own, act_other, mid_own, mid_other, w_own, w_other):
    rows, half = mid_own.shape
    vmem = pl.BlockSpec(memory_space=pltpu.VMEM)
    return pl.pallas_call(
        finish_kernel,
        in_specs=[pl.BlockSpec(memory_space=pltpu.SMEM)] + [vmem] * 6,
        out_specs=vmem,
        out_shape=jax.ShapeDtypeStruct((2 * rows, half), BF16),
        compiler_params=pltpu.CompilerParams(vmem_limit_bytes=VMEM_LIMIT),
        name="finish",
    )(meta, act_own, act_other, mid_own, mid_other, w_own, w_other)


def local(
    blocks,
    frames,
    segment_ids,
    utt_valid,
    attn_gain,
    qkv_weight,
    out_weight,
    conv_gain,
    pointwise_in,
    depthwise,
    mid_gain,
    pointwise_out,
):
    rows = frames.shape[0]

    def swap(value):
        return lax.ppermute(value, "head", [(0, 1), (1, 0)])

    def shift(value, step):
        pairs = [(i, i - step if i % 2 == 0 else i + step) for i in range(blocks)]
        return lax.ppermute(value, "tm", [p for p in pairs if 0 <= p[1] < blocks])

    def exchange(value):
        return lax.ppermute(value, "tm", [(i, i ^ 1) for i in range(blocks)])

    block = lax.axis_index("tm").astype(jnp.int32)
    column = block % 2
    meta = jnp.stack([
        lax.axis_index("head").astype(jnp.int32),
        column,
        block * rows,
        (block + 1 - 2 * column) * rows,
    ])
    ids = jnp.arange(utt_valid.shape[0], dtype=jnp.int32)
    counts = jnp.sum((segment_ids[None, :] == ids[:, None]).astype(jnp.int32), axis=1)
    counts = lax.all_to_all(
        jnp.broadcast_to(counts[None, :], (blocks, counts.shape[0])), "tm", 0, 0
    )
    other = swap(frames)
    keep, query, send, passed = project(meta, frames, other, attn_gain, qkv_weight)
    pair = exchange(send)
    far_pair = shift(keep, 2)
    far_own = shift(passed, 1)

    pointwise = pointwise_in.transpose(1, 0, 2)
    out_weight, pointwise, depthwise, mid_gain, pointwise_out, _ = lax.optimization_barrier(
        (out_weight, pointwise, depthwise, mid_gain, pointwise_out, keep)
    )
    out_other = swap(out_weight)
    pointwise_other = swap(pointwise)
    depthwise_other = swap(depthwise)
    mid_gain_other = swap(mid_gain)
    pointwise_out_other = swap(pointwise_out)
    lo_own, hi_own, lo_pair, hi_pair = bounds(meta, counts, utt_valid, rows)
    pair, out_other, pointwise_other, depthwise_other, mid_gain_other, pointwise_out_other = (
        lax.optimization_barrier(
            (pair, out_other, pointwise_other, depthwise_other, mid_gain_other,
             pointwise_out_other)
        )
    )

    pair_context = attend(column.reshape(1), pair, pair, keep, far_pair, lo_pair, hi_pair)
    pair_context = exchange(pair_context)
    context = attend((1 - column).reshape(1), query, keep, pair, far_own, lo_own, hi_own)
    contexts = (context, pair_context, swap(context), swap(pair_context))
    glu, edge, mid_keep, mid_send = gated(
        meta, contexts, frames, other, out_weight, out_other, conv_gain,
        pointwise, pointwise_other, lo_own, hi_own,
    )
    edges = [(2 * i, 2 * (i - 1) + 1) for i in range(1, blocks)]
    edges += [(2 * i + 1, 2 * (i + 1)) for i in range(blocks - 1)]
    edge = lax.ppermute(edge, ("tm", "head"), edges)
    mid_other = swap(mid_send)
    act = convolve(
        meta, glu, edge, lo_own, hi_own, depthwise, depthwise_other, mid_gain, mid_gain_other
    )
    act_other = swap(act)
    return finish(
        meta, act, act_other, mid_keep, mid_other, pointwise_out, pointwise_out_other
    )


def solution(mesh):
    in_specs = (
        P(("grp", "tm"), "head"),
        P(("grp", "tm")),
        P("grp"),
        P(),
        P(None, None, "head"),
        P("head", None),
        P(),
        P(None, None, "head"),
        P(None, "head"),
        P("head"),
        P("head", None),
    )
    out_specs = P(("grp", "tm"), "head")
    return jax.shard_map(
        functools.partial(local, mesh.shape["tm"]),
        mesh=mesh,
        in_specs=in_specs,
        out_specs=out_specs,
        check_vma=False,
    )
```

time: 71.4 us -> 67.3 us (0.943)
  blocking collectives: 30.8 us -> 13.4 us
  Pallas kernels: 16.9 us -> 25 us
  waiting for transfers between devices: 3.21 us -> 10.7 us
  other arithmetic: 2.54 us -> 0.2 us
    psum x1 -> x0, blocking collectives: 30.8 us -> none  [local(): counts = lax.psum(jnp.sum(onehot.astype(jnp.int32), axis=0), 'tm')]
    all_to_all x0 -> x1, blocking collectives: none -> 13.4 us  [local(): lax.all_to_all(jnp.broadcast_to(counts[None, :], (blocks, counts.shape[0]...]
    pallas_call x1 -> x3, Pallas kernels: 5.99 us -> 12.2 us  [the longest x2 7.48 us: attend(): pl.pallas_call(attend_kernel, in_specs=[pl.BlockSpec(memory_space=pltpu.S...]
    ppermute x2 -> x4, waiting for transfers between devices: 0.01 us -> 4.53 us  [the longest x2 4.52 us: exchange(): return lax.ppermute(value, 'tm', [(i, i ^ 1) for i in range(blocks)])]
    ppermute x9 -> x10, waiting for transfers between devices: 3.2 us -> 6.17 us  [swap(): return lax.ppermute(value, 'head', [(0, 1), (1, 0)])]
    select_n x2 -> x0, other arithmetic: 2.15 us -> none  [the longest x1 1.15 us: local(): lo = jnp.where(valid, lo, 0)]
    reduce_sum x2 -> x0, local copies, waits for them, and re-layouts: 1.74 us -> none  [the longest x1 0.89 us: local(): hi = jnp.sum(jnp.where(onehot, stops[None, :] - origin, 0), axis=1)]
    unnamed x25 -> x43, local copies, waits for them, and re-layouts: 3.26 us -> 4.73 us
  transfers between devices with their start and end apart: 12 -> 15, of which waited for: 4 -> 8; matrix products, arithmetic and copies ran while one was open for 8% -> 3% of each run, Pallas kernels for 17% -> 24%
where the time goes in v3:
time: 67.3 us; the launch traced here: 67.1 us
  Pallas kernels  25 us (37%)
  blocking collectives  13.4 us (20%)
  starting transfers between devices  12.9 us (19%)
  waiting for transfers between devices  10.7 us (16%)
  local copies, waits for them, and re-layouts  4.74 us (7%)
    all_to_all x1, blocking collectives, local(): lax.all_to_all(jnp.broadcast_to(counts[None, :], (blocks, counts.shape[0]...  13.4 us
    pallas_call x2, Pallas kernels, attend(): pl.pallas_call(attend_kernel, in_specs=[pl.BlockSpec(memory_space=pltpu.S...  7.48 us
    ppermute x10, waiting for transfers between devices, swap(): return lax.ppermute(value, 'head', [(0, 1), (1, 0)])  6.17 us
    ppermute x10, starting transfers between devices, swap(): return lax.ppermute(value, 'head', [(0, 1), (1, 0)])  6.12 us
    pallas_call x1, Pallas kernels, bounds(): pl.pallas_call(bounds_kernel, in_specs=[smem] * 3, out_specs=[vmem] * 4,...  4.76 us
    unnamed x43, local copies, waits for them, and re-layouts  4.73 us
    ppermute x2, waiting for transfers between devices, exchange(): return lax.ppermute(value, 'tm', [(i, i ^ 1) for i in range(blocks)])  4.52 us
    pallas_call x1, Pallas kernels, convolve(): pl.pallas_call(conv_kernel, in_specs=[pl.BlockSpec(memory_space=pltpu.SME...  4.18 us
  transfers between devices with their start and end apart: 15, of which 8 were waited for; matrix products, arithmetic and copies ran while one was open for 3% of the time, Pallas kernels for 24%

profile of v3, /device:TPU:0, one launch (start us, length us, event | category | flops | bytes accessed | tf_op | source)
XLA Modules:
  0.0 67.1 jit_solution(1526361289864032843)
XLA Ops:
  0.5 1.5 %copy.16 = bf16[1024,2,256]{2,0,1:T(8,128)(2,1)S(1)} copy(bf16[1024,2,256]{2,1,0:T(2,128)(2,1)} %param.18) | data formatting | bytes 2097152 | tf_op args[7]
  2.5 3.8 %project.1 = (bf16[512,256]{1,0:T(8,128)(2,1)S(1)}, bf16[512,128]{1,0:T(8,128)(2,1)S(1)}, bf16[512,384]{1,0:T(8,128)(2,1)S(1)}, bf16[512,256]{1,0:T(8,128)(2,1)}) custom-call(s32[4]{0:T(128)S(1)} %pad_add_fusion.meta, bf16[512,512]{1,0:T(8,128)(2,1)S(1)} %copy-done.1, bf16[512,512]{1,0:T(8,128)(2,1)} %collective-permute-done.other_ref.x_other, ...), custom_call_target="tpu_custom_call" | custom-call | tf_op jit(solution)/shard_map/project/pallas_call | solution.py:87
  6.7 2.6 %collective-permute-start.1 = (bf16[512,384]{1,0:T(8,128)(2,1)S(1)}, bf16[512,384]{1,0:T(8,128)(2,1)S(1)}, u32[]{:S(2)}, u32[]{:S(2)}) collective-permute-start(bf16[512,384]{1,0:T(8,128)(2,1)S(1)} %get-tuple-element.30), channel_id=1, source_target_pairs={{0,2},{2,0},{4,6},{6,4},{8,10},{10,8},{12,14},{14,12},{1,3},{3,1},... | collective-permute-start | bytes 1179656 | tf_op jit(solution)/shard_map/ppermute | solution.py:409
  9.9 2.1 %collective-permute-done.5 = f32[256]{0:T(256)S(1)} collective-permute-done((f32[256]{0:T(256)S(1)}, f32[256]{0:T(256)S(1)}, u32[]{:S(2)}, u32[]{:S(2)}) %collective-permute-start.5) | collective-permute-done | bytes 1056 | tf_op jit(solution)/shard_map/ppermute | solution.py:402
  12.1 1.1 %collective-permute-done.4.dw_other = f32[31,256]{1,0:T(8,128)S(1)} collective-permute-done((f32[31,256]{1,0:T(8,128)S(1)}, f32[31,256]{1,0:T(8,128)S(1)}, u32[]{:S(2)}, u32[]{:S(2)}) %collective-permute-start.4) | collective-permute-done | bytes 31776 | tf_op jit(solution)/shard_map/ppermute | solution.py:402
  13.8 1.3 %collective-permute-start.8 = (bf16[512,256]{1,0:T(8,128)(2,1)S(1)}, bf16[512,256]{1,0:T(8,128)(2,1)S(1)}, u32[]{:S(2)}, u32[]{:S(2)}) collective-permute-start(bf16[512,256]{1,0:T(8,128)(2,1)S(1)} %get-tuple-element.29.center.side_a), channel_id=1, source_target_pairs={{2,6},{4,0},{6,10},{8,4},{10,14},{12,8},{3,7},{5,1},{7,11},{9,5},{... | collective-permute-start | bytes 786440 | tf_op jit(solution)/shard_map/ppermute | solution.py:406
  15.1 3.9 %collective-permute-done.1.side_a.query.center = bf16[512,384]{1,0:T(8,128)(2,1)S(1)} collective-permute-done((bf16[512,384]{1,0:T(8,128)(2,1)S(1)}, bf16[512,384]{1,0:T(8,128)(2,1)S(1)}, u32[]{:S(2)}, u32[]{:S(2)}) %collective-permute-start.1) | collective-permute-done | bytes 393248 | tf_op jit(solution)/shard_map/ppermute | solution.py:409
  19.0 1.4 %collective-permute-start.7 = (bf16[512,256]{1,0:T(8,128)(2,1)}, bf16[512,256]{1,0:T(8,128)(2,1)}, u32[]{:S(2)}, u32[]{:S(2)}) collective-permute-start(bf16[512,256]{1,0:T(8,128)(2,1)} %get-tuple-element.37), channel_id=1, source_target_pairs={{2,4},{4,2},{6,8},{8,6},{10,12},{12,10},{3,5},{5,3},{7,9},{9,7},{1... | collective-permute-start | bytes 786440 | tf_op jit(solution)/shard_map/ppermute | solution.py:406
  20.5 13.4 %all_to_all.8 = s32[8,1,16]{2,1,0:T(1,128)S(1)} all-to-all(s32[8,1,16]{2,1,0:T(1,128)S(1)} %broadcast_in_dim.2), channel_id=1, replica_groups=mesh['grp'=2,'tm'=8,'head'=2] {'tm'}, dimensions={0} | all-to-all | bytes 1024 | tf_op jit(solution)/shard_map/all_to_all | solution.py:421
  33.9 4.8 %bounds.1 = (s32[512,128]{1,0:T(8,128)S(1)}, s32[512,128]{1,0:T(8,128)S(1)}, s32[512,128]{1,0:T(8,128)S(1)}, s32[512,128]{1,0:T(8,128)S(1)}) custom-call(s32[4]{0:T(128)S(1)} %pad_add_fusion.meta, s32[8,16]{1,0:T(8,128)S(1)} %bitcast.20, s32[16]{0:T(128)S(1)} %copy-done.19), custom_call_target="tpu_custom_call" | custom-call | tf_op jit(solution)/shard_map/bounds/pallas_call | solution.py:127
  38.7 0.8 %copy-done.6 = bf16[256,1024]{1,0:T(8,128)(2,1)} copy-done((bf16[256,1024]{1,0:T(8,128)(2,1)}, bf16[256,1024]{1,0:T(8,128)(2,1)S(1)}, u32[]{:S(2)}) %copy-start.6) | copy-done | bytes 524312
  39.5 0.8 %copy-done.10 = bf16[256,1024]{1,0:T(8,128)(2,1)} copy-done((bf16[256,1024]{1,0:T(8,128)(2,1)}, bf16[256,1024]{1,0:T(8,128)(2,1)S(1)}, u32[]{:S(2)}) %copy-start.10) | copy-done | bytes 524312
  40.2 1.0 %copy-done.2 = bf16[2,1024,256]{2,1,0:T(8,128)(2,1)} copy-done((bf16[2,1024,256]{2,1,0:T(8,128)(2,1)}, bf16[2,1024,256]{2,1,0:T(8,128)(2,1)S(1)}, u32[]{:S(2)}) %copy-start.2) | copy-done | bytes 1048600
  41.2 3.5 %attend.3 = bf16[512,128]{1,0:T(8,128)(2,1)} custom-call(s32[1]{0:T(128)} %bitcast.1.a_high, bf16[512,384]{1,0:T(8,128)(2,1)S(1)} %collective-permute-done.1.side_a.query.center, bf16[512,384]{1,0:T(8,128)(2,1)S(1)} %collective-permute-done.1.side_a.query.center, bf16[512,256]{1,0:T(8,128)(2,1)S(1)} %get-tuple-element.29.center.side_a, ...), custom_call_target="tpu_custom_call" | custom-call | tf_op jit(solution)/shard_map/attend/pallas_call | solution.py:188
  45.3 4.0 %attend.2.mine_own = bf16[512,128]{1,0:T(8,128)(2,1)S(1)} custom-call(s32[1]{0:T(128)} %bitcast.4.a_high, bf16[512,128]{1,0:T(8,128)(2,1)S(1)} %get-tuple-element.28.query, bf16[512,256]{1,0:T(8,128)(2,1)S(1)} %get-tuple-element.29.center.side_a, bf16[512,384]{1,0:T(8,128)(2,1)S(1)} %collective-permute-done.1.side_a.query.center, ...), custom_call_target="tpu_custom_call" | custom-call | tf_op jit(solution)/shard_map/attend/pallas_call | solution.py:188
  50.1 0.7 %collective-permute-done.10.mine_other = bf16[512,128]{1,0:T(8,128)(2,1)S(1)} collective-permute-done((bf16[512,128]{1,0:T(8,128)(2,1)S(1)}, bf16[512,128]{1,0:T(8,128)(2,1)S(1)}, u32[]{:S(2)}, u32[]{:S(2)}) %collective-permute-start.10) | collective-permute-done | bytes 131104 | tf_op jit(solution)/shard_map/ppermute | solution.py:402
  50.7 0.9 %collective-permute-done.11.pair_other = bf16[512,128]{1,0:T(8,128)(2,1)S(1)} collective-permute-done((bf16[512,128]{1,0:T(8,128)(2,1)}, bf16[512,128]{1,0:T(8,128)(2,1)S(1)}, u32[]{:S(2)}, u32[]{:S(2)}) %collective-permute-start.11) | collective-permute-done | bytes 131104 | tf_op jit(solution)/shard_map/ppermute | solution.py:402
  51.7 2.9 %gated.1 = (bf16[272,512]{1,0:T(8,128)(2,1)S(1)}, bf16[16,512]{1,0:T(8,128)(2,1)S(1)}, bf16[256,512]{1,0:T(8,128)(2,1)S(1)}, bf16[256,512]{1,0:T(8,128)(2,1)S(1)}) custom-call(s32[4]{0:T(128)S(1)} %pad_add_fusion.meta, bf16[512,128]{1,0:T(8,128)(2,1)S(1)} %attend.2.mine_own, bf16[512,128]{1,0:T(8,128)(2,1)} %collective-permute-done.9.pair_own, ...), custom_call_target="tpu_custom_call" | custom-call | tf_op jit(solution)/shard_map/gated/pallas_call | solution.py:280
  54.6 0.8 %collective-permute-start.12 = (bf16[16,512]{1,0:T(8,128)(2,1)S(1)}, bf16[16,512]{1,0:T(8,128)(2,1)S(1)}, u32[]{:S(2)}, u32[]{:S(2)}) collective-permute-start(bf16[16,512]{1,0:T(8,128)(2,1)S(1)} %get-tuple-element.45), channel_id=1, source_target_pairs={{2,1},{4,3},{6,5},{8,7},{10,9},{12,11},{14,13},{1,2},{3,4},{5,6},{... | collective-permute-start | bytes 49160 | tf_op jit(solution)/shard_map/ppermute | solution.py:457
  55.4 2.4 %collective-permute-start.14 = (bf16[256,512]{1,0:T(8,128)(2,1)S(1)}, bf16[256,512]{1,0:T(8,128)(2,1)S(1)}, u32[]{:S(2)}, u32[]{:S(2)}) collective-permute-start(bf16[256,512]{1,0:T(8,128)(2,1)S(1)} %get-tuple-element.49), channel_id=1, source_target_pairs={{0,1},{1,0},{2,3},{3,2},{4,5},{5,4},{6,7},{7,6},{8,9},{9,8},{10,11... | collective-permute-start | bytes 786440 | tf_op jit(solution)/shard_map/ppermute | solution.py:402
  57.9 4.2 %convolve.1.act_own = bf16[256,512]{1,0:T(8,128)(2,1)S(1)} custom-call(s32[4]{0:T(128)S(1)} %pad_add_fusion.meta, bf16[272,512]{1,0:T(8,128)(2,1)S(1)} %get-tuple-element.44.glu_ref, bf16[16,512]{1,0:T(8,128)(2,1)S(1)} %collective-permute-done.12.edge_ref, s32[512,128]{1,0:T(8,128)S(1)} %get-tuple-element.38.lo_ref, ...), custom_call_target="tpu_custom_call" | custom-call | tf_op jit(solution)/shard_map/convolve/pallas_call | solution.py:341
  62.1 2.0 %collective-permute-start.13 = (bf16[256,512]{1,0:T(8,128)(2,1)S(1)}, bf16[256,512]{1,0:T(8,128)(2,1)S(1)}, u32[]{:S(2)}, u32[]{:S(2)}) collective-permute-start(bf16[256,512]{1,0:T(8,128)(2,1)S(1)} %convolve.1.act_own), channel_id=1, source_target_pairs={{0,1},{1,0},{2,3},{3,2},{4,5},{5,4},{6,7},{7,6},{8,9},{9,8},{10,11... | collective-permute-start | bytes 786440 | tf_op jit(solution)/shard_map/ppermute | solution.py:402
  64.0 1.2 %collective-permute-done.13.act_other = bf16[256,512]{1,0:T(8,128)(2,1)S(1)} collective-permute-done((bf16[256,512]{1,0:T(8,128)(2,1)S(1)}, bf16[256,512]{1,0:T(8,128)(2,1)S(1)}, u32[]{:S(2)}, u32[]{:S(2)}) %collective-permute-start.13) | collective-permute-done | bytes 262176 | tf_op jit(solution)/shard_map/ppermute | solution.py:402
  65.2 1.8 %finish.1 = bf16[512,512]{1,0:T(8,128)(2,1)} custom-call(s32[4]{0:T(128)S(1)} %pad_add_fusion.meta, bf16[256,512]{1,0:T(8,128)(2,1)S(1)} %convolve.1.act_own, bf16[256,512]{1,0:T(8,128)(2,1)S(1)} %collective-permute-done.13.act_other, bf16[256,512]{1,0:T(8,128)(2,1)S(1)} %get-tuple-element.48.mid_own, ...), custom_call_target="tpu_custom_call" | custom-call | tf_op jit(solution)/shard_map/finish/pallas_call | solution.py:375
  (60 shorter events, 4.2 us)
Async XLA Ops:
  0.0 2.4 %collective-permute-start = (bf16[512,512]{1,0:T(8,128)(2,1)}, bf16[512,512]{1,0:T(8,128)(2,1)}, u32[]{:S(2)}, u32[]{:S(2)}) collective-permute-start(bf16[512,512]{1,0:T(8,128)(2,1)} %x_own.1), channel_id=1, source_target_pairs={{0,1},{1,0},{2,3},{3,2},{4,5},{5,4},{6,7},{7,6},{8,9},{9,8},{10,11... | collective-permute-start | bytes 1572872 | tf_op jit(solution)/shard_map/ppermute | solution.py:402
  2.4 7.0 %copy-start.8 = (bf16[256,1024]{1,0:T(8,128)(2,1)S(1)}, bf16[256,1024]{1,0:T(8,128)(2,1)}, u32[]{:S(2)}) copy-start(bf16[256,1024]{1,0:T(8,128)(2,1)} %w_own) | copy-start | bytes 1572868
  2.4 7.4 %copy-start.18 = (f32[256]{0:T(256)S(1)}, f32[256]{0:T(256)}, u32[]{:S(2)}) copy-start(f32[256]{0:T(256)} %param.20) | copy-start | bytes 3076
  2.4 9.6 %copy-start.12 = (f32[31,256]{1,0:T(8,128)S(1)}, f32[31,256]{1,0:T(8,128)}, u32[]{:S(2)}) copy-start(f32[31,256]{1,0:T(8,128)} %dw_own) | copy-start | bytes 95236
  2.5 17.9 %copy-start.20 = (s32[512]{0:T(512)S(1)}, s32[512]{0:T(512)}, u32[]{:S(2)}) copy-start(s32[512]{0:T(512)} %param.12) | copy-start | bytes 6148
  2.5 31.4 %copy-start.19 = (s32[16]{0:T(128)S(1)}, s32[16]{0:T(128)}, u32[]{:S(2)}) copy-start(s32[16]{0:T(128)} %valid.1) | copy-start | bytes 196
  6.3 33.9 %collective-permute-start.3 = (bf16[2,1024,256]{2,1,0:T(8,128)(2,1)S(1)}, bf16[2,1024,256]{2,1,0:T(8,128)(2,1)S(1)}, u32[]{:S(2)}, u32[]{:S(2)}) collective-permute-start(bf16[2,1024,256]{2,1,0:T(8,128)(2,1)S(1)} %bitcast.18), channel_id=1, source_target_pairs={{0,1},{1,0},{2,3},{3,2},{4,5},{5,4},{6,7},{7,6},{8,9},{9,8},{10,11... | collective-permute-start | bytes 3145736 | tf_op jit(solution)/shard_map/ppermute | solution.py:402
  6.7 12.3 %collective-permute-start.1 = (bf16[512,384]{1,0:T(8,128)(2,1)S(1)}, bf16[512,384]{1,0:T(8,128)(2,1)S(1)}, u32[]{:S(2)}, u32[]{:S(2)}) collective-permute-start(bf16[512,384]{1,0:T(8,128)(2,1)S(1)} %get-tuple-element.30), channel_id=1, source_target_pairs={{0,2},{2,0},{4,6},{6,4},{8,10},{10,8},{12,14},{14,12},{1,3},{3,1},... | collective-permute-start | bytes 1179656 | tf_op jit(solution)/shard_map/ppermute | solution.py:409
  9.3 29.3 %collective-permute-start.2 = (bf16[256,1024]{1,0:T(8,128)(2,1)S(1)}, bf16[256,1024]{1,0:T(8,128)(2,1)S(1)}, u32[]{:S(2)}, u32[]{:S(2)}) collective-permute-start(bf16[256,1024]{1,0:T(8,128)(2,1)S(1)} %copy-done.4), channel_id=1, source_target_pairs={{0,1},{1,0},{2,3},{3,2},{4,5},{5,4},{6,7},{7,6},{8,9},{9,8},{10,11... | collective-permute-start | bytes 1572872 | tf_op jit(solution)/shard_map/ppermute | solution.py:402
  9.4 30.0 %collective-permute-start.6 = (bf16[256,1024]{1,0:T(8,128)(2,1)S(1)}, bf16[256,1024]{1,0:T(8,128)(2,1)S(1)}, u32[]{:S(2)}, u32[]{:S(2)}) collective-permute-start(bf16[256,1024]{1,0:T(8,128)(2,1)S(1)} %copy-done.8), channel_id=1, source_target_pairs={{0,1},{1,0},{2,3},{3,2},{4,5},{5,4},{6,7},{7,6},{8,9},{9,8},{10,11... | collective-permute-start | bytes 1572872 | tf_op jit(solution)/shard_map/ppermute | solution.py:402
  9.9 2.1 %collective-permute-start.5 = (f32[256]{0:T(256)S(1)}, f32[256]{0:T(256)S(1)}, u32[]{:S(2)}, u32[]{:S(2)}) collective-permute-start(f32[256]{0:T(256)S(1)} %copy-done.18), channel_id=1, source_target_pairs={{0,1},{1,0},{2,3},{3,2},{4,5},{5,4},{6,7},{7,6},{8,9},{9,8},{10,11... | collective-permute-start | bytes 3080 | tf_op jit(solution)/shard_map/ppermute | solution.py:402
  12.0 1.2 %collective-permute-start.4 = (f32[31,256]{1,0:T(8,128)S(1)}, f32[31,256]{1,0:T(8,128)S(1)}, u32[]{:S(2)}, u32[]{:S(2)}) collective-permute-start(f32[31,256]{1,0:T(8,128)S(1)} %copy-done.12), channel_id=1, source_target_pairs={{0,1},{1,0},{2,3},{3,2},{4,5},{5,4},{6,7},{7,6},{8,9},{9,8},{10,11... | collective-permute-start | bytes 95240 | tf_op jit(solution)/shard_map/ppermute | solution.py:402
  13.8 27.4 %collective-permute-start.8 = (bf16[512,256]{1,0:T(8,128)(2,1)S(1)}, bf16[512,256]{1,0:T(8,128)(2,1)S(1)}, u32[]{:S(2)}, u32[]{:S(2)}) collective-permute-start(bf16[512,256]{1,0:T(8,128)(2,1)S(1)} %get-tuple-element.29.center.side_a), channel_id=1, source_target_pairs={{2,6},{4,0},{6,10},{8,4},{10,14},{12,8},{3,7},{5,1},{7,11},{9,5},{... | collective-permute-start | bytes 786440 | tf_op jit(solution)/shard_map/ppermute | solution.py:406
  19.0 26.4 %collective-permute-start.7 = (bf16[512,256]{1,0:T(8,128)(2,1)}, bf16[512,256]{1,0:T(8,128)(2,1)}, u32[]{:S(2)}, u32[]{:S(2)}) collective-permute-start(bf16[512,256]{1,0:T(8,128)(2,1)} %get-tuple-element.37), channel_id=1, source_target_pairs={{2,4},{4,2},{6,8},{8,6},{10,12},{12,10},{3,5},{5,3},{7,9},{9,7},{1... | collective-permute-start | bytes 786440 | tf_op jit(solution)/shard_map/ppermute | solution.py:406
  41.2 10.4 %copy-start.5 = (bf16[256,1024]{1,0:T(8,128)(2,1)S(1)}, bf16[256,1024]{1,0:T(8,128)(2,1)}, u32[]{:S(2)}) copy-start(bf16[256,1024]{1,0:T(8,128)(2,1)} %out_own) | copy-start | bytes 1572868
  41.2 10.4 %copy-start.17 = (f32[1024]{0:T(1024)S(1)}, f32[1024]{0:T(1024)}, u32[]{:S(2)}) copy-start(f32[1024]{0:T(1024)} %param.17) | copy-start | bytes 12292
  44.7 5.3 %collective-permute-start.9 = (bf16[512,128]{1,0:T(8,128)(2,1)}, bf16[512,128]{1,0:T(8,128)(2,1)}, u32[]{:S(2)}, u32[]{:S(2)}) collective-permute-start(bf16[512,128]{1,0:T(8,128)(2,1)} %attend.3), channel_id=1, source_target_pairs={{0,2},{2,0},{4,6},{6,4},{8,10},{10,8},{12,14},{14,12},{1,3},{3,1},... | collective-permute-start | bytes 393224 | tf_op jit(solution)/shard_map/ppermute | solution.py:409
  49.3 1.4 %collective-permute-start.10 = (bf16[512,128]{1,0:T(8,128)(2,1)S(1)}, bf16[512,128]{1,0:T(8,128)(2,1)S(1)}, u32[]{:S(2)}, u32[]{:S(2)}) collective-permute-start(bf16[512,128]{1,0:T(8,128)(2,1)S(1)} %attend.2.mine_own), channel_id=1, source_target_pairs={{0,1},{1,0},{2,3},{3,2},{4,5},{5,4},{6,7},{7,6},{8,9},{9,8},{10,11... | collective-permute-start | bytes 393224 | tf_op jit(solution)/shard_map/ppermute | solution.py:402
  50.1 1.6 %collective-permute-start.11 = (bf16[512,128]{1,0:T(8,128)(2,1)}, bf16[512,128]{1,0:T(8,128)(2,1)S(1)}, u32[]{:S(2)}, u32[]{:S(2)}) collective-permute-start(bf16[512,128]{1,0:T(8,128)(2,1)} %collective-permute-done.9.pair_own), channel_id=1, source_target_pairs={{0,1},{1,0},{2,3},{3,2},{4,5},{5,4},{6,7},{7,6},{8,9},{9,8},{10,11... | collective-permute-start | bytes 393224 | tf_op jit(solution)/shard_map/ppermute | solution.py:402
  51.7 13.5 %copy-start.9 = (bf16[256,1024]{1,0:T(8,128)(2,1)S(1)}, bf16[256,1024]{1,0:T(8,128)(2,1)}, u32[]{:S(2)}) copy-start(bf16[256,1024]{1,0:T(8,128)(2,1)} %w_own) | copy-start | bytes 1572868
  51.7 13.5 %copy-start.11 = (bf16[256,1024]{1,0:T(8,128)(2,1)S(1)}, bf16[256,1024]{1,0:T(8,128)(2,1)}, u32[]{:S(2)}) copy-start(bf16[256,1024]{1,0:T(8,128)(2,1)} %copy-done.10) | copy-start | bytes 1572868
  54.6 3.3 %collective-permute-start.12 = (bf16[16,512]{1,0:T(8,128)(2,1)S(1)}, bf16[16,512]{1,0:T(8,128)(2,1)S(1)}, u32[]{:S(2)}, u32[]{:S(2)}) collective-permute-start(bf16[16,512]{1,0:T(8,128)(2,1)S(1)} %get-tuple-element.45), channel_id=1, source_target_pairs={{2,1},{4,3},{6,5},{8,7},{10,9},{12,11},{14,13},{1,2},{3,4},{5,6},{... | collective-permute-start | bytes 49160 | tf_op jit(solution)/shard_map/ppermute | solution.py:457
  55.4 8.6 %collective-permute-start.14 = (bf16[256,512]{1,0:T(8,128)(2,1)S(1)}, bf16[256,512]{1,0:T(8,128)(2,1)S(1)}, u32[]{:S(2)}, u32[]{:S(2)}) collective-permute-start(bf16[256,512]{1,0:T(8,128)(2,1)S(1)} %get-tuple-element.49), channel_id=1, source_target_pairs={{0,1},{1,0},{2,3},{3,2},{4,5},{5,4},{6,7},{7,6},{8,9},{9,8},{10,11... | collective-permute-start | bytes 786440 | tf_op jit(solution)/shard_map/ppermute | solution.py:402
  62.1 3.1 %collective-permute-start.13 = (bf16[256,512]{1,0:T(8,128)(2,1)S(1)}, bf16[256,512]{1,0:T(8,128)(2,1)S(1)}, u32[]{:S(2)}, u32[]{:S(2)}) collective-permute-start(bf16[256,512]{1,0:T(8,128)(2,1)S(1)} %convolve.1.act_own), channel_id=1, source_target_pairs={{0,1},{1,0},{2,3},{3,2},{4,5},{5,4},{6,7},{7,6},{8,9},{9,8},{10,11... | collective-permute-start | bytes 786440 | tf_op jit(solution)/shard_map/ppermute | solution.py:402
  (12 other events, 42.4 us)

commit v4 on v3

v4 whole, which is shorter than its diff:
```python
import functools
import math

import jax
import jax.numpy as jnp
from jax import lax
from jax.experimental import pallas as pl
from jax.experimental.pallas import tpu as pltpu
from jax.sharding import PartitionSpec as P

HEAD_DIM = 64
CONV_CH = 512
KERNEL = 31
WIN = 512
EDGE = 16
NEG = -1e30
EXP_SCALE = HEAD_DIM ** (-0.5) * math.log2(math.e)
F32 = jnp.float32
BF16 = jnp.bfloat16
VMEM_LIMIT = 16 * 1024 * 1024


def dot(a, b):
    return jnp.dot(a, b, preferred_element_type=F32)


def normalize_halves(own, other, gain_own, gain_other):
    width = own.shape[1] + other.shape[1]
    mean = (
        jnp.sum(own, axis=1, keepdims=True) + jnp.sum(other, axis=1, keepdims=True)
    ) / width
    own = own - mean
    other = other - mean
    spread = (
        jnp.sum(own * own, axis=1, keepdims=True) + jnp.sum(other * other, axis=1, keepdims=True)
    ) / width
    scale = lax.rsqrt(spread + 1e-05)
    return (own * scale * gain_own).astype(BF16), (other * scale * gain_other).astype(BF16)


def qkv_kernel(
    meta, own_ref, other_ref, gain_ref, w_ref, keep_ref, query_ref, send_ref, pass_ref
):
    h = meta[0]
    first = meta[1] == 0
    rows = own_ref.shape[0]
    tile = 256
    for at in range(0, rows, tile):
        here = slice(at, at + tile)
        n_own, n_other = normalize_halves(
            own_ref[here, :].astype(F32), other_ref[here, :].astype(F32),
            gain_ref[h], gain_ref[1 - h],
        )
        for slot, part in enumerate((1, 2, 0)):
            value = (dot(n_own, w_ref[part, h]) + dot(n_other, w_ref[part, 1 - h])).astype(BF16)
            sub = value.shape[1] // 2
            cols = slice(slot * sub, slot * sub + sub)
            keep = jnp.where(first, value[:, :sub], value[:, sub:])
            send = jnp.where(first, value[:, sub:], value[:, :sub])
            send_ref[here, cols] = send
            if slot < 2:
                keep_ref[here, cols] = keep
                pass_ref[here, cols] = send
            else:
                query_ref[here, :] = keep


def project(meta, frames, other, gain, weight):
    rows, half = frames.shape
    width = weight.shape[2]
    vmem = pl.BlockSpec(memory_space=pltpu.VMEM)
    return pl.pallas_call(
        qkv_kernel,
        in_specs=[pl.BlockSpec(memory_space=pltpu.SMEM)] + [vmem] * 4,
        out_specs=[vmem] * 4,
        out_shape=[
            jax.ShapeDtypeStruct((rows, width), BF16),
            jax.ShapeDtypeStruct((rows, width // 2), BF16),
            jax.ShapeDtypeStruct((rows, 3 * width // 2), BF16),
            jax.ShapeDtypeStruct((rows, width), BF16),
        ],
        compiler_params=pltpu.CompilerParams(vmem_limit_bytes=VMEM_LIMIT),
        name="project",
    )(meta, frames, other, gain.reshape(2, 1, half),
      weight.transpose(1, 0, 2).reshape(3, 2, half, width))


def bounds_kernel(meta, counts, valid, own_ref, pair_ref):
    utts = valid.shape[1]
    rows = own_ref.shape[0]
    square = (utts, utts)
    sub = lax.broadcasted_iota(jnp.int32, square, 0)
    lane = lax.broadcasted_iota(jnp.int32, square, 1)
    total = jnp.sum(counts[...].astype(F32), axis=0, keepdims=True)
    limit = jnp.broadcast_to(jnp.minimum(total, valid[...].astype(F32)), square)
    total = jnp.broadcast_to(total, square)
    start = jnp.sum(jnp.where(lane < sub, total, 0.0), axis=1, keepdims=True)
    stop = start + jnp.sum(jnp.where(lane == sub, limit, 0.0), axis=1, keepdims=True)
    at = lax.broadcasted_iota(jnp.int32, (utts, rows), 1).astype(F32)
    for slot, ref in enumerate((own_ref, pair_ref)):
        origin = meta[2 + slot].astype(F32)
        lo = start - origin
        hi = stop - origin
        inside = (at >= lo) & (at < hi)
        low = jnp.sum(jnp.where(inside, lo, 0.0), axis=0, keepdims=True)
        high = jnp.sum(jnp.where(inside, hi, 0.0), axis=0, keepdims=True)
        both = jnp.concatenate([low, high, jnp.zeros((126, rows), F32)], axis=0)
        ref[...] = both.T.astype(jnp.int32)


def bounds(meta, counts, valid, rows):
    vmem = pl.BlockSpec(memory_space=pltpu.VMEM)
    return pl.pallas_call(
        bounds_kernel,
        in_specs=[pl.BlockSpec(memory_space=pltpu.SMEM), vmem, vmem],
        out_specs=[vmem] * 2,
        out_shape=[jax.ShapeDtypeStruct((rows, 128), jnp.int32)] * 2,
        compiler_params=pltpu.CompilerParams(vmem_limit_bytes=VMEM_LIMIT),
        name="bounds",
    )(meta, counts, valid.reshape(1, -1))


def attend_kernel(a_high, query, center, side_a, side_b, run_ref, out_ref):
    rows = center.shape[0]
    width = center.shape[1] // 2 if query.shape[1] < center.shape[1] else center.shape[1] // 3
    q_cols = slice(query.shape[1] - width, query.shape[1])
    tile = rows // 2
    lane = lax.broadcasted_iota(jnp.int32, (tile, width), 1)

    def run(low_ref, high_ref):
        for block in range(2):
            at = block * tile
            pieces = (
                ((low_ref, 0, rows, -rows), (center, 0, rows, 0), (high_ref, 0, tile, rows))
                if block == 0
                else ((low_ref, tile, tile, -rows), (center, 0, rows, 0), (high_ref, 0, rows, rows))
            )
            position = lax.broadcasted_iota(jnp.int32, (tile, 1), 0) + at
            lo = run_ref[at : at + tile, 0:1]
            hi = run_ref[at : at + tile, 1:2]
            near_lo = jnp.maximum(lo, position - WIN)
            near_hi = jnp.minimum(hi, position + (WIN + 1))
            biases = []
            for _, first, size, origin in pieces:
                u = lax.broadcasted_iota(jnp.int32, (tile, size), 1) + (origin + first)
                biases.append(jnp.where((u >= near_lo) & (u < near_hi), 0.0, NEG))
            q = query[at : at + tile, q_cols]
            outs = []
            for sub in range(2):
                q_sub = jnp.where((lane >= HEAD_DIM) == (sub == 1), q, jnp.zeros_like(q))
                scores = []
                for (ref, first, size, _), bias in zip(pieces, biases):
                    s = lax.dot_general(
                        q_sub, ref[first : first + size, :width], (((1,), (1,)), ((), ())),
                        preferred_element_type=F32,
                    )
                    scores.append(s + bias)
                peak = functools.reduce(
                    jnp.maximum, [jnp.max(s, axis=1, keepdims=True) for s in scores]
                )
                total = jnp.zeros((tile, 1), F32)
                context = jnp.zeros((tile, width), F32)
                for (ref, first, size, _), s in zip(pieces, scores):
                    expw = jnp.exp2((s - peak) * EXP_SCALE)
                    total = total + jnp.sum(expw, axis=1, keepdims=True)
                    context = context + dot(
                        expw.astype(BF16), ref[first : first + size, width : 2 * width]
                    )
                outs.append(context / jnp.maximum(total, 1.0))
            joined = jnp.where(lane >= HEAD_DIM, outs[1], outs[0])
            out_ref[at : at + tile, :] = jnp.where(hi > lo, joined, 0.0).astype(BF16)

    @pl.when(a_high[0] == 1)
    def _():
        run(side_b, side_a)

    @pl.when(a_high[0] == 0)
    def _():
        run(side_a, side_b)


def attend(a_high, query, center, side_a, side_b, runs):
    rows, width = side_b.shape[0], side_b.shape[1] // 2
    vmem = pl.BlockSpec(memory_space=pltpu.VMEM)
    return pl.pallas_call(
        attend_kernel,
        in_specs=[pl.BlockSpec(memory_space=pltpu.SMEM)] + [vmem] * 5,
        out_specs=vmem,
        out_shape=jax.ShapeDtypeStruct((rows, width), BF16),
        compiler_params=pltpu.CompilerParams(vmem_limit_bytes=VMEM_LIMIT),
        name="attend",
    )(a_high, query, center, side_a, side_b, runs)


def gate_kernel(
    meta,
    mine_own, pair_own, mine_other, pair_other,
    x_own, x_other,
    out_own, out_other,
    gain_ref,
    in_own, in_other,
    run_ref,
    glu_ref, edge_ref, mid_keep, mid_send,
):
    h = meta[0]
    first = meta[1] == 0
    half = x_own.shape[1]
    rows = glu_ref.shape[0]
    here = pl.ds(pl.multiple_of(h * (rows - 2 * EDGE), EDGE), rows)

    def joined(mine, pair):
        mine = mine[here, :]
        pair = pair[here, :]
        return jnp.concatenate(
            [jnp.where(first, mine, pair), jnp.where(first, pair, mine)], axis=1
        )

    c_own = joined(mine_own, pair_own)
    c_other = joined(mine_other, pair_other)
    own_cols = pl.ds(pl.multiple_of(h * half, half), half)
    other_cols = pl.ds(pl.multiple_of((1 - h) * half, half), half)

    def mid(cols, x_ref):
        first = dot(c_own, out_own[:, cols]).astype(BF16).astype(F32)
        second = dot(c_other, out_other[:, cols]).astype(BF16).astype(F32)
        return (x_ref[here, :].astype(F32) + (first + second)).astype(BF16)

    m_own = mid(own_cols, x_own)
    m_other = mid(other_cols, x_other)
    keep = rows - EDGE

    @pl.when(h == 0)
    def _():
        mid_keep[...] = m_own[:keep]
        mid_send[...] = m_other[:keep]

    @pl.when(h == 1)
    def _():
        mid_keep[...] = m_own[EDGE:]
        mid_send[...] = m_other[EDGE:]

    n_own, n_other = normalize_halves(
        m_own.astype(F32), m_other.astype(F32), gain_ref[h], gain_ref[1 - h]
    )
    run = run_ref[here, :]
    valid = run[:, 1:2] > run[:, 0:1]
    glus = []
    for w_ref in (in_own, in_other):
        value = dot(n_own, w_ref[0, own_cols, :]) + dot(n_other, w_ref[0, other_cols, :])
        gate = dot(n_own, w_ref[1, own_cols, :]) + dot(n_other, w_ref[1, other_cols, :])
        glu = value / (1.0 + jnp.exp(-gate))
        glus.append(jnp.where(valid, glu, 0.0).astype(BF16))
    chan = glus[0].shape[1]
    glu_ref[:, :chan] = glus[0]
    glu_ref[:, chan:] = glus[1]

    @pl.when(h == 0)
    def _():
        edge_ref[:, :chan] = glus[1][:EDGE]
        edge_ref[:, chan:] = glus[0][:EDGE]

    @pl.when(h == 1)
    def _():
        edge_ref[:, :chan] = glus[1][rows - EDGE :]
        edge_ref[:, chan:] = glus[0][rows - EDGE :]


def gated(meta, contexts, x_own, x_other, out_own, out_other, gain, in_own, in_other, runs):
    rows = x_own.shape[0] // 2 + EDGE
    half = x_own.shape[1]
    chan = in_own.shape[2]
    vmem = pl.BlockSpec(memory_space=pltpu.VMEM)
    return pl.pallas_call(
        gate_kernel,
        in_specs=[pl.BlockSpec(memory_space=pltpu.SMEM)] + [vmem] * 12,
        out_specs=[vmem] * 4,
        out_shape=[
            jax.ShapeDtypeStruct((rows, 2 * chan), BF16),
            jax.ShapeDtypeStruct((EDGE, 2 * chan), BF16),
            jax.ShapeDtypeStruct((rows - EDGE, half), BF16),
            jax.ShapeDtypeStruct((rows - EDGE, half), BF16),
        ],
        compiler_params=pltpu.CompilerParams(vmem_limit_bytes=VMEM_LIMIT),
        name="gated",
    )(meta, *contexts, x_own, x_other, out_own, out_other,
      gain.reshape(2, 1, half), in_own, in_other, runs)


def conv_kernel(meta, glu_ref, edge_ref, run_ref, dw_own, dw_other, act_ref, ext):
    h = meta[0]
    rows, width = act_ref.shape
    chan = width // 2
    got = glu_ref.shape[0]
    ext[pl.ds(pl.multiple_of((1 - h) * EDGE, EDGE), got), :] = glu_ref[...].astype(F32)
    ext[pl.ds(pl.multiple_of(h * got, EDGE), EDGE), :] = edge_ref[...].astype(F32)
    first = pl.multiple_of(h * rows, rows)
    at = lax.broadcasted_iota(jnp.int32, (rows, 128), 0) + first
    run = run_ref[pl.ds(first, rows), :]
    low = jnp.broadcast_to(run[:, 0:1], (rows, 128)) - at
    high = jnp.broadcast_to(run[:, 1:2], (rows, 128)) - at
    reach = KERNEL // 2
    step = 64
    for base in range(0, rows, step):
        low_b = low[base : base + step]
        high_b = high[base : base + step]
        sums = jnp.zeros((step, 128), F32)
        squares = jnp.zeros((step, 128), F32)
        results = []
        for col in range(0, width, 128):
            dw_ref, c = (dw_own, col) if col < chan else (dw_other, col - chan)
            total = jnp.zeros((step, 128), F32)
            for tap in range(KERNEL):
                shift = tap - reach
                row = base + EDGE + shift
                piece = ext[row : row + step, col : col + 128]
                same = (low_b <= shift) & (high_b > shift)
                total = total + jnp.where(same, piece, 0.0) * dw_ref[tap : tap + 1, c : c + 128]
            sums = sums + total
            squares = squares + total * total
            results.append(total)
        mean = jnp.sum(sums, axis=1, keepdims=True) / CONV_CH
        square = jnp.sum(squares, axis=1, keepdims=True) / CONV_CH
        scale = lax.rsqrt(square - mean * mean + 1e-05)
        for col, total in zip(range(0, width, 128), results):
            dw_ref, c = (dw_own, col) if col < chan else (dw_other, col - chan)
            y = (total - mean) * scale * dw_ref[KERNEL : KERNEL + 1, c : c + 128]
            act_ref[base : base + step, col : col + 128] = (y / (1.0 + jnp.exp(-y))).astype(BF16)


def convolve(meta, glu, edge, runs, taps_own, taps_other):
    rows = glu.shape[0] - EDGE
    width = glu.shape[1]
    vmem = pl.BlockSpec(memory_space=pltpu.VMEM)
    return pl.pallas_call(
        conv_kernel,
        in_specs=[pl.BlockSpec(memory_space=pltpu.SMEM)] + [vmem] * 5,
        out_specs=vmem,
        out_shape=jax.ShapeDtypeStruct((rows, width), BF16),
        scratch_shapes=[pltpu.VMEM((rows + 2 * EDGE, width), F32)],
        compiler_params=pltpu.CompilerParams(vmem_limit_bytes=VMEM_LIMIT),
        name="convolve",
    )(meta, glu, edge, runs, taps_own, taps_other)


def finish_kernel(meta, act_own, act_other, mid_own, mid_other, w_own, w_other, out_ref):
    h = meta[0]
    rows, chan2 = act_own.shape
    chan = chan2 // 2
    half = out_ref.shape[1]
    cols = pl.ds(pl.multiple_of(h * half, half), half)
    w_a = w_own[:, cols]
    w_b = w_other[:, cols]

    def rows_of(act, mid, flip):
        first = dot(act[:, :chan], w_b if flip else w_a).astype(BF16).astype(F32)
        second = dot(act[:, chan:], w_a if flip else w_b).astype(BF16).astype(F32)
        return (mid[...].astype(F32) + (first + second)).astype(BF16)

    out_ref[pl.ds(pl.multiple_of(h * rows, rows), rows), :] = rows_of(act_own, mid_own, False)
    out_ref[pl.ds(pl.multiple_of((1 - h) * rows, rows), rows), :] = rows_of(
        act_other, mid_other, True
    )


def finish(meta, act_own, act_other, mid_own, mid_other, w_own, w_other):
    rows, half = mid_own.shape
    vmem = pl.BlockSpec(memory_space=pltpu.VMEM)
    return pl.pallas_call(
        finish_kernel,
        in_specs=[pl.BlockSpec(memory_space=pltpu.SMEM)] + [vmem] * 6,
        out_specs=vmem,
        out_shape=jax.ShapeDtypeStruct((2 * rows, half), BF16),
        compiler_params=pltpu.CompilerParams(vmem_limit_bytes=VMEM_LIMIT),
        name="finish",
    )(meta, act_own, act_other, mid_own, mid_other, w_own, w_other)


def local(
    blocks,
    frames,
    segment_ids,
    utt_valid,
    attn_gain,
    qkv_weight,
    out_weight,
    conv_gain,
    pointwise_in,
    depthwise,
    mid_gain,
    pointwise_out,
):
    rows = frames.shape[0]

    def swap(value):
        return lax.ppermute(value, "head", [(0, 1), (1, 0)])

    def shift(value, step):
        pairs = [(i, i - step if i % 2 == 0 else i + step) for i in range(blocks)]
        return lax.ppermute(value, "tm", [p for p in pairs if 0 <= p[1] < blocks])

    def exchange(value):
        return lax.ppermute(value, "tm", [(i, i ^ 1) for i in range(blocks)])

    block = lax.axis_index("tm").astype(jnp.int32)
    column = block % 2
    meta = jnp.stack([
        lax.axis_index("head").astype(jnp.int32),
        column,
        block * rows,
        (block + 1 - 2 * column) * rows,
    ])
    other = swap(frames)
    keep, query, send, passed = project(meta, frames, other, attn_gain, qkv_weight)
    far_own = shift(passed, 1)
    pair = exchange(send)
    far_pair = shift(keep, 2)

    segment_ids, _ = lax.optimization_barrier((segment_ids, passed))
    ids = jnp.arange(utt_valid.shape[0], dtype=jnp.int32)
    counts = jnp.sum((segment_ids[None, :] == ids[:, None]).astype(jnp.int32), axis=1)
    counts = lax.all_to_all(
        jnp.broadcast_to(counts[None, :], (blocks, counts.shape[0])), "tm", 0, 0
    )
    pointwise = pointwise_in.transpose(1, 0, 2)
    taps = jnp.concatenate([depthwise, mid_gain[None, :]], axis=0)
    out_weight, pointwise, taps, pointwise_out, _ = lax.optimization_barrier(
        (out_weight, pointwise, taps, pointwise_out, keep)
    )
    pointwise_other = swap(pointwise)
    out_other = swap(out_weight)
    pointwise_out_other = swap(pointwise_out)
    taps_other = swap(taps)
    runs, pair_runs = bounds(meta, counts, utt_valid, rows)

    pair_context = attend(column.reshape(1), pair, pair, keep, far_pair, pair_runs)
    pair_context = exchange(pair_context)
    context = attend((1 - column).reshape(1), query, keep, pair, far_own, runs)
    contexts = (context, pair_context, swap(context), swap(pair_context))
    glu, edge, mid_keep, mid_send = gated(
        meta, contexts, frames, other, out_weight, out_other, conv_gain,
        pointwise, pointwise_other, runs,
    )
    edges = [(2 * i, 2 * (i - 1) + 1) for i in range(1, blocks)]
    edges += [(2 * i + 1, 2 * (i + 1)) for i in range(blocks - 1)]
    edge = lax.ppermute(edge, ("tm", "head"), edges)
    mid_other = swap(mid_send)
    act = convolve(meta, glu, edge, runs, taps, taps_other)
    act_other = swap(act)
    return finish(
        meta, act, act_other, mid_keep, mid_other, pointwise_out, pointwise_out_other
    )


def solution(mesh):
    in_specs = (
        P(("grp", "tm"), "head"),
        P(("grp", "tm")),
        P("grp"),
        P(),
        P(None, None, "head"),
        P("head", None),
        P(),
        P(None, None, "head"),
        P(None, "head"),
        P("head"),
        P("head", None),
    )
    out_specs = P(("grp", "tm"), "head")
    return jax.shard_map(
        functools.partial(local, mesh.shape["tm"]),
        mesh=mesh,
        in_specs=in_specs,
        out_specs=out_specs,
        check_vma=False,
    )
```

time: 67.3 us -> 55.2 us (0.82)
  waiting for transfers between devices: 10.7 us -> 2.29 us
  Pallas kernels: 25 us -> 20.5 us
  local copies, waits for them, and re-layouts: 4.74 us -> 2.44 us
  blocking collectives: 13.4 us -> 14.7 us
  starting transfers between devices: 12.9 us -> 14 us
    pallas_call x2, Pallas kernels: 8.6 us -> 3.43 us  [the longest x1 2.59 us: project(): pl.pallas_call(qkv_kernel, in_specs=[pl.BlockSpec(memory_space=pltpu.SMEM...]
    ppermute x2, waiting for transfers between devices: 4.52 us -> 0.01 us  [exchange(): return lax.ppermute(value, 'tm', [(i, i ^ 1) for i in range(blocks)])]
    ppermute x10 -> x9, waiting for transfers between devices: 6.17 us -> 2.28 us  [swap(): return lax.ppermute(value, 'head', [(0, 1), (1, 0)])]
    unnamed x43 -> x25, local copies, waits for them, and re-layouts: 4.73 us -> 2.44 us
    all_to_all x1, blocking collectives: 13.4 us -> 14.7 us  [local(): lax.all_to_all(jnp.broadcast_to(counts[None, :], (blocks, counts.shape[0]...]
    ppermute x2, starting transfers between devices: 3.24 us -> 4.38 us  [exchange(): return lax.ppermute(value, 'tm', [(i, i ^ 1) for i in range(blocks)])]
    ppermute x10 -> x9, starting transfers between devices: 6.12 us -> 6.33 us  [swap(): return lax.ppermute(value, 'head', [(0, 1), (1, 0)])]
  transfers between devices with their start and end apart: 15 -> 14, of which waited for: 8 -> 3; matrix products, arithmetic and copies ran while one was open for 3% -> 4% of each run, Pallas kernels for 24% -> 28%
where the time goes in v4:
time: 55.2 us; the launch traced here: 54.9 us
  Pallas kernels  20.5 us (37%)
  blocking collectives  14.7 us (27%)
  starting transfers between devices  14 us (25%)
  local copies, waits for them, and re-layouts  2.44 us (4%)
  waiting for transfers between devices  2.29 us (4%)
  other arithmetic  0.82 us (1%)
    all_to_all x1, blocking collectives, local(): lax.all_to_all(jnp.broadcast_to(counts[None, :], (blocks, counts.shape[0]...  14.7 us
    pallas_call x2, Pallas kernels, attend(): pl.pallas_call(attend_kernel, in_specs=[pl.BlockSpec(memory_space=pltpu.S...  7.09 us
    ppermute x9, starting transfers between devices, swap(): return lax.ppermute(value, 'head', [(0, 1), (1, 0)])  6.33 us
    ppermute x2, starting transfers between devices, exchange(): return lax.ppermute(value, 'tm', [(i, i ^ 1) for i in range(blocks)])  4.38 us
    pallas_call x1, Pallas kernels, convolve(): pl.pallas_call(conv_kernel, in_specs=[pl.BlockSpec(memory_space=pltpu.SME...  4.36 us
    pallas_call x1, Pallas kernels, gated(): pl.pallas_call(gate_kernel, in_specs=[pl.BlockSpec(memory_space=pltpu.SME...  3.09 us
    ppermute x2, starting transfers between devices, shift(): return lax.ppermute(value, 'tm', [p for p in pairs if 0 <= p[1] < blocks])  2.66 us
    pallas_call x1, Pallas kernels, project(): pl.pallas_call(qkv_kernel, in_specs=[pl.BlockSpec(memory_space=pltpu.SMEM...  2.59 us
  transfers between devices with their start and end apart: 14, of which 3 were waited for; matrix products, arithmetic and copies ran while one was open for 4% of the time, Pallas kernels for 28%

profile of v4, /device:TPU:0, one launch (start us, length us, event | category | flops | bytes accessed | tf_op | source)
XLA Modules:
  0.0 54.9 jit_solution(18283406289680236503)
XLA Ops:
  0.0 0.5 collective-permute-start
  0.5 1.5 %copy.16 = bf16[1024,2,256]{2,0,1:T(8,128)(2,1)S(1)} copy(bf16[1024,2,256]{2,1,0:T(2,128)(2,1)} %param.18) | data formatting | bytes 2097152 | tf_op args[7]
  2.1 0.6 %pad_maximum_fusion.dw_own = f32[32,256]{1,0:T(8,128)} fusion(f32[1,256]{1,0:T(1,128)S(1)} %bitcast.23, f32[31,256]{1,0:T(8,128)S(1)} %copy-done.9), kind=kLoop, calls=%fused_computation.1 | loop fusion | flops 8192 | bytes 65536 | tf_op jit(solution)/shard_map/concatenate | solution.py:425
  2.8 2.6 %project.1 = (bf16[512,256]{1,0:T(8,128)(2,1)S(1)}, bf16[512,128]{1,0:T(8,128)(2,1)S(1)}, bf16[512,384]{1,0:T(8,128)(2,1)S(1)}, bf16[512,256]{1,0:T(8,128)(2,1)}) custom-call(s32[4]{0:T(128)S(1)} %pad_add_fusion.meta, bf16[512,512]{1,0:T(8,128)(2,1)S(1)} %copy-done, bf16[512,512]{1,0:T(8,128)(2,1)S(1)} %collective-permute-done.other_ref.x_other, ...), custom_call_target="tpu_custom_call" | custom-call | tf_op jit(solution)/shard_map/project/pallas_call | solution.py:72
  5.4 2.9 %collective-permute-start.1 = (bf16[512,384]{1,0:T(8,128)(2,1)S(1)}, bf16[512,384]{1,0:T(8,128)(2,1)S(1)}, u32[]{:S(2)}, u32[]{:S(2)}) collective-permute-start(bf16[512,384]{1,0:T(8,128)(2,1)S(1)} %get-tuple-element.22), channel_id=1, source_target_pairs={{0,2},{2,0},{4,6},{6,4},{8,10},{10,8},{12,14},{14,12},{1,3},{3,1},... | collective-permute-start | bytes 1179656 | tf_op jit(solution)/shard_map/ppermute | solution.py:402
  8.4 1.3 %collective-permute-start.3 = (bf16[512,256]{1,0:T(8,128)(2,1)S(1)}, bf16[512,256]{1,0:T(8,128)(2,1)S(1)}, u32[]{:S(2)}, u32[]{:S(2)}) collective-permute-start(bf16[512,256]{1,0:T(8,128)(2,1)S(1)} %get-tuple-element.21.center.side_a), channel_id=1, source_target_pairs={{2,6},{4,0},{6,10},{8,4},{10,14},{12,8},{3,7},{5,1},{7,11},{9,5},{... | collective-permute-start | bytes 786440 | tf_op jit(solution)/shard_map/ppermute | solution.py:399
  9.8 1.4 %collective-permute-start.2 = (bf16[512,256]{1,0:T(8,128)(2,1)}, bf16[512,256]{1,0:T(8,128)(2,1)}, u32[]{:S(2)}, u32[]{:S(2)}) collective-permute-start(bf16[512,256]{1,0:T(8,128)(2,1)} %get-tuple-element.23), channel_id=1, source_target_pairs={{2,4},{4,2},{6,8},{8,6},{10,12},{12,10},{3,5},{5,3},{7,9},{9,7},{1... | collective-permute-start | bytes 786440 | tf_op jit(solution)/shard_map/ppermute | solution.py:399
  11.3 14.7 %all_to_all.8 = s32[8,1,16]{2,1,0:T(1,128)S(1)} all-to-all(s32[8,1,16]{2,1,0:T(1,128)S(1)} %broadcast_in_dim.4), channel_id=1, replica_groups=mesh['grp'=2,'tm'=8,'head'=2] {'tm'}, dimensions={0} | all-to-all | bytes 1024 | tf_op jit(solution)/shard_map/all_to_all | solution.py:421
  25.9 0.8 %bounds.1 = (s32[512,128]{1,0:T(8,128)S(1)}, s32[512,128]{1,0:T(8,128)S(1)}) custom-call(s32[4]{0:T(128)S(1)} %pad_add_fusion.meta, s32[8,16]{1,0:T(8,128)S(1)} %bitcast.19, s32[1,16]{1,0:T(1,128)S(1)} %bitcast.22), custom_call_target="tpu_custom_call" | custom-call | tf_op jit(solution)/shard_map/bounds/pallas_call | solution.py:113
  26.8 3.3 %attend.3 = bf16[512,128]{1,0:T(8,128)(2,1)} custom-call(s32[1]{0:T(128)} %bitcast.1.a_high, bf16[512,384]{1,0:T(8,128)(2,1)S(1)} %collective-permute-done.1.side_a.query.center, bf16[512,384]{1,0:T(8,128)(2,1)S(1)} %collective-permute-done.1.side_a.query.center, bf16[512,256]{1,0:T(8,128)(2,1)S(1)} %get-tuple-element.21.center.side_a, ...), custom_call_target="tpu_custom_call" | custom-call | tf_op jit(solution)/shard_map/attend/pallas_call | solution.py:185
  30.1 1.4 %collective-permute-start.4 = (bf16[512,128]{1,0:T(8,128)(2,1)}, bf16[512,128]{1,0:T(8,128)(2,1)}, u32[]{:S(2)}, u32[]{:S(2)}) collective-permute-start(bf16[512,128]{1,0:T(8,128)(2,1)} %attend.3), channel_id=1, source_target_pairs={{0,2},{2,0},{4,6},{6,4},{8,10},{10,8},{12,14},{14,12},{1,3},{3,1},... | collective-permute-start | bytes 393224 | tf_op jit(solution)/shard_map/ppermute | solution.py:402
  31.6 0.9 %copy-done.5 = bf16[512,128]{1,0:T(8,128)(2,1)S(1)} copy-done((bf16[512,128]{1,0:T(8,128)(2,1)S(1)}, bf16[512,128]{1,0:T(8,128)(2,1)}, u32[]{:S(2)}) %copy-start.5) | copy-done | bytes 131096
  32.5 3.8 %attend.2.mine_own = bf16[512,128]{1,0:T(8,128)(2,1)S(1)} custom-call(s32[1]{0:T(128)} %bitcast.4.a_high, bf16[512,128]{1,0:T(8,128)(2,1)S(1)} %copy-done.5, bf16[512,256]{1,0:T(8,128)(2,1)S(1)} %get-tuple-element.21.center.side_a, bf16[512,384]{1,0:T(8,128)(2,1)S(1)} %collective-permute-done.1.side_a.query.center, ...), custom_call_target="tpu_custom_call" | custom-call | tf_op jit(solution)/shard_map/attend/pallas_call | solution.py:185
  36.3 0.6 %collective-permute-start.5 = (bf16[512,128]{1,0:T(8,128)(2,1)S(1)}, bf16[512,128]{1,0:T(8,128)(2,1)S(1)}, u32[]{:S(2)}, u32[]{:S(2)}) collective-permute-start(bf16[512,128]{1,0:T(8,128)(2,1)S(1)} %attend.2.mine_own), channel_id=1, source_target_pairs={{0,1},{1,0},{2,3},{3,2},{4,5},{5,4},{6,7},{7,6},{8,9},{9,8},{10,11... | collective-permute-start | bytes 393224 | tf_op jit(solution)/shard_map/ppermute | solution.py:395
  36.9 0.9 %collective-permute-done.5.mine_other = bf16[512,128]{1,0:T(8,128)(2,1)S(1)} collective-permute-done((bf16[512,128]{1,0:T(8,128)(2,1)S(1)}, bf16[512,128]{1,0:T(8,128)(2,1)S(1)}, u32[]{:S(2)}, u32[]{:S(2)}) %collective-permute-start.5) | collective-permute-done | bytes 131104 | tf_op jit(solution)/shard_map/ppermute | solution.py:395
  37.8 0.4 collective-permute-start.10
  38.2 0.2 collective-permute-done.6.pair_other
  38.4 3.1 %gated.1 = (bf16[272,512]{1,0:T(8,128)(2,1)S(1)}, bf16[16,512]{1,0:T(8,128)(2,1)S(1)}, bf16[256,512]{1,0:T(8,128)(2,1)S(1)}, bf16[256,512]{1,0:T(8,128)(2,1)S(1)}) custom-call(s32[4]{0:T(128)S(1)} %pad_add_fusion.meta, bf16[512,128]{1,0:T(8,128)(2,1)S(1)} %attend.2.mine_own, bf16[512,128]{1,0:T(8,128)(2,1)} %collective-permute-done.4.pair_own, ...), custom_call_target="tpu_custom_call" | custom-call | tf_op jit(solution)/shard_map/gated/pallas_call | solution.py:273
  41.5 0.7 %collective-permute-start.9 = (bf16[16,512]{1,0:T(8,128)(2,1)S(1)}, bf16[16,512]{1,0:T(8,128)(2,1)S(1)}, u32[]{:S(2)}, u32[]{:S(2)}) collective-permute-start(bf16[16,512]{1,0:T(8,128)(2,1)S(1)} %get-tuple-element.30), channel_id=1, source_target_pairs={{2,1},{4,3},{6,5},{8,7},{10,9},{12,11},{14,13},{1,2},{3,4},{5,6},{... | collective-permute-start | bytes 49160 | tf_op jit(solution)/shard_map/ppermute | solution.py:445
  42.2 1.8 %collective-permute-start.12 = (bf16[256,512]{1,0:T(8,128)(2,1)S(1)}, bf16[256,512]{1,0:T(8,128)(2,1)S(1)}, u32[]{:S(2)}, u32[]{:S(2)}) collective-permute-start(bf16[256,512]{1,0:T(8,128)(2,1)S(1)} %get-tuple-element.33), channel_id=1, source_target_pairs={{0,1},{1,0},{2,3},{3,2},{4,5},{5,4},{6,7},{7,6},{8,9},{9,8},{10,11... | collective-permute-start | bytes 786440 | tf_op jit(solution)/shard_map/ppermute | solution.py:395
  44.0 4.4 %convolve.1.act_own = bf16[256,512]{1,0:T(8,128)(2,1)S(1)} custom-call(s32[4]{0:T(128)S(1)} %pad_add_fusion.meta, bf16[272,512]{1,0:T(8,128)(2,1)S(1)} %get-tuple-element.29.glu_ref, bf16[16,512]{1,0:T(8,128)(2,1)S(1)} %collective-permute-done.9.edge_ref, s32[512,128]{1,0:T(8,128)S(1)} %get-tuple-element.25.run_ref, f32[32,256]{1,0:T(8,128)S(1)} %copy-done.3, ...), custom_call_target="tpu_custom_call" | custom-call | tf_op jit(solution)/shard_map/convolve/pallas_call | solution.py:334
  48.4 2.8 %collective-permute-start.11 = (bf16[256,512]{1,0:T(8,128)(2,1)S(1)}, bf16[256,512]{1,0:T(8,128)(2,1)S(1)}, u32[]{:S(2)}, u32[]{:S(2)}) collective-permute-start(bf16[256,512]{1,0:T(8,128)(2,1)S(1)} %convolve.1.act_own), channel_id=1, source_target_pairs={{0,1},{1,0},{2,3},{3,2},{4,5},{5,4},{6,7},{7,6},{8,9},{9,8},{10,11... | collective-permute-start | bytes 786440 | tf_op jit(solution)/shard_map/ppermute | solution.py:395
  51.2 1.2 %collective-permute-done.11.act_other = bf16[256,512]{1,0:T(8,128)(2,1)S(1)} collective-permute-done((bf16[256,512]{1,0:T(8,128)(2,1)S(1)}, bf16[256,512]{1,0:T(8,128)(2,1)S(1)}, u32[]{:S(2)}, u32[]{:S(2)}) %collective-permute-start.11) | collective-permute-done | bytes 262176 | tf_op jit(solution)/shard_map/ppermute | solution.py:395
  52.4 2.5 %finish.1 = bf16[512,512]{1,0:T(8,128)(2,1)} custom-call(s32[4]{0:T(128)S(1)} %pad_add_fusion.meta, bf16[256,512]{1,0:T(8,128)(2,1)S(1)} %convolve.1.act_own, bf16[256,512]{1,0:T(8,128)(2,1)S(1)} %collective-permute-done.11.act_other, bf16[256,512]{1,0:T(8,128)(2,1)S(1)} %get-tuple-element.32.mid_own, ...), custom_call_target="tpu_custom_call" | custom-call | tf_op jit(solution)/shard_map/finish/pallas_call | solution.py:368
  (41 shorter events, 0.5 us)
Async XLA Ops:
  0.0 2.8 %copy-start = (bf16[512,512]{1,0:T(8,128)(2,1)S(1)}, bf16[512,512]{1,0:T(8,128)(2,1)}, u32[]{:S(2)}) copy-start(bf16[512,512]{1,0:T(8,128)(2,1)} %x_own.1) | copy-start | bytes 1572868
  0.0 2.1 %copy-start.9 = (f32[31,256]{1,0:T(8,128)S(1)}, f32[31,256]{1,0:T(8,128)}, u32[]{:S(2)}) copy-start(f32[31,256]{1,0:T(8,128)} %param.19) | copy-start | bytes 95236
  0.0 2.8 %copy-start.6 = (f32[1024]{0:T(1024)S(1)}, f32[1024]{0:T(1024)}, u32[]{:S(2)}) copy-start(f32[1024]{0:T(1024)} %param.14) | copy-start | bytes 12292
  0.0 2.8 %collective-permute-start = (bf16[512,512]{1,0:T(8,128)(2,1)}, bf16[512,512]{1,0:T(8,128)(2,1)S(1)}, u32[]{:S(2)}, u32[]{:S(2)}) collective-permute-start(bf16[512,512]{1,0:T(8,128)(2,1)} %x_own.1), channel_id=1, source_target_pairs={{0,1},{1,0},{2,3},{3,2},{4,5},{5,4},{6,7},{7,6},{8,9},{9,8},{10,11... | collective-permute-start | bytes 1572872 | tf_op jit(solution)/shard_map/ppermute | solution.py:395
  0.5 2.2 %copy-start.1 = (bf16[1024,3,256]{2,0,1:T(8,128)(2,1)S(1)}, bf16[1024,3,256]{2,0,1:T(8,128)(2,1)}, u32[]{:S(2)}) copy-start(bf16[1024,3,256]{2,0,1:T(8,128)(2,1)} %param.15) | copy-start | bytes 4718596
  2.0 7.6 %copy-start.2 = (bf16[256,1024]{1,0:T(8,128)(2,1)S(1)}, bf16[256,1024]{1,0:T(8,128)(2,1)}, u32[]{:S(2)}) copy-start(bf16[256,1024]{1,0:T(8,128)(2,1)} %out_own) | copy-start | bytes 1572868
  2.0 9.1 %copy-start.10 = (s32[512]{0:T(512)S(1)}, s32[512]{0:T(512)}, u32[]{:S(2)}) copy-start(s32[512]{0:T(512)} %param.12) | copy-start | bytes 6148
  2.0 23.9 %copy-start.8 = (s32[16]{0:T(128)S(1)}, s32[16]{0:T(128)}, u32[]{:S(2)}) copy-start(s32[16]{0:T(128)} %param.13) | copy-start | bytes 196
  5.4 24.7 %copy-start.4 = (bf16[512,128]{1,0:T(8,128)(2,1)}, bf16[512,128]{1,0:T(8,128)(2,1)S(1)}, u32[]{:S(2)}) copy-start(bf16[512,128]{1,0:T(8,128)(2,1)S(1)} %get-tuple-element.20.query) | copy-start | bytes 393220
  5.4 33.0 %collective-permute-start.8 = (bf16[2,1024,256]{2,1,0:T(8,128)(2,1)S(1)}, bf16[2,1024,256]{2,1,0:T(8,128)(2,1)}, u32[]{:S(2)}, u32[]{:S(2)}) collective-permute-start(bf16[2,1024,256]{2,1,0:T(8,128)(2,1)S(1)} %bitcast.16), channel_id=1, source_target_pairs={{0,1},{1,0},{2,3},{3,2},{4,5},{5,4},{6,7},{7,6},{8,9},{9,8},{10,11... | collective-permute-start | bytes 3145736 | tf_op jit(solution)/shard_map/ppermute | solution.py:395
  5.4 21.3 %collective-permute-start.1 = (bf16[512,384]{1,0:T(8,128)(2,1)S(1)}, bf16[512,384]{1,0:T(8,128)(2,1)S(1)}, u32[]{:S(2)}, u32[]{:S(2)}) collective-permute-start(bf16[512,384]{1,0:T(8,128)(2,1)S(1)} %get-tuple-element.22), channel_id=1, source_target_pairs={{0,2},{2,0},{4,6},{6,4},{8,10},{10,8},{12,14},{14,12},{1,3},{3,1},... | collective-permute-start | bytes 1179656 | tf_op jit(solution)/shard_map/ppermute | solution.py:402
  8.4 18.4 %collective-permute-start.3 = (bf16[512,256]{1,0:T(8,128)(2,1)S(1)}, bf16[512,256]{1,0:T(8,128)(2,1)S(1)}, u32[]{:S(2)}, u32[]{:S(2)}) collective-permute-start(bf16[512,256]{1,0:T(8,128)(2,1)S(1)} %get-tuple-element.21.center.side_a), channel_id=1, source_target_pairs={{2,6},{4,0},{6,10},{8,4},{10,14},{12,8},{3,7},{5,1},{7,11},{9,5},{... | collective-permute-start | bytes 786440 | tf_op jit(solution)/shard_map/ppermute | solution.py:399
  9.7 28.5 %collective-permute-start.7 = (bf16[256,1024]{1,0:T(8,128)(2,1)S(1)}, bf16[256,1024]{1,0:T(8,128)(2,1)}, u32[]{:S(2)}, u32[]{:S(2)}) collective-permute-start(bf16[256,1024]{1,0:T(8,128)(2,1)S(1)} %copy-done.2), channel_id=1, source_target_pairs={{0,1},{1,0},{2,3},{3,2},{4,5},{5,4},{6,7},{7,6},{8,9},{9,8},{10,11... | collective-permute-start | bytes 1572872 | tf_op jit(solution)/shard_map/ppermute | solution.py:395
  9.8 21.8 %collective-permute-start.2 = (bf16[512,256]{1,0:T(8,128)(2,1)}, bf16[512,256]{1,0:T(8,128)(2,1)}, u32[]{:S(2)}, u32[]{:S(2)}) collective-permute-start(bf16[512,256]{1,0:T(8,128)(2,1)} %get-tuple-element.23), channel_id=1, source_target_pairs={{2,4},{4,2},{6,8},{8,6},{10,12},{12,10},{3,5},{5,3},{7,9},{9,7},{1... | collective-permute-start | bytes 786440 | tf_op jit(solution)/shard_map/ppermute | solution.py:399
  26.8 11.6 %copy-start.7 = (f32[1024]{0:T(1024)S(1)}, f32[1024]{0:T(1024)}, u32[]{:S(2)}) copy-start(f32[1024]{0:T(1024)} %param.17) | copy-start | bytes 12292
  30.1 6.7 %collective-permute-start.4 = (bf16[512,128]{1,0:T(8,128)(2,1)}, bf16[512,128]{1,0:T(8,128)(2,1)}, u32[]{:S(2)}, u32[]{:S(2)}) collective-permute-start(bf16[512,128]{1,0:T(8,128)(2,1)} %attend.3), channel_id=1, source_target_pairs={{0,2},{2,0},{4,6},{6,4},{8,10},{10,8},{12,14},{14,12},{1,3},{3,1},... | collective-permute-start | bytes 393224 | tf_op jit(solution)/shard_map/ppermute | solution.py:402
  31.6 19.6 %collective-permute-start.13 = (bf16[256,1024]{1,0:T(8,128)(2,1)}, bf16[256,1024]{1,0:T(8,128)(2,1)}, u32[]{:S(2)}, u32[]{:S(2)}) collective-permute-start(bf16[256,1024]{1,0:T(8,128)(2,1)} %w_own), channel_id=1, source_target_pairs={{0,1},{1,0},{2,3},{3,2},{4,5},{5,4},{6,7},{7,6},{8,9},{9,8},{10,11... | collective-permute-start | bytes 1572872 | tf_op jit(solution)/shard_map/ppermute | solution.py:395
  36.3 1.6 %collective-permute-start.5 = (bf16[512,128]{1,0:T(8,128)(2,1)S(1)}, bf16[512,128]{1,0:T(8,128)(2,1)S(1)}, u32[]{:S(2)}, u32[]{:S(2)}) collective-permute-start(bf16[512,128]{1,0:T(8,128)(2,1)S(1)} %attend.2.mine_own), channel_id=1, source_target_pairs={{0,1},{1,0},{2,3},{3,2},{4,5},{5,4},{6,7},{7,6},{8,9},{9,8},{10,11... | collective-permute-start | bytes 393224 | tf_op jit(solution)/shard_map/ppermute | solution.py:395
  36.8 1.6 %collective-permute-start.6 = (bf16[512,128]{1,0:T(8,128)(2,1)}, bf16[512,128]{1,0:T(8,128)(2,1)S(1)}, u32[]{:S(2)}, u32[]{:S(2)}) collective-permute-start(bf16[512,128]{1,0:T(8,128)(2,1)} %collective-permute-done.4.pair_own), channel_id=1, source_target_pairs={{0,1},{1,0},{2,3},{3,2},{4,5},{5,4},{6,7},{7,6},{8,9},{9,8},{10,11... | collective-permute-start | bytes 393224 | tf_op jit(solution)/shard_map/ppermute | solution.py:395
  37.8 6.2 %collective-permute-start.10 = (f32[32,256]{1,0:T(8,128)}, f32[32,256]{1,0:T(8,128)S(1)}, u32[]{:S(2)}, u32[]{:S(2)}) collective-permute-start(f32[32,256]{1,0:T(8,128)} %pad_maximum_fusion.dw_own), channel_id=1, source_target_pairs={{0,1},{1,0},{2,3},{3,2},{4,5},{5,4},{6,7},{7,6},{8,9},{9,8},{10,11... | collective-permute-start | bytes 98312 | tf_op jit(solution)/shard_map/ppermute | solution.py:395
  38.4 5.6 %copy-start.3 = (f32[32,256]{1,0:T(8,128)S(1)}, f32[32,256]{1,0:T(8,128)}, u32[]{:S(2)}) copy-start(f32[32,256]{1,0:T(8,128)} %pad_maximum_fusion.dw_own) | copy-start | bytes 98308
  41.5 2.5 %collective-permute-start.9 = (bf16[16,512]{1,0:T(8,128)(2,1)S(1)}, bf16[16,512]{1,0:T(8,128)(2,1)S(1)}, u32[]{:S(2)}, u32[]{:S(2)}) collective-permute-start(bf16[16,512]{1,0:T(8,128)(2,1)S(1)} %get-tuple-element.30), channel_id=1, source_target_pairs={{2,1},{4,3},{6,5},{8,7},{10,9},{12,11},{14,13},{1,2},{3,4},{5,6},{... | collective-permute-start | bytes 49160 | tf_op jit(solution)/shard_map/ppermute | solution.py:445
  42.2 9.0 %collective-permute-start.12 = (bf16[256,512]{1,0:T(8,128)(2,1)S(1)}, bf16[256,512]{1,0:T(8,128)(2,1)S(1)}, u32[]{:S(2)}, u32[]{:S(2)}) collective-permute-start(bf16[256,512]{1,0:T(8,128)(2,1)S(1)} %get-tuple-element.33), channel_id=1, source_target_pairs={{0,1},{1,0},{2,3},{3,2},{4,5},{5,4},{6,7},{7,6},{8,9},{9,8},{10,11... | collective-permute-start | bytes 786440 | tf_op jit(solution)/shard_map/ppermute | solution.py:395
  48.4 4.0 %collective-permute-start.11 = (bf16[256,512]{1,0:T(8,128)(2,1)S(1)}, bf16[256,512]{1,0:T(8,128)(2,1)S(1)}, u32[]{:S(2)}, u32[]{:S(2)}) collective-permute-start(bf16[256,512]{1,0:T(8,128)(2,1)S(1)} %convolve.1.act_own), channel_id=1, source_target_pairs={{0,1},{1,0},{2,3},{3,2},{4,5},{5,4},{6,7},{7,6},{8,9},{9,8},{10,11... | collective-permute-start | bytes 786440 | tf_op jit(solution)/shard_map/ppermute | solution.py:395
  (2 other events, 3.0 us)

commit v5 on v4

--- a/solution.py
+++ b/solution.py
@@ -13,11 +13,18 @@
 KERNEL = 31
 WIN = 512
 EDGE = 16
+SENT = 64
 NEG = -1e30
 EXP_SCALE = HEAD_DIM ** (-0.5) * math.log2(math.e)
 F32 = jnp.float32
 BF16 = jnp.bfloat16
 VMEM_LIMIT = 16 * 1024 * 1024
+
+
+def weight(microseconds):
+    return pl.CostEstimate(
+        flops=int(microseconds * 1.15e9), bytes_accessed=0, transcendentals=0
+    )
 
 
 def dot(a, b):
@@ -65,9 +72,9 @@
                 query_ref[here, :] = keep
 
 
-def project(meta, frames, other, gain, weight):
+def project(meta, frames, other, gain, qkv):
     rows, half = frames.shape
-    width = weight.shape[2]
+    width = qkv.shape[2]
     vmem = pl.BlockSpec(memory_space=pltpu.VMEM)
     return pl.pallas_call(
         qkv_kernel,
@@ -80,9 +87,10 @@
             jax.ShapeDtypeStruct((rows, width), BF16),
         ],
         compiler_params=pltpu.CompilerParams(vmem_limit_bytes=VMEM_LIMIT),
+        cost_estimate=weight(3),
         name="project",
     )(meta, frames, other, gain.reshape(2, 1, half),
-      weight.transpose(1, 0, 2).reshape(3, 2, half, width))
+      qkv.transpose(1, 0, 2).reshape(3, 2, half, width))
 
 
 def bounds_kernel(meta, counts, valid, own_ref, pair_ref):
@@ -116,6 +124,7 @@
         out_specs=[vmem] * 2,
         out_shape=[jax.ShapeDtypeStruct((rows, 128), jnp.int32)] * 2,
         compiler_params=pltpu.CompilerParams(vmem_limit_bytes=VMEM_LIMIT),
+        cost_estimate=weight(1),
         name="bounds",
     )(meta, counts, valid.reshape(1, -1))
 
@@ -188,6 +197,7 @@
         out_specs=vmem,
         out_shape=jax.ShapeDtypeStruct((rows, width), BF16),
         compiler_params=pltpu.CompilerParams(vmem_limit_bytes=VMEM_LIMIT),
+        cost_estimate=weight(3),
         name="attend",
     )(a_high, query, center, side_a, side_b, runs)
 
@@ -256,13 +266,13 @@
 
     @pl.when(h == 0)
     def _():
-        edge_ref[:, :chan] = glus[1][:EDGE]
-        edge_ref[:, chan:] = glus[0][:EDGE]
+        edge_ref[:, :chan] = glus[1][:SENT]
+        edge_ref[:, chan:] = glus[0][:SENT]
 
     @pl.when(h == 1)
     def _():
-        edge_ref[:, :chan] = glus[1][rows - EDGE :]
-        edge_ref[:, chan:] = glus[0][rows - EDGE :]
+        edge_ref[:, :chan] = glus[1][rows - SENT :]
+        edge_ref[:, chan:] = glus[0][rows - SENT :]
 
 
 def gated(meta, contexts, x_own, x_other, out_own, out_other, gain, in_own, in_other, runs):
@@ -276,103 +286,166 @@
         out_specs=[vmem] * 4,
         out_shape=[
             jax.ShapeDtypeStruct((rows, 2 * chan), BF16),
-            jax.ShapeDtypeStruct((EDGE, 2 * chan), BF16),
+            jax.ShapeDtypeStruct((SENT, 2 * chan), BF16),
             jax.ShapeDtypeStruct((rows - EDGE, half), BF16),
             jax.ShapeDtypeStruct((rows - EDGE, half), BF16),
         ],
         compiler_params=pltpu.CompilerParams(vmem_limit_bytes=VMEM_LIMIT),
+        cost_estimate=weight(3),
         name="gated",
     )(meta, *contexts, x_own, x_other, out_own, out_other,
       gain.reshape(2, 1, half), in_own, in_other, runs)
 
 
-def conv_kernel(meta, glu_ref, edge_ref, run_ref, dw_own, dw_other, act_ref, ext):
+def conv_rows(shifted, low, high, taps, out_ref, rows):
+    width = out_ref.shape[1]
+    chan = width // 2
+    reach = KERNEL // 2
+    step = min(32, rows)
+    cols = range(0, width, 128)
+    weights = [
+        [
+            (taps[0] if col < chan else taps[1])[tap : tap + 1, col % chan : col % chan + 128]
+            for col in cols
+        ]
+        for tap in range(KERNEL + 1)
+    ]
+    for base in range(0, rows, step):
+        totals = [jnp.zeros((step, 128), F32) for _ in cols]
+        for tap in range(KERNEL):
+            shift = tap - reach
+            same = (low[base : base + step] <= shift) & (high[base : base + step] > shift)
+            row = base + EDGE + shift
+            first = row - row % 8
+            for index, col in enumerate(cols):
+                piece = shifted[row % 8, first : first + step, col : col + 128]
+                totals[index] = totals[index] + jnp.where(same, piece, 0.0) * weights[tap][index]
+        mean = jnp.sum(sum(totals), axis=1, keepdims=True) / CONV_CH
+        square = jnp.sum(sum(t * t for t in totals), axis=1, keepdims=True) / CONV_CH
+        scale = lax.rsqrt(square - mean * mean + 1e-05)
+        for index, col in enumerate(cols):
+            y = (totals[index] - mean) * scale * weights[KERNEL][index]
+            out_ref[base : base + step, col : col + 128] = (y / (1.0 + jnp.exp(-y))).astype(BF16)
+
+
+def run_offsets(run_ref, first, rows):
+    run = run_ref[pl.ds(first, rows), :]
+    at = lax.broadcasted_iota(jnp.int32, (rows, 128), 0) + first
+    low = jnp.broadcast_to(run[:, 0:1], (rows, 128)) - at
+    high = jnp.broadcast_to(run[:, 1:2], (rows, 128)) - at
+    return low, high
+
+
+def conv_kernel(meta, glu_ref, run_ref, taps_own, taps_other, act_ref, ext, shifted):
     h = meta[0]
     rows, width = act_ref.shape
-    chan = width // 2
     got = glu_ref.shape[0]
+    ext[pl.ds(pl.multiple_of(h * got, EDGE), EDGE), :] = jnp.zeros((EDGE, width), F32)
     ext[pl.ds(pl.multiple_of((1 - h) * EDGE, EDGE), got), :] = glu_ref[...].astype(F32)
-    ext[pl.ds(pl.multiple_of(h * got, EDGE), EDGE), :] = edge_ref[...].astype(F32)
-    first = pl.multiple_of(h * rows, rows)
-    at = lax.broadcasted_iota(jnp.int32, (rows, 128), 0) + first
-    run = run_ref[pl.ds(first, rows), :]
-    low = jnp.broadcast_to(run[:, 0:1], (rows, 128)) - at
-    high = jnp.broadcast_to(run[:, 1:2], (rows, 128)) - at
-    reach = KERNEL // 2
-    step = 64
-    for base in range(0, rows, step):
-        low_b = low[base : base + step]
-        high_b = high[base : base + step]
-        sums = jnp.zeros((step, 128), F32)
-        squares = jnp.zeros((step, 128), F32)
-        results = []
-        for col in range(0, width, 128):
-            dw_ref, c = (dw_own, col) if col < chan else (dw_other, col - chan)
-            total = jnp.zeros((step, 128), F32)
-            for tap in range(KERNEL):
-                shift = tap - reach
-                row = base + EDGE + shift
-                piece = ext[row : row + step, col : col + 128]
-                same = (low_b <= shift) & (high_b > shift)
-                total = total + jnp.where(same, piece, 0.0) * dw_ref[tap : tap + 1, c : c + 128]
-            sums = sums + total
-            squares = squares + total * total
-            results.append(total)
-        mean = jnp.sum(sums, axis=1, keepdims=True) / CONV_CH
-        square = jnp.sum(squares, axis=1, keepdims=True) / CONV_CH
-        scale = lax.rsqrt(square - mean * mean + 1e-05)
-        for col, total in zip(range(0, width, 128), results):
-            dw_ref, c = (dw_own, col) if col < chan else (dw_other, col - chan)
-            y = (total - mean) * scale * dw_ref[KERNEL : KERNEL + 1, c : c + 128]
-            act_ref[base : base + step, col : col + 128] = (y / (1.0 + jnp.exp(-y))).astype(BF16)
-
-
-def convolve(meta, glu, edge, runs, taps_own, taps_other):
+    size = shifted.shape[1]
+    for s in range(8):
+        shifted[s] = ext[s : s + size, :]
+    low, high = run_offsets(run_ref, pl.multiple_of(h * rows, rows), rows)
+    conv_rows(shifted, low, high, (taps_own, taps_other), act_ref, rows)
+
+
+def convolve(meta, glu, runs, taps_own, taps_other):
     rows = glu.shape[0] - EDGE
     width = glu.shape[1]
     vmem = pl.BlockSpec(memory_space=pltpu.VMEM)
     return pl.pallas_call(
         conv_kernel,
+        in_specs=[pl.BlockSpec(memory_space=pltpu.SMEM)] + [vmem] * 4,
+        out_specs=vmem,
+        out_shape=jax.ShapeDtypeStruct((rows, width), BF16),
+        scratch_shapes=[
+            pltpu.VMEM((rows + 2 * EDGE, width), F32),
+            pltpu.VMEM((8, rows + 2 * EDGE - 8, width), F32),
+        ],
+        compiler_params=pltpu.CompilerParams(vmem_limit_bytes=VMEM_LIMIT),
+        cost_estimate=weight(3),
+        name="convolve",
+    )(meta, glu, runs, taps_own, taps_other)
+
+
+def rim_kernel(meta, glu_ref, edge_ref, run_ref, taps_own, taps_other, act_ref, ext, shifted):
+    h = meta[0]
+    got = glu_ref.shape[0]
+    near = 2 * EDGE
+    ext[pl.ds(pl.multiple_of(h * near, EDGE), EDGE), :] = edge_ref[
+        pl.ds(pl.multiple_of((1 - h) * (SENT - EDGE), EDGE), EDGE), :
+    ].astype(F32)
+    ext[pl.ds(pl.multiple_of((1 - h) * EDGE, EDGE), near), :] = glu_ref[
+        pl.ds(pl.multiple_of(h * (got - near), EDGE), near), :
+    ].astype(F32)
+    size = shifted.shape[1]
+    for s in range(8):
+        shifted[s] = ext[s : s + size, :]
+    first = pl.multiple_of(h * (run_ref.shape[0] - EDGE), EDGE)
+    low, high = run_offsets(run_ref, first, EDGE)
+    conv_rows(shifted, low, high, (taps_own, taps_other), act_ref, EDGE)
+
+
+def rim(meta, glu, edge, runs, taps_own, taps_other):
+    width = glu.shape[1]
+    vmem = pl.BlockSpec(memory_space=pltpu.VMEM)
+    return pl.pallas_call(
+        rim_kernel,
         in_specs=[pl.BlockSpec(memory_space=pltpu.SMEM)] + [vmem] * 5,
         out_specs=vmem,
-        out_shape=jax.ShapeDtypeStruct((rows, width), BF16),
-        scratch_shapes=[pltpu.VMEM((rows + 2 * EDGE, width), F32)],
-        compiler_params=pltpu.CompilerParams(vmem_limit_bytes=VMEM_LIMIT),
-        name="convolve",
+        out_shape=jax.ShapeDtypeStruct((EDGE, width), BF16),
+        scratch_shapes=[
+            pltpu.VMEM((3 * EDGE, width), F32),
+            pltpu.VMEM((8, 3 * EDGE - 8, width), F32),
+        ],
+        compiler_params=pltpu.CompilerParams(vmem_limit_bytes=VMEM_LIMIT),
+        cost_estimate=weight(1),
+        name="rim",
     )(meta, glu, edge, runs, taps_own, taps_other)
 
 
-def finish_kernel(meta, act_own, act_other, mid_own, mid_other, w_own, w_other, out_ref):
+def last_product(act_ref, rim_ref, rim_at, mid_ref, w_first, w_second, cols, act):
+    chan = act_ref.shape[1] // 2
+    act[...] = act_ref[...]
+    act[pl.ds(rim_at, EDGE), :] = rim_ref[...]
+    first = dot(act[:, :chan], w_first[:, cols]).astype(BF16).astype(F32)
+    second = dot(act[:, chan:], w_second[:, cols]).astype(BF16).astype(F32)
+    return (mid_ref[...].astype(F32) + (first + second)).astype(BF16)
+
+
+def finish_own_kernel(meta, act_ref, rim_ref, mid_ref, w_own, w_other, out_ref, act):
     h = meta[0]
-    rows, chan2 = act_own.shape
-    chan = chan2 // 2
-    half = out_ref.shape[1]
-    cols = pl.ds(pl.multiple_of(h * half, half), half)
-    w_a = w_own[:, cols]
-    w_b = w_other[:, cols]
-
-    def rows_of(act, mid, flip):
-        first = dot(act[:, :chan], w_b if flip else w_a).astype(BF16).astype(F32)
-        second = dot(act[:, chan:], w_a if flip else w_b).astype(BF16).astype(F32)
-        return (mid[...].astype(F32) + (first + second)).astype(BF16)
-
-    out_ref[pl.ds(pl.multiple_of(h * rows, rows), rows), :] = rows_of(act_own, mid_own, False)
-    out_ref[pl.ds(pl.multiple_of((1 - h) * rows, rows), rows), :] = rows_of(
-        act_other, mid_other, True
-    )
-
-
-def finish(meta, act_own, act_other, mid_own, mid_other, w_own, w_other):
-    rows, half = mid_own.shape
-    vmem = pl.BlockSpec(memory_space=pltpu.VMEM)
-    return pl.pallas_call(
-        finish_kernel,
-        in_specs=[pl.BlockSpec(memory_space=pltpu.SMEM)] + [vmem] * 6,
+    rows, half = out_ref.shape
+    out_ref[...] = last_product(
+        act_ref, rim_ref, pl.multiple_of(h * (rows - EDGE), EDGE), mid_ref, w_own, w_other,
+        pl.ds(pl.multiple_of(h * half, half), half), act,
+    )
+
+
+def finish_kernel(meta, act_ref, rim_ref, mid_ref, w_own, w_other, done_ref, out_ref, act):
+    h = meta[0]
+    rows, half = done_ref.shape
+    out_ref[pl.ds(pl.multiple_of(h * rows, rows), rows), :] = done_ref[...]
+    out_ref[pl.ds(pl.multiple_of((1 - h) * rows, rows), rows), :] = last_product(
+        act_ref, rim_ref, pl.multiple_of((1 - h) * (rows - EDGE), EDGE), mid_ref, w_other, w_own,
+        pl.ds(pl.multiple_of(h * half, half), half), act,
+    )
+
+
+def finish(meta, act, rim_act, mid, w_own, w_other, done=None):
+    rows, half = mid.shape
+    vmem = pl.BlockSpec(memory_space=pltpu.VMEM)
+    args = (act, rim_act, mid, w_own, w_other) + (() if done is None else (done,))
+    return pl.pallas_call(
+        finish_own_kernel if done is None else finish_kernel,
+        in_specs=[pl.BlockSpec(memory_space=pltpu.SMEM)] + [vmem] * len(args),
         out_specs=vmem,
-        out_shape=jax.ShapeDtypeStruct((2 * rows, half), BF16),
-        compiler_params=pltpu.CompilerParams(vmem_limit_bytes=VMEM_LIMIT),
-        name="finish",
-    )(meta, act_own, act_other, mid_own, mid_other, w_own, w_other)
+        out_shape=jax.ShapeDtypeStruct((rows if done is None else 2 * rows, half), BF16),
+        scratch_shapes=[pltpu.VMEM(act.shape, BF16)],
+        compiler_params=pltpu.CompilerParams(vmem_limit_bytes=VMEM_LIMIT),
+        cost_estimate=weight(1.2),
+        name="finish_own" if done is None else "finish",
+    )(meta, *args)
 
 
 def local(
@@ -422,10 +495,10 @@
         jnp.broadcast_to(counts[None, :], (blocks, counts.shape[0])), "tm", 0, 0
     )
     pointwise = pointwise_in.transpose(1, 0, 2)
+    out_weight, pointwise, depthwise, mid_gain, pointwise_out, _ = lax.optimization_barrier(
+        (out_weight, pointwise, depthwise, mid_gain, pointwise_out, keep)
+    )
     taps = jnp.concatenate([depthwise, mid_gain[None, :]], axis=0)
-    out_weight, pointwise, taps, pointwise_out, _ = lax.optimization_barrier(
-        (out_weight, pointwise, taps, pointwise_out, keep)
-    )
     pointwise_other = swap(pointwise)
     out_other = swap(out_weight)
     pointwise_out_other = swap(pointwise_out)
@@ -436,6 +509,9 @@
     pair_context = exchange(pair_context)
     context = attend((1 - column).reshape(1), query, keep, pair, far_own, runs)
     contexts = (context, pair_context, swap(context), swap(pair_context))
+    contexts, pointwise_out_other, taps_other = lax.optimization_barrier(
+        (contexts, pointwise_out_other, taps_other)
+    )
     glu, edge, mid_keep, mid_send = gated(
         meta, contexts, frames, other, out_weight, out_other, conv_gain,
         pointwise, pointwise_other, runs,
@@ -444,10 +520,13 @@
     edges += [(2 * i + 1, 2 * (i + 1)) for i in range(blocks - 1)]
     edge = lax.ppermute(edge, ("tm", "head"), edges)
     mid_other = swap(mid_send)
-    act = convolve(meta, glu, edge, runs, taps, taps_other)
+    act = convolve(meta, glu, runs, taps, taps_other)
     act_other = swap(act)
+    rim_act = rim(meta, glu, edge, runs, taps, taps_other)
+    rim_other = swap(rim_act)
+    done = finish(meta, act, rim_act, mid_keep, pointwise_out, pointwise_out_other)
     return finish(
-        meta, act, act_other, mid_keep, mid_other, pointwise_out, pointwise_out_other
+        meta, act_other, rim_other, mid_other, pointwise_out, pointwise_out_other, done
     )
 
 

time: 55.2 us -> 55.7 us (level)
  blocking collectives: 14.7 us -> 0 us
  waiting for transfers between devices: 2.29 us -> 9.11 us
  starting transfers between devices: 14 us -> 20.5 us
  local copies, waits for them, and re-layouts: 2.44 us -> 4.87 us
  other arithmetic: 0.82 us -> 0.2 us
    all_to_all x1 -> x0, blocking collectives: 14.7 us -> none  [local(): lax.all_to_all(jnp.broadcast_to(counts[None, :], (blocks, counts.shape[0]...]
    all_to_all x0 -> x1, starting transfers between devices: none -> 8.06 us  [local(): lax.all_to_all(jnp.broadcast_to(counts[None, :], (blocks, counts.shape[0]...]
    all_to_all x0 -> x1, waiting for transfers between devices: none -> 6.15 us  [local(): lax.all_to_all(jnp.broadcast_to(counts[None, :], (blocks, counts.shape[0]...]
    unnamed x25 -> x29, local copies, waits for them, and re-layouts: 2.44 us -> 4.28 us
    ppermute x9 -> x10, starting transfers between devices: 6.33 us -> 4.84 us  [swap(): return lax.ppermute(value, 'head', [(0, 1), (1, 0)])]
    pallas_call x1 -> x3, Pallas kernels: 2.49 us -> 3.43 us  [the longest x2 2.59 us: finish(): pl.pallas_call(finish_own_kernel if done is None else finish_kernel, in_s...]
    pallas_call x1, Pallas kernels: 4.36 us -> 3.44 us  [convolve(): pl.pallas_call(conv_kernel, in_specs=[pl.BlockSpec(memory_space=pltpu.SME...]
    pallas_call x1, Pallas kernels: 3.09 us -> 2.21 us  [gated(): pl.pallas_call(gate_kernel, in_specs=[pl.BlockSpec(memory_space=pltpu.SME...]
  transfers between devices with their start and end apart: 14 -> 16, of which waited for: 3 -> 5; matrix products, arithmetic and copies ran while one was open for 4% -> 2% of each run, Pallas kernels for 28% -> 25%
where the time goes in v5:
time: 55.7 us; the launch traced here: 55.3 us
  starting transfers between devices  20.5 us (37%)
  Pallas kernels  20.4 us (37%)
  waiting for transfers between devices  9.11 us (16%)
  local copies, waits for them, and re-layouts  4.87 us (9%)
    all_to_all x1, starting transfers between devices, local(): lax.all_to_all(jnp.broadcast_to(counts[None, :], (blocks, counts.shape[0]...  8.06 us
    pallas_call x2, Pallas kernels, attend(): pl.pallas_call(attend_kernel, in_specs=[pl.BlockSpec(memory_space=pltpu.S...  7.7 us
    all_to_all x1, waiting for transfers between devices, local(): lax.all_to_all(jnp.broadcast_to(counts[None, :], (blocks, counts.shape[0]...  6.15 us
    ppermute x10, starting transfers between devices, swap(): return lax.ppermute(value, 'head', [(0, 1), (1, 0)])  4.84 us
    ppermute x2, starting transfers between devices, exchange(): return lax.ppermute(value, 'tm', [(i, i ^ 1) for i in range(blocks)])  4.3 us
    unnamed x29, local copies, waits for them, and re-layouts  4.28 us
    pallas_call x1, Pallas kernels, convolve(): pl.pallas_call(conv_kernel, in_specs=[pl.BlockSpec(memory_space=pltpu.SME...  3.44 us
    pallas_call x1, Pallas kernels, project(): pl.pallas_call(qkv_kernel, in_specs=[pl.BlockSpec(memory_space=pltpu.SMEM...  2.75 us
  transfers between devices with their start and end apart: 16, of which 5 were waited for; matrix products, arithmetic and copies ran while one was open for 2% of the time, Pallas kernels for 25%

profile of v5, /device:TPU:0, one launch (start us, length us, event | category | flops | bytes accessed | tf_op | source)
XLA Modules:
  0.0 55.3 jit_solution(3955276022988880661)
XLA Ops:
  0.5 1.7 %collective-permute-done.other_ref.x_other = bf16[512,512]{1,0:T(8,128)(2,1)S(1)} collective-permute-done((bf16[512,512]{1,0:T(8,128)(2,1)}, bf16[512,512]{1,0:T(8,128)(2,1)S(1)}, u32[]{:S(2)}, u32[]{:S(2)}) %collective-permute-start) | collective-permute-done | bytes 524320 | tf_op jit(solution)/shard_map/ppermute | solution.py:468
  2.2 1.4 %copy-done = bf16[1024,3,256]{2,0,1:T(8,128)(2,1)S(1)} copy-done((bf16[1024,3,256]{2,0,1:T(8,128)(2,1)S(1)}, bf16[1024,3,256]{2,0,1:T(8,128)(2,1)}, u32[]{:S(2)}) %copy-start) | copy-done | bytes 1572888
  3.6 1.0 %copy-done.1 = bf16[512,512]{1,0:T(8,128)(2,1)S(1)} copy-done((bf16[512,512]{1,0:T(8,128)(2,1)S(1)}, bf16[512,512]{1,0:T(8,128)(2,1)}, u32[]{:S(2)}) %copy-start.1) | copy-done | bytes 524312
  4.7 0.7 %copy-done.5 = f32[1024]{0:T(1024)S(1)} copy-done((f32[1024]{0:T(1024)S(1)}, f32[1024]{0:T(1024)}, u32[]{:S(2)}) %copy-start.5) | copy-done | bytes 4120
  5.3 2.7 %project.1 = (bf16[512,256]{1,0:T(8,128)(2,1)}, bf16[512,128]{1,0:T(8,128)(2,1)S(1)}, bf16[512,384]{1,0:T(8,128)(2,1)S(1)}, bf16[512,256]{1,0:T(8,128)(2,1)}) custom-call(s32[4]{0:T(128)S(1)} %pad_add_fusion.meta, bf16[512,512]{1,0:T(8,128)(2,1)S(1)} %copy-done.1, bf16[512,512]{1,0:T(8,128)(2,1)S(1)} %collective-permute-done.other_ref.x_other, ...), custom_call_target="tpu_custom_call" | custom-call | flops 3449999872 | tf_op jit(solution)/shard_map/project/pallas_call | solution.py:79
  8.1 0.6 %copy-done.8 = bf16[512,128]{1,0:T(8,128)(2,1)} copy-done((bf16[512,128]{1,0:T(8,128)(2,1)}, bf16[512,128]{1,0:T(8,128)(2,1)S(1)}, u32[]{:S(2)}) %copy-start.8) | copy-done | bytes 131096
  8.7 2.9 %collective-permute-start.1 = (bf16[512,384]{1,0:T(8,128)(2,1)S(1)}, bf16[512,384]{1,0:T(8,128)(2,1)S(1)}, u32[]{:S(2)}, u32[]{:S(2)}) collective-permute-start(bf16[512,384]{1,0:T(8,128)(2,1)S(1)} %get-tuple-element.29), channel_id=1, source_target_pairs={{0,2},{2,0},{4,6},{6,4},{8,10},{10,8},{12,14},{14,12},{1,3},{3,1},... | collective-permute-start | bytes 1179656 | tf_op jit(solution)/shard_map/ppermute | solution.py:475
  11.8 1.4 %collective-permute-start.2 = (bf16[512,256]{1,0:T(8,128)(2,1)}, bf16[512,256]{1,0:T(8,128)(2,1)}, u32[]{:S(2)}, u32[]{:S(2)}) collective-permute-start(bf16[512,256]{1,0:T(8,128)(2,1)} %get-tuple-element.30), channel_id=1, source_target_pairs={{2,4},{4,2},{6,8},{8,6},{10,12},{12,10},{3,5},{5,3},{7,9},{9,7},{1... | collective-permute-start | bytes 786440 | tf_op jit(solution)/shard_map/ppermute | solution.py:472
  13.2 1.3 %collective-permute-start.3 = (bf16[512,256]{1,0:T(8,128)(2,1)}, bf16[512,256]{1,0:T(8,128)(2,1)}, u32[]{:S(2)}, u32[]{:S(2)}) collective-permute-start(bf16[512,256]{1,0:T(8,128)(2,1)} %get-tuple-element.28.center.side_a), channel_id=1, source_target_pairs={{2,6},{4,0},{6,10},{8,4},{10,14},{12,8},{3,7},{5,1},{7,11},{9,5},{... | collective-permute-start | bytes 786440 | tf_op jit(solution)/shard_map/ppermute | solution.py:472
  14.7 0.6 %broadcast_in_dim.4 = s32[8,1,16]{2,1,0:T(1,128)} broadcast(s32[16]{0:T(128)S(1)} %convert_reduce_fusion), dimensions={2} | broadcast | bytes 576 | tf_op jit(solution)/shard_map/broadcast_in_dim | solution.py:495
  15.3 8.1 %all-to-all-start = ((s32[8,1,16]{2,1,0:T(1,128)}), s32[8,1,16]{2,1,0:T(1,128)S(1)}, u32[]{:S(2)}, u32[]{:S(2)}) async-start(s32[8,1,16]{2,1,0:T(1,128)} %broadcast_in_dim.4), calls=%async_computation | async-start | bytes 8192 | tf_op jit(solution)/shard_map/all_to_all | solution.py:494
  23.7 6.2 %all-to-all-done = s32[8,1,16]{2,1,0:T(1,128)S(1)} async-done(((s32[8,1,16]{2,1,0:T(1,128)}), s32[8,1,16]{2,1,0:T(1,128)S(1)}, u32[]{:S(2)}, u32[]{:S(2)}) %all-to-all-start) | async-done | bytes 544 | tf_op jit(solution)/shard_map/all_to_all | solution.py:494
  29.8 0.8 %bounds.1 = (s32[512,128]{1,0:T(8,128)S(1)}, s32[512,128]{1,0:T(8,128)S(1)}) custom-call(s32[4]{0:T(128)S(1)} %pad_add_fusion.meta, s32[8,16]{1,0:T(8,128)S(1)} %bitcast.18, s32[1,16]{1,0:T(1,128)S(1)} %bitcast.22), custom_call_target="tpu_custom_call" | custom-call | flops 1150000000 | tf_op jit(solution)/shard_map/bounds/pallas_call | solution.py:121
  31.4 3.8 %attend.3 = bf16[512,128]{1,0:T(8,128)(2,1)S(1)} custom-call(s32[1]{0:T(128)} %bitcast.1.a_high, bf16[512,384]{1,0:T(8,128)(2,1)S(1)} %collective-permute-done.1.side_a.query.center, bf16[512,384]{1,0:T(8,128)(2,1)S(1)} %collective-permute-done.1.side_a.query.center, bf16[512,256]{1,0:T(8,128)(2,1)} %get-tuple-element.28.center.side_a, ...), custom_call_target="tpu_custom_call" | custom-call | flops 3449999872 | tf_op jit(solution)/shard_map/attend/pallas_call | solution.py:194
  35.2 1.4 %collective-permute-start.4 = (bf16[512,128]{1,0:T(8,128)(2,1)S(1)}, bf16[512,128]{1,0:T(8,128)(2,1)S(1)}, u32[]{:S(2)}, u32[]{:S(2)}) collective-permute-start(bf16[512,128]{1,0:T(8,128)(2,1)S(1)} %attend.3), channel_id=1, source_target_pairs={{0,2},{2,0},{4,6},{6,4},{8,10},{10,8},{12,14},{14,12},{1,3},{3,1},... | collective-permute-start | bytes 393224 | tf_op jit(solution)/shard_map/ppermute | solution.py:475
  36.5 3.9 %attend.2.mine_own = bf16[512,128]{1,0:T(8,128)(2,1)S(1)} custom-call(s32[1]{0:T(128)} %bitcast.4.a_high, bf16[512,128]{1,0:T(8,128)(2,1)S(1)} %copy-done.9, bf16[512,256]{1,0:T(8,128)(2,1)} %get-tuple-element.28.center.side_a, bf16[512,384]{1,0:T(8,128)(2,1)S(1)} %collective-permute-done.1.side_a.query.center, ...), custom_call_target="tpu_custom_call" | custom-call | flops 3449999872 | tf_op jit(solution)/shard_map/attend/pallas_call | solution.py:194
  41.1 0.8 %collective-permute-done.5.mine_other = bf16[512,128]{1,0:T(8,128)(2,1)S(1)} collective-permute-done((bf16[512,128]{1,0:T(8,128)(2,1)S(1)}, bf16[512,128]{1,0:T(8,128)(2,1)S(1)}, u32[]{:S(2)}, u32[]{:S(2)}) %collective-permute-start.5) | collective-permute-done | bytes 131104 | tf_op jit(solution)/shard_map/ppermute | solution.py:468
  42.2 2.2 %gated.1 = (bf16[272,512]{1,0:T(8,128)(2,1)S(1)}, bf16[64,512]{1,0:T(8,128)(2,1)S(1)}, bf16[256,512]{1,0:T(8,128)(2,1)S(1)}, bf16[256,512]{1,0:T(8,128)(2,1)S(1)}) custom-call(s32[4]{0:T(128)S(1)} %pad_add_fusion.meta, bf16[512,128]{1,0:T(8,128)(2,1)S(1)} %attend.2.mine_own, bf16[512,128]{1,0:T(8,128)(2,1)S(1)} %collective-permute-done.4.pair_own, ...), custom_call_target="tpu_custom_call" | custom-call | flops 3449999872 | tf_op jit(solution)/shard_map/gated/pallas_call | solution.py:283
  44.4 0.7 %collective-permute-start.12 = (bf16[64,512]{1,0:T(8,128)(2,1)S(1)}, bf16[64,512]{1,0:T(8,128)(2,1)S(1)}, u32[]{:S(2)}, u32[]{:S(2)}) collective-permute-start(bf16[64,512]{1,0:T(8,128)(2,1)S(1)} %get-tuple-element.45), channel_id=1, source_target_pairs={{2,1},{4,3},{6,5},{8,7},{10,9},{12,11},{14,13},{1,2},{3,4},{5,6},{... | collective-permute-start | bytes 196616 | tf_op jit(solution)/shard_map/ppermute | solution.py:521
  45.0 3.4 %convolve.1.act_ref = bf16[256,512]{1,0:T(8,128)(2,1)S(1)} custom-call(s32[4]{0:T(128)S(1)} %pad_add_fusion.meta, bf16[272,512]{1,0:T(8,128)(2,1)S(1)} %get-tuple-element.43.glu_ref, s32[512,128]{1,0:T(8,128)S(1)} %get-tuple-element.32.run_ref, f32[32,256]{1,0:T(8,128)S(1)} %pad_maximum_fusion.taps_own, f32[32,256]{1,0:T(8,128)S(1)} %collective-permute-done.8.taps_other), custom_call_target="tpu_custom_call" | custom-call | flops 3449999872 | tf_op jit(solution)/shard_map/convolve/pallas_call | solution.py:356
  48.5 2.7 %collective-permute-start.11 = (bf16[256,512]{1,0:T(8,128)(2,1)S(1)}, bf16[256,512]{1,0:T(8,128)(2,1)S(1)}, u32[]{:S(2)}, u32[]{:S(2)}) collective-permute-start(bf16[256,512]{1,0:T(8,128)(2,1)S(1)} %convolve.1.act_ref), channel_id=1, source_target_pairs={{0,1},{1,0},{2,3},{3,2},{4,5},{5,4},{6,7},{7,6},{8,9},{9,8},{10,11... | collective-permute-start | bytes 786440 | tf_op jit(solution)/shard_map/ppermute | solution.py:468
  51.3 0.8 %rim.1.rim_ref = bf16[16,512]{1,0:T(8,128)(2,1)S(1)} custom-call(s32[4]{0:T(128)S(1)} %pad_add_fusion.meta, bf16[272,512]{1,0:T(8,128)(2,1)S(1)} %get-tuple-element.43.glu_ref, bf16[64,512]{1,0:T(8,128)(2,1)S(1)} %collective-permute-done.12.edge_ref, s32[512,128]{1,0:T(8,128)S(1)} %get-tuple-element.32.run_ref, f32[32,256]{1,0:T(8,128)S(1)} %pad_maximum_fusion.taps_own, ...), custom_call_target="tpu_custom_call" | custom-call | flops 1150000000 | tf_op jit(solution)/shard_map/rim/pallas_call | solution.py:392
  52.7 0.9 %finish_own.1.done_ref = bf16[256,512]{1,0:T(8,128)(2,1)S(1)} custom-call(s32[4]{0:T(128)S(1)} %pad_add_fusion.meta, bf16[256,512]{1,0:T(8,128)(2,1)S(1)} %convolve.1.act_ref, bf16[16,512]{1,0:T(8,128)(2,1)S(1)} %rim.1.rim_ref, bf16[256,512]{1,0:T(8,128)(2,1)S(1)} %get-tuple-element.48.mid_ref, bf16[256,1024]{1,0:T(8,128)(2,1)S(1)} %copy-done.4, ...), custom_call_target="tpu_custom_call" | custom-call | flops 1380000000 | tf_op jit(solution)/shard_map/finish_own/pallas_call | solution.py:439
  53.6 1.7 %finish.1 = bf16[512,512]{1,0:T(8,128)(2,1)} custom-call(s32[4]{0:T(128)S(1)} %pad_add_fusion.meta, bf16[256,512]{1,0:T(8,128)(2,1)S(1)} %collective-permute-done.11.act_ref, bf16[16,512]{1,0:T(8,128)(2,1)S(1)} %collective-permute-done.13.rim_ref, bf16[256,512]{1,0:T(8,128)(2,1)S(1)} %collective-permute-done.14.mid_ref, bf16[256,1024]{1,0:T(8,128)(2,1)S(1)} %copy-done.4, ...), custom_call_target="tpu_custom_call" | custom-call | flops 1380000000 | tf_op jit(solution)/shard_map/finish/pallas_call | solution.py:439
  (50 shorter events, 3.3 us)
Async XLA Ops:
  0.0 2.2 %collective-permute-start = (bf16[512,512]{1,0:T(8,128)(2,1)}, bf16[512,512]{1,0:T(8,128)(2,1)S(1)}, u32[]{:S(2)}, u32[]{:S(2)}) collective-permute-start(bf16[512,512]{1,0:T(8,128)(2,1)} %x_own.1), channel_id=1, source_target_pairs={{0,1},{1,0},{2,3},{3,2},{4,5},{5,4},{6,7},{7,6},{8,9},{9,8},{10,11... | collective-permute-start | bytes 1572872 | tf_op jit(solution)/shard_map/ppermute | solution.py:468
  5.3 6.3 %copy-start.10 = (bf16[1024,2,256]{2,1,0:T(2,128)(2,1)S(1)}, bf16[1024,2,256]{2,1,0:T(2,128)(2,1)}, u32[]{:S(2)}) copy-start(bf16[1024,2,256]{2,1,0:T(2,128)(2,1)} %param.18) | copy-start | bytes 3145732
  8.7 5.8 %copy-start.12 = (s32[512]{0:T(512)S(1)}, s32[512]{0:T(512)}, u32[]{:S(2)}) copy-start(s32[512]{0:T(512)} %param.12) | copy-start | bytes 6148
  8.7 14.6 %copy-start.11 = (f32[31,256]{1,0:T(8,128)S(1)}, f32[31,256]{1,0:T(8,128)}, u32[]{:S(2)}) copy-start(f32[31,256]{1,0:T(8,128)} %param.19) | copy-start | bytes 95236
  8.7 14.6 %copy-start.13 = (f32[256]{0:T(256)S(1)}, f32[256]{0:T(256)}, u32[]{:S(2)}) copy-start(f32[256]{0:T(256)} %param.20) | copy-start | bytes 3076
  8.7 21.1 %copy-start.7 = (s32[16]{0:T(128)S(1)}, s32[16]{0:T(128)}, u32[]{:S(2)}) copy-start(s32[16]{0:T(128)} %param.13) | copy-start | bytes 196
  8.7 22.1 %collective-permute-start.1 = (bf16[512,384]{1,0:T(8,128)(2,1)S(1)}, bf16[512,384]{1,0:T(8,128)(2,1)S(1)}, u32[]{:S(2)}, u32[]{:S(2)}) collective-permute-start(bf16[512,384]{1,0:T(8,128)(2,1)S(1)} %get-tuple-element.29), channel_id=1, source_target_pairs={{0,2},{2,0},{4,6},{6,4},{8,10},{10,8},{12,14},{14,12},{1,3},{3,1},... | collective-permute-start | bytes 1179656 | tf_op jit(solution)/shard_map/ppermute | solution.py:475
  11.8 23.3 %collective-permute-start.2 = (bf16[512,256]{1,0:T(8,128)(2,1)}, bf16[512,256]{1,0:T(8,128)(2,1)}, u32[]{:S(2)}, u32[]{:S(2)}) collective-permute-start(bf16[512,256]{1,0:T(8,128)(2,1)} %get-tuple-element.30), channel_id=1, source_target_pairs={{2,4},{4,2},{6,8},{8,6},{10,12},{12,10},{3,5},{5,3},{7,9},{9,7},{1... | collective-permute-start | bytes 786440 | tf_op jit(solution)/shard_map/ppermute | solution.py:472
  13.2 17.5 %collective-permute-start.3 = (bf16[512,256]{1,0:T(8,128)(2,1)}, bf16[512,256]{1,0:T(8,128)(2,1)}, u32[]{:S(2)}, u32[]{:S(2)}) collective-permute-start(bf16[512,256]{1,0:T(8,128)(2,1)} %get-tuple-element.28.center.side_a), channel_id=1, source_target_pairs={{2,6},{4,0},{6,10},{8,4},{10,14},{12,8},{3,7},{5,1},{7,11},{9,5},{... | collective-permute-start | bytes 786440 | tf_op jit(solution)/shard_map/ppermute | solution.py:472
  14.5 27.6 %collective-permute-start.10 = (bf16[2,1024,256]{2,1,0:T(8,128)(2,1)S(1)}, bf16[2,1024,256]{2,1,0:T(8,128)(2,1)S(1)}, u32[]{:S(2)}, u32[]{:S(2)}) collective-permute-start(bf16[2,1024,256]{2,1,0:T(8,128)(2,1)S(1)} %bitcast.16), channel_id=1, source_target_pairs={{0,1},{1,0},{2,3},{3,2},{4,5},{5,4},{6,7},{7,6},{8,9},{9,8},{10,11... | collective-permute-start | bytes 3145736 | tf_op jit(solution)/shard_map/ppermute | solution.py:468
  15.3 14.5 %all-to-all-start = ((s32[8,1,16]{2,1,0:T(1,128)}), s32[8,1,16]{2,1,0:T(1,128)S(1)}, u32[]{:S(2)}, u32[]{:S(2)}) async-start(s32[8,1,16]{2,1,0:T(1,128)} %broadcast_in_dim.4), calls=%async_computation | async-start | bytes 8192 | tf_op jit(solution)/shard_map/all_to_all | solution.py:494
  23.4 17.1 %collective-permute-start.8 = (f32[32,256]{1,0:T(8,128)S(1)}, f32[32,256]{1,0:T(8,128)S(1)}, u32[]{:S(2)}, u32[]{:S(2)}) collective-permute-start(f32[32,256]{1,0:T(8,128)S(1)} %pad_maximum_fusion.taps_own), channel_id=1, source_target_pairs={{0,1},{1,0},{2,3},{3,2},{4,5},{5,4},{6,7},{7,6},{8,9},{9,8},{10,11... | collective-permute-start | bytes 98312 | tf_op jit(solution)/shard_map/ppermute | solution.py:468
  30.9 11.3 %collective-permute-start.9 = (bf16[256,1024]{1,0:T(8,128)(2,1)S(1)}, bf16[256,1024]{1,0:T(8,128)(2,1)S(1)}, u32[]{:S(2)}, u32[]{:S(2)}) collective-permute-start(bf16[256,1024]{1,0:T(8,128)(2,1)S(1)} %copy-done.3), channel_id=1, source_target_pairs={{0,1},{1,0},{2,3},{3,2},{4,5},{5,4},{6,7},{7,6},{8,9},{9,8},{10,11... | collective-permute-start | bytes 1572872 | tf_op jit(solution)/shard_map/ppermute | solution.py:468
  31.0 10.9 %collective-permute-start.7 = (bf16[256,1024]{1,0:T(8,128)(2,1)S(1)}, bf16[256,1024]{1,0:T(8,128)(2,1)S(1)}, u32[]{:S(2)}, u32[]{:S(2)}) collective-permute-start(bf16[256,1024]{1,0:T(8,128)(2,1)S(1)} %copy-done.4), channel_id=1, source_target_pairs={{0,1},{1,0},{2,3},{3,2},{4,5},{5,4},{6,7},{7,6},{8,9},{9,8},{10,11... | collective-permute-start | bytes 1572872 | tf_op jit(solution)/shard_map/ppermute | solution.py:468
  31.4 5.1 %copy-start.9 = (bf16[512,128]{1,0:T(8,128)(2,1)S(1)}, bf16[512,128]{1,0:T(8,128)(2,1)}, u32[]{:S(2)}) copy-start(bf16[512,128]{1,0:T(8,128)(2,1)} %copy-done.8) | copy-start | bytes 393220
  35.2 5.6 %collective-permute-start.4 = (bf16[512,128]{1,0:T(8,128)(2,1)S(1)}, bf16[512,128]{1,0:T(8,128)(2,1)S(1)}, u32[]{:S(2)}, u32[]{:S(2)}) collective-permute-start(bf16[512,128]{1,0:T(8,128)(2,1)S(1)} %attend.3), channel_id=1, source_target_pairs={{0,2},{2,0},{4,6},{6,4},{8,10},{10,8},{12,14},{14,12},{1,3},{3,1},... | collective-permute-start | bytes 393224 | tf_op jit(solution)/shard_map/ppermute | solution.py:475
  36.5 5.6 %copy-start.2 = (bf16[512,512]{1,0:T(8,128)(2,1)S(1)}, bf16[512,512]{1,0:T(8,128)(2,1)}, u32[]{:S(2)}) copy-start(bf16[512,512]{1,0:T(8,128)(2,1)} %x_own.1) | copy-start | bytes 1572868
  36.5 5.6 %copy-start.6 = (f32[1024]{0:T(1024)S(1)}, f32[1024]{0:T(1024)}, u32[]{:S(2)}) copy-start(f32[1024]{0:T(1024)} %param.17) | copy-start | bytes 12292
  40.5 1.4 %collective-permute-start.5 = (bf16[512,128]{1,0:T(8,128)(2,1)S(1)}, bf16[512,128]{1,0:T(8,128)(2,1)S(1)}, u32[]{:S(2)}, u32[]{:S(2)}) collective-permute-start(bf16[512,128]{1,0:T(8,128)(2,1)S(1)} %attend.2.mine_own), channel_id=1, source_target_pairs={{0,1},{1,0},{2,3},{3,2},{4,5},{5,4},{6,7},{7,6},{8,9},{9,8},{10,11... | collective-permute-start | bytes 393224 | tf_op jit(solution)/shard_map/ppermute | solution.py:468
  40.8 1.3 %collective-permute-start.6 = (bf16[512,128]{1,0:T(8,128)(2,1)S(1)}, bf16[512,128]{1,0:T(8,128)(2,1)S(1)}, u32[]{:S(2)}, u32[]{:S(2)}) collective-permute-start(bf16[512,128]{1,0:T(8,128)(2,1)S(1)} %collective-permute-done.4.pair_own), channel_id=1, source_target_pairs={{0,1},{1,0},{2,3},{3,2},{4,5},{5,4},{6,7},{7,6},{8,9},{9,8},{10,11... | collective-permute-start | bytes 393224 | tf_op jit(solution)/shard_map/ppermute | solution.py:468
  44.4 6.9 %collective-permute-start.12 = (bf16[64,512]{1,0:T(8,128)(2,1)S(1)}, bf16[64,512]{1,0:T(8,128)(2,1)S(1)}, u32[]{:S(2)}, u32[]{:S(2)}) collective-permute-start(bf16[64,512]{1,0:T(8,128)(2,1)S(1)} %get-tuple-element.45), channel_id=1, source_target_pairs={{2,1},{4,3},{6,5},{8,7},{10,9},{12,11},{14,13},{1,2},{3,4},{5,6},{... | collective-permute-start | bytes 196616 | tf_op jit(solution)/shard_map/ppermute | solution.py:521
  48.5 5.1 %collective-permute-start.11 = (bf16[256,512]{1,0:T(8,128)(2,1)S(1)}, bf16[256,512]{1,0:T(8,128)(2,1)S(1)}, u32[]{:S(2)}, u32[]{:S(2)}) collective-permute-start(bf16[256,512]{1,0:T(8,128)(2,1)S(1)} %convolve.1.act_ref), channel_id=1, source_target_pairs={{0,1},{1,0},{2,3},{3,2},{4,5},{5,4},{6,7},{7,6},{8,9},{9,8},{10,11... | collective-permute-start | bytes 786440 | tf_op jit(solution)/shard_map/ppermute | solution.py:468
  51.2 2.4 %collective-permute-start.14 = (bf16[256,512]{1,0:T(8,128)(2,1)S(1)}, bf16[256,512]{1,0:T(8,128)(2,1)S(1)}, u32[]{:S(2)}, u32[]{:S(2)}) collective-permute-start(bf16[256,512]{1,0:T(8,128)(2,1)S(1)} %get-tuple-element.46), channel_id=1, source_target_pairs={{0,1},{1,0},{2,3},{3,2},{4,5},{5,4},{6,7},{7,6},{8,9},{9,8},{10,11... | collective-permute-start | bytes 786440 | tf_op jit(solution)/shard_map/ppermute | solution.py:468
  52.2 1.4 %collective-permute-start.13 = (bf16[16,512]{1,0:T(8,128)(2,1)S(1)}, bf16[16,512]{1,0:T(8,128)(2,1)S(1)}, u32[]{:S(2)}, u32[]{:S(2)}) collective-permute-start(bf16[16,512]{1,0:T(8,128)(2,1)S(1)} %rim.1.rim_ref), channel_id=1, source_target_pairs={{0,1},{1,0},{2,3},{3,2},{4,5},{5,4},{6,7},{7,6},{8,9},{9,8},{10,11... | collective-permute-start | bytes 49160 | tf_op jit(solution)/shard_map/ppermute | solution.py:468
  (6 other events, 6.0 us)

commit v6 on v5

--- a/solution.py
+++ b/solution.py
@@ -87,7 +87,6 @@
             jax.ShapeDtypeStruct((rows, width), BF16),
         ],
         compiler_params=pltpu.CompilerParams(vmem_limit_bytes=VMEM_LIMIT),
-        cost_estimate=weight(3),
         name="project",
     )(meta, frames, other, gain.reshape(2, 1, half),
       qkv.transpose(1, 0, 2).reshape(3, 2, half, width))
@@ -124,7 +123,6 @@
         out_specs=[vmem] * 2,
         out_shape=[jax.ShapeDtypeStruct((rows, 128), jnp.int32)] * 2,
         compiler_params=pltpu.CompilerParams(vmem_limit_bytes=VMEM_LIMIT),
-        cost_estimate=weight(1),
         name="bounds",
     )(meta, counts, valid.reshape(1, -1))
 
@@ -197,7 +195,6 @@
         out_specs=vmem,
         out_shape=jax.ShapeDtypeStruct((rows, width), BF16),
         compiler_params=pltpu.CompilerParams(vmem_limit_bytes=VMEM_LIMIT),
-        cost_estimate=weight(3),
         name="attend",
     )(a_high, query, center, side_a, side_b, runs)
 
@@ -291,7 +288,6 @@
             jax.ShapeDtypeStruct((rows - EDGE, half), BF16),
         ],
         compiler_params=pltpu.CompilerParams(vmem_limit_bytes=VMEM_LIMIT),
-        cost_estimate=weight(3),
         name="gated",
     )(meta, *contexts, x_own, x_other, out_own, out_other,
       gain.reshape(2, 1, half), in_own, in_other, runs)
@@ -495,18 +491,21 @@
         jnp.broadcast_to(counts[None, :], (blocks, counts.shape[0])), "tm", 0, 0
     )
     pointwise = pointwise_in.transpose(1, 0, 2)
-    out_weight, pointwise, depthwise, mid_gain, pointwise_out, _ = lax.optimization_barrier(
-        (out_weight, pointwise, depthwise, mid_gain, pointwise_out, keep)
-    )
-    taps = jnp.concatenate([depthwise, mid_gain[None, :]], axis=0)
+    out_weight, pointwise, _ = lax.optimization_barrier((out_weight, pointwise, keep))
     pointwise_other = swap(pointwise)
     out_other = swap(out_weight)
+    runs, pair_runs = bounds(meta, counts, utt_valid, rows)
+    pair, far_pair, far_own, runs, pair_runs = lax.optimization_barrier(
+        (pair, far_pair, far_own, runs, pair_runs)
+    )
+    pair_context = attend(column.reshape(1), pair, pair, keep, far_pair, pair_runs)
+    depthwise, mid_gain, pointwise_out, pair_context = lax.optimization_barrier(
+        (depthwise, mid_gain, pointwise_out, pair_context)
+    )
+    pair_context = exchange(pair_context)
+    taps = jnp.concatenate([depthwise, mid_gain[None, :]], axis=0)
     pointwise_out_other = swap(pointwise_out)
     taps_other = swap(taps)
-    runs, pair_runs = bounds(meta, counts, utt_valid, rows)
-
-    pair_context = attend(column.reshape(1), pair, pair, keep, far_pair, pair_runs)
-    pair_context = exchange(pair_context)
     context = attend((1 - column).reshape(1), query, keep, pair, far_own, runs)
     contexts = (context, pair_context, swap(context), swap(pair_context))
     contexts, pointwise_out_other, taps_other = lax.optimization_barrier(

time: 55.7 us -> 54.7 us (0.982)
  blocking collectives: 0 us -> 15.8 us
  starting transfers between devices: 20.5 us -> 11.1 us
  waiting for transfers between devices: 9.11 us -> 1.66 us
  local copies, waits for them, and re-layouts: 4.87 us -> 4.04 us
  other arithmetic: 0.2 us -> 0.81 us
    all_to_all x0 -> x1, blocking collectives: none -> 15.8 us  [local(): lax.all_to_all(jnp.broadcast_to(counts[None, :], (blocks, counts.shape[0]...]
    all_to_all x1 -> x0, starting transfers between devices: 8.06 us -> none  [local(): lax.all_to_all(jnp.broadcast_to(counts[None, :], (blocks, counts.shape[0]...]
    all_to_all x1 -> x0, waiting for transfers between devices: 6.15 us -> none  [local(): lax.all_to_all(jnp.broadcast_to(counts[None, :], (blocks, counts.shape[0]...]
    pallas_call x2, Pallas kernels: 7.7 us -> 6.3 us  [attend(): pl.pallas_call(attend_kernel, in_specs=[pl.BlockSpec(memory_space=pltpu.S...]
    pallas_call x2, Pallas kernels: 2.59 us -> 3.92 us  [finish(): pl.pallas_call(finish_own_kernel if done is None else finish_kernel, in_s...]
    ppermute x10, waiting for transfers between devices: 2.74 us -> 1.65 us  [swap(): return lax.ppermute(value, 'head', [(0, 1), (1, 0)])]
    pallas_call x1, Pallas kernels: 2.21 us -> 3.09 us  [gated(): pl.pallas_call(gate_kernel, in_specs=[pl.BlockSpec(memory_space=pltpu.SME...]
    pallas_call x1, Pallas kernels: 2.75 us -> 1.94 us  [project(): pl.pallas_call(qkv_kernel, in_specs=[pl.BlockSpec(memory_space=pltpu.SMEM...]
  transfers between devices with their start and end apart: 16 -> 15, of which waited for: 5 -> 3; matrix products, arithmetic and copies ran while one was open for 2% -> 4% of each run, Pallas kernels for 25% -> 24%
where the time goes in v6:
time: 54.7 us; the launch traced here: 54.3 us
  Pallas kernels  20.7 us (38%)
  blocking collectives  15.8 us (29%)
  starting transfers between devices  11.1 us (20%)
  local copies, waits for them, and re-layouts  4.04 us (7%)
  waiting for transfers between devices  1.66 us (3%)
  other arithmetic  0.81 us (1%)
    all_to_all x1, blocking collectives, local(): lax.all_to_all(jnp.broadcast_to(counts[None, :], (blocks, counts.shape[0]...  15.8 us
    pallas_call x2, Pallas kernels, attend(): pl.pallas_call(attend_kernel, in_specs=[pl.BlockSpec(memory_space=pltpu.S...  6.3 us
    ppermute x10, starting transfers between devices, swap(): return lax.ppermute(value, 'head', [(0, 1), (1, 0)])  4.4 us
    ppermute x2, starting transfers between devices, exchange(): return lax.ppermute(value, 'tm', [(i, i ^ 1) for i in range(blocks)])  4.06 us
    unnamed x27, local copies, waits for them, and re-layouts  4.03 us
    pallas_call x2, Pallas kernels, finish(): pl.pallas_call(finish_own_kernel if done is None else finish_kernel, in_s...  3.92 us
    pallas_call x1, Pallas kernels, convolve(): pl.pallas_call(conv_kernel, in_specs=[pl.BlockSpec(memory_space=pltpu.SME...  3.49 us
    pallas_call x1, Pallas kernels, gated(): pl.pallas_call(gate_kernel, in_specs=[pl.BlockSpec(memory_space=pltpu.SME...  3.09 us
  transfers between devices with their start and end apart: 15, of which 3 were waited for; matrix products, arithmetic and copies ran while one was open for 4% of the time, Pallas kernels for 24%

profile of v6, /device:TPU:0, one launch (start us, length us, event | category | flops | bytes accessed | tf_op | source)
XLA Modules:
  0.0 54.3 jit_solution(9180841622483914076)
XLA Ops:
  0.5 1.5 %copy.16 = bf16[1024,2,256]{2,0,1:T(8,128)(2,1)S(1)} copy(bf16[1024,2,256]{2,1,0:T(2,128)(2,1)} %param.18) | data formatting | bytes 2097152 | tf_op args[7]
  2.2 1.9 %project.1 = (bf16[512,256]{1,0:T(8,128)(2,1)S(1)}, bf16[512,128]{1,0:T(8,128)(2,1)S(1)}, bf16[512,384]{1,0:T(8,128)(2,1)S(1)}, bf16[512,256]{1,0:T(8,128)(2,1)S(1)}) custom-call(s32[4]{0:T(128)S(1)} %pad_add_fusion.meta, bf16[512,512]{1,0:T(8,128)(2,1)S(1)} %copy-done, bf16[512,512]{1,0:T(8,128)(2,1)S(1)} %collective-permute-done.other_ref.x_other, ...), custom_call_target="tpu_custom_call" | custom-call | tf_op jit(solution)/shard_map/project/pallas_call | solution.py:79
  4.2 0.6 %copy-done.5 = bf16[512,128]{1,0:T(8,128)(2,1)} copy-done((bf16[512,128]{1,0:T(8,128)(2,1)}, bf16[512,128]{1,0:T(8,128)(2,1)S(1)}, u32[]{:S(2)}) %copy-start.5) | copy-done | bytes 131096
  5.2 2.6 %collective-permute-start.1 = (bf16[512,384]{1,0:T(8,128)(2,1)S(1)}, bf16[512,384]{1,0:T(8,128)(2,1)S(1)}, u32[]{:S(2)}, u32[]{:S(2)}) collective-permute-start(bf16[512,384]{1,0:T(8,128)(2,1)S(1)} %get-tuple-element.35), channel_id=1, source_target_pairs={{0,2},{2,0},{4,6},{6,4},{8,10},{10,8},{12,14},{14,12},{1,3},{3,1},... | collective-permute-start | bytes 1179656 | tf_op jit(solution)/shard_map/ppermute | solution.py:471
  7.9 0.7 %collective-permute-start.3 = (bf16[512,256]{1,0:T(8,128)(2,1)S(1)}, bf16[512,256]{1,0:T(8,128)(2,1)S(1)}, u32[]{:S(2)}, u32[]{:S(2)}) collective-permute-start(bf16[512,256]{1,0:T(8,128)(2,1)S(1)} %get-tuple-element.36), channel_id=1, source_target_pairs={{2,4},{4,2},{6,8},{8,6},{10,12},{12,10},{3,5},{5,3},{7,9},{9,7},{1... | collective-permute-start | bytes 786440 | tf_op jit(solution)/shard_map/ppermute | solution.py:468
  8.5 1.3 %collective-permute-start.2 = (bf16[512,256]{1,0:T(8,128)(2,1)S(1)}, bf16[512,256]{1,0:T(8,128)(2,1)S(1)}, u32[]{:S(2)}, u32[]{:S(2)}) collective-permute-start(bf16[512,256]{1,0:T(8,128)(2,1)S(1)} %get-tuple-element.34.center.side_a), channel_id=1, source_target_pairs={{2,6},{4,0},{6,10},{8,4},{10,14},{12,8},{3,7},{5,1},{7,11},{9,5},{... | collective-permute-start | bytes 786440 | tf_op jit(solution)/shard_map/ppermute | solution.py:468
  10.0 15.8 %all_to_all.8 = s32[8,1,16]{2,1,0:T(1,128)S(1)} all-to-all(s32[8,1,16]{2,1,0:T(1,128)S(1)} %broadcast_in_dim.4), channel_id=1, replica_groups=mesh['grp'=2,'tm'=8,'head'=2] {'tm'}, dimensions={0} | all-to-all | bytes 1024 | tf_op jit(solution)/shard_map/all_to_all | solution.py:490
  25.7 0.8 %bounds.1 = (s32[512,128]{1,0:T(8,128)S(1)}, s32[512,128]{1,0:T(8,128)S(1)}) custom-call(s32[4]{0:T(128)S(1)} %pad_add_fusion.meta, s32[8,16]{1,0:T(8,128)S(1)} %bitcast.19, s32[1,16]{1,0:T(1,128)S(1)} %bitcast.22), custom_call_target="tpu_custom_call" | custom-call | tf_op jit(solution)/shard_map/bounds/pallas_call | solution.py:120
  26.6 3.4 %attend.3 = bf16[512,128]{1,0:T(8,128)(2,1)} custom-call(s32[1]{0:T(128)} %bitcast.1.a_high, bf16[512,384]{1,0:T(8,128)(2,1)S(1)} %collective-permute-done.1.side_a.query.center, bf16[512,384]{1,0:T(8,128)(2,1)S(1)} %collective-permute-done.1.side_a.query.center, bf16[512,256]{1,0:T(8,128)(2,1)S(1)} %get-tuple-element.34.center.side_a, ...), custom_call_target="tpu_custom_call" | custom-call | tf_op jit(solution)/shard_map/attend/pallas_call | solution.py:192
  30.5 1.4 %collective-permute-start.4 = (bf16[512,128]{1,0:T(8,128)(2,1)}, bf16[512,128]{1,0:T(8,128)(2,1)}, u32[]{:S(2)}, u32[]{:S(2)}) collective-permute-start(bf16[512,128]{1,0:T(8,128)(2,1)} %attend.3), channel_id=1, source_target_pairs={{0,2},{2,0},{4,6},{6,4},{8,10},{10,8},{12,14},{14,12},{1,3},{3,1},... | collective-permute-start | bytes 393224 | tf_op jit(solution)/shard_map/ppermute | solution.py:471
  32.0 0.6 %pad_maximum_fusion.taps_own = f32[32,256]{1,0:T(8,128)} fusion(f32[1,256]{1,0:T(1,128)S(1)} %bitcast.23, f32[31,256]{1,0:T(8,128)S(1)} %copy-done.10), kind=kLoop, calls=%fused_computation.1 | loop fusion | flops 8192 | bytes 65536 | tf_op jit(solution)/shard_map/concatenate | solution.py:506
  32.6 0.9 %copy-done.4 = bf16[512,256]{1,0:T(8,128)(2,1)S(1)} copy-done((bf16[512,256]{1,0:T(8,128)(2,1)S(1)}, bf16[512,256]{1,0:T(8,128)(2,1)}, u32[]{:S(2)}) %copy-start.4) | copy-done | bytes 262168
  33.6 0.9 %copy-done.6 = bf16[512,128]{1,0:T(8,128)(2,1)S(1)} copy-done((bf16[512,128]{1,0:T(8,128)(2,1)S(1)}, bf16[512,128]{1,0:T(8,128)(2,1)}, u32[]{:S(2)}) %copy-start.6) | copy-done | bytes 131096
  34.5 2.9 %attend.2.mine_own = bf16[512,128]{1,0:T(8,128)(2,1)S(1)} custom-call(s32[1]{0:T(128)} %bitcast.4.a_high, bf16[512,128]{1,0:T(8,128)(2,1)S(1)} %copy-done.6, bf16[512,256]{1,0:T(8,128)(2,1)S(1)} %get-tuple-element.34.center.side_a, bf16[512,384]{1,0:T(8,128)(2,1)S(1)} %collective-permute-done.1.side_a.query.center, bf16[512,256]{1,0:T(8,128)(2,1)S(1)} %copy-done.4, ...), custom_call_target="tpu_custom_call" | custom-call | tf_op jit(solution)/shard_map/attend/pallas_call | solution.py:192
  37.4 0.6 %collective-permute-start.5 = (bf16[512,128]{1,0:T(8,128)(2,1)S(1)}, bf16[512,128]{1,0:T(8,128)(2,1)S(1)}, u32[]{:S(2)}, u32[]{:S(2)}) collective-permute-start(bf16[512,128]{1,0:T(8,128)(2,1)S(1)} %attend.2.mine_own), channel_id=1, source_target_pairs={{0,1},{1,0},{2,3},{3,2},{4,5},{5,4},{6,7},{7,6},{8,9},{9,8},{10,11... | collective-permute-start | bytes 393224 | tf_op jit(solution)/shard_map/ppermute | solution.py:464
  38.0 0.9 %collective-permute-done.5.mine_other = bf16[512,128]{1,0:T(8,128)(2,1)S(1)} collective-permute-done((bf16[512,128]{1,0:T(8,128)(2,1)S(1)}, bf16[512,128]{1,0:T(8,128)(2,1)S(1)}, u32[]{:S(2)}, u32[]{:S(2)}) %collective-permute-start.5) | collective-permute-done | bytes 131104 | tf_op jit(solution)/shard_map/ppermute | solution.py:464
  38.9 0.6 %collective-permute-done.6.pair_other = bf16[512,128]{1,0:T(8,128)(2,1)S(1)} collective-permute-done((bf16[512,128]{1,0:T(8,128)(2,1)}, bf16[512,128]{1,0:T(8,128)(2,1)S(1)}, u32[]{:S(2)}, u32[]{:S(2)}) %collective-permute-start.6) | collective-permute-done | bytes 131104 | tf_op jit(solution)/shard_map/ppermute | solution.py:464
  39.5 3.1 %gated.1 = (bf16[272,512]{1,0:T(8,128)(2,1)S(1)}, bf16[64,512]{1,0:T(8,128)(2,1)S(1)}, bf16[256,512]{1,0:T(8,128)(2,1)S(1)}, bf16[256,512]{1,0:T(8,128)(2,1)S(1)}) custom-call(s32[4]{0:T(128)S(1)} %pad_add_fusion.meta, bf16[512,128]{1,0:T(8,128)(2,1)S(1)} %attend.2.mine_own, bf16[512,128]{1,0:T(8,128)(2,1)} %collective-permute-done.4.pair_own, ...), custom_call_target="tpu_custom_call" | custom-call | tf_op jit(solution)/shard_map/gated/pallas_call | solution.py:280
  42.6 0.7 %collective-permute-start.12 = (bf16[64,512]{1,0:T(8,128)(2,1)S(1)}, bf16[64,512]{1,0:T(8,128)(2,1)S(1)}, u32[]{:S(2)}, u32[]{:S(2)}) collective-permute-start(bf16[64,512]{1,0:T(8,128)(2,1)S(1)} %get-tuple-element.57), channel_id=1, source_target_pairs={{2,1},{4,3},{6,5},{8,7},{10,9},{12,11},{14,13},{1,2},{3,4},{5,6},{... | collective-permute-start | bytes 196616 | tf_op jit(solution)/shard_map/ppermute | solution.py:520
  43.3 3.5 %convolve.1.act_ref = bf16[256,512]{1,0:T(8,128)(2,1)S(1)} custom-call(s32[4]{0:T(128)S(1)} %pad_add_fusion.meta, bf16[272,512]{1,0:T(8,128)(2,1)S(1)} %get-tuple-element.55.glu_ref, s32[512,128]{1,0:T(8,128)S(1)} %get-tuple-element.42.run_ref, f32[32,256]{1,0:T(8,128)} %pad_maximum_fusion.taps_own, f32[32,256]{1,0:T(8,128)} %collective-permute-done.8.taps_other), custom_call_target="tpu_custom_call" | custom-call | flops 3449999872 | tf_op jit(solution)/shard_map/convolve/pallas_call | solution.py:352
  46.8 1.8 %collective-permute-start.11 = (bf16[256,512]{1,0:T(8,128)(2,1)S(1)}, bf16[256,512]{1,0:T(8,128)(2,1)S(1)}, u32[]{:S(2)}, u32[]{:S(2)}) collective-permute-start(bf16[256,512]{1,0:T(8,128)(2,1)S(1)} %convolve.1.act_ref), channel_id=1, source_target_pairs={{0,1},{1,0},{2,3},{3,2},{4,5},{5,4},{6,7},{7,6},{8,9},{9,8},{10,11... | collective-permute-start | bytes 786440 | tf_op jit(solution)/shard_map/ppermute | solution.py:464
  48.7 1.1 %rim.1.rim_ref = bf16[16,512]{1,0:T(8,128)(2,1)S(1)} custom-call(s32[4]{0:T(128)S(1)} %pad_add_fusion.meta, bf16[272,512]{1,0:T(8,128)(2,1)S(1)} %get-tuple-element.55.glu_ref, bf16[64,512]{1,0:T(8,128)(2,1)S(1)} %collective-permute-done.12.edge_ref, s32[512,128]{1,0:T(8,128)S(1)} %get-tuple-element.42.run_ref, f32[32,256]{1,0:T(8,128)} %pad_maximum_fusion.taps_own, ...), custom_call_target="tpu_custom_call" | custom-call | flops 1150000000 | tf_op jit(solution)/shard_map/rim/pallas_call | solution.py:388
  50.3 1.6 %finish_own.1.done_ref = bf16[256,512]{1,0:T(8,128)(2,1)S(1)} custom-call(s32[4]{0:T(128)S(1)} %pad_add_fusion.meta, bf16[256,512]{1,0:T(8,128)(2,1)S(1)} %convolve.1.act_ref, bf16[16,512]{1,0:T(8,128)(2,1)S(1)} %rim.1.rim_ref, bf16[256,512]{1,0:T(8,128)(2,1)S(1)} %get-tuple-element.60.mid_ref, bf16[256,1024]{1,0:T(8,128)(2,1)} %w_own.1, ...), custom_call_target="tpu_custom_call" | custom-call | flops 1380000000 | tf_op jit(solution)/shard_map/finish_own/pallas_call | solution.py:435
  51.9 2.4 %finish.1 = bf16[512,512]{1,0:T(8,128)(2,1)} custom-call(s32[4]{0:T(128)S(1)} %pad_add_fusion.meta, bf16[256,512]{1,0:T(8,128)(2,1)S(1)} %collective-permute-done.11.act_ref, bf16[16,512]{1,0:T(8,128)(2,1)S(1)} %collective-permute-done.13.rim_ref, bf16[256,512]{1,0:T(8,128)(2,1)S(1)} %collective-permute-done.14.mid_ref, bf16[256,1024]{1,0:T(8,128)(2,1)} %w_own.1, ...), custom_call_target="tpu_custom_call" | custom-call | flops 1380000000 | tf_op jit(solution)/shard_map/finish/pallas_call | solution.py:435
  (47 shorter events, 2.5 us)
Async XLA Ops:
  0.0 2.2 %copy-start = (bf16[512,512]{1,0:T(8,128)(2,1)S(1)}, bf16[512,512]{1,0:T(8,128)(2,1)}, u32[]{:S(2)}) copy-start(bf16[512,512]{1,0:T(8,128)(2,1)} %x_own.1) | copy-start | bytes 1572868
  0.0 2.2 %copy-start.7 = (f32[1024]{0:T(1024)S(1)}, f32[1024]{0:T(1024)}, u32[]{:S(2)}) copy-start(f32[1024]{0:T(1024)} %param.14) | copy-start | bytes 12292
  0.0 2.2 %collective-permute-start = (bf16[512,512]{1,0:T(8,128)(2,1)}, bf16[512,512]{1,0:T(8,128)(2,1)S(1)}, u32[]{:S(2)}, u32[]{:S(2)}) collective-permute-start(bf16[512,512]{1,0:T(8,128)(2,1)} %x_own.1), channel_id=1, source_target_pairs={{0,1},{1,0},{2,3},{3,2},{4,5},{5,4},{6,7},{7,6},{8,9},{9,8},{10,11... | collective-permute-start | bytes 1572872 | tf_op jit(solution)/shard_map/ppermute | solution.py:464
  1.9 7.9 %copy-start.11 = (s32[512]{0:T(512)S(1)}, s32[512]{0:T(512)}, u32[]{:S(2)}) copy-start(s32[512]{0:T(512)} %param.12) | copy-start | bytes 6148
  2.0 23.8 %copy-start.9 = (s32[16]{0:T(128)S(1)}, s32[16]{0:T(128)}, u32[]{:S(2)}) copy-start(s32[16]{0:T(128)} %param.13) | copy-start | bytes 196
  2.2 27.8 %copy-start.2 = (bf16[256,1024]{1,0:T(8,128)(2,1)S(1)}, bf16[256,1024]{1,0:T(8,128)(2,1)}, u32[]{:S(2)}) copy-start(bf16[256,1024]{1,0:T(8,128)(2,1)} %out_own) | copy-start | bytes 1572868
  2.2 29.8 %copy-start.10 = (f32[31,256]{1,0:T(8,128)S(1)}, f32[31,256]{1,0:T(8,128)}, u32[]{:S(2)}) copy-start(f32[31,256]{1,0:T(8,128)} %param.19) | copy-start | bytes 95236
  2.2 29.8 %copy-start.12 = (f32[256]{0:T(256)S(1)}, f32[256]{0:T(256)}, u32[]{:S(2)}) copy-start(f32[256]{0:T(256)} %param.20) | copy-start | bytes 3076
  4.8 34.7 %collective-permute-start.10 = (bf16[2,1024,256]{2,1,0:T(8,128)(2,1)S(1)}, bf16[2,1024,256]{2,1,0:T(8,128)(2,1)}, u32[]{:S(2)}, u32[]{:S(2)}) collective-permute-start(bf16[2,1024,256]{2,1,0:T(8,128)(2,1)S(1)} %bitcast.16), channel_id=1, source_target_pairs={{0,1},{1,0},{2,3},{3,2},{4,5},{5,4},{6,7},{7,6},{8,9},{9,8},{10,11... | collective-permute-start | bytes 3145736 | tf_op jit(solution)/shard_map/ppermute | solution.py:464
  5.2 21.4 %collective-permute-start.1 = (bf16[512,384]{1,0:T(8,128)(2,1)S(1)}, bf16[512,384]{1,0:T(8,128)(2,1)S(1)}, u32[]{:S(2)}, u32[]{:S(2)}) collective-permute-start(bf16[512,384]{1,0:T(8,128)(2,1)S(1)} %get-tuple-element.35), channel_id=1, source_target_pairs={{0,2},{2,0},{4,6},{6,4},{8,10},{10,8},{12,14},{14,12},{1,3},{3,1},... | collective-permute-start | bytes 1179656 | tf_op jit(solution)/shard_map/ppermute | solution.py:471
  7.9 18.7 %collective-permute-start.3 = (bf16[512,256]{1,0:T(8,128)(2,1)S(1)}, bf16[512,256]{1,0:T(8,128)(2,1)S(1)}, u32[]{:S(2)}, u32[]{:S(2)}) collective-permute-start(bf16[512,256]{1,0:T(8,128)(2,1)S(1)} %get-tuple-element.36), channel_id=1, source_target_pairs={{2,4},{4,2},{6,8},{8,6},{10,12},{12,10},{3,5},{5,3},{7,9},{9,7},{1... | collective-permute-start | bytes 786440 | tf_op jit(solution)/shard_map/ppermute | solution.py:468
  8.5 18.1 %collective-permute-start.2 = (bf16[512,256]{1,0:T(8,128)(2,1)S(1)}, bf16[512,256]{1,0:T(8,128)(2,1)S(1)}, u32[]{:S(2)}, u32[]{:S(2)}) collective-permute-start(bf16[512,256]{1,0:T(8,128)(2,1)S(1)} %get-tuple-element.34.center.side_a), channel_id=1, source_target_pairs={{2,6},{4,0},{6,10},{8,4},{10,14},{12,8},{3,7},{5,1},{7,11},{9,5},{... | collective-permute-start | bytes 786440 | tf_op jit(solution)/shard_map/ppermute | solution.py:468
  26.6 3.4 %copy-start.3 = (bf16[512,256]{1,0:T(8,128)(2,1)}, bf16[512,256]{1,0:T(8,128)(2,1)S(1)}, u32[]{:S(2)}) copy-start(bf16[512,256]{1,0:T(8,128)(2,1)S(1)} %collective-permute-done.3.side_b) | copy-start | bytes 786436
  26.6 12.9 %copy-start.8 = (f32[1024]{0:T(1024)S(1)}, f32[1024]{0:T(1024)}, u32[]{:S(2)}) copy-start(f32[1024]{0:T(1024)} %param.17) | copy-start | bytes 12292
  30.0 9.5 %collective-permute-start.7 = (bf16[256,1024]{1,0:T(8,128)(2,1)}, bf16[256,1024]{1,0:T(8,128)(2,1)}, u32[]{:S(2)}, u32[]{:S(2)}) collective-permute-start(bf16[256,1024]{1,0:T(8,128)(2,1)} %w_own.1), channel_id=1, source_target_pairs={{0,1},{1,0},{2,3},{3,2},{4,5},{5,4},{6,7},{7,6},{8,9},{9,8},{10,11... | collective-permute-start | bytes 1572872 | tf_op jit(solution)/shard_map/ppermute | solution.py:464
  30.0 9.5 %collective-permute-start.9 = (bf16[256,1024]{1,0:T(8,128)(2,1)S(1)}, bf16[256,1024]{1,0:T(8,128)(2,1)}, u32[]{:S(2)}, u32[]{:S(2)}) collective-permute-start(bf16[256,1024]{1,0:T(8,128)(2,1)S(1)} %copy-done.2), channel_id=1, source_target_pairs={{0,1},{1,0},{2,3},{3,2},{4,5},{5,4},{6,7},{7,6},{8,9},{9,8},{10,11... | collective-permute-start | bytes 1572872 | tf_op jit(solution)/shard_map/ppermute | solution.py:464
  30.5 7.4 %collective-permute-start.4 = (bf16[512,128]{1,0:T(8,128)(2,1)}, bf16[512,128]{1,0:T(8,128)(2,1)}, u32[]{:S(2)}, u32[]{:S(2)}) collective-permute-start(bf16[512,128]{1,0:T(8,128)(2,1)} %attend.3), channel_id=1, source_target_pairs={{0,2},{2,0},{4,6},{6,4},{8,10},{10,8},{12,14},{14,12},{1,3},{3,1},... | collective-permute-start | bytes 393224 | tf_op jit(solution)/shard_map/ppermute | solution.py:471
  32.6 4.8 %collective-permute-start.8 = (f32[32,256]{1,0:T(8,128)}, f32[32,256]{1,0:T(8,128)}, u32[]{:S(2)}, u32[]{:S(2)}) collective-permute-start(f32[32,256]{1,0:T(8,128)} %pad_maximum_fusion.taps_own), channel_id=1, source_target_pairs={{0,1},{1,0},{2,3},{3,2},{4,5},{5,4},{6,7},{7,6},{8,9},{9,8},{10,11... | collective-permute-start | bytes 98312 | tf_op jit(solution)/shard_map/ppermute | solution.py:464
  37.4 1.6 %collective-permute-start.5 = (bf16[512,128]{1,0:T(8,128)(2,1)S(1)}, bf16[512,128]{1,0:T(8,128)(2,1)S(1)}, u32[]{:S(2)}, u32[]{:S(2)}) collective-permute-start(bf16[512,128]{1,0:T(8,128)(2,1)S(1)} %attend.2.mine_own), channel_id=1, source_target_pairs={{0,1},{1,0},{2,3},{3,2},{4,5},{5,4},{6,7},{7,6},{8,9},{9,8},{10,11... | collective-permute-start | bytes 393224 | tf_op jit(solution)/shard_map/ppermute | solution.py:464
  38.0 1.6 %collective-permute-start.6 = (bf16[512,128]{1,0:T(8,128)(2,1)}, bf16[512,128]{1,0:T(8,128)(2,1)S(1)}, u32[]{:S(2)}, u32[]{:S(2)}) collective-permute-start(bf16[512,128]{1,0:T(8,128)(2,1)} %collective-permute-done.4.pair_own), channel_id=1, source_target_pairs={{0,1},{1,0},{2,3},{3,2},{4,5},{5,4},{6,7},{7,6},{8,9},{9,8},{10,11... | collective-permute-start | bytes 393224 | tf_op jit(solution)/shard_map/ppermute | solution.py:464
  42.6 6.1 %collective-permute-start.12 = (bf16[64,512]{1,0:T(8,128)(2,1)S(1)}, bf16[64,512]{1,0:T(8,128)(2,1)S(1)}, u32[]{:S(2)}, u32[]{:S(2)}) collective-permute-start(bf16[64,512]{1,0:T(8,128)(2,1)S(1)} %get-tuple-element.57), channel_id=1, source_target_pairs={{2,1},{4,3},{6,5},{8,7},{10,9},{12,11},{14,13},{1,2},{3,4},{5,6},{... | collective-permute-start | bytes 196616 | tf_op jit(solution)/shard_map/ppermute | solution.py:520
  46.8 5.1 %collective-permute-start.11 = (bf16[256,512]{1,0:T(8,128)(2,1)S(1)}, bf16[256,512]{1,0:T(8,128)(2,1)S(1)}, u32[]{:S(2)}, u32[]{:S(2)}) collective-permute-start(bf16[256,512]{1,0:T(8,128)(2,1)S(1)} %convolve.1.act_ref), channel_id=1, source_target_pairs={{0,1},{1,0},{2,3},{3,2},{4,5},{5,4},{6,7},{7,6},{8,9},{9,8},{10,11... | collective-permute-start | bytes 786440 | tf_op jit(solution)/shard_map/ppermute | solution.py:464
  48.6 3.2 %collective-permute-start.14 = (bf16[256,512]{1,0:T(8,128)(2,1)S(1)}, bf16[256,512]{1,0:T(8,128)(2,1)S(1)}, u32[]{:S(2)}, u32[]{:S(2)}) collective-permute-start(bf16[256,512]{1,0:T(8,128)(2,1)S(1)} %get-tuple-element.58), channel_id=1, source_target_pairs={{0,1},{1,0},{2,3},{3,2},{4,5},{5,4},{6,7},{7,6},{8,9},{9,8},{10,11... | collective-permute-start | bytes 786440 | tf_op jit(solution)/shard_map/ppermute | solution.py:464
  49.8 2.1 %collective-permute-start.13 = (bf16[16,512]{1,0:T(8,128)(2,1)S(1)}, bf16[16,512]{1,0:T(8,128)(2,1)S(1)}, u32[]{:S(2)}, u32[]{:S(2)}) collective-permute-start(bf16[16,512]{1,0:T(8,128)(2,1)S(1)} %rim.1.rim_ref), channel_id=1, source_target_pairs={{0,1},{1,0},{2,3},{3,2},{4,5},{5,4},{6,7},{7,6},{8,9},{9,8},{10,11... | collective-permute-start | bytes 49160 | tf_op jit(solution)/shard_map/ppermute | solution.py:464
  (4 other events, 4.3 us)

commit v7 on v6

--- a/solution.py
+++ b/solution.py
@@ -46,10 +46,24 @@
 
 
 def qkv_kernel(
-    meta, own_ref, other_ref, gain_ref, w_ref, keep_ref, query_ref, send_ref, pass_ref
+    meta, own_hbm, other_hbm, gain_ref, w_hbm, _, keep_ref, query_ref, send_ref, pass_ref,
+    own_ref, other_ref, w_ref, sems,
 ):
     h = meta[0]
     first = meta[1] == 0
+    order = (1, 2, 0)
+    frames_in = [
+        pltpu.make_async_copy(own_hbm, own_ref, sems.at[0]),
+        pltpu.make_async_copy(other_hbm, other_ref, sems.at[1]),
+    ]
+    weights_in = [
+        pltpu.make_async_copy(w_hbm.at[part], w_ref.at[part], sems.at[2 + slot])
+        for slot, part in enumerate(order)
+    ]
+    for copy in frames_in + weights_in:
+        copy.start()
+    for copy in frames_in:
+        copy.wait()
     rows = own_ref.shape[0]
     tile = 256
     for at in range(0, rows, tile):
@@ -58,7 +72,9 @@
             own_ref[here, :].astype(F32), other_ref[here, :].astype(F32),
             gain_ref[h], gain_ref[1 - h],
         )
-        for slot, part in enumerate((1, 2, 0)):
+        for slot, part in enumerate(order):
+            if at == 0:
+                weights_in[slot].wait()
             value = (dot(n_own, w_ref[part, h]) + dot(n_other, w_ref[part, 1 - h])).astype(BF16)
             sub = value.shape[1] // 2
             cols = slice(slot * sub, slot * sub + sub)
@@ -72,13 +88,15 @@
                 query_ref[here, :] = keep
 
 
-def project(meta, frames, other, gain, qkv):
+def project(meta, frames, other, gain, qkv, early):
     rows, half = frames.shape
     width = qkv.shape[2]
     vmem = pl.BlockSpec(memory_space=pltpu.VMEM)
+    hbm = pl.BlockSpec(memory_space=pltpu.HBM)
     return pl.pallas_call(
         qkv_kernel,
-        in_specs=[pl.BlockSpec(memory_space=pltpu.SMEM)] + [vmem] * 4,
+        in_specs=[pl.BlockSpec(memory_space=pltpu.SMEM), hbm, hbm, vmem, hbm]
+        + [pl.BlockSpec(memory_space=pl.ANY)],
         out_specs=[vmem] * 4,
         out_shape=[
             jax.ShapeDtypeStruct((rows, width), BF16),
@@ -86,10 +104,16 @@
             jax.ShapeDtypeStruct((rows, 3 * width // 2), BF16),
             jax.ShapeDtypeStruct((rows, width), BF16),
         ],
+        scratch_shapes=[
+            pltpu.VMEM((rows, half), BF16),
+            pltpu.VMEM((rows, half), BF16),
+            pltpu.VMEM((3, 2, half, width), BF16),
+            pltpu.SemaphoreType.DMA((5,)),
+        ],
         compiler_params=pltpu.CompilerParams(vmem_limit_bytes=VMEM_LIMIT),
         name="project",
     )(meta, frames, other, gain.reshape(2, 1, half),
-      qkv.transpose(1, 0, 2).reshape(3, 2, half, width))
+      qkv.transpose(1, 0, 2).reshape(3, 2, half, width), early)
 
 
 def bounds_kernel(meta, counts, valid, own_ref, pair_ref):
@@ -195,6 +219,7 @@
         out_specs=vmem,
         out_shape=jax.ShapeDtypeStruct((rows, width), BF16),
         compiler_params=pltpu.CompilerParams(vmem_limit_bytes=VMEM_LIMIT),
+        cost_estimate=weight(3),
         name="attend",
     )(a_high, query, center, side_a, side_b, runs)
 
@@ -222,14 +247,15 @@
             [jnp.where(first, mine, pair), jnp.where(first, pair, mine)], axis=1
         )
 
+    depth = 2 * mine_own.shape[1]
     c_own = joined(mine_own, pair_own)
     c_other = joined(mine_other, pair_other)
     own_cols = pl.ds(pl.multiple_of(h * half, half), half)
     other_cols = pl.ds(pl.multiple_of((1 - h) * half, half), half)
 
     def mid(cols, x_ref):
-        first = dot(c_own, out_own[:, cols]).astype(BF16).astype(F32)
-        second = dot(c_other, out_other[:, cols]).astype(BF16).astype(F32)
+        first = dot(c_own, out_own[:depth, cols]).astype(BF16).astype(F32)
+        second = dot(c_other, out_other[:depth, cols]).astype(BF16).astype(F32)
         return (x_ref[here, :].astype(F32) + (first + second)).astype(BF16)
 
     m_own = mid(own_cols, x_own)
@@ -288,6 +314,7 @@
             jax.ShapeDtypeStruct((rows - EDGE, half), BF16),
         ],
         compiler_params=pltpu.CompilerParams(vmem_limit_bytes=VMEM_LIMIT),
+        cost_estimate=weight(3),
         name="gated",
     )(meta, *contexts, x_own, x_other, out_own, out_other,
       gain.reshape(2, 1, half), in_own, in_other, runs)
@@ -404,8 +431,9 @@
     chan = act_ref.shape[1] // 2
     act[...] = act_ref[...]
     act[pl.ds(rim_at, EDGE), :] = rim_ref[...]
-    first = dot(act[:, :chan], w_first[:, cols]).astype(BF16).astype(F32)
-    second = dot(act[:, chan:], w_second[:, cols]).astype(BF16).astype(F32)
+    below = w_first.shape[0] - chan
+    first = dot(act[:, :chan], w_first[below:, cols]).astype(BF16).astype(F32)
+    second = dot(act[:, chan:], w_second[below:, cols]).astype(BF16).astype(F32)
     return (mid_ref[...].astype(F32) + (first + second)).astype(BF16)
 
 
@@ -479,7 +507,10 @@
         (block + 1 - 2 * column) * rows,
     ])
     other = swap(frames)
-    keep, query, send, passed = project(meta, frames, other, attn_gain, qkv_weight)
+    pointwise = pointwise_in.transpose(1, 0, 2)
+    keep, query, send, passed = project(
+        meta, frames, other, attn_gain, qkv_weight, pointwise
+    )
     far_own = shift(passed, 1)
     pair = exchange(send)
     far_pair = shift(keep, 2)
@@ -490,27 +521,23 @@
     counts = lax.all_to_all(
         jnp.broadcast_to(counts[None, :], (blocks, counts.shape[0])), "tm", 0, 0
     )
-    pointwise = pointwise_in.transpose(1, 0, 2)
-    out_weight, pointwise, _ = lax.optimization_barrier((out_weight, pointwise, keep))
+    taps = jnp.concatenate([depthwise, mid_gain[None, :]], axis=0)
+    out_weight, pointwise, taps, keep = lax.optimization_barrier(
+        (out_weight, pointwise, taps, keep)
+    )
     pointwise_other = swap(pointwise)
     out_other = swap(out_weight)
     runs, pair_runs = bounds(meta, counts, utt_valid, rows)
+    taps, pointwise_out, runs = lax.optimization_barrier((taps, pointwise_out, runs))
+    taps_other = swap(taps)
+    pointwise_out_other = swap(pointwise_out)
     pair, far_pair, far_own, runs, pair_runs = lax.optimization_barrier(
         (pair, far_pair, far_own, runs, pair_runs)
     )
     pair_context = attend(column.reshape(1), pair, pair, keep, far_pair, pair_runs)
-    depthwise, mid_gain, pointwise_out, pair_context = lax.optimization_barrier(
-        (depthwise, mid_gain, pointwise_out, pair_context)
-    )
     pair_context = exchange(pair_context)
-    taps = jnp.concatenate([depthwise, mid_gain[None, :]], axis=0)
-    pointwise_out_other = swap(pointwise_out)
-    taps_other = swap(taps)
     context = attend((1 - column).reshape(1), query, keep, pair, far_own, runs)
     contexts = (context, pair_context, swap(context), swap(pair_context))
-    contexts, pointwise_out_other, taps_other = lax.optimization_barrier(
-        (contexts, pointwise_out_other, taps_other)
-    )
     glu, edge, mid_keep, mid_send = gated(
         meta, contexts, frames, other, out_weight, out_other, conv_gain,
         pointwise, pointwise_other, runs,

time: 54.7 us -> 54.5 us (level)
  blocking collectives: 15.8 us -> 0 us
  starting transfers between devices: 11.1 us -> 20.5 us
  waiting for transfers between devices: 1.66 us -> 7.57 us
  Pallas kernels: 20.7 us -> 23 us
  local copies, waits for them, and re-layouts: 4.04 us -> 2.77 us
  other arithmetic: 0.81 us -> 0.21 us
    all_to_all x1 -> x0, blocking collectives: 15.8 us -> none  [local(): lax.all_to_all(jnp.broadcast_to(counts[None, :], (blocks, counts.shape[0]...]
    all_to_all x0 -> x1, starting transfers between devices: none -> 8.64 us  [local(): lax.all_to_all(jnp.broadcast_to(counts[None, :], (blocks, counts.shape[0]...]
    all_to_all x0 -> x1, waiting for transfers between devices: none -> 6.45 us  [local(): lax.all_to_all(jnp.broadcast_to(counts[None, :], (blocks, counts.shape[0]...]
    pallas_call x1, Pallas kernels: 1.94 us -> 4.67 us  [project(): pl.pallas_call(qkv_kernel, in_specs=[pl.BlockSpec(memory_space=pltpu.SMEM...]
    unnamed x27 -> x25, local copies, waits for them, and re-layouts: 4.03 us -> 2.16 us
    pallas_call x2, Pallas kernels: 6.3 us -> 7.7 us  [attend(): pl.pallas_call(attend_kernel, in_specs=[pl.BlockSpec(memory_space=pltpu.S...]
    pallas_call x2, Pallas kernels: 3.92 us -> 2.58 us  [finish(): pl.pallas_call(finish_own_kernel if done is None else finish_kernel, in_s...]
    ppermute x2, starting transfers between devices: 1.96 us -> 2.67 us  [shift(): return lax.ppermute(value, 'tm', [p for p in pairs if 0 <= p[1] < blocks])]
  transfers between devices with their start and end apart: 15 -> 16, of which waited for: 3 -> 3; matrix products, arithmetic and copies ran while one was open for 4% -> 4% of each run, Pallas kernels for 24% -> 31%
where the time goes in v7:
time: 54.5 us; the launch traced here: 54.2 us
  Pallas kernels  23 us (42%)
  starting transfers between devices  20.5 us (38%)
  waiting for transfers between devices  7.57 us (14%)
  local copies, waits for them, and re-layouts  2.77 us (5%)
    all_to_all x1, starting transfers between devices, local(): lax.all_to_all(jnp.broadcast_to(counts[None, :], (blocks, counts.shape[0]...  8.64 us
    pallas_call x2, Pallas kernels, attend(): pl.pallas_call(attend_kernel, in_specs=[pl.BlockSpec(memory_space=pltpu.S...  7.7 us
    all_to_all x1, waiting for transfers between devices, local(): lax.all_to_all(jnp.broadcast_to(counts[None, :], (blocks, counts.shape[0]...  6.45 us
    pallas_call x1, Pallas kernels, project(): pl.pallas_call(qkv_kernel, in_specs=[pl.BlockSpec(memory_space=pltpu.SMEM...  4.67 us
    ppermute x2, starting transfers between devices, exchange(): return lax.ppermute(value, 'tm', [(i, i ^ 1) for i in range(blocks)])  4.37 us
    ppermute x10, starting transfers between devices, swap(): return lax.ppermute(value, 'head', [(0, 1), (1, 0)])  4.14 us
    pallas_call x1, Pallas kernels, convolve(): pl.pallas_call(conv_kernel, in_specs=[pl.BlockSpec(memory_space=pltpu.SME...  3.45 us
    pallas_call x1, Pallas kernels, gated(): pl.pallas_call(gate_kernel, in_specs=[pl.BlockSpec(memory_space=pltpu.SME...  2.86 us
  transfers between devices with their start and end apart: 16, of which 3 were waited for; matrix products, arithmetic and copies ran while one was open for 4% of the time, Pallas kernels for 31%

profile of v7, /device:TPU:0, one launch (start us, length us, event | category | flops | bytes accessed | tf_op | source)
XLA Modules:
  0.0 54.2 jit_solution(17942271757803195735)
XLA Ops:
  0.0 0.5 collective-permute-start
  0.5 1.5 %copy.16 = bf16[1024,2,256]{2,0,1:T(8,128)(2,1)S(1)} copy(bf16[1024,2,256]{2,1,0:T(2,128)(2,1)} %param.18) | data formatting | bytes 2097152 | tf_op args[7]
  2.5 4.7 %project.1 = (bf16[512,256]{1,0:T(8,128)(2,1)}, bf16[512,128]{1,0:T(8,128)(2,1)S(1)}, bf16[512,384]{1,0:T(8,128)(2,1)}, bf16[512,256]{1,0:T(8,128)(2,1)}) custom-call(s32[4]{0:T(128)S(1)} %pad_add_fusion.meta, bf16[512,512]{1,0:T(8,128)(2,1)S(1)} %copy-done.1, bf16[512,512]{1,0:T(8,128)(2,1)} %collective-permute-done.other_hbm.x_other, ...), custom_call_target="tpu_custom_call" | custom-call | tf_op jit(solution)/shard_map/project/pallas_call | solution.py:96
  7.2 0.6 %copy-done.6 = bf16[512,128]{1,0:T(8,128)(2,1)} copy-done((bf16[512,128]{1,0:T(8,128)(2,1)}, bf16[512,128]{1,0:T(8,128)(2,1)S(1)}, u32[]{:S(2)}) %copy-start.6) | copy-done | bytes 131096
  7.8 2.9 %collective-permute-start.1 = (bf16[512,384]{1,0:T(8,128)(2,1)}, bf16[512,384]{1,0:T(8,128)(2,1)S(1)}, u32[]{:S(2)}, u32[]{:S(2)}) collective-permute-start(bf16[512,384]{1,0:T(8,128)(2,1)} %get-tuple-element.31), channel_id=1, source_target_pairs={{0,2},{2,0},{4,6},{6,4},{8,10},{10,8},{12,14},{14,12},{1,3},{3,1},... | collective-permute-start | bytes 1179656 | tf_op jit(solution)/shard_map/ppermute | solution.py:499
  10.7 1.3 %collective-permute-start.2 = (bf16[512,256]{1,0:T(8,128)(2,1)}, bf16[512,256]{1,0:T(8,128)(2,1)}, u32[]{:S(2)}, u32[]{:S(2)}) collective-permute-start(bf16[512,256]{1,0:T(8,128)(2,1)} %get-tuple-element.30.center.side_a), channel_id=1, source_target_pairs={{2,6},{4,0},{6,10},{8,4},{10,14},{12,8},{3,7},{5,1},{7,11},{9,5},{... | collective-permute-start | bytes 786440 | tf_op jit(solution)/shard_map/ppermute | solution.py:496
  12.0 1.4 %collective-permute-start.3 = (bf16[512,256]{1,0:T(8,128)(2,1)}, bf16[512,256]{1,0:T(8,128)(2,1)}, u32[]{:S(2)}, u32[]{:S(2)}) collective-permute-start(bf16[512,256]{1,0:T(8,128)(2,1)} %get-tuple-element.32), channel_id=1, source_target_pairs={{2,4},{4,2},{6,8},{8,6},{10,12},{12,10},{3,5},{5,3},{7,9},{9,7},{1... | collective-permute-start | bytes 786440 | tf_op jit(solution)/shard_map/ppermute | solution.py:496
  13.5 0.6 %broadcast_in_dim.5 = s32[8,1,16]{2,1,0:T(1,128)} broadcast(s32[16]{0:T(128)S(1)} %convert_reduce_fusion), dimensions={2} | broadcast | bytes 576 | tf_op jit(solution)/shard_map/broadcast_in_dim | solution.py:522
  14.1 8.6 %all-to-all-start = ((s32[8,1,16]{2,1,0:T(1,128)}), s32[8,1,16]{2,1,0:T(1,128)S(1)}, u32[]{:S(2)}, u32[]{:S(2)}) async-start(s32[8,1,16]{2,1,0:T(1,128)} %broadcast_in_dim.5), calls=%async_computation | async-start | bytes 8192 | tf_op jit(solution)/shard_map/all_to_all | solution.py:521
  22.8 6.4 %all-to-all-done = s32[8,1,16]{2,1,0:T(1,128)S(1)} async-done(((s32[8,1,16]{2,1,0:T(1,128)}), s32[8,1,16]{2,1,0:T(1,128)S(1)}, u32[]{:S(2)}, u32[]{:S(2)}) %all-to-all-start) | async-done | bytes 544 | tf_op jit(solution)/shard_map/all_to_all | solution.py:521
  29.2 0.8 %bounds.1 = (s32[512,128]{1,0:T(8,128)S(1)}, s32[512,128]{1,0:T(8,128)S(1)}) custom-call(s32[4]{0:T(128)S(1)} %pad_add_fusion.meta, s32[8,16]{1,0:T(8,128)S(1)} %bitcast.20, s32[1,16]{1,0:T(1,128)S(1)} %bitcast.22), custom_call_target="tpu_custom_call" | custom-call | tf_op jit(solution)/shard_map/bounds/pallas_call | solution.py:144
  30.1 3.7 %attend.3 = bf16[512,128]{1,0:T(8,128)(2,1)S(1)} custom-call(s32[1]{0:T(128)} %bitcast.1.a_high, bf16[512,384]{1,0:T(8,128)(2,1)S(1)} %collective-permute-done.1.side_a.query.center, bf16[512,384]{1,0:T(8,128)(2,1)S(1)} %collective-permute-done.1.side_a.query.center, bf16[512,256]{1,0:T(8,128)(2,1)} %get-tuple-element.30.center.side_a, ...), custom_call_target="tpu_custom_call" | custom-call | flops 3449999872 | tf_op jit(solution)/shard_map/attend/pallas_call | solution.py:216
  33.9 1.5 %collective-permute-start.4 = (bf16[512,128]{1,0:T(8,128)(2,1)S(1)}, bf16[512,128]{1,0:T(8,128)(2,1)S(1)}, u32[]{:S(2)}, u32[]{:S(2)}) collective-permute-start(bf16[512,128]{1,0:T(8,128)(2,1)S(1)} %attend.3), channel_id=1, source_target_pairs={{0,2},{2,0},{4,6},{6,4},{8,10},{10,8},{12,14},{14,12},{1,3},{3,1},... | collective-permute-start | bytes 393224 | tf_op jit(solution)/shard_map/ppermute | solution.py:499
  35.4 4.0 %attend.2.mine_own = bf16[512,128]{1,0:T(8,128)(2,1)S(1)} custom-call(s32[1]{0:T(128)} %bitcast.4.a_high, bf16[512,128]{1,0:T(8,128)(2,1)S(1)} %copy-done.7, bf16[512,256]{1,0:T(8,128)(2,1)} %get-tuple-element.30.center.side_a, bf16[512,384]{1,0:T(8,128)(2,1)S(1)} %collective-permute-done.1.side_a.query.center, ...), custom_call_target="tpu_custom_call" | custom-call | flops 3449999872 | tf_op jit(solution)/shard_map/attend/pallas_call | solution.py:216
  39.5 0.5 collective-permute-start.6
  40.0 0.7 %collective-permute-done.5.mine_other = bf16[512,128]{1,0:T(8,128)(2,1)S(1)} collective-permute-done((bf16[512,128]{1,0:T(8,128)(2,1)S(1)}, bf16[512,128]{1,0:T(8,128)(2,1)S(1)}, u32[]{:S(2)}, u32[]{:S(2)}) %collective-permute-start.5) | collective-permute-done | bytes 131104 | tf_op jit(solution)/shard_map/ppermute | solution.py:492
  41.0 2.9 %gated.1 = (bf16[272,512]{1,0:T(8,128)(2,1)S(1)}, bf16[64,512]{1,0:T(8,128)(2,1)S(1)}, bf16[256,512]{1,0:T(8,128)(2,1)S(1)}, bf16[256,512]{1,0:T(8,128)(2,1)S(1)}) custom-call(s32[4]{0:T(128)S(1)} %pad_add_fusion.meta, bf16[512,128]{1,0:T(8,128)(2,1)S(1)} %attend.2.mine_own, bf16[512,128]{1,0:T(8,128)(2,1)S(1)} %collective-permute-done.4.pair_own, ...), custom_call_target="tpu_custom_call" | custom-call | flops 3449999872 | tf_op jit(solution)/shard_map/gated/pallas_call | solution.py:306
  43.9 0.7 %collective-permute-start.11 = (bf16[64,512]{1,0:T(8,128)(2,1)S(1)}, bf16[64,512]{1,0:T(8,128)(2,1)S(1)}, u32[]{:S(2)}, u32[]{:S(2)}) collective-permute-start(bf16[64,512]{1,0:T(8,128)(2,1)S(1)} %get-tuple-element.47), channel_id=1, source_target_pairs={{2,1},{4,3},{6,5},{8,7},{10,9},{12,11},{14,13},{1,2},{3,4},{5,6},{... | collective-permute-start | bytes 196616 | tf_op jit(solution)/shard_map/ppermute | solution.py:547
  44.5 3.5 %convolve.1.act_ref = bf16[256,512]{1,0:T(8,128)(2,1)S(1)} custom-call(s32[4]{0:T(128)S(1)} %pad_add_fusion.meta, bf16[272,512]{1,0:T(8,128)(2,1)S(1)} %get-tuple-element.45.glu_ref, s32[512,128]{1,0:T(8,128)S(1)} %get-tuple-element.40.run_ref, f32[32,256]{1,0:T(8,128)S(1)} %pad_maximum_fusion.taps_own, f32[32,256]{1,0:T(8,128)S(1)} %collective-permute-done.9.taps_other), custom_call_target="tpu_custom_call" | custom-call | flops 3449999872 | tf_op jit(solution)/shard_map/convolve/pallas_call | solution.py:379
  48.0 2.2 %collective-permute-start.10 = (bf16[256,512]{1,0:T(8,128)(2,1)S(1)}, bf16[256,512]{1,0:T(8,128)(2,1)S(1)}, u32[]{:S(2)}, u32[]{:S(2)}) collective-permute-start(bf16[256,512]{1,0:T(8,128)(2,1)S(1)} %convolve.1.act_ref), channel_id=1, source_target_pairs={{0,1},{1,0},{2,3},{3,2},{4,5},{5,4},{6,7},{7,6},{8,9},{9,8},{10,11... | collective-permute-start | bytes 786440 | tf_op jit(solution)/shard_map/ppermute | solution.py:492
  50.3 0.8 %rim.1.rim_ref = bf16[16,512]{1,0:T(8,128)(2,1)S(1)} custom-call(s32[4]{0:T(128)S(1)} %pad_add_fusion.meta, bf16[272,512]{1,0:T(8,128)(2,1)S(1)} %get-tuple-element.45.glu_ref, bf16[64,512]{1,0:T(8,128)(2,1)S(1)} %collective-permute-done.11.edge_ref, s32[512,128]{1,0:T(8,128)S(1)} %get-tuple-element.40.run_ref, f32[32,256]{1,0:T(8,128)S(1)} %pad_maximum_fusion.taps_own, ...), custom_call_target="tpu_custom_call" | custom-call | flops 1150000000 | tf_op jit(solution)/shard_map/rim/pallas_call | solution.py:415
  51.1 0.5 collective-permute-start.12
  51.6 0.9 %finish_own.1.done_ref = bf16[256,512]{1,0:T(8,128)(2,1)S(1)} custom-call(s32[4]{0:T(128)S(1)} %pad_add_fusion.meta, bf16[256,512]{1,0:T(8,128)(2,1)S(1)} %convolve.1.act_ref, bf16[16,512]{1,0:T(8,128)(2,1)S(1)} %rim.1.rim_ref, bf16[256,512]{1,0:T(8,128)(2,1)S(1)} %get-tuple-element.50.mid_ref, bf16[256,1024]{1,0:T(8,128)(2,1)S(1)} %copy-done.5, ...), custom_call_target="tpu_custom_call" | custom-call | flops 1380000000 | tf_op jit(solution)/shard_map/finish_own/pallas_call | solution.py:463
  52.5 1.7 %finish.1 = bf16[512,512]{1,0:T(8,128)(2,1)} custom-call(s32[4]{0:T(128)S(1)} %pad_add_fusion.meta, bf16[256,512]{1,0:T(8,128)(2,1)S(1)} %collective-permute-done.10.act_ref, bf16[16,512]{1,0:T(8,128)(2,1)S(1)} %collective-permute-done.12.rim_ref, bf16[256,512]{1,0:T(8,128)(2,1)S(1)} %collective-permute-done.13.mid_ref, bf16[256,1024]{1,0:T(8,128)(2,1)S(1)} %copy-done.5, ...), custom_call_target="tpu_custom_call" | custom-call | flops 1380000000 | tf_op jit(solution)/shard_map/finish/pallas_call | solution.py:463
  (46 shorter events, 1.1 us)
Async XLA Ops:
  0.0 2.4 %collective-permute-start = (bf16[512,512]{1,0:T(8,128)(2,1)}, bf16[512,512]{1,0:T(8,128)(2,1)}, u32[]{:S(2)}, u32[]{:S(2)}) collective-permute-start(bf16[512,512]{1,0:T(8,128)(2,1)} %x_own.1), channel_id=1, source_target_pairs={{0,1},{1,0},{2,3},{3,2},{4,5},{5,4},{6,7},{7,6},{8,9},{9,8},{10,11... | collective-permute-start | bytes 1572872 | tf_op jit(solution)/shard_map/ppermute | solution.py:492
  2.4 8.2 %copy-start.9 = (f32[31,256]{1,0:T(8,128)S(1)}, f32[31,256]{1,0:T(8,128)}, u32[]{:S(2)}) copy-start(f32[31,256]{1,0:T(8,128)} %param.19) | copy-start | bytes 95236
  2.4 8.2 %copy-start.11 = (f32[256]{0:T(256)S(1)}, f32[256]{0:T(256)}, u32[]{:S(2)}) copy-start(f32[256]{0:T(256)} %param.20) | copy-start | bytes 3076
  2.4 11.0 %copy-start.10 = (s32[512]{0:T(512)S(1)}, s32[512]{0:T(512)}, u32[]{:S(2)}) copy-start(s32[512]{0:T(512)} %param.12) | copy-start | bytes 6148
  2.4 26.8 %copy-start.3 = (s32[16]{0:T(128)S(1)}, s32[16]{0:T(128)}, u32[]{:S(2)}) copy-start(s32[16]{0:T(128)} %param.13) | copy-start | bytes 196
  7.8 22.3 %collective-permute-start.1 = (bf16[512,384]{1,0:T(8,128)(2,1)}, bf16[512,384]{1,0:T(8,128)(2,1)S(1)}, u32[]{:S(2)}, u32[]{:S(2)}) collective-permute-start(bf16[512,384]{1,0:T(8,128)(2,1)} %get-tuple-element.31), channel_id=1, source_target_pairs={{0,2},{2,0},{4,6},{6,4},{8,10},{10,8},{12,14},{14,12},{1,3},{3,1},... | collective-permute-start | bytes 1179656 | tf_op jit(solution)/shard_map/ppermute | solution.py:499
  10.7 30.3 %collective-permute-start.8 = (bf16[2,1024,256]{2,1,0:T(8,128)(2,1)S(1)}, bf16[2,1024,256]{2,1,0:T(8,128)(2,1)S(1)}, u32[]{:S(2)}, u32[]{:S(2)}) collective-permute-start(bf16[2,1024,256]{2,1,0:T(8,128)(2,1)S(1)} %bitcast.17), channel_id=1, source_target_pairs={{0,1},{1,0},{2,3},{3,2},{4,5},{5,4},{6,7},{7,6},{8,9},{9,8},{10,11... | collective-permute-start | bytes 3145736 | tf_op jit(solution)/shard_map/ppermute | solution.py:492
  10.7 19.4 %collective-permute-start.2 = (bf16[512,256]{1,0:T(8,128)(2,1)}, bf16[512,256]{1,0:T(8,128)(2,1)}, u32[]{:S(2)}, u32[]{:S(2)}) collective-permute-start(bf16[512,256]{1,0:T(8,128)(2,1)} %get-tuple-element.30.center.side_a), channel_id=1, source_target_pairs={{2,6},{4,0},{6,10},{8,4},{10,14},{12,8},{3,7},{5,1},{7,11},{9,5},{... | collective-permute-start | bytes 786440 | tf_op jit(solution)/shard_map/ppermute | solution.py:496
  12.0 18.1 %collective-permute-start.3 = (bf16[512,256]{1,0:T(8,128)(2,1)}, bf16[512,256]{1,0:T(8,128)(2,1)}, u32[]{:S(2)}, u32[]{:S(2)}) collective-permute-start(bf16[512,256]{1,0:T(8,128)(2,1)} %get-tuple-element.32), channel_id=1, source_target_pairs={{2,4},{4,2},{6,8},{8,6},{10,12},{12,10},{3,5},{5,3},{7,9},{9,7},{1... | collective-permute-start | bytes 786440 | tf_op jit(solution)/shard_map/ppermute | solution.py:496
  14.1 15.1 %all-to-all-start = ((s32[8,1,16]{2,1,0:T(1,128)}), s32[8,1,16]{2,1,0:T(1,128)S(1)}, u32[]{:S(2)}, u32[]{:S(2)}) async-start(s32[8,1,16]{2,1,0:T(1,128)} %broadcast_in_dim.5), calls=%async_computation | async-start | bytes 8192 | tf_op jit(solution)/shard_map/all_to_all | solution.py:521
  22.8 18.2 %collective-permute-start.7 = (bf16[256,1024]{1,0:T(8,128)(2,1)}, bf16[256,1024]{1,0:T(8,128)(2,1)}, u32[]{:S(2)}, u32[]{:S(2)}) collective-permute-start(bf16[256,1024]{1,0:T(8,128)(2,1)} %out_own), channel_id=1, source_target_pairs={{0,1},{1,0},{2,3},{3,2},{4,5},{5,4},{6,7},{7,6},{8,9},{9,8},{10,11... | collective-permute-start | bytes 1572872 | tf_op jit(solution)/shard_map/ppermute | solution.py:492
  30.1 5.3 %copy-start.7 = (bf16[512,128]{1,0:T(8,128)(2,1)S(1)}, bf16[512,128]{1,0:T(8,128)(2,1)}, u32[]{:S(2)}) copy-start(bf16[512,128]{1,0:T(8,128)(2,1)} %copy-done.6) | copy-start | bytes 393220
  33.9 5.6 %collective-permute-start.4 = (bf16[512,128]{1,0:T(8,128)(2,1)S(1)}, bf16[512,128]{1,0:T(8,128)(2,1)S(1)}, u32[]{:S(2)}, u32[]{:S(2)}) collective-permute-start(bf16[512,128]{1,0:T(8,128)(2,1)S(1)} %attend.3), channel_id=1, source_target_pairs={{0,2},{2,0},{4,6},{6,4},{8,10},{10,8},{12,14},{14,12},{1,3},{3,1},... | collective-permute-start | bytes 393224 | tf_op jit(solution)/shard_map/ppermute | solution.py:499
  35.4 5.4 %copy-start.5 = (bf16[256,1024]{1,0:T(8,128)(2,1)S(1)}, bf16[256,1024]{1,0:T(8,128)(2,1)}, u32[]{:S(2)}) copy-start(bf16[256,1024]{1,0:T(8,128)(2,1)} %w_own.1) | copy-start | bytes 1572868
  35.4 5.6 %copy-start.4 = (bf16[256,1024]{1,0:T(8,128)(2,1)S(1)}, bf16[256,1024]{1,0:T(8,128)(2,1)}, u32[]{:S(2)}) copy-start(bf16[256,1024]{1,0:T(8,128)(2,1)} %out_own) | copy-start | bytes 1572868
  35.4 5.6 %copy-start.8 = (f32[1024]{0:T(1024)S(1)}, f32[1024]{0:T(1024)}, u32[]{:S(2)}) copy-start(f32[1024]{0:T(1024)} %param.17) | copy-start | bytes 12292
  39.4 1.4 %collective-permute-start.5 = (bf16[512,128]{1,0:T(8,128)(2,1)S(1)}, bf16[512,128]{1,0:T(8,128)(2,1)S(1)}, u32[]{:S(2)}, u32[]{:S(2)}) collective-permute-start(bf16[512,128]{1,0:T(8,128)(2,1)S(1)} %attend.2.mine_own), channel_id=1, source_target_pairs={{0,1},{1,0},{2,3},{3,2},{4,5},{5,4},{6,7},{7,6},{8,9},{9,8},{10,11... | collective-permute-start | bytes 393224 | tf_op jit(solution)/shard_map/ppermute | solution.py:492
  39.5 1.5 %collective-permute-start.6 = (bf16[512,128]{1,0:T(8,128)(2,1)S(1)}, bf16[512,128]{1,0:T(8,128)(2,1)S(1)}, u32[]{:S(2)}, u32[]{:S(2)}) collective-permute-start(bf16[512,128]{1,0:T(8,128)(2,1)S(1)} %collective-permute-done.4.pair_own), channel_id=1, source_target_pairs={{0,1},{1,0},{2,3},{3,2},{4,5},{5,4},{6,7},{7,6},{8,9},{9,8},{10,11... | collective-permute-start | bytes 393224 | tf_op jit(solution)/shard_map/ppermute | solution.py:492
  40.0 4.6 %collective-permute-start.9 = (f32[32,256]{1,0:T(8,128)S(1)}, f32[32,256]{1,0:T(8,128)S(1)}, u32[]{:S(2)}, u32[]{:S(2)}) collective-permute-start(f32[32,256]{1,0:T(8,128)S(1)} %pad_maximum_fusion.taps_own), channel_id=1, source_target_pairs={{0,1},{1,0},{2,3},{3,2},{4,5},{5,4},{6,7},{7,6},{8,9},{9,8},{10,11... | collective-permute-start | bytes 98312 | tf_op jit(solution)/shard_map/ppermute | solution.py:492
  40.8 10.8 %collective-permute-start.14 = (bf16[256,1024]{1,0:T(8,128)(2,1)S(1)}, bf16[256,1024]{1,0:T(8,128)(2,1)S(1)}, u32[]{:S(2)}, u32[]{:S(2)}) collective-permute-start(bf16[256,1024]{1,0:T(8,128)(2,1)S(1)} %copy-done.5), channel_id=1, source_target_pairs={{0,1},{1,0},{2,3},{3,2},{4,5},{5,4},{6,7},{7,6},{8,9},{9,8},{10,11... | collective-permute-start | bytes 1572872 | tf_op jit(solution)/shard_map/ppermute | solution.py:492
  43.9 6.4 %collective-permute-start.11 = (bf16[64,512]{1,0:T(8,128)(2,1)S(1)}, bf16[64,512]{1,0:T(8,128)(2,1)S(1)}, u32[]{:S(2)}, u32[]{:S(2)}) collective-permute-start(bf16[64,512]{1,0:T(8,128)(2,1)S(1)} %get-tuple-element.47), channel_id=1, source_target_pairs={{2,1},{4,3},{6,5},{8,7},{10,9},{12,11},{14,13},{1,2},{3,4},{5,6},{... | collective-permute-start | bytes 196616 | tf_op jit(solution)/shard_map/ppermute | solution.py:547
  48.0 4.5 %collective-permute-start.10 = (bf16[256,512]{1,0:T(8,128)(2,1)S(1)}, bf16[256,512]{1,0:T(8,128)(2,1)S(1)}, u32[]{:S(2)}, u32[]{:S(2)}) collective-permute-start(bf16[256,512]{1,0:T(8,128)(2,1)S(1)} %convolve.1.act_ref), channel_id=1, source_target_pairs={{0,1},{1,0},{2,3},{3,2},{4,5},{5,4},{6,7},{7,6},{8,9},{9,8},{10,11... | collective-permute-start | bytes 786440 | tf_op jit(solution)/shard_map/ppermute | solution.py:492
  50.2 2.4 %collective-permute-start.13 = (bf16[256,512]{1,0:T(8,128)(2,1)S(1)}, bf16[256,512]{1,0:T(8,128)(2,1)S(1)}, u32[]{:S(2)}, u32[]{:S(2)}) collective-permute-start(bf16[256,512]{1,0:T(8,128)(2,1)S(1)} %get-tuple-element.48), channel_id=1, source_target_pairs={{0,1},{1,0},{2,3},{3,2},{4,5},{5,4},{6,7},{7,6},{8,9},{9,8},{10,11... | collective-permute-start | bytes 786440 | tf_op jit(solution)/shard_map/ppermute | solution.py:492
  51.1 1.4 %collective-permute-start.12 = (bf16[16,512]{1,0:T(8,128)(2,1)S(1)}, bf16[16,512]{1,0:T(8,128)(2,1)S(1)}, u32[]{:S(2)}, u32[]{:S(2)}) collective-permute-start(bf16[16,512]{1,0:T(8,128)(2,1)S(1)} %rim.1.rim_ref), channel_id=1, source_target_pairs={{0,1},{1,0},{2,3},{3,2},{4,5},{5,4},{6,7},{7,6},{8,9},{9,8},{10,11... | collective-permute-start | bytes 49160 | tf_op jit(solution)/shard_map/ppermute | solution.py:492
  (4 other events, 7.9 us)

commit v8 on v7

--- a/solution.py
+++ b/solution.py
@@ -24,6 +24,12 @@
 def weight(microseconds):
     return pl.CostEstimate(
         flops=int(microseconds * 1.15e9), bytes_accessed=0, transcendentals=0
+    )
+
+
+def traffic(microseconds):
+    return pl.CostEstimate(
+        flops=0, bytes_accessed=int(microseconds * 3.69e6), transcendentals=0
     )
 
 
@@ -46,24 +52,10 @@
 
 
 def qkv_kernel(
-    meta, own_hbm, other_hbm, gain_ref, w_hbm, _, keep_ref, query_ref, send_ref, pass_ref,
-    own_ref, other_ref, w_ref, sems,
+    meta, own_ref, other_ref, gain_ref, w_ref, _, keep_ref, query_ref, send_ref, pass_ref
 ):
     h = meta[0]
     first = meta[1] == 0
-    order = (1, 2, 0)
-    frames_in = [
-        pltpu.make_async_copy(own_hbm, own_ref, sems.at[0]),
-        pltpu.make_async_copy(other_hbm, other_ref, sems.at[1]),
-    ]
-    weights_in = [
-        pltpu.make_async_copy(w_hbm.at[part], w_ref.at[part], sems.at[2 + slot])
-        for slot, part in enumerate(order)
-    ]
-    for copy in frames_in + weights_in:
-        copy.start()
-    for copy in frames_in:
-        copy.wait()
     rows = own_ref.shape[0]
     tile = 256
     for at in range(0, rows, tile):
@@ -72,9 +64,7 @@
             own_ref[here, :].astype(F32), other_ref[here, :].astype(F32),
             gain_ref[h], gain_ref[1 - h],
         )
-        for slot, part in enumerate(order):
-            if at == 0:
-                weights_in[slot].wait()
+        for slot, part in enumerate((1, 2, 0)):
             value = (dot(n_own, w_ref[part, h]) + dot(n_other, w_ref[part, 1 - h])).astype(BF16)
             sub = value.shape[1] // 2
             cols = slice(slot * sub, slot * sub + sub)
@@ -92,10 +82,10 @@
     rows, half = frames.shape
     width = qkv.shape[2]
     vmem = pl.BlockSpec(memory_space=pltpu.VMEM)
-    hbm = pl.BlockSpec(memory_space=pltpu.HBM)
     return pl.pallas_call(
         qkv_kernel,
-        in_specs=[pl.BlockSpec(memory_space=pltpu.SMEM), hbm, hbm, vmem, hbm]
+        in_specs=[pl.BlockSpec(memory_space=pltpu.SMEM)]
+        + [vmem] * 4
         + [pl.BlockSpec(memory_space=pl.ANY)],
         out_specs=[vmem] * 4,
         out_shape=[
@@ -103,12 +93,6 @@
             jax.ShapeDtypeStruct((rows, width // 2), BF16),
             jax.ShapeDtypeStruct((rows, 3 * width // 2), BF16),
             jax.ShapeDtypeStruct((rows, width), BF16),
-        ],
-        scratch_shapes=[
-            pltpu.VMEM((rows, half), BF16),
-            pltpu.VMEM((rows, half), BF16),
-            pltpu.VMEM((3, 2, half, width), BF16),
-            pltpu.SemaphoreType.DMA((5,)),
         ],
         compiler_params=pltpu.CompilerParams(vmem_limit_bytes=VMEM_LIMIT),
         name="project",
@@ -219,7 +203,7 @@
         out_specs=vmem,
         out_shape=jax.ShapeDtypeStruct((rows, width), BF16),
         compiler_params=pltpu.CompilerParams(vmem_limit_bytes=VMEM_LIMIT),
-        cost_estimate=weight(3),
+        cost_estimate=traffic(3),
         name="attend",
     )(a_high, query, center, side_a, side_b, runs)
 
@@ -314,7 +298,7 @@
             jax.ShapeDtypeStruct((rows - EDGE, half), BF16),
         ],
         compiler_params=pltpu.CompilerParams(vmem_limit_bytes=VMEM_LIMIT),
-        cost_estimate=weight(3),
+        cost_estimate=traffic(3),
         name="gated",
     )(meta, *contexts, x_own, x_other, out_own, out_other,
       gain.reshape(2, 1, half), in_own, in_other, runs)

time: 54.5 us -> 51.4 us (0.943)
  blocking collectives: 0 us -> 15.3 us
  starting transfers between devices: 20.5 us -> 10.8 us
  waiting for transfers between devices: 7.57 us -> 1.03 us
  Pallas kernels: 23 us -> 18.8 us
  local copies, waits for them, and re-layouts: 2.77 us -> 4.04 us
  other arithmetic: 0.21 us -> 0.82 us
    all_to_all x0 -> x1, blocking collectives: none -> 15.3 us  [local(): lax.all_to_all(jnp.broadcast_to(counts[None, :], (blocks, counts.shape[0]...]
    all_to_all x1 -> x0, starting transfers between devices: 8.64 us -> none  [local(): lax.all_to_all(jnp.broadcast_to(counts[None, :], (blocks, counts.shape[0]...]
    all_to_all x1 -> x0, waiting for transfers between devices: 6.45 us -> none  [local(): lax.all_to_all(jnp.broadcast_to(counts[None, :], (blocks, counts.shape[0]...]
    pallas_call x1, Pallas kernels: 4.67 us -> 1.94 us  [project(): pl.pallas_call(qkv_kernel, in_specs=[pl.BlockSpec(memory_space=pltpu.SMEM...]
    unnamed x25 -> x31, local copies, waits for them, and re-layouts: 2.16 us -> 4.03 us
    pallas_call x2, Pallas kernels: 7.7 us -> 6.27 us  [attend(): pl.pallas_call(attend_kernel, in_specs=[pl.BlockSpec(memory_space=pltpu.S...]
    ppermute x2, starting transfers between devices: 2.67 us -> 1.96 us  [shift(): return lax.ppermute(value, 'tm', [p for p in pairs if 0 <= p[1] < blocks])]
    concatenate x1, other arithmetic: 0.01 us -> 0.62 us  [local(): taps = jnp.concatenate([depthwise, mid_gain[None, :]], axis=0)]
  transfers between devices with their start and end apart: 16 -> 15, of which waited for: 3 -> 2; matrix products, arithmetic and copies ran while one was open for 4% -> 5% of each run, Pallas kernels for 31% -> 30%
where the time goes in v8:
time: 51.4 us; the launch traced here: 51.1 us
  Pallas kernels  18.8 us (37%)
  blocking collectives  15.3 us (30%)
  starting transfers between devices  10.8 us (21%)
  local copies, waits for them, and re-layouts  4.04 us (8%)
  waiting for transfers between devices  1.03 us (2%)
  other arithmetic  0.82 us (2%)
    all_to_all x1, blocking collectives, local(): lax.all_to_all(jnp.broadcast_to(counts[None, :], (blocks, counts.shape[0]...  15.3 us
    pallas_call x2, Pallas kernels, attend(): pl.pallas_call(attend_kernel, in_specs=[pl.BlockSpec(memory_space=pltpu.S...  6.27 us
    ppermute x2, starting transfers between devices, exchange(): return lax.ppermute(value, 'tm', [(i, i ^ 1) for i in range(blocks)])  4.4 us
    unnamed x31, local copies, waits for them, and re-layouts  4.03 us
    ppermute x10, starting transfers between devices, swap(): return lax.ppermute(value, 'head', [(0, 1), (1, 0)])  3.81 us
    pallas_call x1, Pallas kernels, convolve(): pl.pallas_call(conv_kernel, in_specs=[pl.BlockSpec(memory_space=pltpu.SME...  3.24 us
    pallas_call x1, Pallas kernels, gated(): pl.pallas_call(gate_kernel, in_specs=[pl.BlockSpec(memory_space=pltpu.SME...  3.1 us
    pallas_call x2, Pallas kernels, finish(): pl.pallas_call(finish_own_kernel if done is None else finish_kernel, in_s...  2.59 us
  transfers between devices with their start and end apart: 15, of which 2 were waited for; matrix products, arithmetic and copies ran while one was open for 5% of the time, Pallas kernels for 30%

profile of v8, /device:TPU:0, one launch (start us, length us, event | category | flops | bytes accessed | tf_op | source)
XLA Modules:
  0.0 51.1 jit_solution(6716728393262064168)
XLA Ops:
  0.0 0.5 %collective-permute-start = (bf16[512,512]{1,0:T(8,128)(2,1)}, bf16[512,512]{1,0:T(8,128)(2,1)S(1)}, u32[]{:S(2)}, u32[]{:S(2)}) collective-permute-start(bf16[512,512]{1,0:T(8,128)(2,1)} %x_own.1), channel_id=1, source_target_pairs={{0,1},{1,0},{2,3},{3,2},{4,5},{5,4},{6,7},{7,6},{8,9},{9,8},{10,11... | collective-permute-start | bytes 1572872 | tf_op jit(solution)/shard_map/ppermute | solution.py:476
  0.5 1.5 %copy.16 = bf16[1024,2,256]{2,0,1:T(8,128)(2,1)S(1)} copy(bf16[1024,2,256]{2,1,0:T(2,128)(2,1)} %param.18) | data formatting | bytes 2097152 | tf_op args[7]
  2.1 0.6 %pad_maximum_fusion.taps_own = f32[32,256]{1,0:T(8,128)} fusion(f32[1,256]{1,0:T(1,128)S(1)} %bitcast.24, f32[31,256]{1,0:T(8,128)S(1)} %copy-done.12), kind=kLoop, calls=%fused_computation.1 | loop fusion | flops 8192 | bytes 65536 | tf_op jit(solution)/shard_map/concatenate | solution.py:508
  2.8 1.9 %project.1 = (bf16[512,256]{1,0:T(8,128)(2,1)S(1)}, bf16[512,128]{1,0:T(8,128)(2,1)S(1)}, bf16[512,384]{1,0:T(8,128)(2,1)S(1)}, bf16[512,256]{1,0:T(8,128)(2,1)S(1)}) custom-call(s32[4]{0:T(128)S(1)} %pad_add_fusion.meta, bf16[512,512]{1,0:T(8,128)(2,1)S(1)} %copy-done, bf16[512,512]{1,0:T(8,128)(2,1)S(1)} %collective-permute-done.other_ref.x_other, ...), custom_call_target="tpu_custom_call" | custom-call | tf_op jit(solution)/shard_map/project/pallas_call | solution.py:85
  4.8 0.6 %copy-done.5 = bf16[512,128]{1,0:T(8,128)(2,1)} copy-done((bf16[512,128]{1,0:T(8,128)(2,1)}, bf16[512,128]{1,0:T(8,128)(2,1)S(1)}, u32[]{:S(2)}) %copy-start.5) | copy-done | bytes 131096
  5.5 2.9 %collective-permute-start.1 = (bf16[512,384]{1,0:T(8,128)(2,1)S(1)}, bf16[512,384]{1,0:T(8,128)(2,1)S(1)}, u32[]{:S(2)}, u32[]{:S(2)}) collective-permute-start(bf16[512,384]{1,0:T(8,128)(2,1)S(1)} %get-tuple-element.31), channel_id=1, source_target_pairs={{0,2},{2,0},{4,6},{6,4},{8,10},{10,8},{12,14},{14,12},{1,3},{3,1},... | collective-permute-start | bytes 1179656 | tf_op jit(solution)/shard_map/ppermute | solution.py:483
  8.4 1.3 %collective-permute-start.2 = (bf16[512,256]{1,0:T(8,128)(2,1)S(1)}, bf16[512,256]{1,0:T(8,128)(2,1)S(1)}, u32[]{:S(2)}, u32[]{:S(2)}) collective-permute-start(bf16[512,256]{1,0:T(8,128)(2,1)S(1)} %get-tuple-element.30.center.side_a), channel_id=1, source_target_pairs={{2,6},{4,0},{6,10},{8,4},{10,14},{12,8},{3,7},{5,1},{7,11},{9,5},{... | collective-permute-start | bytes 786440 | tf_op jit(solution)/shard_map/ppermute | solution.py:480
  9.7 0.7 %collective-permute-start.3 = (bf16[512,256]{1,0:T(8,128)(2,1)S(1)}, bf16[512,256]{1,0:T(8,128)(2,1)S(1)}, u32[]{:S(2)}, u32[]{:S(2)}) collective-permute-start(bf16[512,256]{1,0:T(8,128)(2,1)S(1)} %get-tuple-element.32), channel_id=1, source_target_pairs={{2,4},{4,2},{6,8},{8,6},{10,12},{12,10},{3,5},{5,3},{7,9},{9,7},{1... | collective-permute-start | bytes 786440 | tf_op jit(solution)/shard_map/ppermute | solution.py:480
  10.6 15.3 %all_to_all.8 = s32[8,1,16]{2,1,0:T(1,128)S(1)} all-to-all(s32[8,1,16]{2,1,0:T(1,128)S(1)} %broadcast_in_dim.5), channel_id=1, replica_groups=mesh['grp'=2,'tm'=8,'head'=2] {'tm'}, dimensions={0} | all-to-all | bytes 1024 | tf_op jit(solution)/shard_map/all_to_all | solution.py:505
  25.9 0.8 %bounds.1 = (s32[512,128]{1,0:T(8,128)S(1)}, s32[512,128]{1,0:T(8,128)S(1)}) custom-call(s32[4]{0:T(128)S(1)} %pad_add_fusion.meta, s32[8,16]{1,0:T(8,128)S(1)} %bitcast.20, s32[1,16]{1,0:T(1,128)S(1)} %bitcast.23), custom_call_target="tpu_custom_call" | custom-call | tf_op jit(solution)/shard_map/bounds/pallas_call | solution.py:128
  26.8 3.4 %attend.3 = bf16[512,128]{1,0:T(8,128)(2,1)} custom-call(s32[1]{0:T(128)} %bitcast.1.a_high, bf16[512,384]{1,0:T(8,128)(2,1)S(1)} %collective-permute-done.1.side_a.query.center, bf16[512,384]{1,0:T(8,128)(2,1)S(1)} %collective-permute-done.1.side_a.query.center, bf16[512,256]{1,0:T(8,128)(2,1)S(1)} %get-tuple-element.30.center.side_a, ...), custom_call_target="tpu_custom_call" | custom-call | bytes 11070000 | tf_op jit(solution)/shard_map/attend/pallas_call | solution.py:200
  30.2 1.5 %collective-permute-start.4 = (bf16[512,128]{1,0:T(8,128)(2,1)}, bf16[512,128]{1,0:T(8,128)(2,1)}, u32[]{:S(2)}, u32[]{:S(2)}) collective-permute-start(bf16[512,128]{1,0:T(8,128)(2,1)} %attend.3), channel_id=1, source_target_pairs={{0,2},{2,0},{4,6},{6,4},{8,10},{10,8},{12,14},{14,12},{1,3},{3,1},... | collective-permute-start | bytes 393224 | tf_op jit(solution)/shard_map/ppermute | solution.py:483
  31.7 0.9 %copy-done.4 = bf16[512,256]{1,0:T(8,128)(2,1)S(1)} copy-done((bf16[512,256]{1,0:T(8,128)(2,1)S(1)}, bf16[512,256]{1,0:T(8,128)(2,1)}, u32[]{:S(2)}) %copy-start.4) | copy-done | bytes 262168
  32.6 0.9 %copy-done.6 = bf16[512,128]{1,0:T(8,128)(2,1)S(1)} copy-done((bf16[512,128]{1,0:T(8,128)(2,1)S(1)}, bf16[512,128]{1,0:T(8,128)(2,1)}, u32[]{:S(2)}) %copy-start.6) | copy-done | bytes 131096
  33.5 2.9 %attend.2.mine_own = bf16[512,128]{1,0:T(8,128)(2,1)S(1)} custom-call(s32[1]{0:T(128)} %bitcast.4.a_high, bf16[512,128]{1,0:T(8,128)(2,1)S(1)} %copy-done.6, bf16[512,256]{1,0:T(8,128)(2,1)S(1)} %get-tuple-element.30.center.side_a, bf16[512,384]{1,0:T(8,128)(2,1)S(1)} %collective-permute-done.1.side_a.query.center, bf16[512,256]{1,0:T(8,128)(2,1)S(1)} %copy-done.4, ...), custom_call_target="tpu_custom_call" | custom-call | bytes 11070000 | tf_op jit(solution)/shard_map/attend/pallas_call | solution.py:200
  36.5 0.5 collective-permute-start.6
  37.1 0.7 %collective-permute-done.5.mine_other = bf16[512,128]{1,0:T(8,128)(2,1)S(1)} collective-permute-done((bf16[512,128]{1,0:T(8,128)(2,1)S(1)}, bf16[512,128]{1,0:T(8,128)(2,1)S(1)}, u32[]{:S(2)}, u32[]{:S(2)}) %collective-permute-start.5) | collective-permute-done | bytes 131104 | tf_op jit(solution)/shard_map/ppermute | solution.py:476
  38.3 3.1 %gated.1 = (bf16[272,512]{1,0:T(8,128)(2,1)S(1)}, bf16[64,512]{1,0:T(8,128)(2,1)S(1)}, bf16[256,512]{1,0:T(8,128)(2,1)S(1)}, bf16[256,512]{1,0:T(8,128)(2,1)S(1)}) custom-call(s32[4]{0:T(128)S(1)} %pad_add_fusion.meta, bf16[512,128]{1,0:T(8,128)(2,1)S(1)} %attend.2.mine_own, bf16[512,128]{1,0:T(8,128)(2,1)} %collective-permute-done.4.pair_own, ...), custom_call_target="tpu_custom_call" | custom-call | bytes 11070000 | tf_op jit(solution)/shard_map/gated/pallas_call | solution.py:290
  41.4 0.7 %collective-permute-start.11 = (bf16[64,512]{1,0:T(8,128)(2,1)S(1)}, bf16[64,512]{1,0:T(8,128)(2,1)S(1)}, u32[]{:S(2)}, u32[]{:S(2)}) collective-permute-start(bf16[64,512]{1,0:T(8,128)(2,1)S(1)} %get-tuple-element.47), channel_id=1, source_target_pairs={{2,1},{4,3},{6,5},{8,7},{10,9},{12,11},{14,13},{1,2},{3,4},{5,6},{... | collective-permute-start | bytes 196616 | tf_op jit(solution)/shard_map/ppermute | solution.py:531
  42.1 3.2 %convolve.1.act_ref = bf16[256,512]{1,0:T(8,128)(2,1)S(1)} custom-call(s32[4]{0:T(128)S(1)} %pad_add_fusion.meta, bf16[272,512]{1,0:T(8,128)(2,1)S(1)} %get-tuple-element.45.glu_ref, s32[512,128]{1,0:T(8,128)S(1)} %get-tuple-element.40.run_ref, f32[32,256]{1,0:T(8,128)S(1)} %copy-done.7, f32[32,256]{1,0:T(8,128)S(1)} %collective-permute-done.9.taps_other), custom_call_target="tpu_custom_call" | custom-call | flops 3449999872 | tf_op jit(solution)/shard_map/convolve/pallas_call | solution.py:363
  45.3 1.8 %collective-permute-start.10 = (bf16[256,512]{1,0:T(8,128)(2,1)S(1)}, bf16[256,512]{1,0:T(8,128)(2,1)S(1)}, u32[]{:S(2)}, u32[]{:S(2)}) collective-permute-start(bf16[256,512]{1,0:T(8,128)(2,1)S(1)} %convolve.1.act_ref), channel_id=1, source_target_pairs={{0,1},{1,0},{2,3},{3,2},{4,5},{5,4},{6,7},{7,6},{8,9},{9,8},{10,11... | collective-permute-start | bytes 786440 | tf_op jit(solution)/shard_map/ppermute | solution.py:476
  47.2 0.8 %rim.1.rim_ref = bf16[16,512]{1,0:T(8,128)(2,1)S(1)} custom-call(s32[4]{0:T(128)S(1)} %pad_add_fusion.meta, bf16[272,512]{1,0:T(8,128)(2,1)S(1)} %get-tuple-element.45.glu_ref, bf16[64,512]{1,0:T(8,128)(2,1)S(1)} %collective-permute-done.11.edge_ref, s32[512,128]{1,0:T(8,128)S(1)} %get-tuple-element.40.run_ref, f32[32,256]{1,0:T(8,128)S(1)} %copy-done.7, ...), custom_call_target="tpu_custom_call" | custom-call | flops 1150000000 | tf_op jit(solution)/shard_map/rim/pallas_call | solution.py:399
  48.5 0.9 %finish_own.1.done_ref = bf16[256,512]{1,0:T(8,128)(2,1)S(1)} custom-call(s32[4]{0:T(128)S(1)} %pad_add_fusion.meta, bf16[256,512]{1,0:T(8,128)(2,1)S(1)} %convolve.1.act_ref, bf16[16,512]{1,0:T(8,128)(2,1)S(1)} %rim.1.rim_ref, bf16[256,512]{1,0:T(8,128)(2,1)S(1)} %get-tuple-element.50.mid_ref, bf16[256,1024]{1,0:T(8,128)(2,1)S(1)} %copy-done.11, ...), custom_call_target="tpu_custom_call" | custom-call | flops 1380000000 | tf_op jit(solution)/shard_map/finish_own/pallas_call | solution.py:447
  49.4 1.7 %finish.1 = bf16[512,512]{1,0:T(8,128)(2,1)} custom-call(s32[4]{0:T(128)S(1)} %pad_add_fusion.meta, bf16[256,512]{1,0:T(8,128)(2,1)S(1)} %collective-permute-done.10.act_ref, bf16[16,512]{1,0:T(8,128)(2,1)S(1)} %collective-permute-done.12.rim_ref, bf16[256,512]{1,0:T(8,128)(2,1)S(1)} %collective-permute-done.13.mid_ref, bf16[256,1024]{1,0:T(8,128)(2,1)S(1)} %copy-done.11, ...), custom_call_target="tpu_custom_call" | custom-call | flops 1380000000 | tf_op jit(solution)/shard_map/finish/pallas_call | solution.py:447
  (51 shorter events, 1.6 us)
Async XLA Ops:
  0.0 2.7 %copy-start = (bf16[512,512]{1,0:T(8,128)(2,1)S(1)}, bf16[512,512]{1,0:T(8,128)(2,1)}, u32[]{:S(2)}) copy-start(bf16[512,512]{1,0:T(8,128)(2,1)} %x_own.1) | copy-start | bytes 1572868
  0.0 2.7 %copy-start.8 = (f32[1024]{0:T(1024)S(1)}, f32[1024]{0:T(1024)}, u32[]{:S(2)}) copy-start(f32[1024]{0:T(1024)} %param.14) | copy-start | bytes 12292
  0.0 2.7 %collective-permute-start = (bf16[512,512]{1,0:T(8,128)(2,1)}, bf16[512,512]{1,0:T(8,128)(2,1)S(1)}, u32[]{:S(2)}, u32[]{:S(2)}) collective-permute-start(bf16[512,512]{1,0:T(8,128)(2,1)} %x_own.1), channel_id=1, source_target_pairs={{0,1},{1,0},{2,3},{3,2},{4,5},{5,4},{6,7},{7,6},{8,9},{9,8},{10,11... | collective-permute-start | bytes 1572872 | tf_op jit(solution)/shard_map/ppermute | solution.py:476
  0.5 2.2 %copy-start.1 = (bf16[1024,3,256]{2,0,1:T(8,128)(2,1)S(1)}, bf16[1024,3,256]{2,0,1:T(8,128)(2,1)}, u32[]{:S(2)}) copy-start(bf16[1024,3,256]{2,0,1:T(8,128)(2,1)} %param.15) | copy-start | bytes 4718596
  2.8 7.6 %copy-start.2 = (bf16[256,1024]{1,0:T(8,128)(2,1)S(1)}, bf16[256,1024]{1,0:T(8,128)(2,1)}, u32[]{:S(2)}) copy-start(bf16[256,1024]{1,0:T(8,128)(2,1)} %out_own) | copy-start | bytes 1572868
  2.8 7.7 %copy-start.13 = (s32[512]{0:T(512)S(1)}, s32[512]{0:T(512)}, u32[]{:S(2)}) copy-start(s32[512]{0:T(512)} %param.12) | copy-start | bytes 6148
  2.8 23.1 %copy-start.10 = (s32[16]{0:T(128)S(1)}, s32[16]{0:T(128)}, u32[]{:S(2)}) copy-start(s32[16]{0:T(128)} %param.13) | copy-start | bytes 196
  5.4 32.9 %collective-permute-start.8 = (bf16[2,1024,256]{2,1,0:T(8,128)(2,1)S(1)}, bf16[2,1024,256]{2,1,0:T(8,128)(2,1)}, u32[]{:S(2)}, u32[]{:S(2)}) collective-permute-start(bf16[2,1024,256]{2,1,0:T(8,128)(2,1)S(1)} %bitcast.17), channel_id=1, source_target_pairs={{0,1},{1,0},{2,3},{3,2},{4,5},{5,4},{6,7},{7,6},{8,9},{9,8},{10,11... | collective-permute-start | bytes 3145736 | tf_op jit(solution)/shard_map/ppermute | solution.py:476
  5.5 21.4 %collective-permute-start.1 = (bf16[512,384]{1,0:T(8,128)(2,1)S(1)}, bf16[512,384]{1,0:T(8,128)(2,1)S(1)}, u32[]{:S(2)}, u32[]{:S(2)}) collective-permute-start(bf16[512,384]{1,0:T(8,128)(2,1)S(1)} %get-tuple-element.31), channel_id=1, source_target_pairs={{0,2},{2,0},{4,6},{6,4},{8,10},{10,8},{12,14},{14,12},{1,3},{3,1},... | collective-permute-start | bytes 1179656 | tf_op jit(solution)/shard_map/ppermute | solution.py:483
  8.4 18.4 %collective-permute-start.2 = (bf16[512,256]{1,0:T(8,128)(2,1)S(1)}, bf16[512,256]{1,0:T(8,128)(2,1)S(1)}, u32[]{:S(2)}, u32[]{:S(2)}) collective-permute-start(bf16[512,256]{1,0:T(8,128)(2,1)S(1)} %get-tuple-element.30.center.side_a), channel_id=1, source_target_pairs={{2,6},{4,0},{6,10},{8,4},{10,14},{12,8},{3,7},{5,1},{7,11},{9,5},{... | collective-permute-start | bytes 786440 | tf_op jit(solution)/shard_map/ppermute | solution.py:480
  9.7 17.1 %collective-permute-start.3 = (bf16[512,256]{1,0:T(8,128)(2,1)S(1)}, bf16[512,256]{1,0:T(8,128)(2,1)S(1)}, u32[]{:S(2)}, u32[]{:S(2)}) collective-permute-start(bf16[512,256]{1,0:T(8,128)(2,1)S(1)} %get-tuple-element.32), channel_id=1, source_target_pairs={{2,4},{4,2},{6,8},{8,6},{10,12},{12,10},{3,5},{5,3},{7,9},{9,7},{1... | collective-permute-start | bytes 786440 | tf_op jit(solution)/shard_map/ppermute | solution.py:480
  10.4 27.6 %collective-permute-start.7 = (bf16[256,1024]{1,0:T(8,128)(2,1)S(1)}, bf16[256,1024]{1,0:T(8,128)(2,1)}, u32[]{:S(2)}, u32[]{:S(2)}) collective-permute-start(bf16[256,1024]{1,0:T(8,128)(2,1)S(1)} %copy-done.2), channel_id=1, source_target_pairs={{0,1},{1,0},{2,3},{3,2},{4,5},{5,4},{6,7},{7,6},{8,9},{9,8},{10,11... | collective-permute-start | bytes 1572872 | tf_op jit(solution)/shard_map/ppermute | solution.py:476
  26.8 3.4 %copy-start.3 = (bf16[512,256]{1,0:T(8,128)(2,1)}, bf16[512,256]{1,0:T(8,128)(2,1)S(1)}, u32[]{:S(2)}) copy-start(bf16[512,256]{1,0:T(8,128)(2,1)S(1)} %collective-permute-done.3.side_b) | copy-start | bytes 786436
  26.8 11.4 %copy-start.9 = (f32[1024]{0:T(1024)S(1)}, f32[1024]{0:T(1024)}, u32[]{:S(2)}) copy-start(f32[1024]{0:T(1024)} %param.17) | copy-start | bytes 12292
  30.2 6.3 %collective-permute-start.4 = (bf16[512,128]{1,0:T(8,128)(2,1)}, bf16[512,128]{1,0:T(8,128)(2,1)}, u32[]{:S(2)}, u32[]{:S(2)}) collective-permute-start(bf16[512,128]{1,0:T(8,128)(2,1)} %attend.3), channel_id=1, source_target_pairs={{0,2},{2,0},{4,6},{6,4},{8,10},{10,8},{12,14},{14,12},{1,3},{3,1},... | collective-permute-start | bytes 393224 | tf_op jit(solution)/shard_map/ppermute | solution.py:483
  36.4 1.4 %collective-permute-start.5 = (bf16[512,128]{1,0:T(8,128)(2,1)S(1)}, bf16[512,128]{1,0:T(8,128)(2,1)S(1)}, u32[]{:S(2)}, u32[]{:S(2)}) collective-permute-start(bf16[512,128]{1,0:T(8,128)(2,1)S(1)} %attend.2.mine_own), channel_id=1, source_target_pairs={{0,1},{1,0},{2,3},{3,2},{4,5},{5,4},{6,7},{7,6},{8,9},{9,8},{10,11... | collective-permute-start | bytes 393224 | tf_op jit(solution)/shard_map/ppermute | solution.py:476
  36.5 1.7 %collective-permute-start.6 = (bf16[512,128]{1,0:T(8,128)(2,1)}, bf16[512,128]{1,0:T(8,128)(2,1)S(1)}, u32[]{:S(2)}, u32[]{:S(2)}) collective-permute-start(bf16[512,128]{1,0:T(8,128)(2,1)} %collective-permute-done.4.pair_own), channel_id=1, source_target_pairs={{0,1},{1,0},{2,3},{3,2},{4,5},{5,4},{6,7},{7,6},{8,9},{9,8},{10,11... | collective-permute-start | bytes 393224 | tf_op jit(solution)/shard_map/ppermute | solution.py:476
  37.0 11.5 %collective-permute-start.14 = (bf16[256,1024]{1,0:T(8,128)(2,1)}, bf16[256,1024]{1,0:T(8,128)(2,1)S(1)}, u32[]{:S(2)}, u32[]{:S(2)}) collective-permute-start(bf16[256,1024]{1,0:T(8,128)(2,1)} %w_own.1), channel_id=1, source_target_pairs={{0,1},{1,0},{2,3},{3,2},{4,5},{5,4},{6,7},{7,6},{8,9},{9,8},{10,11... | collective-permute-start | bytes 1572872 | tf_op jit(solution)/shard_map/ppermute | solution.py:476
  37.8 4.2 %collective-permute-start.9 = (f32[32,256]{1,0:T(8,128)}, f32[32,256]{1,0:T(8,128)S(1)}, u32[]{:S(2)}, u32[]{:S(2)}) collective-permute-start(f32[32,256]{1,0:T(8,128)} %pad_maximum_fusion.taps_own), channel_id=1, source_target_pairs={{0,1},{1,0},{2,3},{3,2},{4,5},{5,4},{6,7},{7,6},{8,9},{9,8},{10,11... | collective-permute-start | bytes 98312 | tf_op jit(solution)/shard_map/ppermute | solution.py:476
  38.3 3.8 %copy-start.7 = (f32[32,256]{1,0:T(8,128)S(1)}, f32[32,256]{1,0:T(8,128)}, u32[]{:S(2)}) copy-start(f32[32,256]{1,0:T(8,128)} %pad_maximum_fusion.taps_own) | copy-start | bytes 98308
  41.4 5.8 %collective-permute-start.11 = (bf16[64,512]{1,0:T(8,128)(2,1)S(1)}, bf16[64,512]{1,0:T(8,128)(2,1)S(1)}, u32[]{:S(2)}, u32[]{:S(2)}) collective-permute-start(bf16[64,512]{1,0:T(8,128)(2,1)S(1)} %get-tuple-element.47), channel_id=1, source_target_pairs={{2,1},{4,3},{6,5},{8,7},{10,9},{12,11},{14,13},{1,2},{3,4},{5,6},{... | collective-permute-start | bytes 196616 | tf_op jit(solution)/shard_map/ppermute | solution.py:531
  45.3 4.1 %collective-permute-start.10 = (bf16[256,512]{1,0:T(8,128)(2,1)S(1)}, bf16[256,512]{1,0:T(8,128)(2,1)S(1)}, u32[]{:S(2)}, u32[]{:S(2)}) collective-permute-start(bf16[256,512]{1,0:T(8,128)(2,1)S(1)} %convolve.1.act_ref), channel_id=1, source_target_pairs={{0,1},{1,0},{2,3},{3,2},{4,5},{5,4},{6,7},{7,6},{8,9},{9,8},{10,11... | collective-permute-start | bytes 786440 | tf_op jit(solution)/shard_map/ppermute | solution.py:476
  47.1 2.3 %collective-permute-start.13 = (bf16[256,512]{1,0:T(8,128)(2,1)S(1)}, bf16[256,512]{1,0:T(8,128)(2,1)S(1)}, u32[]{:S(2)}, u32[]{:S(2)}) collective-permute-start(bf16[256,512]{1,0:T(8,128)(2,1)S(1)} %get-tuple-element.48), channel_id=1, source_target_pairs={{0,1},{1,0},{2,3},{3,2},{4,5},{5,4},{6,7},{7,6},{8,9},{9,8},{10,11... | collective-permute-start | bytes 786440 | tf_op jit(solution)/shard_map/ppermute | solution.py:476
  48.0 1.4 %collective-permute-start.12 = (bf16[16,512]{1,0:T(8,128)(2,1)S(1)}, bf16[16,512]{1,0:T(8,128)(2,1)S(1)}, u32[]{:S(2)}, u32[]{:S(2)}) collective-permute-start(bf16[16,512]{1,0:T(8,128)(2,1)S(1)} %rim.1.rim_ref), channel_id=1, source_target_pairs={{0,1},{1,0},{2,3},{3,2},{4,5},{5,4},{6,7},{7,6},{8,9},{9,8},{10,11... | collective-permute-start | bytes 49160 | tf_op jit(solution)/shard_map/ppermute | solution.py:476
  (6 other events, 8.1 us)

commit v9 on v8

--- a/solution.py
+++ b/solution.py
@@ -100,7 +100,8 @@
       qkv.transpose(1, 0, 2).reshape(3, 2, half, width), early)
 
 
-def bounds_kernel(meta, counts, valid, own_ref, pair_ref):
+def bounds_kernel(meta, counts, valid, *refs):
+    own_ref, pair_ref = refs[-2:]
     utts = valid.shape[1]
     rows = own_ref.shape[0]
     square = (utts, utts)
@@ -123,19 +124,21 @@
         ref[...] = both.T.astype(jnp.int32)
 
 
-def bounds(meta, counts, valid, rows):
-    vmem = pl.BlockSpec(memory_space=pltpu.VMEM)
+def bounds(meta, counts, valid, rows, held):
+    vmem = pl.BlockSpec(memory_space=pltpu.VMEM)
+    anywhere = [pl.BlockSpec(memory_space=pl.ANY)] * len(held)
     return pl.pallas_call(
         bounds_kernel,
-        in_specs=[pl.BlockSpec(memory_space=pltpu.SMEM), vmem, vmem],
+        in_specs=[pl.BlockSpec(memory_space=pltpu.SMEM), vmem, vmem] + anywhere,
         out_specs=[vmem] * 2,
         out_shape=[jax.ShapeDtypeStruct((rows, 128), jnp.int32)] * 2,
         compiler_params=pltpu.CompilerParams(vmem_limit_bytes=VMEM_LIMIT),
         name="bounds",
-    )(meta, counts, valid.reshape(1, -1))
-
-
-def attend_kernel(a_high, query, center, side_a, side_b, run_ref, out_ref):
+    )(meta, counts, valid.reshape(1, -1), *held)
+
+
+def attend_kernel(a_high, query, center, side_a, side_b, run_ref, *refs):
+    out_ref = refs[-1]
     rows = center.shape[0]
     width = center.shape[1] // 2 if query.shape[1] < center.shape[1] else center.shape[1] // 3
     q_cols = slice(query.shape[1] - width, query.shape[1])
@@ -194,18 +197,19 @@
         run(side_a, side_b)
 
 
-def attend(a_high, query, center, side_a, side_b, runs):
+def attend(a_high, query, center, side_a, side_b, runs, held):
+    anywhere = [pl.BlockSpec(memory_space=pl.ANY)] * len(held)
     rows, width = side_b.shape[0], side_b.shape[1] // 2
     vmem = pl.BlockSpec(memory_space=pltpu.VMEM)
     return pl.pallas_call(
         attend_kernel,
-        in_specs=[pl.BlockSpec(memory_space=pltpu.SMEM)] + [vmem] * 5,
+        in_specs=[pl.BlockSpec(memory_space=pltpu.SMEM)] + [vmem] * 5 + anywhere,
         out_specs=vmem,
         out_shape=jax.ShapeDtypeStruct((rows, width), BF16),
         compiler_params=pltpu.CompilerParams(vmem_limit_bytes=VMEM_LIMIT),
         cost_estimate=traffic(3),
         name="attend",
-    )(a_high, query, center, side_a, side_b, runs)
+    )(a_high, query, center, side_a, side_b, runs, *held)
 
 
 def gate_kernel(
@@ -511,16 +515,19 @@
     )
     pointwise_other = swap(pointwise)
     out_other = swap(out_weight)
-    runs, pair_runs = bounds(meta, counts, utt_valid, rows)
+    runs, pair_runs = bounds(meta, counts, utt_valid, rows, (query,))
     taps, pointwise_out, runs = lax.optimization_barrier((taps, pointwise_out, runs))
     taps_other = swap(taps)
     pointwise_out_other = swap(pointwise_out)
     pair, far_pair, far_own, runs, pair_runs = lax.optimization_barrier(
         (pair, far_pair, far_own, runs, pair_runs)
     )
-    pair_context = attend(column.reshape(1), pair, pair, keep, far_pair, pair_runs)
+    weights = (pointwise_other, out_other)
+    pair_context = attend(
+        column.reshape(1), pair, pair, keep, far_pair, pair_runs, (query, far_own, *weights)
+    )
     pair_context = exchange(pair_context)
-    context = attend((1 - column).reshape(1), query, keep, pair, far_own, runs)
+    context = attend((1 - column).reshape(1), query, keep, pair, far_own, runs, weights)
     contexts = (context, pair_context, swap(context), swap(pair_context))
     glu, edge, mid_keep, mid_send = gated(
         meta, contexts, frames, other, out_weight, out_other, conv_gain,

time: 51.4 us -> 54.8 us (1.066)
  local copies, waits for them, and re-layouts: 4.04 us -> 6.78 us
  starting transfers between devices: 10.8 us -> 11.4 us
    unnamed x31 -> x47, local copies, waits for them, and re-layouts: 4.03 us -> 6.77 us
    ppermute x10, starting transfers between devices: 3.81 us -> 4.76 us  [swap(): return lax.ppermute(value, 'head', [(0, 1), (1, 0)])]
  transfers between devices with their start and end apart: 15 -> 15, of which waited for: 2 -> 2; matrix products, arithmetic and copies ran while one was open for 5% -> 4% of each run, Pallas kernels for 30% -> 21%
where the time goes in v9:
time: 54.8 us; the launch traced here: 54.5 us
  Pallas kernels  18.7 us (34%)
  blocking collectives  15.8 us (29%)
  starting transfers between devices  11.4 us (21%)
  local copies, waits for them, and re-layouts  6.78 us (12%)
  other arithmetic  0.82 us (1%)
  waiting for transfers between devices  0.75 us (1%)
    all_to_all x1, blocking collectives, local(): lax.all_to_all(jnp.broadcast_to(counts[None, :], (blocks, counts.shape[0]...  15.8 us
    unnamed x47, local copies, waits for them, and re-layouts  6.77 us
    pallas_call x2, Pallas kernels, attend(): pl.pallas_call(attend_kernel, in_specs=[pl.BlockSpec(memory_space=pltpu.S...  6.24 us
    ppermute x10, starting transfers between devices, swap(): return lax.ppermute(value, 'head', [(0, 1), (1, 0)])  4.76 us
    ppermute x2, starting transfers between devices, exchange(): return lax.ppermute(value, 'tm', [(i, i ^ 1) for i in range(blocks)])  4 us
    pallas_call x1, Pallas kernels, convolve(): pl.pallas_call(conv_kernel, in_specs=[pl.BlockSpec(memory_space=pltpu.SME...  3.59 us
    pallas_call x1, Pallas kernels, gated(): pl.pallas_call(gate_kernel, in_specs=[pl.BlockSpec(memory_space=pltpu.SME...  2.6 us
    pallas_call x2, Pallas kernels, finish(): pl.pallas_call(finish_own_kernel if done is None else finish_kernel, in_s...  2.59 us
  transfers between devices with their start and end apart: 15, of which 2 were waited for; matrix products, arithmetic and copies ran while one was open for 4% of the time, Pallas kernels for 21%

profile of v9, /device:TPU:0, one launch (start us, length us, event | category | flops | bytes accessed | tf_op | source)
XLA Modules:
  0.0 54.5 jit_solution(17461764687779813020)
XLA Ops:
  0.5 1.5 %copy.16 = bf16[1024,2,256]{2,0,1:T(8,128)(2,1)S(1)} copy(bf16[1024,2,256]{2,1,0:T(2,128)(2,1)} %param.18) | data formatting | bytes 2097152 | tf_op args[7]
  2.1 0.6 %pad_maximum_fusion.taps_own = f32[32,256]{1,0:T(8,128)} fusion(f32[1,256]{1,0:T(1,128)S(1)} %bitcast.24, f32[31,256]{1,0:T(8,128)S(1)} %copy-done.20), kind=kLoop, calls=%fused_computation.1 | loop fusion | flops 8192 | bytes 65536 | tf_op jit(solution)/shard_map/concatenate | solution.py:512
  2.8 2.0 %project.1 = (bf16[512,256]{1,0:T(8,128)(2,1)S(1)}, bf16[512,128]{1,0:T(8,128)(2,1)S(1)}, bf16[512,384]{1,0:T(8,128)(2,1)S(1)}, bf16[512,256]{1,0:T(8,128)(2,1)S(1)}) custom-call(s32[4]{0:T(128)S(1)} %pad_add_fusion.meta, bf16[512,512]{1,0:T(8,128)(2,1)S(1)} %copy-done, bf16[512,512]{1,0:T(8,128)(2,1)S(1)} %collective-permute-done.other_ref.x_other, ...), custom_call_target="tpu_custom_call" | custom-call | tf_op jit(solution)/shard_map/project/pallas_call | solution.py:85
  5.4 2.6 %collective-permute-start.1 = (bf16[512,384]{1,0:T(8,128)(2,1)S(1)}, bf16[512,384]{1,0:T(8,128)(2,1)S(1)}, u32[]{:S(2)}, u32[]{:S(2)}) collective-permute-start(bf16[512,384]{1,0:T(8,128)(2,1)S(1)} %get-tuple-element.31), channel_id=1, source_target_pairs={{0,2},{2,0},{4,6},{6,4},{8,10},{10,8},{12,14},{14,12},{1,3},{3,1},... | collective-permute-start | bytes 1179656 | tf_op jit(solution)/shard_map/ppermute | solution.py:487
  7.9 1.3 %collective-permute-start.2 = (bf16[512,256]{1,0:T(8,128)(2,1)S(1)}, bf16[512,256]{1,0:T(8,128)(2,1)S(1)}, u32[]{:S(2)}, u32[]{:S(2)}) collective-permute-start(bf16[512,256]{1,0:T(8,128)(2,1)S(1)} %get-tuple-element.30.center.side_a), channel_id=1, source_target_pairs={{2,6},{4,0},{6,10},{8,4},{10,14},{12,8},{3,7},{5,1},{7,11},{9,5},{... | collective-permute-start | bytes 786440 | tf_op jit(solution)/shard_map/ppermute | solution.py:484
  9.2 0.7 %collective-permute-start.3 = (bf16[512,256]{1,0:T(8,128)(2,1)S(1)}, bf16[512,256]{1,0:T(8,128)(2,1)S(1)}, u32[]{:S(2)}, u32[]{:S(2)}) collective-permute-start(bf16[512,256]{1,0:T(8,128)(2,1)S(1)} %get-tuple-element.32), channel_id=1, source_target_pairs={{2,4},{4,2},{6,8},{8,6},{10,12},{12,10},{3,5},{5,3},{7,9},{9,7},{1... | collective-permute-start | bytes 786440 | tf_op jit(solution)/shard_map/ppermute | solution.py:484
  10.0 15.8 %all_to_all.8 = s32[8,1,16]{2,1,0:T(1,128)S(1)} all-to-all(s32[8,1,16]{2,1,0:T(1,128)S(1)} %broadcast_in_dim.5), channel_id=1, replica_groups=mesh['grp'=2,'tm'=8,'head'=2] {'tm'}, dimensions={0} | all-to-all | bytes 1024 | tf_op jit(solution)/shard_map/all_to_all | solution.py:509
  25.9 0.8 %bounds.1 = (s32[512,128]{1,0:T(8,128)S(1)}, s32[512,128]{1,0:T(8,128)S(1)}) custom-call(s32[4]{0:T(128)S(1)} %pad_add_fusion.meta, s32[8,16]{1,0:T(8,128)S(1)} %bitcast.20, s32[1,16]{1,0:T(1,128)S(1)} %bitcast.23, bf16[512,128]{1,0:T(8,128)(2,1)S(1)} %get-tuple-element.28.refs_0_.query), custom_call_target="tpu_custom_call" | custom-call | tf_op jit(solution)/shard_map/bounds/pallas_call | solution.py:130
  26.7 0.7 %copy-done.6 = s32[512,128]{1,0:T(8,128)} copy-done((s32[512,128]{1,0:T(8,128)}, s32[512,128]{1,0:T(8,128)S(1)}, u32[]{:S(2)}) %copy-start.6) | copy-done | bytes 262168
  27.5 3.4 %attend.3 = bf16[512,128]{1,0:T(8,128)(2,1)} custom-call(s32[1]{0:T(128)} %bitcast.1.a_high, bf16[512,384]{1,0:T(8,128)(2,1)S(1)} %collective-permute-done.1.side_a.query.center, bf16[512,384]{1,0:T(8,128)(2,1)S(1)} %collective-permute-done.1.side_a.query.center, bf16[512,256]{1,0:T(8,128)(2,1)S(1)} %get-tuple-element.30.center.side_a, ...), custom_call_target="tpu_custom_call" | custom-call | bytes 11070000 | tf_op jit(solution)/shard_map/attend/pallas_call | solution.py:204
  30.9 0.7 %copy-done.9 = bf16[512,256]{1,0:T(8,128)(2,1)} copy-done((bf16[512,256]{1,0:T(8,128)(2,1)}, bf16[512,256]{1,0:T(8,128)(2,1)S(1)}, u32[]{:S(2)}) %copy-start.9) | copy-done | bytes 262168
  31.6 1.4 %collective-permute-start.6 = (bf16[512,128]{1,0:T(8,128)(2,1)}, bf16[512,128]{1,0:T(8,128)(2,1)}, u32[]{:S(2)}, u32[]{:S(2)}) collective-permute-start(bf16[512,128]{1,0:T(8,128)(2,1)} %attend.3), channel_id=1, source_target_pairs={{0,2},{2,0},{4,6},{6,4},{8,10},{10,8},{12,14},{14,12},{1,3},{3,1},... | collective-permute-start | bytes 393224 | tf_op jit(solution)/shard_map/ppermute | solution.py:487
  33.0 1.0 %copy-done.5 = bf16[512,128]{1,0:T(8,128)(2,1)S(1)} copy-done((bf16[512,128]{1,0:T(8,128)(2,1)S(1)}, bf16[512,128]{1,0:T(8,128)(2,1)}, u32[]{:S(2)}) %copy-start.5) | copy-done | bytes 131096
  34.0 0.9 %copy-done.7 = s32[512,128]{1,0:T(8,128)S(1)} copy-done((s32[512,128]{1,0:T(8,128)S(1)}, s32[512,128]{1,0:T(8,128)}, u32[]{:S(2)}) %copy-start.7) | copy-done | bytes 262168
  34.9 0.9 %copy-done.10 = bf16[512,256]{1,0:T(8,128)(2,1)S(1)} copy-done((bf16[512,256]{1,0:T(8,128)(2,1)S(1)}, bf16[512,256]{1,0:T(8,128)(2,1)}, u32[]{:S(2)}) %copy-start.10) | copy-done | bytes 262168
  35.9 0.9 %copy-done.12 = bf16[512,256]{1,0:T(8,128)(2,1)S(1)} copy-done((bf16[512,256]{1,0:T(8,128)(2,1)S(1)}, bf16[512,256]{1,0:T(8,128)(2,1)}, u32[]{:S(2)}) %copy-start.12) | copy-done | bytes 262168
  36.8 2.8 %attend.2.mine_own = bf16[512,128]{1,0:T(8,128)(2,1)S(1)} custom-call(s32[1]{0:T(128)} %bitcast.4.a_high, bf16[512,128]{1,0:T(8,128)(2,1)S(1)} %copy-done.5, bf16[512,256]{1,0:T(8,128)(2,1)S(1)} %copy-done.10, bf16[512,384]{1,0:T(8,128)(2,1)S(1)} %collective-permute-done.1.side_a.query.center, bf16[512,256]{1,0:T(8,128)(2,1)S(1)} %copy-done.12, ...), custom_call_target="tpu_custom_call" | custom-call | bytes 11070000 | tf_op jit(solution)/shard_map/attend/pallas_call | solution.py:204
  41.5 2.6 %gated.1 = (bf16[272,512]{1,0:T(8,128)(2,1)S(1)}, bf16[64,512]{1,0:T(8,128)(2,1)S(1)}, bf16[256,512]{1,0:T(8,128)(2,1)S(1)}, bf16[256,512]{1,0:T(8,128)(2,1)S(1)}) custom-call(s32[4]{0:T(128)S(1)} %pad_add_fusion.meta, bf16[512,128]{1,0:T(8,128)(2,1)S(1)} %attend.2.mine_own, bf16[512,128]{1,0:T(8,128)(2,1)} %collective-permute-done.6.pair_own, ...), custom_call_target="tpu_custom_call" | custom-call | bytes 11070000 | tf_op jit(solution)/shard_map/gated/pallas_call | solution.py:294
  44.1 0.7 %collective-permute-start.11 = (bf16[64,512]{1,0:T(8,128)(2,1)S(1)}, bf16[64,512]{1,0:T(8,128)(2,1)S(1)}, u32[]{:S(2)}, u32[]{:S(2)}) collective-permute-start(bf16[64,512]{1,0:T(8,128)(2,1)S(1)} %get-tuple-element.47), channel_id=1, source_target_pairs={{2,1},{4,3},{6,5},{8,7},{10,9},{12,11},{14,13},{1,2},{3,4},{5,6},{... | collective-permute-start | bytes 196616 | tf_op jit(solution)/shard_map/ppermute | solution.py:538
  44.8 3.6 %convolve.1.act_ref = bf16[256,512]{1,0:T(8,128)(2,1)S(1)} custom-call(s32[4]{0:T(128)S(1)} %pad_add_fusion.meta, bf16[272,512]{1,0:T(8,128)(2,1)S(1)} %get-tuple-element.45.glu_ref, s32[512,128]{1,0:T(8,128)S(1)} %copy-done.8, f32[32,256]{1,0:T(8,128)S(1)} %copy-done.15, f32[32,256]{1,0:T(8,128)S(1)} %collective-permute-done.9.taps_other), custom_call_target="tpu_custom_call" | custom-call | flops 3449999872 | tf_op jit(solution)/shard_map/convolve/pallas_call | solution.py:367
  48.4 2.0 %collective-permute-start.10 = (bf16[256,512]{1,0:T(8,128)(2,1)S(1)}, bf16[256,512]{1,0:T(8,128)(2,1)S(1)}, u32[]{:S(2)}, u32[]{:S(2)}) collective-permute-start(bf16[256,512]{1,0:T(8,128)(2,1)S(1)} %convolve.1.act_ref), channel_id=1, source_target_pairs={{0,1},{1,0},{2,3},{3,2},{4,5},{5,4},{6,7},{7,6},{8,9},{9,8},{10,11... | collective-permute-start | bytes 786440 | tf_op jit(solution)/shard_map/ppermute | solution.py:480
  50.5 0.9 %rim.1.rim_ref = bf16[16,512]{1,0:T(8,128)(2,1)S(1)} custom-call(s32[4]{0:T(128)S(1)} %pad_add_fusion.meta, bf16[272,512]{1,0:T(8,128)(2,1)S(1)} %get-tuple-element.45.glu_ref, bf16[64,512]{1,0:T(8,128)(2,1)S(1)} %collective-permute-done.11.edge_ref, s32[512,128]{1,0:T(8,128)S(1)} %copy-done.8, f32[32,256]{1,0:T(8,128)S(1)} %copy-done.15, ...), custom_call_target="tpu_custom_call" | custom-call | flops 1150000000 | tf_op jit(solution)/shard_map/rim/pallas_call | solution.py:403
  51.9 0.9 %finish_own.1.done_ref = bf16[256,512]{1,0:T(8,128)(2,1)S(1)} custom-call(s32[4]{0:T(128)S(1)} %pad_add_fusion.meta, bf16[256,512]{1,0:T(8,128)(2,1)S(1)} %convolve.1.act_ref, bf16[16,512]{1,0:T(8,128)(2,1)S(1)} %rim.1.rim_ref, bf16[256,512]{1,0:T(8,128)(2,1)S(1)} %get-tuple-element.50.mid_ref, bf16[256,1024]{1,0:T(8,128)(2,1)S(1)} %copy-done.19, ...), custom_call_target="tpu_custom_call" | custom-call | flops 1380000000 | tf_op jit(solution)/shard_map/finish_own/pallas_call | solution.py:451
  52.8 1.7 %finish.1 = bf16[512,512]{1,0:T(8,128)(2,1)} custom-call(s32[4]{0:T(128)S(1)} %pad_add_fusion.meta, bf16[256,512]{1,0:T(8,128)(2,1)S(1)} %collective-permute-done.10.act_ref, bf16[16,512]{1,0:T(8,128)(2,1)S(1)} %collective-permute-done.12.rim_ref, bf16[256,512]{1,0:T(8,128)(2,1)S(1)} %collective-permute-done.13.mid_ref, bf16[256,1024]{1,0:T(8,128)(2,1)S(1)} %copy-done.19, ...), custom_call_target="tpu_custom_call" | custom-call | flops 1380000000 | tf_op jit(solution)/shard_map/finish/pallas_call | solution.py:451
  (67 shorter events, 3.8 us)
Async XLA Ops:
  0.0 2.7 %collective-permute-start = (bf16[512,512]{1,0:T(8,128)(2,1)}, bf16[512,512]{1,0:T(8,128)(2,1)S(1)}, u32[]{:S(2)}, u32[]{:S(2)}) collective-permute-start(bf16[512,512]{1,0:T(8,128)(2,1)} %x_own.1), channel_id=1, source_target_pairs={{0,1},{1,0},{2,3},{3,2},{4,5},{5,4},{6,7},{7,6},{8,9},{9,8},{10,11... | collective-permute-start | bytes 1572872 | tf_op jit(solution)/shard_map/ppermute | solution.py:480
  2.8 7.1 %copy-start.21 = (s32[512]{0:T(512)S(1)}, s32[512]{0:T(512)}, u32[]{:S(2)}) copy-start(s32[512]{0:T(512)} %param.12) | copy-start | bytes 6148
  2.8 23.1 %copy-start.18 = (s32[16]{0:T(128)S(1)}, s32[16]{0:T(128)}, u32[]{:S(2)}) copy-start(s32[16]{0:T(128)} %param.13) | copy-start | bytes 196
  4.8 26.1 %copy-start.4 = (bf16[512,128]{1,0:T(8,128)(2,1)}, bf16[512,128]{1,0:T(8,128)(2,1)S(1)}, u32[]{:S(2)}) copy-start(bf16[512,128]{1,0:T(8,128)(2,1)S(1)} %get-tuple-element.28.refs_0_.query) | copy-start | bytes 393220
  4.8 22.7 %collective-permute-start.4 = (bf16[2,1024,256]{2,1,0:T(8,128)(2,1)S(1)}, bf16[2,1024,256]{2,1,0:T(8,128)(2,1)S(1)}, u32[]{:S(2)}, u32[]{:S(2)}) collective-permute-start(bf16[2,1024,256]{2,1,0:T(8,128)(2,1)S(1)} %bitcast.17), channel_id=1, source_target_pairs={{0,1},{1,0},{2,3},{3,2},{4,5},{5,4},{6,7},{7,6},{8,9},{9,8},{10,11... | collective-permute-start | bytes 3145736 | tf_op jit(solution)/shard_map/ppermute | solution.py:480
  4.9 22.5 %collective-permute-start.5 = (bf16[256,1024]{1,0:T(8,128)(2,1)S(1)}, bf16[256,1024]{1,0:T(8,128)(2,1)S(1)}, u32[]{:S(2)}, u32[]{:S(2)}) collective-permute-start(bf16[256,1024]{1,0:T(8,128)(2,1)S(1)} %copy-done.13), channel_id=1, source_target_pairs={{0,1},{1,0},{2,3},{3,2},{4,5},{5,4},{6,7},{7,6},{8,9},{9,8},{10,11... | collective-permute-start | bytes 1572872 | tf_op jit(solution)/shard_map/ppermute | solution.py:480
  5.4 22.1 %collective-permute-start.1 = (bf16[512,384]{1,0:T(8,128)(2,1)S(1)}, bf16[512,384]{1,0:T(8,128)(2,1)S(1)}, u32[]{:S(2)}, u32[]{:S(2)}) collective-permute-start(bf16[512,384]{1,0:T(8,128)(2,1)S(1)} %get-tuple-element.31), channel_id=1, source_target_pairs={{0,2},{2,0},{4,6},{6,4},{8,10},{10,8},{12,14},{14,12},{1,3},{3,1},... | collective-permute-start | bytes 1179656 | tf_op jit(solution)/shard_map/ppermute | solution.py:487
  7.9 19.5 %collective-permute-start.2 = (bf16[512,256]{1,0:T(8,128)(2,1)S(1)}, bf16[512,256]{1,0:T(8,128)(2,1)S(1)}, u32[]{:S(2)}, u32[]{:S(2)}) collective-permute-start(bf16[512,256]{1,0:T(8,128)(2,1)S(1)} %get-tuple-element.30.center.side_a), channel_id=1, source_target_pairs={{2,6},{4,0},{6,10},{8,4},{10,14},{12,8},{3,7},{5,1},{7,11},{9,5},{... | collective-permute-start | bytes 786440 | tf_op jit(solution)/shard_map/ppermute | solution.py:484
  9.2 18.2 %collective-permute-start.3 = (bf16[512,256]{1,0:T(8,128)(2,1)S(1)}, bf16[512,256]{1,0:T(8,128)(2,1)S(1)}, u32[]{:S(2)}, u32[]{:S(2)}) collective-permute-start(bf16[512,256]{1,0:T(8,128)(2,1)S(1)} %get-tuple-element.32), channel_id=1, source_target_pairs={{2,4},{4,2},{6,8},{8,6},{10,12},{12,10},{3,5},{5,3},{7,9},{9,7},{1... | collective-permute-start | bytes 786440 | tf_op jit(solution)/shard_map/ppermute | solution.py:484
  27.4 3.4 %copy-start.11 = (bf16[512,256]{1,0:T(8,128)(2,1)}, bf16[512,256]{1,0:T(8,128)(2,1)S(1)}, u32[]{:S(2)}) copy-start(bf16[512,256]{1,0:T(8,128)(2,1)S(1)} %collective-permute-done.3.side_b.refs_1_) | copy-start | bytes 786436
  27.5 14.1 %copy-start.17 = (f32[1024]{0:T(1024)S(1)}, f32[1024]{0:T(1024)}, u32[]{:S(2)}) copy-start(f32[1024]{0:T(1024)} %param.17) | copy-start | bytes 12292
  31.6 8.2 %collective-permute-start.6 = (bf16[512,128]{1,0:T(8,128)(2,1)}, bf16[512,128]{1,0:T(8,128)(2,1)}, u32[]{:S(2)}, u32[]{:S(2)}) collective-permute-start(bf16[512,128]{1,0:T(8,128)(2,1)} %attend.3), channel_id=1, source_target_pairs={{0,2},{2,0},{4,6},{6,4},{8,10},{10,8},{12,14},{14,12},{1,3},{3,1},... | collective-permute-start | bytes 393224 | tf_op jit(solution)/shard_map/ppermute | solution.py:487
  33.0 8.5 %copy-start.2 = (bf16[512,512]{1,0:T(8,128)(2,1)S(1)}, bf16[512,512]{1,0:T(8,128)(2,1)}, u32[]{:S(2)}) copy-start(bf16[512,512]{1,0:T(8,128)(2,1)} %copy-done.1) | copy-start | bytes 1572868
  36.8 3.4 %copy-start.19 = (bf16[256,1024]{1,0:T(8,128)(2,1)S(1)}, bf16[256,1024]{1,0:T(8,128)(2,1)}, u32[]{:S(2)}) copy-start(bf16[256,1024]{1,0:T(8,128)(2,1)} %w_own.1) | copy-start | bytes 1572868
  36.8 3.5 %copy-start.15 = (f32[32,256]{1,0:T(8,128)S(1)}, f32[32,256]{1,0:T(8,128)}, u32[]{:S(2)}) copy-start(f32[32,256]{1,0:T(8,128)} %pad_maximum_fusion.taps_own) | copy-start | bytes 98308
  36.8 4.7 %copy-start.14 = (bf16[256,1024]{1,0:T(8,128)(2,1)S(1)}, bf16[256,1024]{1,0:T(8,128)(2,1)}, u32[]{:S(2)}) copy-start(bf16[256,1024]{1,0:T(8,128)(2,1)} %out_own) | copy-start | bytes 1572868
  39.7 1.4 %collective-permute-start.7 = (bf16[512,128]{1,0:T(8,128)(2,1)S(1)}, bf16[512,128]{1,0:T(8,128)(2,1)S(1)}, u32[]{:S(2)}, u32[]{:S(2)}) collective-permute-start(bf16[512,128]{1,0:T(8,128)(2,1)S(1)} %attend.2.mine_own), channel_id=1, source_target_pairs={{0,1},{1,0},{2,3},{3,2},{4,5},{5,4},{6,7},{7,6},{8,9},{9,8},{10,11... | collective-permute-start | bytes 393224 | tf_op jit(solution)/shard_map/ppermute | solution.py:480
  39.8 1.7 %collective-permute-start.8 = (bf16[512,128]{1,0:T(8,128)(2,1)}, bf16[512,128]{1,0:T(8,128)(2,1)S(1)}, u32[]{:S(2)}, u32[]{:S(2)}) collective-permute-start(bf16[512,128]{1,0:T(8,128)(2,1)} %collective-permute-done.6.pair_own), channel_id=1, source_target_pairs={{0,1},{1,0},{2,3},{3,2},{4,5},{5,4},{6,7},{7,6},{8,9},{9,8},{10,11... | collective-permute-start | bytes 393224 | tf_op jit(solution)/shard_map/ppermute | solution.py:480
  40.3 11.6 %collective-permute-start.14 = (bf16[256,1024]{1,0:T(8,128)(2,1)S(1)}, bf16[256,1024]{1,0:T(8,128)(2,1)S(1)}, u32[]{:S(2)}, u32[]{:S(2)}) collective-permute-start(bf16[256,1024]{1,0:T(8,128)(2,1)S(1)} %copy-done.19), channel_id=1, source_target_pairs={{0,1},{1,0},{2,3},{3,2},{4,5},{5,4},{6,7},{7,6},{8,9},{9,8},{10,11... | collective-permute-start | bytes 1572872 | tf_op jit(solution)/shard_map/ppermute | solution.py:480
  40.4 4.4 %collective-permute-start.9 = (f32[32,256]{1,0:T(8,128)S(1)}, f32[32,256]{1,0:T(8,128)S(1)}, u32[]{:S(2)}, u32[]{:S(2)}) collective-permute-start(f32[32,256]{1,0:T(8,128)S(1)} %copy-done.15), channel_id=1, source_target_pairs={{0,1},{1,0},{2,3},{3,2},{4,5},{5,4},{6,7},{7,6},{8,9},{9,8},{10,11... | collective-permute-start | bytes 98312 | tf_op jit(solution)/shard_map/ppermute | solution.py:480
  44.1 6.4 %collective-permute-start.11 = (bf16[64,512]{1,0:T(8,128)(2,1)S(1)}, bf16[64,512]{1,0:T(8,128)(2,1)S(1)}, u32[]{:S(2)}, u32[]{:S(2)}) collective-permute-start(bf16[64,512]{1,0:T(8,128)(2,1)S(1)} %get-tuple-element.47), channel_id=1, source_target_pairs={{2,1},{4,3},{6,5},{8,7},{10,9},{12,11},{14,13},{1,2},{3,4},{5,6},{... | collective-permute-start | bytes 196616 | tf_op jit(solution)/shard_map/ppermute | solution.py:538
  48.4 4.4 %collective-permute-start.10 = (bf16[256,512]{1,0:T(8,128)(2,1)S(1)}, bf16[256,512]{1,0:T(8,128)(2,1)S(1)}, u32[]{:S(2)}, u32[]{:S(2)}) collective-permute-start(bf16[256,512]{1,0:T(8,128)(2,1)S(1)} %convolve.1.act_ref), channel_id=1, source_target_pairs={{0,1},{1,0},{2,3},{3,2},{4,5},{5,4},{6,7},{7,6},{8,9},{9,8},{10,11... | collective-permute-start | bytes 786440 | tf_op jit(solution)/shard_map/ppermute | solution.py:480
  50.4 2.4 %collective-permute-start.13 = (bf16[256,512]{1,0:T(8,128)(2,1)S(1)}, bf16[256,512]{1,0:T(8,128)(2,1)S(1)}, u32[]{:S(2)}, u32[]{:S(2)}) collective-permute-start(bf16[256,512]{1,0:T(8,128)(2,1)S(1)} %get-tuple-element.48), channel_id=1, source_target_pairs={{0,1},{1,0},{2,3},{3,2},{4,5},{5,4},{6,7},{7,6},{8,9},{9,8},{10,11... | collective-permute-start | bytes 786440 | tf_op jit(solution)/shard_map/ppermute | solution.py:480
  51.4 1.4 %collective-permute-start.12 = (bf16[16,512]{1,0:T(8,128)(2,1)S(1)}, bf16[16,512]{1,0:T(8,128)(2,1)S(1)}, u32[]{:S(2)}, u32[]{:S(2)}) collective-permute-start(bf16[16,512]{1,0:T(8,128)(2,1)S(1)} %rim.1.rim_ref), channel_id=1, source_target_pairs={{0,1},{1,0},{2,3},{3,2},{4,5},{5,4},{6,7},{7,6},{8,9},{9,8},{10,11... | collective-permute-start | bytes 49160 | tf_op jit(solution)/shard_map/ppermute | solution.py:480
  (14 other events, 24.6 us)

commit v10 on v9

--- a/solution.py
+++ b/solution.py
@@ -18,7 +18,7 @@
 EXP_SCALE = HEAD_DIM ** (-0.5) * math.log2(math.e)
 F32 = jnp.float32
 BF16 = jnp.bfloat16
-VMEM_LIMIT = 16 * 1024 * 1024
+VMEM_LIMIT = 8 * 1024 * 1024
 
 
 def weight(microseconds):

time: 54.8 us -> 54.8 us (level)
  no operation moved by 1% of the time
where the time goes in v10:
time: 54.8 us; the launch traced here: 54.4 us
  Pallas kernels  18.6 us (34%)
  blocking collectives  15.8 us (29%)
  starting transfers between devices  11.4 us (21%)
  local copies, waits for them, and re-layouts  6.78 us (12%)
  other arithmetic  0.82 us (1%)
  waiting for transfers between devices  0.75 us (1%)
    all_to_all x1, blocking collectives, local(): lax.all_to_all(jnp.broadcast_to(counts[None, :], (blocks, counts.shape[0]...  15.8 us
    unnamed x47, local copies, waits for them, and re-layouts  6.77 us
    pallas_call x2, Pallas kernels, attend(): pl.pallas_call(attend_kernel, in_specs=[pl.BlockSpec(memory_space=pltpu.S...  6.25 us
    ppermute x10, starting transfers between devices, swap(): return lax.ppermute(value, 'head', [(0, 1), (1, 0)])  4.77 us
    ppermute x2, starting transfers between devices, exchange(): return lax.ppermute(value, 'tm', [(i, i ^ 1) for i in range(blocks)])  4 us
    pallas_call x1, Pallas kernels, convolve(): pl.pallas_call(conv_kernel, in_specs=[pl.BlockSpec(memory_space=pltpu.SME...  3.59 us
    pallas_call x1, Pallas kernels, gated(): pl.pallas_call(gate_kernel, in_specs=[pl.BlockSpec(memory_space=pltpu.SME...  2.6 us
    pallas_call x2, Pallas kernels, finish(): pl.pallas_call(finish_own_kernel if done is None else finish_kernel, in_s...  2.59 us
  transfers between devices with their start and end apart: 15, of which 2 were waited for; matrix products, arithmetic and copies ran while one was open for 4% of the time, Pallas kernels for 21%

profile of v10, /device:TPU:0, one launch (start us, length us, event | category | flops | bytes accessed | tf_op | source)
XLA Modules:
  0.0 54.4 jit_solution(6547482866506375768)
XLA Ops:
  0.5 1.5 %copy.16 = bf16[1024,2,256]{2,0,1:T(8,128)(2,1)S(1)} copy(bf16[1024,2,256]{2,1,0:T(2,128)(2,1)} %param.18) | data formatting | bytes 2097152 | tf_op args[7]
  2.1 0.6 %pad_maximum_fusion.taps_own = f32[32,256]{1,0:T(8,128)} fusion(f32[1,256]{1,0:T(1,128)S(1)} %bitcast.24, f32[31,256]{1,0:T(8,128)S(1)} %copy-done.20), kind=kLoop, calls=%fused_computation.1 | loop fusion | flops 8192 | bytes 65536 | tf_op jit(solution)/shard_map/concatenate | solution.py:512
  2.8 1.9 %project.1 = (bf16[512,256]{1,0:T(8,128)(2,1)S(1)}, bf16[512,128]{1,0:T(8,128)(2,1)S(1)}, bf16[512,384]{1,0:T(8,128)(2,1)S(1)}, bf16[512,256]{1,0:T(8,128)(2,1)S(1)}) custom-call(s32[4]{0:T(128)S(1)} %pad_add_fusion.meta, bf16[512,512]{1,0:T(8,128)(2,1)S(1)} %copy-done, bf16[512,512]{1,0:T(8,128)(2,1)S(1)} %collective-permute-done.other_ref.x_other, ...), custom_call_target="tpu_custom_call" | custom-call | tf_op jit(solution)/shard_map/project/pallas_call | solution.py:85
  5.3 2.6 %collective-permute-start.1 = (bf16[512,384]{1,0:T(8,128)(2,1)S(1)}, bf16[512,384]{1,0:T(8,128)(2,1)S(1)}, u32[]{:S(2)}, u32[]{:S(2)}) collective-permute-start(bf16[512,384]{1,0:T(8,128)(2,1)S(1)} %get-tuple-element.31), channel_id=1, source_target_pairs={{0,2},{2,0},{4,6},{6,4},{8,10},{10,8},{12,14},{14,12},{1,3},{3,1},... | collective-permute-start | bytes 1179656 | tf_op jit(solution)/shard_map/ppermute | solution.py:487
  7.9 1.3 %collective-permute-start.2 = (bf16[512,256]{1,0:T(8,128)(2,1)S(1)}, bf16[512,256]{1,0:T(8,128)(2,1)S(1)}, u32[]{:S(2)}, u32[]{:S(2)}) collective-permute-start(bf16[512,256]{1,0:T(8,128)(2,1)S(1)} %get-tuple-element.30.center.side_a), channel_id=1, source_target_pairs={{2,6},{4,0},{6,10},{8,4},{10,14},{12,8},{3,7},{5,1},{7,11},{9,5},{... | collective-permute-start | bytes 786440 | tf_op jit(solution)/shard_map/ppermute | solution.py:484
  9.1 0.7 %collective-permute-start.3 = (bf16[512,256]{1,0:T(8,128)(2,1)S(1)}, bf16[512,256]{1,0:T(8,128)(2,1)S(1)}, u32[]{:S(2)}, u32[]{:S(2)}) collective-permute-start(bf16[512,256]{1,0:T(8,128)(2,1)S(1)} %get-tuple-element.32), channel_id=1, source_target_pairs={{2,4},{4,2},{6,8},{8,6},{10,12},{12,10},{3,5},{5,3},{7,9},{9,7},{1... | collective-permute-start | bytes 786440 | tf_op jit(solution)/shard_map/ppermute | solution.py:484
  10.0 15.8 %all_to_all.8 = s32[8,1,16]{2,1,0:T(1,128)S(1)} all-to-all(s32[8,1,16]{2,1,0:T(1,128)S(1)} %broadcast_in_dim.5), channel_id=1, replica_groups=mesh['grp'=2,'tm'=8,'head'=2] {'tm'}, dimensions={0} | all-to-all | bytes 1024 | tf_op jit(solution)/shard_map/all_to_all | solution.py:509
  25.8 0.8 %bounds.1 = (s32[512,128]{1,0:T(8,128)S(1)}, s32[512,128]{1,0:T(8,128)S(1)}) custom-call(s32[4]{0:T(128)S(1)} %pad_add_fusion.meta, s32[8,16]{1,0:T(8,128)S(1)} %bitcast.20, s32[1,16]{1,0:T(1,128)S(1)} %bitcast.23, bf16[512,128]{1,0:T(8,128)(2,1)S(1)} %get-tuple-element.28.refs_0_.query), custom_call_target="tpu_custom_call" | custom-call | tf_op jit(solution)/shard_map/bounds/pallas_call | solution.py:130
  26.6 0.7 %copy-done.6 = s32[512,128]{1,0:T(8,128)} copy-done((s32[512,128]{1,0:T(8,128)}, s32[512,128]{1,0:T(8,128)S(1)}, u32[]{:S(2)}) %copy-start.6) | copy-done | bytes 262168
  27.4 3.4 %attend.3 = bf16[512,128]{1,0:T(8,128)(2,1)} custom-call(s32[1]{0:T(128)} %bitcast.1.a_high, bf16[512,384]{1,0:T(8,128)(2,1)S(1)} %collective-permute-done.1.side_a.query.center, bf16[512,384]{1,0:T(8,128)(2,1)S(1)} %collective-permute-done.1.side_a.query.center, bf16[512,256]{1,0:T(8,128)(2,1)S(1)} %get-tuple-element.30.center.side_a, ...), custom_call_target="tpu_custom_call" | custom-call | bytes 11070000 | tf_op jit(solution)/shard_map/attend/pallas_call | solution.py:204
  30.8 0.7 %copy-done.9 = bf16[512,256]{1,0:T(8,128)(2,1)} copy-done((bf16[512,256]{1,0:T(8,128)(2,1)}, bf16[512,256]{1,0:T(8,128)(2,1)S(1)}, u32[]{:S(2)}) %copy-start.9) | copy-done | bytes 262168
  31.5 1.4 %collective-permute-start.6 = (bf16[512,128]{1,0:T(8,128)(2,1)}, bf16[512,128]{1,0:T(8,128)(2,1)}, u32[]{:S(2)}, u32[]{:S(2)}) collective-permute-start(bf16[512,128]{1,0:T(8,128)(2,1)} %attend.3), channel_id=1, source_target_pairs={{0,2},{2,0},{4,6},{6,4},{8,10},{10,8},{12,14},{14,12},{1,3},{3,1},... | collective-permute-start | bytes 393224 | tf_op jit(solution)/shard_map/ppermute | solution.py:487
  32.9 1.0 %copy-done.5 = bf16[512,128]{1,0:T(8,128)(2,1)S(1)} copy-done((bf16[512,128]{1,0:T(8,128)(2,1)S(1)}, bf16[512,128]{1,0:T(8,128)(2,1)}, u32[]{:S(2)}) %copy-start.5) | copy-done | bytes 131096
  33.9 0.9 %copy-done.7 = s32[512,128]{1,0:T(8,128)S(1)} copy-done((s32[512,128]{1,0:T(8,128)S(1)}, s32[512,128]{1,0:T(8,128)}, u32[]{:S(2)}) %copy-start.7) | copy-done | bytes 262168
  34.9 0.9 %copy-done.10 = bf16[512,256]{1,0:T(8,128)(2,1)S(1)} copy-done((bf16[512,256]{1,0:T(8,128)(2,1)S(1)}, bf16[512,256]{1,0:T(8,128)(2,1)}, u32[]{:S(2)}) %copy-start.10) | copy-done | bytes 262168
  35.8 0.9 %copy-done.12 = bf16[512,256]{1,0:T(8,128)(2,1)S(1)} copy-done((bf16[512,256]{1,0:T(8,128)(2,1)S(1)}, bf16[512,256]{1,0:T(8,128)(2,1)}, u32[]{:S(2)}) %copy-start.12) | copy-done | bytes 262168
  36.8 2.8 %attend.2.mine_own = bf16[512,128]{1,0:T(8,128)(2,1)S(1)} custom-call(s32[1]{0:T(128)} %bitcast.4.a_high, bf16[512,128]{1,0:T(8,128)(2,1)S(1)} %copy-done.5, bf16[512,256]{1,0:T(8,128)(2,1)S(1)} %copy-done.10, bf16[512,384]{1,0:T(8,128)(2,1)S(1)} %collective-permute-done.1.side_a.query.center, bf16[512,256]{1,0:T(8,128)(2,1)S(1)} %copy-done.12, ...), custom_call_target="tpu_custom_call" | custom-call | bytes 11070000 | tf_op jit(solution)/shard_map/attend/pallas_call | solution.py:204
  41.5 2.6 %gated.1 = (bf16[272,512]{1,0:T(8,128)(2,1)S(1)}, bf16[64,512]{1,0:T(8,128)(2,1)S(1)}, bf16[256,512]{1,0:T(8,128)(2,1)S(1)}, bf16[256,512]{1,0:T(8,128)(2,1)S(1)}) custom-call(s32[4]{0:T(128)S(1)} %pad_add_fusion.meta, bf16[512,128]{1,0:T(8,128)(2,1)S(1)} %attend.2.mine_own, bf16[512,128]{1,0:T(8,128)(2,1)} %collective-permute-done.6.pair_own, ...), custom_call_target="tpu_custom_call" | custom-call | bytes 11070000 | tf_op jit(solution)/shard_map/gated/pallas_call | solution.py:294
  44.1 0.7 %collective-permute-start.11 = (bf16[64,512]{1,0:T(8,128)(2,1)S(1)}, bf16[64,512]{1,0:T(8,128)(2,1)S(1)}, u32[]{:S(2)}, u32[]{:S(2)}) collective-permute-start(bf16[64,512]{1,0:T(8,128)(2,1)S(1)} %get-tuple-element.47), channel_id=1, source_target_pairs={{2,1},{4,3},{6,5},{8,7},{10,9},{12,11},{14,13},{1,2},{3,4},{5,6},{... | collective-permute-start | bytes 196616 | tf_op jit(solution)/shard_map/ppermute | solution.py:538
  44.8 3.6 %convolve.1.act_ref = bf16[256,512]{1,0:T(8,128)(2,1)S(1)} custom-call(s32[4]{0:T(128)S(1)} %pad_add_fusion.meta, bf16[272,512]{1,0:T(8,128)(2,1)S(1)} %get-tuple-element.45.glu_ref, s32[512,128]{1,0:T(8,128)S(1)} %copy-done.8, f32[32,256]{1,0:T(8,128)S(1)} %copy-done.15, f32[32,256]{1,0:T(8,128)S(1)} %collective-permute-done.9.taps_other), custom_call_target="tpu_custom_call" | custom-call | flops 3449999872 | tf_op jit(solution)/shard_map/convolve/pallas_call | solution.py:367
  48.3 2.0 %collective-permute-start.10 = (bf16[256,512]{1,0:T(8,128)(2,1)S(1)}, bf16[256,512]{1,0:T(8,128)(2,1)S(1)}, u32[]{:S(2)}, u32[]{:S(2)}) collective-permute-start(bf16[256,512]{1,0:T(8,128)(2,1)S(1)} %convolve.1.act_ref), channel_id=1, source_target_pairs={{0,1},{1,0},{2,3},{3,2},{4,5},{5,4},{6,7},{7,6},{8,9},{9,8},{10,11... | collective-permute-start | bytes 786440 | tf_op jit(solution)/shard_map/ppermute | solution.py:480
  50.4 0.9 %rim.1.rim_ref = bf16[16,512]{1,0:T(8,128)(2,1)S(1)} custom-call(s32[4]{0:T(128)S(1)} %pad_add_fusion.meta, bf16[272,512]{1,0:T(8,128)(2,1)S(1)} %get-tuple-element.45.glu_ref, bf16[64,512]{1,0:T(8,128)(2,1)S(1)} %collective-permute-done.11.edge_ref, s32[512,128]{1,0:T(8,128)S(1)} %copy-done.8, f32[32,256]{1,0:T(8,128)S(1)} %copy-done.15, ...), custom_call_target="tpu_custom_call" | custom-call | flops 1150000000 | tf_op jit(solution)/shard_map/rim/pallas_call | solution.py:403
  51.8 0.9 %finish_own.1.done_ref = bf16[256,512]{1,0:T(8,128)(2,1)S(1)} custom-call(s32[4]{0:T(128)S(1)} %pad_add_fusion.meta, bf16[256,512]{1,0:T(8,128)(2,1)S(1)} %convolve.1.act_ref, bf16[16,512]{1,0:T(8,128)(2,1)S(1)} %rim.1.rim_ref, bf16[256,512]{1,0:T(8,128)(2,1)S(1)} %get-tuple-element.50.mid_ref, bf16[256,1024]{1,0:T(8,128)(2,1)S(1)} %copy-done.19, ...), custom_call_target="tpu_custom_call" | custom-call | flops 1380000000 | tf_op jit(solution)/shard_map/finish_own/pallas_call | solution.py:451
  52.7 1.7 %finish.1 = bf16[512,512]{1,0:T(8,128)(2,1)} custom-call(s32[4]{0:T(128)S(1)} %pad_add_fusion.meta, bf16[256,512]{1,0:T(8,128)(2,1)S(1)} %collective-permute-done.10.act_ref, bf16[16,512]{1,0:T(8,128)(2,1)S(1)} %collective-permute-done.12.rim_ref, bf16[256,512]{1,0:T(8,128)(2,1)S(1)} %collective-permute-done.13.mid_ref, bf16[256,1024]{1,0:T(8,128)(2,1)S(1)} %copy-done.19, ...), custom_call_target="tpu_custom_call" | custom-call | flops 1380000000 | tf_op jit(solution)/shard_map/finish/pallas_call | solution.py:451
  (67 shorter events, 3.8 us)
Async XLA Ops:
  0.0 2.7 %collective-permute-start = (bf16[512,512]{1,0:T(8,128)(2,1)}, bf16[512,512]{1,0:T(8,128)(2,1)S(1)}, u32[]{:S(2)}, u32[]{:S(2)}) collective-permute-start(bf16[512,512]{1,0:T(8,128)(2,1)} %x_own.1), channel_id=1, source_target_pairs={{0,1},{1,0},{2,3},{3,2},{4,5},{5,4},{6,7},{7,6},{8,9},{9,8},{10,11... | collective-permute-start | bytes 1572872 | tf_op jit(solution)/shard_map/ppermute | solution.py:480
  2.8 7.1 %copy-start.21 = (s32[512]{0:T(512)S(1)}, s32[512]{0:T(512)}, u32[]{:S(2)}) copy-start(s32[512]{0:T(512)} %param.12) | copy-start | bytes 6148
  2.8 23.0 %copy-start.18 = (s32[16]{0:T(128)S(1)}, s32[16]{0:T(128)}, u32[]{:S(2)}) copy-start(s32[16]{0:T(128)} %param.13) | copy-start | bytes 196
  4.7 26.1 %copy-start.4 = (bf16[512,128]{1,0:T(8,128)(2,1)}, bf16[512,128]{1,0:T(8,128)(2,1)S(1)}, u32[]{:S(2)}) copy-start(bf16[512,128]{1,0:T(8,128)(2,1)S(1)} %get-tuple-element.28.refs_0_.query) | copy-start | bytes 393220
  4.7 22.7 %collective-permute-start.4 = (bf16[2,1024,256]{2,1,0:T(8,128)(2,1)S(1)}, bf16[2,1024,256]{2,1,0:T(8,128)(2,1)S(1)}, u32[]{:S(2)}, u32[]{:S(2)}) collective-permute-start(bf16[2,1024,256]{2,1,0:T(8,128)(2,1)S(1)} %bitcast.17), channel_id=1, source_target_pairs={{0,1},{1,0},{2,3},{3,2},{4,5},{5,4},{6,7},{7,6},{8,9},{9,8},{10,11... | collective-permute-start | bytes 3145736 | tf_op jit(solution)/shard_map/ppermute | solution.py:480
  4.8 22.5 %collective-permute-start.5 = (bf16[256,1024]{1,0:T(8,128)(2,1)S(1)}, bf16[256,1024]{1,0:T(8,128)(2,1)S(1)}, u32[]{:S(2)}, u32[]{:S(2)}) collective-permute-start(bf16[256,1024]{1,0:T(8,128)(2,1)S(1)} %copy-done.13), channel_id=1, source_target_pairs={{0,1},{1,0},{2,3},{3,2},{4,5},{5,4},{6,7},{7,6},{8,9},{9,8},{10,11... | collective-permute-start | bytes 1572872 | tf_op jit(solution)/shard_map/ppermute | solution.py:480
  5.3 22.1 %collective-permute-start.1 = (bf16[512,384]{1,0:T(8,128)(2,1)S(1)}, bf16[512,384]{1,0:T(8,128)(2,1)S(1)}, u32[]{:S(2)}, u32[]{:S(2)}) collective-permute-start(bf16[512,384]{1,0:T(8,128)(2,1)S(1)} %get-tuple-element.31), channel_id=1, source_target_pairs={{0,2},{2,0},{4,6},{6,4},{8,10},{10,8},{12,14},{14,12},{1,3},{3,1},... | collective-permute-start | bytes 1179656 | tf_op jit(solution)/shard_map/ppermute | solution.py:487
  7.9 19.5 %collective-permute-start.2 = (bf16[512,256]{1,0:T(8,128)(2,1)S(1)}, bf16[512,256]{1,0:T(8,128)(2,1)S(1)}, u32[]{:S(2)}, u32[]{:S(2)}) collective-permute-start(bf16[512,256]{1,0:T(8,128)(2,1)S(1)} %get-tuple-element.30.center.side_a), channel_id=1, source_target_pairs={{2,6},{4,0},{6,10},{8,4},{10,14},{12,8},{3,7},{5,1},{7,11},{9,5},{... | collective-permute-start | bytes 786440 | tf_op jit(solution)/shard_map/ppermute | solution.py:484
  9.1 18.2 %collective-permute-start.3 = (bf16[512,256]{1,0:T(8,128)(2,1)S(1)}, bf16[512,256]{1,0:T(8,128)(2,1)S(1)}, u32[]{:S(2)}, u32[]{:S(2)}) collective-permute-start(bf16[512,256]{1,0:T(8,128)(2,1)S(1)} %get-tuple-element.32), channel_id=1, source_target_pairs={{2,4},{4,2},{6,8},{8,6},{10,12},{12,10},{3,5},{5,3},{7,9},{9,7},{1... | collective-permute-start | bytes 786440 | tf_op jit(solution)/shard_map/ppermute | solution.py:484
  27.3 3.5 %copy-start.11 = (bf16[512,256]{1,0:T(8,128)(2,1)}, bf16[512,256]{1,0:T(8,128)(2,1)S(1)}, u32[]{:S(2)}) copy-start(bf16[512,256]{1,0:T(8,128)(2,1)S(1)} %collective-permute-done.3.side_b.refs_1_) | copy-start | bytes 786436
  27.4 14.1 %copy-start.17 = (f32[1024]{0:T(1024)S(1)}, f32[1024]{0:T(1024)}, u32[]{:S(2)}) copy-start(f32[1024]{0:T(1024)} %param.17) | copy-start | bytes 12292
  31.5 8.2 %collective-permute-start.6 = (bf16[512,128]{1,0:T(8,128)(2,1)}, bf16[512,128]{1,0:T(8,128)(2,1)}, u32[]{:S(2)}, u32[]{:S(2)}) collective-permute-start(bf16[512,128]{1,0:T(8,128)(2,1)} %attend.3), channel_id=1, source_target_pairs={{0,2},{2,0},{4,6},{6,4},{8,10},{10,8},{12,14},{14,12},{1,3},{3,1},... | collective-permute-start | bytes 393224 | tf_op jit(solution)/shard_map/ppermute | solution.py:487
  32.9 8.5 %copy-start.2 = (bf16[512,512]{1,0:T(8,128)(2,1)S(1)}, bf16[512,512]{1,0:T(8,128)(2,1)}, u32[]{:S(2)}) copy-start(bf16[512,512]{1,0:T(8,128)(2,1)} %copy-done.1) | copy-start | bytes 1572868
  36.8 3.4 %copy-start.19 = (bf16[256,1024]{1,0:T(8,128)(2,1)S(1)}, bf16[256,1024]{1,0:T(8,128)(2,1)}, u32[]{:S(2)}) copy-start(bf16[256,1024]{1,0:T(8,128)(2,1)} %w_own.1) | copy-start | bytes 1572868
  36.8 3.5 %copy-start.15 = (f32[32,256]{1,0:T(8,128)S(1)}, f32[32,256]{1,0:T(8,128)}, u32[]{:S(2)}) copy-start(f32[32,256]{1,0:T(8,128)} %pad_maximum_fusion.taps_own) | copy-start | bytes 98308
  36.8 4.7 %copy-start.14 = (bf16[256,1024]{1,0:T(8,128)(2,1)S(1)}, bf16[256,1024]{1,0:T(8,128)(2,1)}, u32[]{:S(2)}) copy-start(bf16[256,1024]{1,0:T(8,128)(2,1)} %out_own) | copy-start | bytes 1572868
  39.6 1.4 %collective-permute-start.7 = (bf16[512,128]{1,0:T(8,128)(2,1)S(1)}, bf16[512,128]{1,0:T(8,128)(2,1)S(1)}, u32[]{:S(2)}, u32[]{:S(2)}) collective-permute-start(bf16[512,128]{1,0:T(8,128)(2,1)S(1)} %attend.2.mine_own), channel_id=1, source_target_pairs={{0,1},{1,0},{2,3},{3,2},{4,5},{5,4},{6,7},{7,6},{8,9},{9,8},{10,11... | collective-permute-start | bytes 393224 | tf_op jit(solution)/shard_map/ppermute | solution.py:480
  39.7 1.7 %collective-permute-start.8 = (bf16[512,128]{1,0:T(8,128)(2,1)}, bf16[512,128]{1,0:T(8,128)(2,1)S(1)}, u32[]{:S(2)}, u32[]{:S(2)}) collective-permute-start(bf16[512,128]{1,0:T(8,128)(2,1)} %collective-permute-done.6.pair_own), channel_id=1, source_target_pairs={{0,1},{1,0},{2,3},{3,2},{4,5},{5,4},{6,7},{7,6},{8,9},{9,8},{10,11... | collective-permute-start | bytes 393224 | tf_op jit(solution)/shard_map/ppermute | solution.py:480
  40.2 11.6 %collective-permute-start.14 = (bf16[256,1024]{1,0:T(8,128)(2,1)S(1)}, bf16[256,1024]{1,0:T(8,128)(2,1)S(1)}, u32[]{:S(2)}, u32[]{:S(2)}) collective-permute-start(bf16[256,1024]{1,0:T(8,128)(2,1)S(1)} %copy-done.19), channel_id=1, source_target_pairs={{0,1},{1,0},{2,3},{3,2},{4,5},{5,4},{6,7},{7,6},{8,9},{9,8},{10,11... | collective-permute-start | bytes 1572872 | tf_op jit(solution)/shard_map/ppermute | solution.py:480
  40.3 4.4 %collective-permute-start.9 = (f32[32,256]{1,0:T(8,128)S(1)}, f32[32,256]{1,0:T(8,128)S(1)}, u32[]{:S(2)}, u32[]{:S(2)}) collective-permute-start(f32[32,256]{1,0:T(8,128)S(1)} %copy-done.15), channel_id=1, source_target_pairs={{0,1},{1,0},{2,3},{3,2},{4,5},{5,4},{6,7},{7,6},{8,9},{9,8},{10,11... | collective-permute-start | bytes 98312 | tf_op jit(solution)/shard_map/ppermute | solution.py:480
  44.1 6.4 %collective-permute-start.11 = (bf16[64,512]{1,0:T(8,128)(2,1)S(1)}, bf16[64,512]{1,0:T(8,128)(2,1)S(1)}, u32[]{:S(2)}, u32[]{:S(2)}) collective-permute-start(bf16[64,512]{1,0:T(8,128)(2,1)S(1)} %get-tuple-element.47), channel_id=1, source_target_pairs={{2,1},{4,3},{6,5},{8,7},{10,9},{12,11},{14,13},{1,2},{3,4},{5,6},{... | collective-permute-start | bytes 196616 | tf_op jit(solution)/shard_map/ppermute | solution.py:538
  48.3 4.4 %collective-permute-start.10 = (bf16[256,512]{1,0:T(8,128)(2,1)S(1)}, bf16[256,512]{1,0:T(8,128)(2,1)S(1)}, u32[]{:S(2)}, u32[]{:S(2)}) collective-permute-start(bf16[256,512]{1,0:T(8,128)(2,1)S(1)} %convolve.1.act_ref), channel_id=1, source_target_pairs={{0,1},{1,0},{2,3},{3,2},{4,5},{5,4},{6,7},{7,6},{8,9},{9,8},{10,11... | collective-permute-start | bytes 786440 | tf_op jit(solution)/shard_map/ppermute | solution.py:480
  50.4 2.4 %collective-permute-start.13 = (bf16[256,512]{1,0:T(8,128)(2,1)S(1)}, bf16[256,512]{1,0:T(8,128)(2,1)S(1)}, u32[]{:S(2)}, u32[]{:S(2)}) collective-permute-start(bf16[256,512]{1,0:T(8,128)(2,1)S(1)} %get-tuple-element.48), channel_id=1, source_target_pairs={{0,1},{1,0},{2,3},{3,2},{4,5},{5,4},{6,7},{7,6},{8,9},{9,8},{10,11... | collective-permute-start | bytes 786440 | tf_op jit(solution)/shard_map/ppermute | solution.py:480
  51.3 1.4 %collective-permute-start.12 = (bf16[16,512]{1,0:T(8,128)(2,1)S(1)}, bf16[16,512]{1,0:T(8,128)(2,1)S(1)}, u32[]{:S(2)}, u32[]{:S(2)}) collective-permute-start(bf16[16,512]{1,0:T(8,128)(2,1)S(1)} %rim.1.rim_ref), channel_id=1, source_target_pairs={{0,1},{1,0},{2,3},{3,2},{4,5},{5,4},{6,7},{7,6},{8,9},{9,8},{10,11... | collective-permute-start | bytes 49160 | tf_op jit(solution)/shard_map/ppermute | solution.py:480
  (14 other events, 24.4 us)

commit v11 on v8

--- a/solution.py
+++ b/solution.py
@@ -52,7 +52,7 @@
 
 
 def qkv_kernel(
-    meta, own_ref, other_ref, gain_ref, w_ref, _, keep_ref, query_ref, send_ref, pass_ref
+    meta, own_ref, other_ref, gain_ref, w_ref, _, keep_ref, hold_ref, send_ref, pass_ref
 ):
     h = meta[0]
     first = meta[1] == 0
@@ -71,11 +71,10 @@
             keep = jnp.where(first, value[:, :sub], value[:, sub:])
             send = jnp.where(first, value[:, sub:], value[:, :sub])
             send_ref[here, cols] = send
+            hold_ref[here, cols] = keep
             if slot < 2:
                 keep_ref[here, cols] = keep
                 pass_ref[here, cols] = send
-            else:
-                query_ref[here, :] = keep
 
 
 def project(meta, frames, other, gain, qkv, early):
@@ -90,7 +89,7 @@
         out_specs=[vmem] * 4,
         out_shape=[
             jax.ShapeDtypeStruct((rows, width), BF16),
-            jax.ShapeDtypeStruct((rows, width // 2), BF16),
+            jax.ShapeDtypeStruct((rows, 3 * width // 2), BF16),
             jax.ShapeDtypeStruct((rows, 3 * width // 2), BF16),
             jax.ShapeDtypeStruct((rows, width), BF16),
         ],
@@ -137,7 +136,7 @@
 
 def attend_kernel(a_high, query, center, side_a, side_b, run_ref, out_ref):
     rows = center.shape[0]
-    width = center.shape[1] // 2 if query.shape[1] < center.shape[1] else center.shape[1] // 3
+    width = center.shape[1] // 3
     q_cols = slice(query.shape[1] - width, query.shape[1])
     tile = rows // 2
     lane = lax.broadcasted_iota(jnp.int32, (tile, width), 1)
@@ -492,7 +491,7 @@
     ])
     other = swap(frames)
     pointwise = pointwise_in.transpose(1, 0, 2)
-    keep, query, send, passed = project(
+    keep, held, send, passed = project(
         meta, frames, other, attn_gain, qkv_weight, pointwise
     )
     far_own = shift(passed, 1)
@@ -515,12 +514,12 @@
     taps, pointwise_out, runs = lax.optimization_barrier((taps, pointwise_out, runs))
     taps_other = swap(taps)
     pointwise_out_other = swap(pointwise_out)
-    pair, far_pair, far_own, runs, pair_runs = lax.optimization_barrier(
-        (pair, far_pair, far_own, runs, pair_runs)
-    )
-    pair_context = attend(column.reshape(1), pair, pair, keep, far_pair, pair_runs)
+    pair, far_pair, runs, pair_runs = lax.optimization_barrier(
+        (pair, far_pair, runs, pair_runs)
+    )
+    pair_context = attend(column.reshape(1), pair, pair, held, far_pair, pair_runs)
     pair_context = exchange(pair_context)
-    context = attend((1 - column).reshape(1), query, keep, pair, far_own, runs)
+    context = attend((1 - column).reshape(1), held, held, pair, far_own, runs)
     contexts = (context, pair_context, swap(context), swap(pair_context))
     glu, edge, mid_keep, mid_send = gated(
         meta, contexts, frames, other, out_weight, out_other, conv_gain,

time: 51.4 us -> 51.4 us (level)
  local copies, waits for them, and re-layouts: 4.04 us -> 1.53 us
  Pallas kernels: 18.8 us -> 20 us
  starting transfers between devices: 10.8 us -> 11.9 us
    unnamed x31 -> x21, local copies, waits for them, and re-layouts: 4.03 us -> 1.53 us
    ppermute x10, starting transfers between devices: 3.81 us -> 4.85 us  [swap(): return lax.ppermute(value, 'head', [(0, 1), (1, 0)])]
    pallas_call x1, Pallas kernels: 1.94 us -> 2.64 us  [project(): pl.pallas_call(qkv_kernel, in_specs=[pl.BlockSpec(memory_space=pltpu.SMEM...]
    ppermute x2, waiting for transfers between devices: 0.01 us -> 0.7 us  [exchange(): return lax.ppermute(value, 'tm', [(i, i ^ 1) for i in range(blocks)])]
  transfers between devices with their start and end apart: 15 -> 15, of which waited for: 2 -> 3; matrix products, arithmetic and copies ran while one was open for 5% -> 4% of each run, Pallas kernels for 30% -> 31%
where the time goes in v11:
time: 51.4 us; the launch traced here: 51.2 us
  Pallas kernels  20 us (39%)
  blocking collectives  15.3 us (30%)
  starting transfers between devices  11.9 us (23%)
  local copies, waits for them, and re-layouts  1.53 us (3%)
  waiting for transfers between devices  1.4 us (3%)
  other arithmetic  0.82 us (2%)
    all_to_all x1, blocking collectives, local(): lax.all_to_all(jnp.broadcast_to(counts[None, :], (blocks, counts.shape[0]...  15.3 us
    pallas_call x2, Pallas kernels, attend(): pl.pallas_call(attend_kernel, in_specs=[pl.BlockSpec(memory_space=pltpu.S...  6.29 us
    ppermute x10, starting transfers between devices, swap(): return lax.ppermute(value, 'head', [(0, 1), (1, 0)])  4.85 us
    ppermute x2, starting transfers between devices, exchange(): return lax.ppermute(value, 'tm', [(i, i ^ 1) for i in range(blocks)])  4.41 us
    pallas_call x1, Pallas kernels, convolve(): pl.pallas_call(conv_kernel, in_specs=[pl.BlockSpec(memory_space=pltpu.SME...  3.61 us
    pallas_call x1, Pallas kernels, gated(): pl.pallas_call(gate_kernel, in_specs=[pl.BlockSpec(memory_space=pltpu.SME...  3.21 us
    pallas_call x1, Pallas kernels, project(): pl.pallas_call(qkv_kernel, in_specs=[pl.BlockSpec(memory_space=pltpu.SMEM...  2.64 us
    pallas_call x2, Pallas kernels, finish(): pl.pallas_call(finish_own_kernel if done is None else finish_kernel, in_s...  2.58 us
  transfers between devices with their start and end apart: 15, of which 3 were waited for; matrix products, arithmetic and copies ran while one was open for 4% of the time, Pallas kernels for 31%

profile of v11, /device:TPU:0, one launch (start us, length us, event | category | flops | bytes accessed | tf_op | source)
XLA Modules:
  0.0 51.2 jit_solution(13871724537441377773)
XLA Ops:
  0.0 0.5 %collective-permute-start = (bf16[512,512]{1,0:T(8,128)(2,1)}, bf16[512,512]{1,0:T(8,128)(2,1)S(1)}, u32[]{:S(2)}, u32[]{:S(2)}) collective-permute-start(bf16[512,512]{1,0:T(8,128)(2,1)} %x_own.1), channel_id=1, source_target_pairs={{0,1},{1,0},{2,3},{3,2},{4,5},{5,4},{6,7},{7,6},{8,9},{9,8},{10,11... | collective-permute-start | bytes 1572872 | tf_op jit(solution)/shard_map/ppermute | solution.py:475
  0.5 1.5 %copy.16 = bf16[1024,2,256]{2,0,1:T(8,128)(2,1)S(1)} copy(bf16[1024,2,256]{2,1,0:T(2,128)(2,1)} %param.18) | data formatting | bytes 2097152 | tf_op args[7]
  2.1 0.6 %pad_maximum_fusion.taps_own = f32[32,256]{1,0:T(8,128)} fusion(f32[1,256]{1,0:T(1,128)S(1)} %bitcast.24, f32[31,256]{1,0:T(8,128)S(1)} %copy-done.7), kind=kLoop, calls=%fused_computation.1 | loop fusion | flops 8192 | bytes 65536 | tf_op jit(solution)/shard_map/concatenate | solution.py:507
  2.8 2.6 %project.1 = (bf16[512,256]{1,0:T(8,128)(2,1)S(1)}, bf16[512,384]{1,0:T(8,128)(2,1)S(1)}, bf16[512,384]{1,0:T(8,128)(2,1)S(1)}, bf16[512,256]{1,0:T(8,128)(2,1)}) custom-call(s32[4]{0:T(128)S(1)} %pad_add_fusion.meta, bf16[512,512]{1,0:T(8,128)(2,1)S(1)} %copy-done, bf16[512,512]{1,0:T(8,128)(2,1)S(1)} %collective-permute-done.other_ref.x_other, ...), custom_call_target="tpu_custom_call" | custom-call | tf_op jit(solution)/shard_map/project/pallas_call | solution.py:84
  5.5 2.9 %collective-permute-start.1 = (bf16[512,384]{1,0:T(8,128)(2,1)S(1)}, bf16[512,384]{1,0:T(8,128)(2,1)S(1)}, u32[]{:S(2)}, u32[]{:S(2)}) collective-permute-start(bf16[512,384]{1,0:T(8,128)(2,1)S(1)} %get-tuple-element.27), channel_id=1, source_target_pairs={{0,2},{2,0},{4,6},{6,4},{8,10},{10,8},{12,14},{14,12},{1,3},{3,1},... | collective-permute-start | bytes 1179656 | tf_op jit(solution)/shard_map/ppermute | solution.py:482
  8.4 1.3 %collective-permute-start.2 = (bf16[512,256]{1,0:T(8,128)(2,1)S(1)}, bf16[512,256]{1,0:T(8,128)(2,1)S(1)}, u32[]{:S(2)}, u32[]{:S(2)}) collective-permute-start(bf16[512,256]{1,0:T(8,128)(2,1)S(1)} %get-tuple-element.28), channel_id=1, source_target_pairs={{2,6},{4,0},{6,10},{8,4},{10,14},{12,8},{3,7},{5,1},{7,11},{9,5},{... | collective-permute-start | bytes 786440 | tf_op jit(solution)/shard_map/ppermute | solution.py:479
  9.8 0.7 %collective-permute-start.3 = (bf16[512,256]{1,0:T(8,128)(2,1)}, bf16[512,256]{1,0:T(8,128)(2,1)S(1)}, u32[]{:S(2)}, u32[]{:S(2)}) collective-permute-start(bf16[512,256]{1,0:T(8,128)(2,1)} %get-tuple-element.30), channel_id=1, source_target_pairs={{2,4},{4,2},{6,8},{8,6},{10,12},{12,10},{3,5},{5,3},{7,9},{9,7},{1... | collective-permute-start | bytes 786440 | tf_op jit(solution)/shard_map/ppermute | solution.py:479
  10.6 15.3 %all_to_all.8 = s32[8,1,16]{2,1,0:T(1,128)S(1)} all-to-all(s32[8,1,16]{2,1,0:T(1,128)S(1)} %broadcast_in_dim.5), channel_id=1, replica_groups=mesh['grp'=2,'tm'=8,'head'=2] {'tm'}, dimensions={0} | all-to-all | bytes 1024 | tf_op jit(solution)/shard_map/all_to_all | solution.py:504
  25.9 0.8 %bounds.1 = (s32[512,128]{1,0:T(8,128)S(1)}, s32[512,128]{1,0:T(8,128)S(1)}) custom-call(s32[4]{0:T(128)S(1)} %pad_add_fusion.meta, s32[8,16]{1,0:T(8,128)S(1)} %bitcast.20, s32[1,16]{1,0:T(1,128)S(1)} %bitcast.23), custom_call_target="tpu_custom_call" | custom-call | tf_op jit(solution)/shard_map/bounds/pallas_call | solution.py:127
  26.8 3.4 %attend.3 = bf16[512,128]{1,0:T(8,128)(2,1)} custom-call(s32[1]{0:T(128)} %bitcast.1.a_high, bf16[512,384]{1,0:T(8,128)(2,1)S(1)} %collective-permute-done.1.side_a.query.center, bf16[512,384]{1,0:T(8,128)(2,1)S(1)} %collective-permute-done.1.side_a.query.center, bf16[512,384]{1,0:T(8,128)(2,1)S(1)} %get-tuple-element.26.query.center.side_a, ...), custom_call_target="tpu_custom_call" | custom-call | bytes 11070000 | tf_op jit(solution)/shard_map/attend/pallas_call | solution.py:199
  30.2 1.5 %collective-permute-start.4 = (bf16[512,128]{1,0:T(8,128)(2,1)}, bf16[512,128]{1,0:T(8,128)(2,1)S(1)}, u32[]{:S(2)}, u32[]{:S(2)}) collective-permute-start(bf16[512,128]{1,0:T(8,128)(2,1)} %attend.3), channel_id=1, source_target_pairs={{0,2},{2,0},{4,6},{6,4},{8,10},{10,8},{12,14},{14,12},{1,3},{3,1},... | collective-permute-start | bytes 393224 | tf_op jit(solution)/shard_map/ppermute | solution.py:482
  31.7 2.9 %attend.2.mine_own = bf16[512,128]{1,0:T(8,128)(2,1)S(1)} custom-call(s32[1]{0:T(128)} %bitcast.4.a_high, bf16[512,384]{1,0:T(8,128)(2,1)S(1)} %get-tuple-element.26.query.center.side_a, bf16[512,384]{1,0:T(8,128)(2,1)S(1)} %get-tuple-element.26.query.center.side_a, bf16[512,384]{1,0:T(8,128)(2,1)S(1)} %collective-permute-done.1.side_a.query.center, ...), custom_call_target="tpu_custom_call" | custom-call | bytes 11070000 | tf_op jit(solution)/shard_map/attend/pallas_call | solution.py:199
  34.7 0.7 %collective-permute-done.4.pair_own = bf16[512,128]{1,0:T(8,128)(2,1)S(1)} collective-permute-done((bf16[512,128]{1,0:T(8,128)(2,1)}, bf16[512,128]{1,0:T(8,128)(2,1)S(1)}, u32[]{:S(2)}, u32[]{:S(2)}) %collective-permute-start.4) | collective-permute-done | bytes 131104 | tf_op jit(solution)/shard_map/ppermute | solution.py:482
  35.4 0.5 collective-permute-start.14
  36.0 0.1 collective-permute-start.9
  36.2 0.6 %collective-permute-done.6.pair_other = bf16[512,128]{1,0:T(8,128)(2,1)S(1)} collective-permute-done((bf16[512,128]{1,0:T(8,128)(2,1)S(1)}, bf16[512,128]{1,0:T(8,128)(2,1)S(1)}, u32[]{:S(2)}, u32[]{:S(2)}) %collective-permute-start.6) | collective-permute-done | bytes 131104 | tf_op jit(solution)/shard_map/ppermute | solution.py:475
  36.7 3.2 %gated.1 = (bf16[272,512]{1,0:T(8,128)(2,1)S(1)}, bf16[64,512]{1,0:T(8,128)(2,1)S(1)}, bf16[256,512]{1,0:T(8,128)(2,1)S(1)}, bf16[256,512]{1,0:T(8,128)(2,1)S(1)}) custom-call(s32[4]{0:T(128)S(1)} %pad_add_fusion.meta, bf16[512,128]{1,0:T(8,128)(2,1)S(1)} %attend.2.mine_own, bf16[512,128]{1,0:T(8,128)(2,1)S(1)} %collective-permute-done.4.pair_own, ...), custom_call_target="tpu_custom_call" | custom-call | bytes 11070000 | tf_op jit(solution)/shard_map/gated/pallas_call | solution.py:289
  39.9 0.7 %collective-permute-start.11 = (bf16[64,512]{1,0:T(8,128)(2,1)S(1)}, bf16[64,512]{1,0:T(8,128)(2,1)S(1)}, u32[]{:S(2)}, u32[]{:S(2)}) collective-permute-start(bf16[64,512]{1,0:T(8,128)(2,1)S(1)} %get-tuple-element.43), channel_id=1, source_target_pairs={{2,1},{4,3},{6,5},{8,7},{10,9},{12,11},{14,13},{1,2},{3,4},{5,6},{... | collective-permute-start | bytes 196616 | tf_op jit(solution)/shard_map/ppermute | solution.py:530
  40.6 3.6 %convolve.1.act_ref = bf16[256,512]{1,0:T(8,128)(2,1)S(1)} custom-call(s32[4]{0:T(128)S(1)} %pad_add_fusion.meta, bf16[272,512]{1,0:T(8,128)(2,1)S(1)} %get-tuple-element.41.glu_ref, s32[512,128]{1,0:T(8,128)S(1)} %get-tuple-element.36.run_ref, f32[32,256]{1,0:T(8,128)S(1)} %copy-done.2, f32[32,256]{1,0:T(8,128)S(1)} %collective-permute-done.9.taps_other), custom_call_target="tpu_custom_call" | custom-call | flops 3449999872 | tf_op jit(solution)/shard_map/convolve/pallas_call | solution.py:362
  44.2 2.9 %collective-permute-start.10 = (bf16[256,512]{1,0:T(8,128)(2,1)S(1)}, bf16[256,512]{1,0:T(8,128)(2,1)S(1)}, u32[]{:S(2)}, u32[]{:S(2)}) collective-permute-start(bf16[256,512]{1,0:T(8,128)(2,1)S(1)} %convolve.1.act_ref), channel_id=1, source_target_pairs={{0,1},{1,0},{2,3},{3,2},{4,5},{5,4},{6,7},{7,6},{8,9},{9,8},{10,11... | collective-permute-start | bytes 786440 | tf_op jit(solution)/shard_map/ppermute | solution.py:475
  47.2 0.9 %rim.1.rim_ref = bf16[16,512]{1,0:T(8,128)(2,1)S(1)} custom-call(s32[4]{0:T(128)S(1)} %pad_add_fusion.meta, bf16[272,512]{1,0:T(8,128)(2,1)S(1)} %get-tuple-element.41.glu_ref, bf16[64,512]{1,0:T(8,128)(2,1)S(1)} %collective-permute-done.11.edge_ref, s32[512,128]{1,0:T(8,128)S(1)} %get-tuple-element.36.run_ref, f32[32,256]{1,0:T(8,128)S(1)} %copy-done.2, ...), custom_call_target="tpu_custom_call" | custom-call | flops 1150000000 | tf_op jit(solution)/shard_map/rim/pallas_call | solution.py:398
  48.1 0.5 collective-permute-start.12
  48.6 0.9 %finish_own.1.done_ref = bf16[256,512]{1,0:T(8,128)(2,1)S(1)} custom-call(s32[4]{0:T(128)S(1)} %pad_add_fusion.meta, bf16[256,512]{1,0:T(8,128)(2,1)S(1)} %convolve.1.act_ref, bf16[16,512]{1,0:T(8,128)(2,1)S(1)} %rim.1.rim_ref, bf16[256,512]{1,0:T(8,128)(2,1)S(1)} %get-tuple-element.46.mid_ref, bf16[256,1024]{1,0:T(8,128)(2,1)S(1)} %copy-done.6, ...), custom_call_target="tpu_custom_call" | custom-call | flops 1380000000 | tf_op jit(solution)/shard_map/finish_own/pallas_call | solution.py:446
  49.5 1.7 %finish.1 = bf16[512,512]{1,0:T(8,128)(2,1)} custom-call(s32[4]{0:T(128)S(1)} %pad_add_fusion.meta, bf16[256,512]{1,0:T(8,128)(2,1)S(1)} %collective-permute-done.10.act_ref, bf16[16,512]{1,0:T(8,128)(2,1)S(1)} %collective-permute-done.12.rim_ref, bf16[256,512]{1,0:T(8,128)(2,1)S(1)} %collective-permute-done.13.mid_ref, bf16[256,1024]{1,0:T(8,128)(2,1)S(1)} %copy-done.6, ...), custom_call_target="tpu_custom_call" | custom-call | flops 1380000000 | tf_op jit(solution)/shard_map/finish/pallas_call | solution.py:446
  (41 shorter events, 0.7 us)
Async XLA Ops:
  0.0 2.7 %copy-start = (bf16[512,512]{1,0:T(8,128)(2,1)S(1)}, bf16[512,512]{1,0:T(8,128)(2,1)}, u32[]{:S(2)}) copy-start(bf16[512,512]{1,0:T(8,128)(2,1)} %x_own.1) | copy-start | bytes 1572868
  0.0 2.1 %copy-start.7 = (f32[31,256]{1,0:T(8,128)S(1)}, f32[31,256]{1,0:T(8,128)}, u32[]{:S(2)}) copy-start(f32[31,256]{1,0:T(8,128)} %param.19) | copy-start | bytes 95236
  0.0 2.7 %copy-start.3 = (f32[1024]{0:T(1024)S(1)}, f32[1024]{0:T(1024)}, u32[]{:S(2)}) copy-start(f32[1024]{0:T(1024)} %param.14) | copy-start | bytes 12292
  0.0 2.7 %collective-permute-start = (bf16[512,512]{1,0:T(8,128)(2,1)}, bf16[512,512]{1,0:T(8,128)(2,1)S(1)}, u32[]{:S(2)}, u32[]{:S(2)}) collective-permute-start(bf16[512,512]{1,0:T(8,128)(2,1)} %x_own.1), channel_id=1, source_target_pairs={{0,1},{1,0},{2,3},{3,2},{4,5},{5,4},{6,7},{7,6},{8,9},{9,8},{10,11... | collective-permute-start | bytes 1572872 | tf_op jit(solution)/shard_map/ppermute | solution.py:475
  0.5 2.2 %copy-start.1 = (bf16[1024,3,256]{2,0,1:T(8,128)(2,1)S(1)}, bf16[1024,3,256]{2,0,1:T(8,128)(2,1)}, u32[]{:S(2)}) copy-start(bf16[1024,3,256]{2,0,1:T(8,128)(2,1)} %param.15) | copy-start | bytes 4718596
  2.8 7.7 %copy-start.8 = (s32[512]{0:T(512)S(1)}, s32[512]{0:T(512)}, u32[]{:S(2)}) copy-start(s32[512]{0:T(512)} %param.12) | copy-start | bytes 6148
  2.8 23.2 %copy-start.5 = (s32[16]{0:T(128)S(1)}, s32[16]{0:T(128)}, u32[]{:S(2)}) copy-start(s32[16]{0:T(128)} %param.13) | copy-start | bytes 196
  5.4 31.3 %collective-permute-start.8 = (bf16[2,1024,256]{2,1,0:T(8,128)(2,1)S(1)}, bf16[2,1024,256]{2,1,0:T(8,128)(2,1)}, u32[]{:S(2)}, u32[]{:S(2)}) collective-permute-start(bf16[2,1024,256]{2,1,0:T(8,128)(2,1)S(1)} %bitcast.17), channel_id=1, source_target_pairs={{0,1},{1,0},{2,3},{3,2},{4,5},{5,4},{6,7},{7,6},{8,9},{9,8},{10,11... | collective-permute-start | bytes 3145736 | tf_op jit(solution)/shard_map/ppermute | solution.py:475
  5.5 21.3 %collective-permute-start.1 = (bf16[512,384]{1,0:T(8,128)(2,1)S(1)}, bf16[512,384]{1,0:T(8,128)(2,1)S(1)}, u32[]{:S(2)}, u32[]{:S(2)}) collective-permute-start(bf16[512,384]{1,0:T(8,128)(2,1)S(1)} %get-tuple-element.27), channel_id=1, source_target_pairs={{0,2},{2,0},{4,6},{6,4},{8,10},{10,8},{12,14},{14,12},{1,3},{3,1},... | collective-permute-start | bytes 1179656 | tf_op jit(solution)/shard_map/ppermute | solution.py:482
  8.4 18.4 %collective-permute-start.2 = (bf16[512,256]{1,0:T(8,128)(2,1)S(1)}, bf16[512,256]{1,0:T(8,128)(2,1)S(1)}, u32[]{:S(2)}, u32[]{:S(2)}) collective-permute-start(bf16[512,256]{1,0:T(8,128)(2,1)S(1)} %get-tuple-element.28), channel_id=1, source_target_pairs={{2,6},{4,0},{6,10},{8,4},{10,14},{12,8},{3,7},{5,1},{7,11},{9,5},{... | collective-permute-start | bytes 786440 | tf_op jit(solution)/shard_map/ppermute | solution.py:479
  9.7 26.5 %collective-permute-start.7 = (bf16[256,1024]{1,0:T(8,128)(2,1)}, bf16[256,1024]{1,0:T(8,128)(2,1)}, u32[]{:S(2)}, u32[]{:S(2)}) collective-permute-start(bf16[256,1024]{1,0:T(8,128)(2,1)} %out_own), channel_id=1, source_target_pairs={{0,1},{1,0},{2,3},{3,2},{4,5},{5,4},{6,7},{7,6},{8,9},{9,8},{10,11... | collective-permute-start | bytes 1572872 | tf_op jit(solution)/shard_map/ppermute | solution.py:475
  9.8 21.9 %collective-permute-start.3 = (bf16[512,256]{1,0:T(8,128)(2,1)}, bf16[512,256]{1,0:T(8,128)(2,1)S(1)}, u32[]{:S(2)}, u32[]{:S(2)}) collective-permute-start(bf16[512,256]{1,0:T(8,128)(2,1)} %get-tuple-element.30), channel_id=1, source_target_pairs={{2,4},{4,2},{6,8},{8,6},{10,12},{12,10},{3,5},{5,3},{7,9},{9,7},{1... | collective-permute-start | bytes 786440 | tf_op jit(solution)/shard_map/ppermute | solution.py:479
  26.8 9.9 %copy-start.4 = (f32[1024]{0:T(1024)S(1)}, f32[1024]{0:T(1024)}, u32[]{:S(2)}) copy-start(f32[1024]{0:T(1024)} %param.17) | copy-start | bytes 12292
  30.2 5.2 %collective-permute-start.4 = (bf16[512,128]{1,0:T(8,128)(2,1)}, bf16[512,128]{1,0:T(8,128)(2,1)S(1)}, u32[]{:S(2)}, u32[]{:S(2)}) collective-permute-start(bf16[512,128]{1,0:T(8,128)(2,1)} %attend.3), channel_id=1, source_target_pairs={{0,2},{2,0},{4,6},{6,4},{8,10},{10,8},{12,14},{14,12},{1,3},{3,1},... | collective-permute-start | bytes 393224 | tf_op jit(solution)/shard_map/ppermute | solution.py:482
  31.7 3.7 %copy-start.6 = (bf16[256,1024]{1,0:T(8,128)(2,1)S(1)}, bf16[256,1024]{1,0:T(8,128)(2,1)}, u32[]{:S(2)}) copy-start(bf16[256,1024]{1,0:T(8,128)(2,1)} %w_own.1) | copy-start | bytes 1572868
  31.7 4.4 %copy-start.2 = (f32[32,256]{1,0:T(8,128)S(1)}, f32[32,256]{1,0:T(8,128)}, u32[]{:S(2)}) copy-start(f32[32,256]{1,0:T(8,128)} %pad_maximum_fusion.taps_own) | copy-start | bytes 98308
  34.6 1.4 %collective-permute-start.5 = (bf16[512,128]{1,0:T(8,128)(2,1)S(1)}, bf16[512,128]{1,0:T(8,128)(2,1)S(1)}, u32[]{:S(2)}, u32[]{:S(2)}) collective-permute-start(bf16[512,128]{1,0:T(8,128)(2,1)S(1)} %attend.2.mine_own), channel_id=1, source_target_pairs={{0,1},{1,0},{2,3},{3,2},{4,5},{5,4},{6,7},{7,6},{8,9},{9,8},{10,11... | collective-permute-start | bytes 393224 | tf_op jit(solution)/shard_map/ppermute | solution.py:475
  35.4 1.3 %collective-permute-start.6 = (bf16[512,128]{1,0:T(8,128)(2,1)S(1)}, bf16[512,128]{1,0:T(8,128)(2,1)S(1)}, u32[]{:S(2)}, u32[]{:S(2)}) collective-permute-start(bf16[512,128]{1,0:T(8,128)(2,1)S(1)} %collective-permute-done.4.pair_own), channel_id=1, source_target_pairs={{0,1},{1,0},{2,3},{3,2},{4,5},{5,4},{6,7},{7,6},{8,9},{9,8},{10,11... | collective-permute-start | bytes 393224 | tf_op jit(solution)/shard_map/ppermute | solution.py:475
  35.4 13.2 %collective-permute-start.14 = (bf16[256,1024]{1,0:T(8,128)(2,1)S(1)}, bf16[256,1024]{1,0:T(8,128)(2,1)S(1)}, u32[]{:S(2)}, u32[]{:S(2)}) collective-permute-start(bf16[256,1024]{1,0:T(8,128)(2,1)S(1)} %copy-done.6), channel_id=1, source_target_pairs={{0,1},{1,0},{2,3},{3,2},{4,5},{5,4},{6,7},{7,6},{8,9},{9,8},{10,11... | collective-permute-start | bytes 1572872 | tf_op jit(solution)/shard_map/ppermute | solution.py:475
  36.0 4.6 %collective-permute-start.9 = (f32[32,256]{1,0:T(8,128)S(1)}, f32[32,256]{1,0:T(8,128)S(1)}, u32[]{:S(2)}, u32[]{:S(2)}) collective-permute-start(f32[32,256]{1,0:T(8,128)S(1)} %copy-done.2), channel_id=1, source_target_pairs={{0,1},{1,0},{2,3},{3,2},{4,5},{5,4},{6,7},{7,6},{8,9},{9,8},{10,11... | collective-permute-start | bytes 98312 | tf_op jit(solution)/shard_map/ppermute | solution.py:475
  39.9 7.3 %collective-permute-start.11 = (bf16[64,512]{1,0:T(8,128)(2,1)S(1)}, bf16[64,512]{1,0:T(8,128)(2,1)S(1)}, u32[]{:S(2)}, u32[]{:S(2)}) collective-permute-start(bf16[64,512]{1,0:T(8,128)(2,1)S(1)} %get-tuple-element.43), channel_id=1, source_target_pairs={{2,1},{4,3},{6,5},{8,7},{10,9},{12,11},{14,13},{1,2},{3,4},{5,6},{... | collective-permute-start | bytes 196616 | tf_op jit(solution)/shard_map/ppermute | solution.py:530
  44.2 5.2 %collective-permute-start.10 = (bf16[256,512]{1,0:T(8,128)(2,1)S(1)}, bf16[256,512]{1,0:T(8,128)(2,1)S(1)}, u32[]{:S(2)}, u32[]{:S(2)}) collective-permute-start(bf16[256,512]{1,0:T(8,128)(2,1)S(1)} %convolve.1.act_ref), channel_id=1, source_target_pairs={{0,1},{1,0},{2,3},{3,2},{4,5},{5,4},{6,7},{7,6},{8,9},{9,8},{10,11... | collective-permute-start | bytes 786440 | tf_op jit(solution)/shard_map/ppermute | solution.py:475
  47.1 2.4 %collective-permute-start.13 = (bf16[256,512]{1,0:T(8,128)(2,1)S(1)}, bf16[256,512]{1,0:T(8,128)(2,1)S(1)}, u32[]{:S(2)}, u32[]{:S(2)}) collective-permute-start(bf16[256,512]{1,0:T(8,128)(2,1)S(1)} %get-tuple-element.44), channel_id=1, source_target_pairs={{0,1},{1,0},{2,3},{3,2},{4,5},{5,4},{6,7},{7,6},{8,9},{9,8},{10,11... | collective-permute-start | bytes 786440 | tf_op jit(solution)/shard_map/ppermute | solution.py:475
  48.1 1.4 %collective-permute-start.12 = (bf16[16,512]{1,0:T(8,128)(2,1)S(1)}, bf16[16,512]{1,0:T(8,128)(2,1)S(1)}, u32[]{:S(2)}, u32[]{:S(2)}) collective-permute-start(bf16[16,512]{1,0:T(8,128)(2,1)S(1)} %rim.1.rim_ref), channel_id=1, source_target_pairs={{0,1},{1,0},{2,3},{3,2},{4,5},{5,4},{6,7},{7,6},{8,9},{9,8},{10,11... | collective-permute-start | bytes 49160 | tf_op jit(solution)/shard_map/ppermute | solution.py:475
  (1 other events, 2.1 us)

commit v12 on v11

--- a/solution.py
+++ b/solution.py
@@ -70,11 +70,12 @@
             cols = slice(slot * sub, slot * sub + sub)
             keep = jnp.where(first, value[:, :sub], value[:, sub:])
             send = jnp.where(first, value[:, sub:], value[:, :sub])
-            send_ref[here, cols] = send
             hold_ref[here, cols] = keep
             if slot < 2:
                 keep_ref[here, cols] = keep
                 pass_ref[here, cols] = send
+            else:
+                send_ref[here, :] = send
 
 
 def project(meta, frames, other, gain, qkv, early):
@@ -90,7 +91,7 @@
         out_shape=[
             jax.ShapeDtypeStruct((rows, width), BF16),
             jax.ShapeDtypeStruct((rows, 3 * width // 2), BF16),
-            jax.ShapeDtypeStruct((rows, 3 * width // 2), BF16),
+            jax.ShapeDtypeStruct((rows, width // 2), BF16),
             jax.ShapeDtypeStruct((rows, width), BF16),
         ],
         compiler_params=pltpu.CompilerParams(vmem_limit_bytes=VMEM_LIMIT),
@@ -136,7 +137,7 @@
 
 def attend_kernel(a_high, query, center, side_a, side_b, run_ref, out_ref):
     rows = center.shape[0]
-    width = center.shape[1] // 3
+    width = side_b.shape[1] // 2
     q_cols = slice(query.shape[1] - width, query.shape[1])
     tile = rows // 2
     lane = lax.broadcasted_iota(jnp.int32, (tile, width), 1)
@@ -494,9 +495,10 @@
     keep, held, send, passed = project(
         meta, frames, other, attn_gain, qkv_weight, pointwise
     )
-    far_own = shift(passed, 1)
-    pair = exchange(send)
+    pair = exchange(passed)
     far_pair = shift(keep, 2)
+    pair_query = exchange(send)
+    far_own = shift(pair, -2)
 
     segment_ids, _ = lax.optimization_barrier((segment_ids, passed))
     ids = jnp.arange(utt_valid.shape[0], dtype=jnp.int32)
@@ -514,10 +516,10 @@
     taps, pointwise_out, runs = lax.optimization_barrier((taps, pointwise_out, runs))
     taps_other = swap(taps)
     pointwise_out_other = swap(pointwise_out)
-    pair, far_pair, runs, pair_runs = lax.optimization_barrier(
-        (pair, far_pair, runs, pair_runs)
-    )
-    pair_context = attend(column.reshape(1), pair, pair, held, far_pair, pair_runs)
+    pair, pair_query, far_pair, far_own, runs, pair_runs = lax.optimization_barrier(
+        (pair, pair_query, far_pair, far_own, runs, pair_runs)
+    )
+    pair_context = attend(column.reshape(1), pair_query, pair, held, far_pair, pair_runs)
     pair_context = exchange(pair_context)
     context = attend((1 - column).reshape(1), held, held, pair, far_own, runs)
     contexts = (context, pair_context, swap(context), swap(pair_context))

time: 51.4 us -> 55.4 us (1.078)
  waiting for transfers between devices: 1.4 us -> 7.22 us
  blocking collectives: 15.3 us -> 11.6 us
  local copies, waits for them, and re-layouts: 1.53 us -> 3.18 us
  starting transfers between devices: 11.9 us -> 13.1 us
  Pallas kernels: 20 us -> 19.1 us
    ppermute x2 -> x3, waiting for transfers between devices: 0.7 us -> 6.11 us  [exchange(): return lax.ppermute(value, 'tm', [(i, i ^ 1) for i in range(blocks)])]
    all_to_all x1, blocking collectives: 15.3 us -> 11.6 us  [local(): lax.all_to_all(jnp.broadcast_to(counts[None, :], (blocks, counts.shape[0]...]
    ppermute x2, starting transfers between devices: 1.96 us -> 5 us  [shift(): return lax.ppermute(value, 'tm', [p for p in pairs if 0 <= p[1] < blocks])]
    unnamed x21 -> x27, local copies, waits for them, and re-layouts: 1.53 us -> 3.18 us
    ppermute x10, starting transfers between devices: 4.85 us -> 3.81 us  [swap(): return lax.ppermute(value, 'head', [(0, 1), (1, 0)])]
    ppermute x2 -> x3, starting transfers between devices: 4.41 us -> 3.58 us  [exchange(): return lax.ppermute(value, 'tm', [(i, i ^ 1) for i in range(blocks)])]
    pallas_call x1, Pallas kernels: 2.64 us -> 1.96 us  [project(): pl.pallas_call(qkv_kernel, in_specs=[pl.BlockSpec(memory_space=pltpu.SMEM...]
  transfers between devices with their start and end apart: 15 -> 16, of which waited for: 3 -> 3; matrix products, arithmetic and copies ran while one was open for 4% -> 4% of each run, Pallas kernels for 31% -> 28%
where the time goes in v12:
time: 55.4 us; the launch traced here: 55.1 us
  Pallas kernels  19.1 us (34%)
  starting transfers between devices  13.1 us (24%)
  blocking collectives  11.6 us (21%)
  waiting for transfers between devices  7.22 us (13%)
  local copies, waits for them, and re-layouts  3.18 us (6%)
  other arithmetic  0.82 us (1%)
    all_to_all x1, blocking collectives, local(): lax.all_to_all(jnp.broadcast_to(counts[None, :], (blocks, counts.shape[0]...  11.6 us
    pallas_call x2, Pallas kernels, attend(): pl.pallas_call(attend_kernel, in_specs=[pl.BlockSpec(memory_space=pltpu.S...  6.14 us
    ppermute x3, waiting for transfers between devices, exchange(): return lax.ppermute(value, 'tm', [(i, i ^ 1) for i in range(blocks)])  6.11 us
    ppermute x2, starting transfers between devices, shift(): return lax.ppermute(value, 'tm', [p for p in pairs if 0 <= p[1] < blocks])  5 us
    ppermute x10, starting transfers between devices, swap(): return lax.ppermute(value, 'head', [(0, 1), (1, 0)])  3.81 us
    pallas_call x1, Pallas kernels, convolve(): pl.pallas_call(conv_kernel, in_specs=[pl.BlockSpec(memory_space=pltpu.SME...  3.59 us
    ppermute x3, starting transfers between devices, exchange(): return lax.ppermute(value, 'tm', [(i, i ^ 1) for i in range(blocks)])  3.58 us
    unnamed x27, local copies, waits for them, and re-layouts  3.18 us
  transfers between devices with their start and end apart: 16, of which 3 were waited for; matrix products, arithmetic and copies ran while one was open for 4% of the time, Pallas kernels for 28%

profile of v12, /device:TPU:0, one launch (start us, length us, event | category | flops | bytes accessed | tf_op | source)
XLA Modules:
  0.0 55.1 jit_solution(15254008281982508192)
XLA Ops:
  0.0 0.5 collective-permute-start
  0.5 1.5 %copy.16 = bf16[1024,2,256]{2,0,1:T(8,128)(2,1)S(1)} copy(bf16[1024,2,256]{2,1,0:T(2,128)(2,1)} %param.18) | data formatting | bytes 2097152 | tf_op args[7]
  2.1 0.6 %pad_maximum_fusion.taps_own = f32[32,256]{1,0:T(8,128)} fusion(f32[1,256]{1,0:T(1,128)S(1)} %bitcast.24, f32[31,256]{1,0:T(8,128)S(1)} %copy-done.10), kind=kLoop, calls=%fused_computation.1 | loop fusion | flops 8192 | bytes 65536 | tf_op jit(solution)/shard_map/concatenate | solution.py:509
  2.8 2.0 %project.1 = (bf16[512,256]{1,0:T(8,128)(2,1)S(1)}, bf16[512,384]{1,0:T(8,128)(2,1)S(1)}, bf16[512,128]{1,0:T(8,128)(2,1)S(1)}, bf16[512,256]{1,0:T(8,128)(2,1)S(1)}) custom-call(s32[4]{0:T(128)S(1)} %pad_add_fusion.meta, bf16[512,512]{1,0:T(8,128)(2,1)S(1)} %copy-done, bf16[512,512]{1,0:T(8,128)(2,1)S(1)} %collective-permute-done.other_ref.x_other, ...), custom_call_target="tpu_custom_call" | custom-call | tf_op jit(solution)/shard_map/project/pallas_call | solution.py:85
  4.9 2.9 %collective-permute-start.1 = (bf16[512,256]{1,0:T(8,128)(2,1)S(1)}, bf16[512,256]{1,0:T(8,128)(2,1)S(1)}, u32[]{:S(2)}, u32[]{:S(2)}) collective-permute-start(bf16[512,256]{1,0:T(8,128)(2,1)S(1)} %get-tuple-element.29), channel_id=1, source_target_pairs={{0,2},{2,0},{4,6},{6,4},{8,10},{10,8},{12,14},{14,12},{1,3},{3,1},... | collective-permute-start | bytes 786440 | tf_op jit(solution)/shard_map/ppermute | solution.py:483
  7.8 1.3 %collective-permute-start.3 = (bf16[512,256]{1,0:T(8,128)(2,1)S(1)}, bf16[512,256]{1,0:T(8,128)(2,1)S(1)}, u32[]{:S(2)}, u32[]{:S(2)}) collective-permute-start(bf16[512,256]{1,0:T(8,128)(2,1)S(1)} %get-tuple-element.31), channel_id=1, source_target_pairs={{2,6},{4,0},{6,10},{8,4},{10,14},{12,8},{3,7},{5,1},{7,11},{9,5},{... | collective-permute-start | bytes 786440 | tf_op jit(solution)/shard_map/ppermute | solution.py:480
  9.1 5.3 %collective-permute-done.1.side_a.center = bf16[512,256]{1,0:T(8,128)(2,1)S(1)} collective-permute-done((bf16[512,256]{1,0:T(8,128)(2,1)S(1)}, bf16[512,256]{1,0:T(8,128)(2,1)S(1)}, u32[]{:S(2)}, u32[]{:S(2)}) %collective-permute-start.1) | collective-permute-done | bytes 262176 | tf_op jit(solution)/shard_map/ppermute | solution.py:483
  14.4 3.7 %collective-permute-start.4 = (bf16[512,256]{1,0:T(8,128)(2,1)S(1)}, bf16[512,256]{1,0:T(8,128)(2,1)S(1)}, u32[]{:S(2)}, u32[]{:S(2)}) collective-permute-start(bf16[512,256]{1,0:T(8,128)(2,1)S(1)} %collective-permute-done.1.side_a.center), channel_id=1, source_target_pairs={{0,4},{4,8},{6,2},{8,12},{10,6},{14,10},{1,5},{5,9},{7,3},{9,13},{... | collective-permute-start | bytes 786440 | tf_op jit(solution)/shard_map/ppermute | solution.py:480
  18.3 11.6 %all_to_all.8 = s32[8,1,16]{2,1,0:T(1,128)S(1)} all-to-all(s32[8,1,16]{2,1,0:T(1,128)S(1)} %broadcast_in_dim.5), channel_id=1, replica_groups=mesh['grp'=2,'tm'=8,'head'=2] {'tm'}, dimensions={0} | all-to-all | bytes 1024 | tf_op jit(solution)/shard_map/all_to_all | solution.py:506
  29.9 0.8 %bounds.1 = (s32[512,128]{1,0:T(8,128)S(1)}, s32[512,128]{1,0:T(8,128)S(1)}) custom-call(s32[4]{0:T(128)S(1)} %pad_add_fusion.meta, s32[8,16]{1,0:T(8,128)S(1)} %bitcast.20, s32[1,16]{1,0:T(1,128)S(1)} %bitcast.23), custom_call_target="tpu_custom_call" | custom-call | tf_op jit(solution)/shard_map/bounds/pallas_call | solution.py:128
  30.8 0.7 %copy-done.3 = bf16[512,256]{1,0:T(8,128)(2,1)} copy-done((bf16[512,256]{1,0:T(8,128)(2,1)}, bf16[512,256]{1,0:T(8,128)(2,1)S(1)}, u32[]{:S(2)}) %copy-start.3) | copy-done | bytes 262168
  31.5 3.3 %attend.3 = bf16[512,128]{1,0:T(8,128)(2,1)} custom-call(s32[1]{0:T(128)} %bitcast.1.a_high, bf16[512,128]{1,0:T(8,128)(2,1)S(1)} %collective-permute-done.2.query, bf16[512,256]{1,0:T(8,128)(2,1)S(1)} %collective-permute-done.1.side_a.center, bf16[512,384]{1,0:T(8,128)(2,1)S(1)} %get-tuple-element.28.query.center.side_a, ...), custom_call_target="tpu_custom_call" | custom-call | bytes 11070000 | tf_op jit(solution)/shard_map/attend/pallas_call | solution.py:200
  34.8 0.6 %collective-permute-start.5 = (bf16[512,128]{1,0:T(8,128)(2,1)}, bf16[512,128]{1,0:T(8,128)(2,1)}, u32[]{:S(2)}, u32[]{:S(2)}) collective-permute-start(bf16[512,128]{1,0:T(8,128)(2,1)} %attend.3), channel_id=1, source_target_pairs={{0,2},{2,0},{4,6},{6,4},{8,10},{10,8},{12,14},{14,12},{1,3},{3,1},... | collective-permute-start | bytes 393224 | tf_op jit(solution)/shard_map/ppermute | solution.py:483
  35.4 0.9 %copy-done.4 = bf16[512,256]{1,0:T(8,128)(2,1)S(1)} copy-done((bf16[512,256]{1,0:T(8,128)(2,1)S(1)}, bf16[512,256]{1,0:T(8,128)(2,1)}, u32[]{:S(2)}) %copy-start.4) | copy-done | bytes 262168
  36.3 2.8 %attend.2.mine_own = bf16[512,128]{1,0:T(8,128)(2,1)S(1)} custom-call(s32[1]{0:T(128)} %bitcast.4.a_high, bf16[512,384]{1,0:T(8,128)(2,1)S(1)} %get-tuple-element.28.query.center.side_a, bf16[512,384]{1,0:T(8,128)(2,1)S(1)} %get-tuple-element.28.query.center.side_a, bf16[512,256]{1,0:T(8,128)(2,1)S(1)} %collective-permute-done.1.side_a.center, ...), custom_call_target="tpu_custom_call" | custom-call | bytes 11070000 | tf_op jit(solution)/shard_map/attend/pallas_call | solution.py:200
  39.2 0.9 %collective-permute-done.5.pair_own = bf16[512,128]{1,0:T(8,128)(2,1)} collective-permute-done((bf16[512,128]{1,0:T(8,128)(2,1)}, bf16[512,128]{1,0:T(8,128)(2,1)}, u32[]{:S(2)}, u32[]{:S(2)}) %collective-permute-start.5) | collective-permute-done | bytes 131104 | tf_op jit(solution)/shard_map/ppermute | solution.py:483
  40.7 1.1 %collective-permute-done.7.pair_other = bf16[512,128]{1,0:T(8,128)(2,1)S(1)} collective-permute-done((bf16[512,128]{1,0:T(8,128)(2,1)}, bf16[512,128]{1,0:T(8,128)(2,1)S(1)}, u32[]{:S(2)}, u32[]{:S(2)}) %collective-permute-start.7) | collective-permute-done | bytes 131104 | tf_op jit(solution)/shard_map/ppermute | solution.py:476
  41.8 3.1 %gated.1 = (bf16[272,512]{1,0:T(8,128)(2,1)S(1)}, bf16[64,512]{1,0:T(8,128)(2,1)S(1)}, bf16[256,512]{1,0:T(8,128)(2,1)S(1)}, bf16[256,512]{1,0:T(8,128)(2,1)S(1)}) custom-call(s32[4]{0:T(128)S(1)} %pad_add_fusion.meta, bf16[512,128]{1,0:T(8,128)(2,1)S(1)} %attend.2.mine_own, bf16[512,128]{1,0:T(8,128)(2,1)} %collective-permute-done.5.pair_own, ...), custom_call_target="tpu_custom_call" | custom-call | bytes 11070000 | tf_op jit(solution)/shard_map/gated/pallas_call | solution.py:290
  44.9 0.7 %collective-permute-start.12 = (bf16[64,512]{1,0:T(8,128)(2,1)S(1)}, bf16[64,512]{1,0:T(8,128)(2,1)S(1)}, u32[]{:S(2)}, u32[]{:S(2)}) collective-permute-start(bf16[64,512]{1,0:T(8,128)(2,1)S(1)} %get-tuple-element.47), channel_id=1, source_target_pairs={{2,1},{4,3},{6,5},{8,7},{10,9},{12,11},{14,13},{1,2},{3,4},{5,6},{... | collective-permute-start | bytes 196616 | tf_op jit(solution)/shard_map/ppermute | solution.py:532
  45.5 3.6 %convolve.1.act_ref = bf16[256,512]{1,0:T(8,128)(2,1)S(1)} custom-call(s32[4]{0:T(128)S(1)} %pad_add_fusion.meta, bf16[272,512]{1,0:T(8,128)(2,1)S(1)} %get-tuple-element.45.glu_ref, s32[512,128]{1,0:T(8,128)S(1)} %get-tuple-element.39.run_ref, f32[32,256]{1,0:T(8,128)S(1)} %copy-done.5, f32[32,256]{1,0:T(8,128)S(1)} %collective-permute-done.10.taps_other), custom_call_target="tpu_custom_call" | custom-call | flops 3449999872 | tf_op jit(solution)/shard_map/convolve/pallas_call | solution.py:363
  49.1 1.9 %collective-permute-start.11 = (bf16[256,512]{1,0:T(8,128)(2,1)S(1)}, bf16[256,512]{1,0:T(8,128)(2,1)S(1)}, u32[]{:S(2)}, u32[]{:S(2)}) collective-permute-start(bf16[256,512]{1,0:T(8,128)(2,1)S(1)} %convolve.1.act_ref), channel_id=1, source_target_pairs={{0,1},{1,0},{2,3},{3,2},{4,5},{5,4},{6,7},{7,6},{8,9},{9,8},{10,11... | collective-permute-start | bytes 786440 | tf_op jit(solution)/shard_map/ppermute | solution.py:476
  51.1 0.9 %rim.1.rim_ref = bf16[16,512]{1,0:T(8,128)(2,1)S(1)} custom-call(s32[4]{0:T(128)S(1)} %pad_add_fusion.meta, bf16[272,512]{1,0:T(8,128)(2,1)S(1)} %get-tuple-element.45.glu_ref, bf16[64,512]{1,0:T(8,128)(2,1)S(1)} %collective-permute-done.12.edge_ref, s32[512,128]{1,0:T(8,128)S(1)} %get-tuple-element.39.run_ref, f32[32,256]{1,0:T(8,128)S(1)} %copy-done.5, ...), custom_call_target="tpu_custom_call" | custom-call | flops 1150000000 | tf_op jit(solution)/shard_map/rim/pallas_call | solution.py:399
  52.5 0.9 %finish_own.1.done_ref = bf16[256,512]{1,0:T(8,128)(2,1)S(1)} custom-call(s32[4]{0:T(128)S(1)} %pad_add_fusion.meta, bf16[256,512]{1,0:T(8,128)(2,1)S(1)} %convolve.1.act_ref, bf16[16,512]{1,0:T(8,128)(2,1)S(1)} %rim.1.rim_ref, bf16[256,512]{1,0:T(8,128)(2,1)S(1)} %get-tuple-element.50.mid_ref, bf16[256,1024]{1,0:T(8,128)(2,1)S(1)} %copy-done.9, ...), custom_call_target="tpu_custom_call" | custom-call | flops 1380000000 | tf_op jit(solution)/shard_map/finish_own/pallas_call | solution.py:447
  53.4 1.7 %finish.1 = bf16[512,512]{1,0:T(8,128)(2,1)} custom-call(s32[4]{0:T(128)S(1)} %pad_add_fusion.meta, bf16[256,512]{1,0:T(8,128)(2,1)S(1)} %collective-permute-done.11.act_ref, bf16[16,512]{1,0:T(8,128)(2,1)S(1)} %collective-permute-done.13.rim_ref, bf16[256,512]{1,0:T(8,128)(2,1)S(1)} %collective-permute-done.14.mid_ref, bf16[256,1024]{1,0:T(8,128)(2,1)S(1)} %copy-done.9, ...), custom_call_target="tpu_custom_call" | custom-call | flops 1380000000 | tf_op jit(solution)/shard_map/finish/pallas_call | solution.py:447
  (49 shorter events, 1.7 us)
Async XLA Ops:
  0.0 2.7 %copy-start = (bf16[512,512]{1,0:T(8,128)(2,1)S(1)}, bf16[512,512]{1,0:T(8,128)(2,1)}, u32[]{:S(2)}) copy-start(bf16[512,512]{1,0:T(8,128)(2,1)} %x_own.1) | copy-start | bytes 1572868
  0.0 2.7 %copy-start.6 = (f32[1024]{0:T(1024)S(1)}, f32[1024]{0:T(1024)}, u32[]{:S(2)}) copy-start(f32[1024]{0:T(1024)} %param.14) | copy-start | bytes 12292
  0.0 2.7 %collective-permute-start = (bf16[512,512]{1,0:T(8,128)(2,1)}, bf16[512,512]{1,0:T(8,128)(2,1)S(1)}, u32[]{:S(2)}, u32[]{:S(2)}) collective-permute-start(bf16[512,512]{1,0:T(8,128)(2,1)} %x_own.1), channel_id=1, source_target_pairs={{0,1},{1,0},{2,3},{3,2},{4,5},{5,4},{6,7},{7,6},{8,9},{9,8},{10,11... | collective-permute-start | bytes 1572872 | tf_op jit(solution)/shard_map/ppermute | solution.py:476
  2.8 5.1 %copy-start.2 = (bf16[256,1024]{1,0:T(8,128)(2,1)S(1)}, bf16[256,1024]{1,0:T(8,128)(2,1)}, u32[]{:S(2)}) copy-start(bf16[256,1024]{1,0:T(8,128)(2,1)} %out_own) | copy-start | bytes 1572868
  2.8 15.4 %copy-start.11 = (s32[512]{0:T(512)S(1)}, s32[512]{0:T(512)}, u32[]{:S(2)}) copy-start(s32[512]{0:T(512)} %param.12) | copy-start | bytes 6148
  2.8 27.1 %copy-start.8 = (s32[16]{0:T(128)S(1)}, s32[16]{0:T(128)}, u32[]{:S(2)}) copy-start(s32[16]{0:T(128)} %param.13) | copy-start | bytes 196
  4.8 37.0 %collective-permute-start.9 = (bf16[2,1024,256]{2,1,0:T(8,128)(2,1)S(1)}, bf16[2,1024,256]{2,1,0:T(8,128)(2,1)}, u32[]{:S(2)}, u32[]{:S(2)}) collective-permute-start(bf16[2,1024,256]{2,1,0:T(8,128)(2,1)S(1)} %bitcast.17), channel_id=1, source_target_pairs={{0,1},{1,0},{2,3},{3,2},{4,5},{5,4},{6,7},{7,6},{8,9},{9,8},{10,11... | collective-permute-start | bytes 3145736 | tf_op jit(solution)/shard_map/ppermute | solution.py:476
  4.9 9.5 %collective-permute-start.1 = (bf16[512,256]{1,0:T(8,128)(2,1)S(1)}, bf16[512,256]{1,0:T(8,128)(2,1)S(1)}, u32[]{:S(2)}, u32[]{:S(2)}) collective-permute-start(bf16[512,256]{1,0:T(8,128)(2,1)S(1)} %get-tuple-element.29), channel_id=1, source_target_pairs={{0,2},{2,0},{4,6},{6,4},{8,10},{10,8},{12,14},{14,12},{1,3},{3,1},... | collective-permute-start | bytes 786440 | tf_op jit(solution)/shard_map/ppermute | solution.py:483
  7.8 32.8 %collective-permute-start.8 = (bf16[256,1024]{1,0:T(8,128)(2,1)S(1)}, bf16[256,1024]{1,0:T(8,128)(2,1)}, u32[]{:S(2)}, u32[]{:S(2)}) collective-permute-start(bf16[256,1024]{1,0:T(8,128)(2,1)S(1)} %copy-done.2), channel_id=1, source_target_pairs={{0,1},{1,0},{2,3},{3,2},{4,5},{5,4},{6,7},{7,6},{8,9},{9,8},{10,11... | collective-permute-start | bytes 1572872 | tf_op jit(solution)/shard_map/ppermute | solution.py:476
  7.8 22.9 %collective-permute-start.3 = (bf16[512,256]{1,0:T(8,128)(2,1)S(1)}, bf16[512,256]{1,0:T(8,128)(2,1)S(1)}, u32[]{:S(2)}, u32[]{:S(2)}) collective-permute-start(bf16[512,256]{1,0:T(8,128)(2,1)S(1)} %get-tuple-element.31), channel_id=1, source_target_pairs={{2,6},{4,0},{6,10},{8,4},{10,14},{12,8},{3,7},{5,1},{7,11},{9,5},{... | collective-permute-start | bytes 786440 | tf_op jit(solution)/shard_map/ppermute | solution.py:480
  14.4 16.4 %collective-permute-start.4 = (bf16[512,256]{1,0:T(8,128)(2,1)S(1)}, bf16[512,256]{1,0:T(8,128)(2,1)S(1)}, u32[]{:S(2)}, u32[]{:S(2)}) collective-permute-start(bf16[512,256]{1,0:T(8,128)(2,1)S(1)} %collective-permute-done.1.side_a.center), channel_id=1, source_target_pairs={{0,4},{4,8},{6,2},{8,12},{10,6},{14,10},{1,5},{5,9},{7,3},{9,13},{... | collective-permute-start | bytes 786440 | tf_op jit(solution)/shard_map/ppermute | solution.py:480
  18.1 12.6 %collective-permute-start.2 = (bf16[512,128]{1,0:T(8,128)(2,1)S(1)}, bf16[512,128]{1,0:T(8,128)(2,1)S(1)}, u32[]{:S(2)}, u32[]{:S(2)}) collective-permute-start(bf16[512,128]{1,0:T(8,128)(2,1)S(1)} %get-tuple-element.30), channel_id=1, source_target_pairs={{0,2},{2,0},{4,6},{6,4},{8,10},{10,8},{12,14},{14,12},{1,3},{3,1},... | collective-permute-start | bytes 393224 | tf_op jit(solution)/shard_map/ppermute | solution.py:483
  31.5 10.3 %copy-start.7 = (f32[1024]{0:T(1024)S(1)}, f32[1024]{0:T(1024)}, u32[]{:S(2)}) copy-start(f32[1024]{0:T(1024)} %param.17) | copy-start | bytes 12292
  34.8 5.3 %collective-permute-start.5 = (bf16[512,128]{1,0:T(8,128)(2,1)}, bf16[512,128]{1,0:T(8,128)(2,1)}, u32[]{:S(2)}, u32[]{:S(2)}) collective-permute-start(bf16[512,128]{1,0:T(8,128)(2,1)} %attend.3), channel_id=1, source_target_pairs={{0,2},{2,0},{4,6},{6,4},{8,10},{10,8},{12,14},{14,12},{1,3},{3,1},... | collective-permute-start | bytes 393224 | tf_op jit(solution)/shard_map/ppermute | solution.py:483
  36.3 3.8 %copy-start.9 = (bf16[256,1024]{1,0:T(8,128)(2,1)S(1)}, bf16[256,1024]{1,0:T(8,128)(2,1)}, u32[]{:S(2)}) copy-start(bf16[256,1024]{1,0:T(8,128)(2,1)} %w_own.1) | copy-start | bytes 1572868
  36.3 4.3 %copy-start.5 = (f32[32,256]{1,0:T(8,128)S(1)}, f32[32,256]{1,0:T(8,128)}, u32[]{:S(2)}) copy-start(f32[32,256]{1,0:T(8,128)} %pad_maximum_fusion.taps_own) | copy-start | bytes 98308
  39.2 1.5 %collective-permute-start.6 = (bf16[512,128]{1,0:T(8,128)(2,1)S(1)}, bf16[512,128]{1,0:T(8,128)(2,1)S(1)}, u32[]{:S(2)}, u32[]{:S(2)}) collective-permute-start(bf16[512,128]{1,0:T(8,128)(2,1)S(1)} %attend.2.mine_own), channel_id=1, source_target_pairs={{0,1},{1,0},{2,3},{3,2},{4,5},{5,4},{6,7},{7,6},{8,9},{9,8},{10,11... | collective-permute-start | bytes 393224 | tf_op jit(solution)/shard_map/ppermute | solution.py:476
  40.1 1.7 %collective-permute-start.7 = (bf16[512,128]{1,0:T(8,128)(2,1)}, bf16[512,128]{1,0:T(8,128)(2,1)S(1)}, u32[]{:S(2)}, u32[]{:S(2)}) collective-permute-start(bf16[512,128]{1,0:T(8,128)(2,1)} %collective-permute-done.5.pair_own), channel_id=1, source_target_pairs={{0,1},{1,0},{2,3},{3,2},{4,5},{5,4},{6,7},{7,6},{8,9},{9,8},{10,11... | collective-permute-start | bytes 393224 | tf_op jit(solution)/shard_map/ppermute | solution.py:476
  40.1 12.4 %collective-permute-start.15 = (bf16[256,1024]{1,0:T(8,128)(2,1)S(1)}, bf16[256,1024]{1,0:T(8,128)(2,1)S(1)}, u32[]{:S(2)}, u32[]{:S(2)}) collective-permute-start(bf16[256,1024]{1,0:T(8,128)(2,1)S(1)} %copy-done.9), channel_id=1, source_target_pairs={{0,1},{1,0},{2,3},{3,2},{4,5},{5,4},{6,7},{7,6},{8,9},{9,8},{10,11... | collective-permute-start | bytes 1572872 | tf_op jit(solution)/shard_map/ppermute | solution.py:476
  40.6 4.9 %collective-permute-start.10 = (f32[32,256]{1,0:T(8,128)S(1)}, f32[32,256]{1,0:T(8,128)S(1)}, u32[]{:S(2)}, u32[]{:S(2)}) collective-permute-start(f32[32,256]{1,0:T(8,128)S(1)} %copy-done.5), channel_id=1, source_target_pairs={{0,1},{1,0},{2,3},{3,2},{4,5},{5,4},{6,7},{7,6},{8,9},{9,8},{10,11... | collective-permute-start | bytes 98312 | tf_op jit(solution)/shard_map/ppermute | solution.py:476
  44.9 6.3 %collective-permute-start.12 = (bf16[64,512]{1,0:T(8,128)(2,1)S(1)}, bf16[64,512]{1,0:T(8,128)(2,1)S(1)}, u32[]{:S(2)}, u32[]{:S(2)}) collective-permute-start(bf16[64,512]{1,0:T(8,128)(2,1)S(1)} %get-tuple-element.47), channel_id=1, source_target_pairs={{2,1},{4,3},{6,5},{8,7},{10,9},{12,11},{14,13},{1,2},{3,4},{5,6},{... | collective-permute-start | bytes 196616 | tf_op jit(solution)/shard_map/ppermute | solution.py:532
  49.1 4.3 %collective-permute-start.11 = (bf16[256,512]{1,0:T(8,128)(2,1)S(1)}, bf16[256,512]{1,0:T(8,128)(2,1)S(1)}, u32[]{:S(2)}, u32[]{:S(2)}) collective-permute-start(bf16[256,512]{1,0:T(8,128)(2,1)S(1)} %convolve.1.act_ref), channel_id=1, source_target_pairs={{0,1},{1,0},{2,3},{3,2},{4,5},{5,4},{6,7},{7,6},{8,9},{9,8},{10,11... | collective-permute-start | bytes 786440 | tf_op jit(solution)/shard_map/ppermute | solution.py:476
  51.1 2.4 %collective-permute-start.14 = (bf16[256,512]{1,0:T(8,128)(2,1)S(1)}, bf16[256,512]{1,0:T(8,128)(2,1)S(1)}, u32[]{:S(2)}, u32[]{:S(2)}) collective-permute-start(bf16[256,512]{1,0:T(8,128)(2,1)S(1)} %get-tuple-element.48), channel_id=1, source_target_pairs={{0,1},{1,0},{2,3},{3,2},{4,5},{5,4},{6,7},{7,6},{8,9},{9,8},{10,11... | collective-permute-start | bytes 786440 | tf_op jit(solution)/shard_map/ppermute | solution.py:476
  52.0 1.4 %collective-permute-start.13 = (bf16[16,512]{1,0:T(8,128)(2,1)S(1)}, bf16[16,512]{1,0:T(8,128)(2,1)S(1)}, u32[]{:S(2)}, u32[]{:S(2)}) collective-permute-start(bf16[16,512]{1,0:T(8,128)(2,1)S(1)} %rim.1.rim_ref), channel_id=1, source_target_pairs={{0,1},{1,0},{2,3},{3,2},{4,5},{5,4},{6,7},{7,6},{8,9},{9,8},{10,11... | collective-permute-start | bytes 49160 | tf_op jit(solution)/shard_map/ppermute | solution.py:476
  (5 other events, 8.1 us)

commit v13 on v12

--- a/solution.py
+++ b/solution.py
@@ -498,7 +498,6 @@
     pair = exchange(passed)
     far_pair = shift(keep, 2)
     pair_query = exchange(send)
-    far_own = shift(pair, -2)
 
     segment_ids, _ = lax.optimization_barrier((segment_ids, passed))
     ids = jnp.arange(utt_valid.shape[0], dtype=jnp.int32)
@@ -506,6 +505,8 @@
     counts = lax.all_to_all(
         jnp.broadcast_to(counts[None, :], (blocks, counts.shape[0])), "tm", 0, 0
     )
+    pair, counts = lax.optimization_barrier((pair, counts))
+    far_own = shift(pair, -2)
     taps = jnp.concatenate([depthwise, mid_gain[None, :]], axis=0)
     out_weight, pointwise, taps, keep = lax.optimization_barrier(
         (out_weight, pointwise, taps, keep)
@@ -516,12 +517,13 @@
     taps, pointwise_out, runs = lax.optimization_barrier((taps, pointwise_out, runs))
     taps_other = swap(taps)
     pointwise_out_other = swap(pointwise_out)
-    pair, pair_query, far_pair, far_own, runs, pair_runs = lax.optimization_barrier(
-        (pair, pair_query, far_pair, far_own, runs, pair_runs)
+    pair, pair_query, far_pair, runs, pair_runs = lax.optimization_barrier(
+        (pair, pair_query, far_pair, runs, pair_runs)
     )
     pair_context = attend(column.reshape(1), pair_query, pair, held, far_pair, pair_runs)
     pair_context = exchange(pair_context)
     context = attend((1 - column).reshape(1), held, held, pair, far_own, runs)
+    context, pair_context = lax.optimization_barrier((context, pair_context))
     contexts = (context, pair_context, swap(context), swap(pair_context))
     glu, edge, mid_keep, mid_send = gated(
         meta, contexts, frames, other, out_weight, out_other, conv_gain,

time: 55.4 us -> 52.9 us (0.955)
  blocking collectives: 11.6 us -> 0 us
  starting transfers between devices: 13.1 us -> 20.4 us
  Pallas kernels: 19.1 us -> 21.8 us
    all_to_all x1 -> x0, blocking collectives: 11.6 us -> none  [local(): lax.all_to_all(jnp.broadcast_to(counts[None, :], (blocks, counts.shape[0]...]
    all_to_all x0 -> x1, starting transfers between devices: none -> 6.65 us  [local(): lax.all_to_all(jnp.broadcast_to(counts[None, :], (blocks, counts.shape[0]...]
    ppermute x3, waiting for transfers between devices: 6.11 us -> 1.43 us  [exchange(): return lax.ppermute(value, 'tm', [(i, i ^ 1) for i in range(blocks)])]
    all_to_all x0 -> x1, waiting for transfers between devices: none -> 4.42 us  [local(): lax.all_to_all(jnp.broadcast_to(counts[None, :], (blocks, counts.shape[0]...]
    pallas_call x2, Pallas kernels: 6.14 us -> 8.18 us  [attend(): pl.pallas_call(attend_kernel, in_specs=[pl.BlockSpec(memory_space=pltpu.S...]
    unnamed x27 -> x25, local copies, waits for them, and re-layouts: 3.18 us -> 2.12 us
    ppermute x3, starting transfers between devices: 3.58 us -> 4.56 us  [exchange(): return lax.ppermute(value, 'tm', [(i, i ^ 1) for i in range(blocks)])]
    pallas_call x1, Pallas kernels: 1.96 us -> 2.67 us  [project(): pl.pallas_call(qkv_kernel, in_specs=[pl.BlockSpec(memory_space=pltpu.SMEM...]
  transfers between devices with their start and end apart: 16 -> 17, of which waited for: 3 -> 4; matrix products, arithmetic and copies ran while one was open for 4% -> 6% of each run, Pallas kernels for 28% -> 33%
where the time goes in v13:
time: 52.9 us; the launch traced here: 52.6 us
  Pallas kernels  21.8 us (41%)
  starting transfers between devices  20.4 us (39%)
  waiting for transfers between devices  6.67 us (13%)
  local copies, waits for them, and re-layouts  2.71 us (5%)
  other arithmetic  0.82 us (2%)
    pallas_call x2, Pallas kernels, attend(): pl.pallas_call(attend_kernel, in_specs=[pl.BlockSpec(memory_space=pltpu.S...  8.18 us
    all_to_all x1, starting transfers between devices, local(): lax.all_to_all(jnp.broadcast_to(counts[None, :], (blocks, counts.shape[0]...  6.65 us
    ppermute x3, starting transfers between devices, exchange(): return lax.ppermute(value, 'tm', [(i, i ^ 1) for i in range(blocks)])  4.56 us
    all_to_all x1, waiting for transfers between devices, local(): lax.all_to_all(jnp.broadcast_to(counts[None, :], (blocks, counts.shape[0]...  4.42 us
    ppermute x2, starting transfers between devices, shift(): return lax.ppermute(value, 'tm', [p for p in pairs if 0 <= p[1] < blocks])  4.32 us
    ppermute x10, starting transfers between devices, swap(): return lax.ppermute(value, 'head', [(0, 1), (1, 0)])  4.18 us
    pallas_call x1, Pallas kernels, convolve(): pl.pallas_call(conv_kernel, in_specs=[pl.BlockSpec(memory_space=pltpu.SME...  3.59 us
    pallas_call x1, Pallas kernels, gated(): pl.pallas_call(gate_kernel, in_specs=[pl.BlockSpec(memory_space=pltpu.SME...  3.08 us
  transfers between devices with their start and end apart: 17, of which 4 were waited for; matrix products, arithmetic and copies ran while one was open for 6% of the time, Pallas kernels for 33%

profile of v13, /device:TPU:0, one launch (start us, length us, event | category | flops | bytes accessed | tf_op | source)
XLA Modules:
  0.0 52.6 jit_solution(4511649033938087501)
XLA Ops:
  0.0 0.5 %collective-permute-start = (bf16[512,512]{1,0:T(8,128)(2,1)}, bf16[512,512]{1,0:T(8,128)(2,1)S(1)}, u32[]{:S(2)}, u32[]{:S(2)}) collective-permute-start(bf16[512,512]{1,0:T(8,128)(2,1)} %x_own.1), channel_id=1, source_target_pairs={{0,1},{1,0},{2,3},{3,2},{4,5},{5,4},{6,7},{7,6},{8,9},{9,8},{10,11... | collective-permute-start | bytes 1572872 | tf_op jit(solution)/shard_map/ppermute | solution.py:476
  0.5 1.5 %copy.16 = bf16[1024,2,256]{2,0,1:T(8,128)(2,1)S(1)} copy(bf16[1024,2,256]{2,1,0:T(2,128)(2,1)} %param.18) | data formatting | bytes 2097152 | tf_op args[7]
  2.1 0.6 %pad_maximum_fusion.taps_own = f32[32,256]{1,0:T(8,128)} fusion(f32[1,256]{1,0:T(1,128)S(1)} %bitcast.24, f32[31,256]{1,0:T(8,128)S(1)} %copy-done.9), kind=kLoop, calls=%fused_computation.1 | loop fusion | flops 8192 | bytes 65536 | tf_op jit(solution)/shard_map/concatenate | solution.py:510
  2.8 2.7 %project.1 = (bf16[512,256]{1,0:T(8,128)(2,1)}, bf16[512,384]{1,0:T(8,128)(2,1)S(1)}, bf16[512,128]{1,0:T(8,128)(2,1)S(1)}, bf16[512,256]{1,0:T(8,128)(2,1)S(1)}) custom-call(s32[4]{0:T(128)S(1)} %pad_add_fusion.meta, bf16[512,512]{1,0:T(8,128)(2,1)S(1)} %copy-done, bf16[512,512]{1,0:T(8,128)(2,1)S(1)} %collective-permute-done.other_ref.x_other, ...), custom_call_target="tpu_custom_call" | custom-call | tf_op jit(solution)/shard_map/project/pallas_call | solution.py:85
  5.5 0.6 %copy-done.8 = bf16[512,128]{1,0:T(8,128)(2,1)} copy-done((bf16[512,128]{1,0:T(8,128)(2,1)}, bf16[512,128]{1,0:T(8,128)(2,1)S(1)}, u32[]{:S(2)}) %copy-start.8) | copy-done | bytes 131096
  6.1 2.5 %collective-permute-start.1 = (bf16[512,256]{1,0:T(8,128)(2,1)S(1)}, bf16[512,256]{1,0:T(8,128)(2,1)S(1)}, u32[]{:S(2)}, u32[]{:S(2)}) collective-permute-start(bf16[512,256]{1,0:T(8,128)(2,1)S(1)} %get-tuple-element.32), channel_id=1, source_target_pairs={{0,2},{2,0},{4,6},{6,4},{8,10},{10,8},{12,14},{14,12},{1,3},{3,1},... | collective-permute-start | bytes 786440 | tf_op jit(solution)/shard_map/ppermute | solution.py:483
  8.8 1.3 %collective-permute-start.3 = (bf16[512,256]{1,0:T(8,128)(2,1)}, bf16[512,256]{1,0:T(8,128)(2,1)}, u32[]{:S(2)}, u32[]{:S(2)}) collective-permute-start(bf16[512,256]{1,0:T(8,128)(2,1)} %get-tuple-element.36), channel_id=1, source_target_pairs={{2,6},{4,0},{6,10},{8,4},{10,14},{12,8},{3,7},{5,1},{7,11},{9,5},{... | collective-permute-start | bytes 786440 | tf_op jit(solution)/shard_map/ppermute | solution.py:480
  10.2 0.6 %broadcast_in_dim.4 = s32[8,1,16]{2,1,0:T(1,128)} broadcast(s32[16]{0:T(128)S(1)} %convert_reduce_fusion), dimensions={2} | broadcast | bytes 576 | tf_op jit(solution)/shard_map/broadcast_in_dim | solution.py:506
  10.8 6.6 %all-to-all-start = ((s32[8,1,16]{2,1,0:T(1,128)}), s32[8,1,16]{2,1,0:T(1,128)S(1)}, u32[]{:S(2)}, u32[]{:S(2)}) async-start(s32[8,1,16]{2,1,0:T(1,128)} %broadcast_in_dim.4), calls=%async_computation | async-start | bytes 8192 | tf_op jit(solution)/shard_map/all_to_all | solution.py:505
  17.5 2.0 %collective-permute-start.2 = (bf16[512,128]{1,0:T(8,128)(2,1)}, bf16[512,128]{1,0:T(8,128)(2,1)}, u32[]{:S(2)}, u32[]{:S(2)}) collective-permute-start(bf16[512,128]{1,0:T(8,128)(2,1)} %copy-done.8), channel_id=1, source_target_pairs={{0,2},{2,0},{4,6},{6,4},{8,10},{10,8},{12,14},{14,12},{1,3},{3,1},... | collective-permute-start | bytes 393224 | tf_op jit(solution)/shard_map/ppermute | solution.py:483
  19.5 4.4 %all-to-all-done = s32[8,1,16]{2,1,0:T(1,128)S(1)} async-done(((s32[8,1,16]{2,1,0:T(1,128)}), s32[8,1,16]{2,1,0:T(1,128)S(1)}, u32[]{:S(2)}, u32[]{:S(2)}) %all-to-all-start) | async-done | bytes 544 | tf_op jit(solution)/shard_map/all_to_all | solution.py:505
  23.9 3.0 %collective-permute-start.4 = (bf16[512,256]{1,0:T(8,128)(2,1)S(1)}, bf16[512,256]{1,0:T(8,128)(2,1)}, u32[]{:S(2)}, u32[]{:S(2)}) collective-permute-start(bf16[512,256]{1,0:T(8,128)(2,1)S(1)} %collective-permute-done.1.side_a.center), channel_id=1, source_target_pairs={{0,4},{4,8},{6,2},{8,12},{10,6},{14,10},{1,5},{5,9},{7,3},{9,13},{... | collective-permute-start | bytes 786440 | tf_op jit(solution)/shard_map/ppermute | solution.py:480
  27.0 0.8 %bounds.1 = (s32[512,128]{1,0:T(8,128)S(1)}, s32[512,128]{1,0:T(8,128)S(1)}) custom-call(s32[4]{0:T(128)S(1)} %pad_add_fusion.meta, s32[8,16]{1,0:T(8,128)S(1)} %bitcast.20, s32[1,16]{1,0:T(1,128)S(1)} %bitcast.23), custom_call_target="tpu_custom_call" | custom-call | tf_op jit(solution)/shard_map/bounds/pallas_call | solution.py:128
  27.9 4.4 %attend.3 = bf16[512,128]{1,0:T(8,128)(2,1)} custom-call(s32[1]{0:T(128)} %bitcast.1.a_high, bf16[512,128]{1,0:T(8,128)(2,1)} %collective-permute-done.2.query, bf16[512,256]{1,0:T(8,128)(2,1)S(1)} %collective-permute-done.1.side_a.center, bf16[512,384]{1,0:T(8,128)(2,1)S(1)} %get-tuple-element.31.query.center.side_a, ...), custom_call_target="tpu_custom_call" | custom-call | bytes 11070000 | tf_op jit(solution)/shard_map/attend/pallas_call | solution.py:200
  32.2 3.8 %attend.2.mine_own = bf16[512,128]{1,0:T(8,128)(2,1)S(1)} custom-call(s32[1]{0:T(128)} %bitcast.4.a_high, bf16[512,384]{1,0:T(8,128)(2,1)S(1)} %get-tuple-element.31.query.center.side_a, bf16[512,384]{1,0:T(8,128)(2,1)S(1)} %get-tuple-element.31.query.center.side_a, bf16[512,256]{1,0:T(8,128)(2,1)S(1)} %collective-permute-done.1.side_a.center, ...), custom_call_target="tpu_custom_call" | custom-call | bytes 11070000 | tf_op jit(solution)/shard_map/attend/pallas_call | solution.py:200
  36.1 1.4 %collective-permute-done.5.pair_own = bf16[512,128]{1,0:T(8,128)(2,1)} collective-permute-done((bf16[512,128]{1,0:T(8,128)(2,1)}, bf16[512,128]{1,0:T(8,128)(2,1)}, u32[]{:S(2)}, u32[]{:S(2)}) %collective-permute-start.5) | collective-permute-done | bytes 131104 | tf_op jit(solution)/shard_map/ppermute | solution.py:483
  37.5 0.5 collective-permute-start.7
  39.3 3.1 %gated.1 = (bf16[272,512]{1,0:T(8,128)(2,1)S(1)}, bf16[64,512]{1,0:T(8,128)(2,1)S(1)}, bf16[256,512]{1,0:T(8,128)(2,1)S(1)}, bf16[256,512]{1,0:T(8,128)(2,1)S(1)}) custom-call(s32[4]{0:T(128)S(1)} %pad_add_fusion.meta, bf16[512,128]{1,0:T(8,128)(2,1)S(1)} %attend.2.mine_own, bf16[512,128]{1,0:T(8,128)(2,1)} %collective-permute-done.5.pair_own, ...), custom_call_target="tpu_custom_call" | custom-call | bytes 11070000 | tf_op jit(solution)/shard_map/gated/pallas_call | solution.py:290
  42.4 0.7 %collective-permute-start.12 = (bf16[64,512]{1,0:T(8,128)(2,1)S(1)}, bf16[64,512]{1,0:T(8,128)(2,1)S(1)}, u32[]{:S(2)}, u32[]{:S(2)}) collective-permute-start(bf16[64,512]{1,0:T(8,128)(2,1)S(1)} %get-tuple-element.53), channel_id=1, source_target_pairs={{2,1},{4,3},{6,5},{8,7},{10,9},{12,11},{14,13},{1,2},{3,4},{5,6},{... | collective-permute-start | bytes 196616 | tf_op jit(solution)/shard_map/ppermute | solution.py:534
  43.1 3.6 %convolve.1.act_ref = bf16[256,512]{1,0:T(8,128)(2,1)S(1)} custom-call(s32[4]{0:T(128)S(1)} %pad_add_fusion.meta, bf16[272,512]{1,0:T(8,128)(2,1)S(1)} %get-tuple-element.51.glu_ref, s32[512,128]{1,0:T(8,128)S(1)} %get-tuple-element.43.run_ref, f32[32,256]{1,0:T(8,128)S(1)} %copy-done.3, f32[32,256]{1,0:T(8,128)S(1)} %collective-permute-done.10.taps_other), custom_call_target="tpu_custom_call" | custom-call | flops 3449999872 | tf_op jit(solution)/shard_map/convolve/pallas_call | solution.py:363
  46.7 1.8 %collective-permute-start.11 = (bf16[256,512]{1,0:T(8,128)(2,1)S(1)}, bf16[256,512]{1,0:T(8,128)(2,1)S(1)}, u32[]{:S(2)}, u32[]{:S(2)}) collective-permute-start(bf16[256,512]{1,0:T(8,128)(2,1)S(1)} %convolve.1.act_ref), channel_id=1, source_target_pairs={{0,1},{1,0},{2,3},{3,2},{4,5},{5,4},{6,7},{7,6},{8,9},{9,8},{10,11... | collective-permute-start | bytes 786440 | tf_op jit(solution)/shard_map/ppermute | solution.py:476
  48.6 0.9 %rim.1.rim_ref = bf16[16,512]{1,0:T(8,128)(2,1)S(1)} custom-call(s32[4]{0:T(128)S(1)} %pad_add_fusion.meta, bf16[272,512]{1,0:T(8,128)(2,1)S(1)} %get-tuple-element.51.glu_ref, bf16[64,512]{1,0:T(8,128)(2,1)S(1)} %collective-permute-done.12.edge_ref, s32[512,128]{1,0:T(8,128)S(1)} %get-tuple-element.43.run_ref, f32[32,256]{1,0:T(8,128)S(1)} %copy-done.3, ...), custom_call_target="tpu_custom_call" | custom-call | flops 1150000000 | tf_op jit(solution)/shard_map/rim/pallas_call | solution.py:399
  50.0 0.9 %finish_own.1.done_ref = bf16[256,512]{1,0:T(8,128)(2,1)S(1)} custom-call(s32[4]{0:T(128)S(1)} %pad_add_fusion.meta, bf16[256,512]{1,0:T(8,128)(2,1)S(1)} %convolve.1.act_ref, bf16[16,512]{1,0:T(8,128)(2,1)S(1)} %rim.1.rim_ref, bf16[256,512]{1,0:T(8,128)(2,1)S(1)} %get-tuple-element.56.mid_ref, bf16[256,1024]{1,0:T(8,128)(2,1)S(1)} %copy-done.7, ...), custom_call_target="tpu_custom_call" | custom-call | flops 1380000000 | tf_op jit(solution)/shard_map/finish_own/pallas_call | solution.py:447
  50.9 1.7 %finish.1 = bf16[512,512]{1,0:T(8,128)(2,1)} custom-call(s32[4]{0:T(128)S(1)} %pad_add_fusion.meta, bf16[256,512]{1,0:T(8,128)(2,1)S(1)} %collective-permute-done.11.act_ref, bf16[16,512]{1,0:T(8,128)(2,1)S(1)} %collective-permute-done.13.rim_ref, bf16[256,512]{1,0:T(8,128)(2,1)S(1)} %collective-permute-done.14.mid_ref, bf16[256,1024]{1,0:T(8,128)(2,1)S(1)} %copy-done.7, ...), custom_call_target="tpu_custom_call" | custom-call | flops 1380000000 | tf_op jit(solution)/shard_map/finish/pallas_call | solution.py:447
  (48 shorter events, 2.4 us)
Async XLA Ops:
  0.0 2.7 %copy-start = (bf16[512,512]{1,0:T(8,128)(2,1)S(1)}, bf16[512,512]{1,0:T(8,128)(2,1)}, u32[]{:S(2)}) copy-start(bf16[512,512]{1,0:T(8,128)(2,1)} %x_own.1) | copy-start | bytes 1572868
  0.0 2.7 %collective-permute-start = (bf16[512,512]{1,0:T(8,128)(2,1)}, bf16[512,512]{1,0:T(8,128)(2,1)S(1)}, u32[]{:S(2)}, u32[]{:S(2)}) collective-permute-start(bf16[512,512]{1,0:T(8,128)(2,1)} %x_own.1), channel_id=1, source_target_pairs={{0,1},{1,0},{2,3},{3,2},{4,5},{5,4},{6,7},{7,6},{8,9},{9,8},{10,11... | collective-permute-start | bytes 1572872 | tf_op jit(solution)/shard_map/ppermute | solution.py:476
  2.8 5.9 %copy-start.2 = (bf16[256,1024]{1,0:T(8,128)(2,1)S(1)}, bf16[256,1024]{1,0:T(8,128)(2,1)}, u32[]{:S(2)}) copy-start(bf16[256,1024]{1,0:T(8,128)(2,1)} %out_own) | copy-start | bytes 1572868
  2.8 7.3 %copy-start.10 = (s32[512]{0:T(512)S(1)}, s32[512]{0:T(512)}, u32[]{:S(2)}) copy-start(s32[512]{0:T(512)} %param.12) | copy-start | bytes 6148
  2.8 24.2 %copy-start.6 = (s32[16]{0:T(128)S(1)}, s32[16]{0:T(128)}, u32[]{:S(2)}) copy-start(s32[16]{0:T(128)} %param.13) | copy-start | bytes 196
  5.5 33.9 %collective-permute-start.9 = (bf16[2,1024,256]{2,1,0:T(8,128)(2,1)S(1)}, bf16[2,1024,256]{2,1,0:T(8,128)(2,1)}, u32[]{:S(2)}, u32[]{:S(2)}) collective-permute-start(bf16[2,1024,256]{2,1,0:T(8,128)(2,1)S(1)} %bitcast.17), channel_id=1, source_target_pairs={{0,1},{1,0},{2,3},{3,2},{4,5},{5,4},{6,7},{7,6},{8,9},{9,8},{10,11... | collective-permute-start | bytes 3145736 | tf_op jit(solution)/shard_map/ppermute | solution.py:476
  6.1 17.8 %collective-permute-start.1 = (bf16[512,256]{1,0:T(8,128)(2,1)S(1)}, bf16[512,256]{1,0:T(8,128)(2,1)S(1)}, u32[]{:S(2)}, u32[]{:S(2)}) collective-permute-start(bf16[512,256]{1,0:T(8,128)(2,1)S(1)} %get-tuple-element.32), channel_id=1, source_target_pairs={{0,2},{2,0},{4,6},{6,4},{8,10},{10,8},{12,14},{14,12},{1,3},{3,1},... | collective-permute-start | bytes 786440 | tf_op jit(solution)/shard_map/ppermute | solution.py:483
  8.6 29.4 %collective-permute-start.8 = (bf16[256,1024]{1,0:T(8,128)(2,1)S(1)}, bf16[256,1024]{1,0:T(8,128)(2,1)}, u32[]{:S(2)}, u32[]{:S(2)}) collective-permute-start(bf16[256,1024]{1,0:T(8,128)(2,1)S(1)} %copy-done.2), channel_id=1, source_target_pairs={{0,1},{1,0},{2,3},{3,2},{4,5},{5,4},{6,7},{7,6},{8,9},{9,8},{10,11... | collective-permute-start | bytes 1572872 | tf_op jit(solution)/shard_map/ppermute | solution.py:476
  8.8 19.0 %collective-permute-start.3 = (bf16[512,256]{1,0:T(8,128)(2,1)}, bf16[512,256]{1,0:T(8,128)(2,1)}, u32[]{:S(2)}, u32[]{:S(2)}) collective-permute-start(bf16[512,256]{1,0:T(8,128)(2,1)} %get-tuple-element.36), channel_id=1, source_target_pairs={{2,6},{4,0},{6,10},{8,4},{10,14},{12,8},{3,7},{5,1},{7,11},{9,5},{... | collective-permute-start | bytes 786440 | tf_op jit(solution)/shard_map/ppermute | solution.py:480
  10.8 13.1 %all-to-all-start = ((s32[8,1,16]{2,1,0:T(1,128)}), s32[8,1,16]{2,1,0:T(1,128)S(1)}, u32[]{:S(2)}, u32[]{:S(2)}) async-start(s32[8,1,16]{2,1,0:T(1,128)} %broadcast_in_dim.4), calls=%async_computation | async-start | bytes 8192 | tf_op jit(solution)/shard_map/all_to_all | solution.py:505
  17.5 10.3 %collective-permute-start.2 = (bf16[512,128]{1,0:T(8,128)(2,1)}, bf16[512,128]{1,0:T(8,128)(2,1)}, u32[]{:S(2)}, u32[]{:S(2)}) collective-permute-start(bf16[512,128]{1,0:T(8,128)(2,1)} %copy-done.8), channel_id=1, source_target_pairs={{0,2},{2,0},{4,6},{6,4},{8,10},{10,8},{12,14},{14,12},{1,3},{3,1},... | collective-permute-start | bytes 393224 | tf_op jit(solution)/shard_map/ppermute | solution.py:483
  23.9 8.3 %collective-permute-start.4 = (bf16[512,256]{1,0:T(8,128)(2,1)S(1)}, bf16[512,256]{1,0:T(8,128)(2,1)}, u32[]{:S(2)}, u32[]{:S(2)}) collective-permute-start(bf16[512,256]{1,0:T(8,128)(2,1)S(1)} %collective-permute-done.1.side_a.center), channel_id=1, source_target_pairs={{0,4},{4,8},{6,2},{8,12},{10,6},{14,10},{1,5},{5,9},{7,3},{9,13},{... | collective-permute-start | bytes 786440 | tf_op jit(solution)/shard_map/ppermute | solution.py:480
  27.8 11.5 %copy-start.5 = (f32[1024]{0:T(1024)S(1)}, f32[1024]{0:T(1024)}, u32[]{:S(2)}) copy-start(f32[1024]{0:T(1024)} %param.17) | copy-start | bytes 12292
  32.2 5.3 %collective-permute-start.5 = (bf16[512,128]{1,0:T(8,128)(2,1)}, bf16[512,128]{1,0:T(8,128)(2,1)}, u32[]{:S(2)}, u32[]{:S(2)}) collective-permute-start(bf16[512,128]{1,0:T(8,128)(2,1)} %attend.3), channel_id=1, source_target_pairs={{0,2},{2,0},{4,6},{6,4},{8,10},{10,8},{12,14},{14,12},{1,3},{3,1},... | collective-permute-start | bytes 393224 | tf_op jit(solution)/shard_map/ppermute | solution.py:483
  32.2 5.8 %copy-start.7 = (bf16[256,1024]{1,0:T(8,128)(2,1)S(1)}, bf16[256,1024]{1,0:T(8,128)(2,1)}, u32[]{:S(2)}) copy-start(bf16[256,1024]{1,0:T(8,128)(2,1)} %w_own.1) | copy-start | bytes 1572868
  32.2 5.8 %copy-start.3 = (f32[32,256]{1,0:T(8,128)S(1)}, f32[32,256]{1,0:T(8,128)}, u32[]{:S(2)}) copy-start(f32[32,256]{1,0:T(8,128)} %pad_maximum_fusion.taps_own) | copy-start | bytes 98308
  37.5 1.5 %collective-permute-start.6 = (bf16[512,128]{1,0:T(8,128)(2,1)S(1)}, bf16[512,128]{1,0:T(8,128)(2,1)S(1)}, u32[]{:S(2)}, u32[]{:S(2)}) collective-permute-start(bf16[512,128]{1,0:T(8,128)(2,1)S(1)} %attend.2.mine_own), channel_id=1, source_target_pairs={{0,1},{1,0},{2,3},{3,2},{4,5},{5,4},{6,7},{7,6},{8,9},{9,8},{10,11... | collective-permute-start | bytes 393224 | tf_op jit(solution)/shard_map/ppermute | solution.py:476
  37.5 1.8 %collective-permute-start.7 = (bf16[512,128]{1,0:T(8,128)(2,1)}, bf16[512,128]{1,0:T(8,128)(2,1)S(1)}, u32[]{:S(2)}, u32[]{:S(2)}) collective-permute-start(bf16[512,128]{1,0:T(8,128)(2,1)} %collective-permute-done.5.pair_own), channel_id=1, source_target_pairs={{0,1},{1,0},{2,3},{3,2},{4,5},{5,4},{6,7},{7,6},{8,9},{9,8},{10,11... | collective-permute-start | bytes 393224 | tf_op jit(solution)/shard_map/ppermute | solution.py:476
  38.0 12.0 %collective-permute-start.15 = (bf16[256,1024]{1,0:T(8,128)(2,1)S(1)}, bf16[256,1024]{1,0:T(8,128)(2,1)S(1)}, u32[]{:S(2)}, u32[]{:S(2)}) collective-permute-start(bf16[256,1024]{1,0:T(8,128)(2,1)S(1)} %copy-done.7), channel_id=1, source_target_pairs={{0,1},{1,0},{2,3},{3,2},{4,5},{5,4},{6,7},{7,6},{8,9},{9,8},{10,11... | collective-permute-start | bytes 1572872 | tf_op jit(solution)/shard_map/ppermute | solution.py:476
  38.0 5.1 %collective-permute-start.10 = (f32[32,256]{1,0:T(8,128)S(1)}, f32[32,256]{1,0:T(8,128)S(1)}, u32[]{:S(2)}, u32[]{:S(2)}) collective-permute-start(f32[32,256]{1,0:T(8,128)S(1)} %copy-done.3), channel_id=1, source_target_pairs={{0,1},{1,0},{2,3},{3,2},{4,5},{5,4},{6,7},{7,6},{8,9},{9,8},{10,11... | collective-permute-start | bytes 98312 | tf_op jit(solution)/shard_map/ppermute | solution.py:476
  42.4 6.2 %collective-permute-start.12 = (bf16[64,512]{1,0:T(8,128)(2,1)S(1)}, bf16[64,512]{1,0:T(8,128)(2,1)S(1)}, u32[]{:S(2)}, u32[]{:S(2)}) collective-permute-start(bf16[64,512]{1,0:T(8,128)(2,1)S(1)} %get-tuple-element.53), channel_id=1, source_target_pairs={{2,1},{4,3},{6,5},{8,7},{10,9},{12,11},{14,13},{1,2},{3,4},{5,6},{... | collective-permute-start | bytes 196616 | tf_op jit(solution)/shard_map/ppermute | solution.py:534
  46.7 4.2 %collective-permute-start.11 = (bf16[256,512]{1,0:T(8,128)(2,1)S(1)}, bf16[256,512]{1,0:T(8,128)(2,1)S(1)}, u32[]{:S(2)}, u32[]{:S(2)}) collective-permute-start(bf16[256,512]{1,0:T(8,128)(2,1)S(1)} %convolve.1.act_ref), channel_id=1, source_target_pairs={{0,1},{1,0},{2,3},{3,2},{4,5},{5,4},{6,7},{7,6},{8,9},{9,8},{10,11... | collective-permute-start | bytes 786440 | tf_op jit(solution)/shard_map/ppermute | solution.py:476
  48.5 2.4 %collective-permute-start.14 = (bf16[256,512]{1,0:T(8,128)(2,1)S(1)}, bf16[256,512]{1,0:T(8,128)(2,1)S(1)}, u32[]{:S(2)}, u32[]{:S(2)}) collective-permute-start(bf16[256,512]{1,0:T(8,128)(2,1)S(1)} %get-tuple-element.54), channel_id=1, source_target_pairs={{0,1},{1,0},{2,3},{3,2},{4,5},{5,4},{6,7},{7,6},{8,9},{9,8},{10,11... | collective-permute-start | bytes 786440 | tf_op jit(solution)/shard_map/ppermute | solution.py:476
  49.5 1.4 %collective-permute-start.13 = (bf16[16,512]{1,0:T(8,128)(2,1)S(1)}, bf16[16,512]{1,0:T(8,128)(2,1)S(1)}, u32[]{:S(2)}, u32[]{:S(2)}) collective-permute-start(bf16[16,512]{1,0:T(8,128)(2,1)S(1)} %rim.1.rim_ref), channel_id=1, source_target_pairs={{0,1},{1,0},{2,3},{3,2},{4,5},{5,4},{6,7},{7,6},{8,9},{9,8},{10,11... | collective-permute-start | bytes 49160 | tf_op jit(solution)/shard_map/ppermute | solution.py:476
  (5 other events, 9.8 us)

commit v14 on v11

--- a/solution.py
+++ b/solution.py
@@ -134,7 +134,8 @@
     )(meta, counts, valid.reshape(1, -1))
 
 
-def attend_kernel(a_high, query, center, side_a, side_b, run_ref, out_ref):
+def attend_kernel(a_high, query, center, side_a, side_b, run_ref, *refs):
+    out_ref = refs[-1]
     rows = center.shape[0]
     width = center.shape[1] // 3
     q_cols = slice(query.shape[1] - width, query.shape[1])
@@ -193,18 +194,19 @@
         run(side_a, side_b)
 
 
-def attend(a_high, query, center, side_a, side_b, runs):
+def attend(a_high, query, center, side_a, side_b, runs, held):
+    anywhere = [pl.BlockSpec(memory_space=pl.ANY)] * len(held)
     rows, width = side_b.shape[0], side_b.shape[1] // 2
     vmem = pl.BlockSpec(memory_space=pltpu.VMEM)
     return pl.pallas_call(
         attend_kernel,
-        in_specs=[pl.BlockSpec(memory_space=pltpu.SMEM)] + [vmem] * 5,
+        in_specs=[pl.BlockSpec(memory_space=pltpu.SMEM)] + [vmem] * 5 + anywhere,
         out_specs=vmem,
         out_shape=jax.ShapeDtypeStruct((rows, width), BF16),
         compiler_params=pltpu.CompilerParams(vmem_limit_bytes=VMEM_LIMIT),
         cost_estimate=traffic(3),
         name="attend",
-    )(a_high, query, center, side_a, side_b, runs)
+    )(a_high, query, center, side_a, side_b, runs, *held)
 
 
 def gate_kernel(
@@ -517,9 +519,9 @@
     pair, far_pair, runs, pair_runs = lax.optimization_barrier(
         (pair, far_pair, runs, pair_runs)
     )
-    pair_context = attend(column.reshape(1), pair, pair, held, far_pair, pair_runs)
+    pair_context = attend(column.reshape(1), pair, pair, held, far_pair, pair_runs, ())
     pair_context = exchange(pair_context)
-    context = attend((1 - column).reshape(1), held, held, pair, far_own, runs)
+    context = attend((1 - column).reshape(1), held, held, pair, far_own, runs, (out_other,))
     contexts = (context, pair_context, swap(context), swap(pair_context))
     glu, edge, mid_keep, mid_send = gated(
         meta, contexts, frames, other, out_weight, out_other, conv_gain,

time: 51.4 us -> 57.7 us (1.12)
  waiting for transfers between devices: 1.4 us -> 4.23 us
  local copies, waits for them, and re-layouts: 1.53 us -> 3.17 us
  Pallas kernels: 20 us -> 20.9 us
  starting transfers between devices: 11.9 us -> 12.7 us
    ppermute x2, waiting for transfers between devices: 0.7 us -> 3.73 us  [exchange(): return lax.ppermute(value, 'tm', [(i, i ^ 1) for i in range(blocks)])]
    unnamed x21 -> x27, local copies, waits for them, and re-layouts: 1.53 us -> 3.17 us
    pallas_call x2, Pallas kernels: 6.29 us -> 7.28 us  [attend(): pl.pallas_call(attend_kernel, in_specs=[pl.BlockSpec(memory_space=pltpu.S...]
    ppermute x2, starting transfers between devices: 1.96 us -> 2.66 us  [shift(): return lax.ppermute(value, 'tm', [p for p in pairs if 0 <= p[1] < blocks])]
  transfers between devices with their start and end apart: 15 -> 15, of which waited for: 3 -> 2; matrix products, arithmetic and copies ran while one was open for 4% -> 4% of each run, Pallas kernels for 31% -> 29%
where the time goes in v14:
time: 57.7 us; the launch traced here: 57.4 us
  Pallas kernels  20.9 us (36%)
  blocking collectives  15.5 us (27%)
  starting transfers between devices  12.7 us (22%)
  waiting for transfers between devices  4.23 us (7%)
  local copies, waits for them, and re-layouts  3.17 us (5%)
  other arithmetic  0.82 us (1%)
    all_to_all x1, blocking collectives, local(): lax.all_to_all(jnp.broadcast_to(counts[None, :], (blocks, counts.shape[0]...  15.5 us
    pallas_call x2, Pallas kernels, attend(): pl.pallas_call(attend_kernel, in_specs=[pl.BlockSpec(memory_space=pltpu.S...  7.28 us
    ppermute x10, starting transfers between devices, swap(): return lax.ppermute(value, 'head', [(0, 1), (1, 0)])  4.94 us
    ppermute x2, starting transfers between devices, exchange(): return lax.ppermute(value, 'tm', [(i, i ^ 1) for i in range(blocks)])  4.39 us
    ppermute x2, waiting for transfers between devices, exchange(): return lax.ppermute(value, 'tm', [(i, i ^ 1) for i in range(blocks)])  3.73 us
    pallas_call x1, Pallas kernels, convolve(): pl.pallas_call(conv_kernel, in_specs=[pl.BlockSpec(memory_space=pltpu.SME...  3.61 us
    unnamed x27, local copies, waits for them, and re-layouts  3.17 us
    pallas_call x1, Pallas kernels, gated(): pl.pallas_call(gate_kernel, in_specs=[pl.BlockSpec(memory_space=pltpu.SME...  3.08 us
  transfers between devices with their start and end apart: 15, of which 2 were waited for; matrix products, arithmetic and copies ran while one was open for 4% of the time, Pallas kernels for 29%

profile of v14, /device:TPU:0, one launch (start us, length us, event | category | flops | bytes accessed | tf_op | source)
XLA Modules:
  0.0 57.4 jit_solution(8693097010812698845)
XLA Ops:
  0.0 0.5 collective-permute-start
  0.5 1.5 %copy.16 = bf16[1024,2,256]{2,0,1:T(8,128)(2,1)S(1)} copy(bf16[1024,2,256]{2,1,0:T(2,128)(2,1)} %param.18) | data formatting | bytes 2097152 | tf_op args[7]
  2.1 0.6 %pad_maximum_fusion.taps_own = f32[32,256]{1,0:T(8,128)} fusion(f32[1,256]{1,0:T(1,128)S(1)} %bitcast.24, f32[31,256]{1,0:T(8,128)S(1)} %copy-done.10), kind=kLoop, calls=%fused_computation.1 | loop fusion | flops 8192 | bytes 65536 | tf_op jit(solution)/shard_map/concatenate | solution.py:509
  2.8 2.6 %project.1 = (bf16[512,256]{1,0:T(8,128)(2,1)S(1)}, bf16[512,384]{1,0:T(8,128)(2,1)S(1)}, bf16[512,384]{1,0:T(8,128)(2,1)S(1)}, bf16[512,256]{1,0:T(8,128)(2,1)}) custom-call(s32[4]{0:T(128)S(1)} %pad_add_fusion.meta, bf16[512,512]{1,0:T(8,128)(2,1)S(1)} %copy-done, bf16[512,512]{1,0:T(8,128)(2,1)S(1)} %collective-permute-done.other_ref.x_other, ...), custom_call_target="tpu_custom_call" | custom-call | tf_op jit(solution)/shard_map/project/pallas_call | solution.py:84
  5.5 2.9 %collective-permute-start.1 = (bf16[512,384]{1,0:T(8,128)(2,1)S(1)}, bf16[512,384]{1,0:T(8,128)(2,1)S(1)}, u32[]{:S(2)}, u32[]{:S(2)}) collective-permute-start(bf16[512,384]{1,0:T(8,128)(2,1)S(1)} %get-tuple-element.27), channel_id=1, source_target_pairs={{0,2},{2,0},{4,6},{6,4},{8,10},{10,8},{12,14},{14,12},{1,3},{3,1},... | collective-permute-start | bytes 1179656 | tf_op jit(solution)/shard_map/ppermute | solution.py:484
  8.4 1.3 %collective-permute-start.2 = (bf16[512,256]{1,0:T(8,128)(2,1)S(1)}, bf16[512,256]{1,0:T(8,128)(2,1)S(1)}, u32[]{:S(2)}, u32[]{:S(2)}) collective-permute-start(bf16[512,256]{1,0:T(8,128)(2,1)S(1)} %get-tuple-element.28), channel_id=1, source_target_pairs={{2,6},{4,0},{6,10},{8,4},{10,14},{12,8},{3,7},{5,1},{7,11},{9,5},{... | collective-permute-start | bytes 786440 | tf_op jit(solution)/shard_map/ppermute | solution.py:481
  9.7 1.4 %collective-permute-start.3 = (bf16[512,256]{1,0:T(8,128)(2,1)}, bf16[512,256]{1,0:T(8,128)(2,1)}, u32[]{:S(2)}, u32[]{:S(2)}) collective-permute-start(bf16[512,256]{1,0:T(8,128)(2,1)} %get-tuple-element.30), channel_id=1, source_target_pairs={{2,4},{4,2},{6,8},{8,6},{10,12},{12,10},{3,5},{5,3},{7,9},{9,7},{1... | collective-permute-start | bytes 786440 | tf_op jit(solution)/shard_map/ppermute | solution.py:481
  11.2 15.5 %all_to_all.8 = s32[8,1,16]{2,1,0:T(1,128)S(1)} all-to-all(s32[8,1,16]{2,1,0:T(1,128)S(1)} %broadcast_in_dim.5), channel_id=1, replica_groups=mesh['grp'=2,'tm'=8,'head'=2] {'tm'}, dimensions={0} | all-to-all | bytes 1024 | tf_op jit(solution)/shard_map/all_to_all | solution.py:506
  26.7 0.8 %bounds.1 = (s32[512,128]{1,0:T(8,128)S(1)}, s32[512,128]{1,0:T(8,128)S(1)}) custom-call(s32[4]{0:T(128)S(1)} %pad_add_fusion.meta, s32[8,16]{1,0:T(8,128)S(1)} %bitcast.20, s32[1,16]{1,0:T(1,128)S(1)} %bitcast.23), custom_call_target="tpu_custom_call" | custom-call | tf_op jit(solution)/shard_map/bounds/pallas_call | solution.py:127
  27.6 0.7 %copy-done.2 = s32[512,128]{1,0:T(8,128)} copy-done((s32[512,128]{1,0:T(8,128)}, s32[512,128]{1,0:T(8,128)S(1)}, u32[]{:S(2)}) %copy-start.2) | copy-done | bytes 262168
  28.3 3.4 %attend.3 = bf16[512,128]{1,0:T(8,128)(2,1)} custom-call(s32[1]{0:T(128)} %bitcast.1.a_high, bf16[512,384]{1,0:T(8,128)(2,1)S(1)} %collective-permute-done.1.side_a.query.center, bf16[512,384]{1,0:T(8,128)(2,1)S(1)} %collective-permute-done.1.side_a.query.center, bf16[512,384]{1,0:T(8,128)(2,1)S(1)} %get-tuple-element.26.query.center.side_a, ...), custom_call_target="tpu_custom_call" | custom-call | bytes 11070000 | tf_op jit(solution)/shard_map/attend/pallas_call | solution.py:201
  31.7 1.4 %collective-permute-start.5 = (bf16[512,128]{1,0:T(8,128)(2,1)}, bf16[512,128]{1,0:T(8,128)(2,1)S(1)}, u32[]{:S(2)}, u32[]{:S(2)}) collective-permute-start(bf16[512,128]{1,0:T(8,128)(2,1)} %attend.3), channel_id=1, source_target_pairs={{0,2},{2,0},{4,6},{6,4},{8,10},{10,8},{12,14},{14,12},{1,3},{3,1},... | collective-permute-start | bytes 393224 | tf_op jit(solution)/shard_map/ppermute | solution.py:484
  33.1 3.7 %collective-permute-done.5.pair_own = bf16[512,128]{1,0:T(8,128)(2,1)S(1)} collective-permute-done((bf16[512,128]{1,0:T(8,128)(2,1)}, bf16[512,128]{1,0:T(8,128)(2,1)S(1)}, u32[]{:S(2)}, u32[]{:S(2)}) %collective-permute-start.5) | collective-permute-done | bytes 131104 | tf_op jit(solution)/shard_map/ppermute | solution.py:484
  36.9 0.9 %copy-done.3 = s32[512,128]{1,0:T(8,128)S(1)} copy-done((s32[512,128]{1,0:T(8,128)S(1)}, s32[512,128]{1,0:T(8,128)}, u32[]{:S(2)}) %copy-start.3) | copy-done | bytes 262168
  37.8 3.9 %attend.2.mine_own = bf16[512,128]{1,0:T(8,128)(2,1)S(1)} custom-call(s32[1]{0:T(128)} %bitcast.4.a_high, bf16[512,384]{1,0:T(8,128)(2,1)S(1)} %get-tuple-element.26.query.center.side_a, bf16[512,384]{1,0:T(8,128)(2,1)S(1)} %get-tuple-element.26.query.center.side_a, bf16[512,384]{1,0:T(8,128)(2,1)S(1)} %collective-permute-done.1.side_a.query.center, ...), custom_call_target="tpu_custom_call" | custom-call | bytes 11070000 | tf_op jit(solution)/shard_map/attend/pallas_call | solution.py:201
  41.7 0.6 %collective-permute-start.6 = (bf16[512,128]{1,0:T(8,128)(2,1)S(1)}, bf16[512,128]{1,0:T(8,128)(2,1)S(1)}, u32[]{:S(2)}, u32[]{:S(2)}) collective-permute-start(bf16[512,128]{1,0:T(8,128)(2,1)S(1)} %attend.2.mine_own), channel_id=1, source_target_pairs={{0,1},{1,0},{2,3},{3,2},{4,5},{5,4},{6,7},{7,6},{8,9},{9,8},{10,11... | collective-permute-start | bytes 393224 | tf_op jit(solution)/shard_map/ppermute | solution.py:477
  43.3 3.1 %gated.1 = (bf16[272,512]{1,0:T(8,128)(2,1)S(1)}, bf16[64,512]{1,0:T(8,128)(2,1)S(1)}, bf16[256,512]{1,0:T(8,128)(2,1)S(1)}, bf16[256,512]{1,0:T(8,128)(2,1)S(1)}) custom-call(s32[4]{0:T(128)S(1)} %pad_add_fusion.meta, bf16[512,128]{1,0:T(8,128)(2,1)S(1)} %attend.2.mine_own, bf16[512,128]{1,0:T(8,128)(2,1)S(1)} %collective-permute-done.5.pair_own, ...), custom_call_target="tpu_custom_call" | custom-call | bytes 11070000 | tf_op jit(solution)/shard_map/gated/pallas_call | solution.py:291
  46.4 0.7 %collective-permute-start.11 = (bf16[64,512]{1,0:T(8,128)(2,1)S(1)}, bf16[64,512]{1,0:T(8,128)(2,1)S(1)}, u32[]{:S(2)}, u32[]{:S(2)}) collective-permute-start(bf16[64,512]{1,0:T(8,128)(2,1)S(1)} %get-tuple-element.43), channel_id=1, source_target_pairs={{2,1},{4,3},{6,5},{8,7},{10,9},{12,11},{14,13},{1,2},{3,4},{5,6},{... | collective-permute-start | bytes 196616 | tf_op jit(solution)/shard_map/ppermute | solution.py:532
  47.1 3.6 %convolve.1.act_ref = bf16[256,512]{1,0:T(8,128)(2,1)S(1)} custom-call(s32[4]{0:T(128)S(1)} %pad_add_fusion.meta, bf16[272,512]{1,0:T(8,128)(2,1)S(1)} %get-tuple-element.41.glu_ref, s32[512,128]{1,0:T(8,128)S(1)} %copy-done.4, f32[32,256]{1,0:T(8,128)S(1)} %copy-done.5, f32[32,256]{1,0:T(8,128)S(1)} %collective-permute-done.9.taps_other), custom_call_target="tpu_custom_call" | custom-call | flops 3449999872 | tf_op jit(solution)/shard_map/convolve/pallas_call | solution.py:364
  50.7 2.7 %collective-permute-start.10 = (bf16[256,512]{1,0:T(8,128)(2,1)S(1)}, bf16[256,512]{1,0:T(8,128)(2,1)S(1)}, u32[]{:S(2)}, u32[]{:S(2)}) collective-permute-start(bf16[256,512]{1,0:T(8,128)(2,1)S(1)} %convolve.1.act_ref), channel_id=1, source_target_pairs={{0,1},{1,0},{2,3},{3,2},{4,5},{5,4},{6,7},{7,6},{8,9},{9,8},{10,11... | collective-permute-start | bytes 786440 | tf_op jit(solution)/shard_map/ppermute | solution.py:477
  53.4 0.9 %rim.1.rim_ref = bf16[16,512]{1,0:T(8,128)(2,1)S(1)} custom-call(s32[4]{0:T(128)S(1)} %pad_add_fusion.meta, bf16[272,512]{1,0:T(8,128)(2,1)S(1)} %get-tuple-element.41.glu_ref, bf16[64,512]{1,0:T(8,128)(2,1)S(1)} %collective-permute-done.11.edge_ref, s32[512,128]{1,0:T(8,128)S(1)} %copy-done.4, f32[32,256]{1,0:T(8,128)S(1)} %copy-done.5, ...), custom_call_target="tpu_custom_call" | custom-call | flops 1150000000 | tf_op jit(solution)/shard_map/rim/pallas_call | solution.py:400
  54.3 0.5 collective-permute-start.12
  54.8 0.9 %finish_own.1.done_ref = bf16[256,512]{1,0:T(8,128)(2,1)S(1)} custom-call(s32[4]{0:T(128)S(1)} %pad_add_fusion.meta, bf16[256,512]{1,0:T(8,128)(2,1)S(1)} %convolve.1.act_ref, bf16[16,512]{1,0:T(8,128)(2,1)S(1)} %rim.1.rim_ref, bf16[256,512]{1,0:T(8,128)(2,1)S(1)} %get-tuple-element.46.mid_ref, bf16[256,1024]{1,0:T(8,128)(2,1)S(1)} %copy-done.9, ...), custom_call_target="tpu_custom_call" | custom-call | flops 1380000000 | tf_op jit(solution)/shard_map/finish_own/pallas_call | solution.py:448
  55.7 1.7 %finish.1 = bf16[512,512]{1,0:T(8,128)(2,1)} custom-call(s32[4]{0:T(128)S(1)} %pad_add_fusion.meta, bf16[256,512]{1,0:T(8,128)(2,1)S(1)} %collective-permute-done.10.act_ref, bf16[16,512]{1,0:T(8,128)(2,1)S(1)} %collective-permute-done.12.rim_ref, bf16[256,512]{1,0:T(8,128)(2,1)S(1)} %collective-permute-done.13.mid_ref, bf16[256,1024]{1,0:T(8,128)(2,1)S(1)} %copy-done.9, ...), custom_call_target="tpu_custom_call" | custom-call | flops 1380000000 | tf_op jit(solution)/shard_map/finish/pallas_call | solution.py:448
  (47 shorter events, 1.4 us)
Async XLA Ops:
  0.0 2.7 %copy-start = (bf16[512,512]{1,0:T(8,128)(2,1)S(1)}, bf16[512,512]{1,0:T(8,128)(2,1)}, u32[]{:S(2)}) copy-start(bf16[512,512]{1,0:T(8,128)(2,1)} %x_own.1) | copy-start | bytes 1572868
  0.0 2.7 %copy-start.6 = (f32[1024]{0:T(1024)S(1)}, f32[1024]{0:T(1024)}, u32[]{:S(2)}) copy-start(f32[1024]{0:T(1024)} %param.14) | copy-start | bytes 12292
  0.0 2.7 %collective-permute-start = (bf16[512,512]{1,0:T(8,128)(2,1)}, bf16[512,512]{1,0:T(8,128)(2,1)S(1)}, u32[]{:S(2)}, u32[]{:S(2)}) collective-permute-start(bf16[512,512]{1,0:T(8,128)(2,1)} %x_own.1), channel_id=1, source_target_pairs={{0,1},{1,0},{2,3},{3,2},{4,5},{5,4},{6,7},{7,6},{8,9},{9,8},{10,11... | collective-permute-start | bytes 1572872 | tf_op jit(solution)/shard_map/ppermute | solution.py:477
  0.5 2.2 %copy-start.1 = (bf16[1024,3,256]{2,0,1:T(8,128)(2,1)S(1)}, bf16[1024,3,256]{2,0,1:T(8,128)(2,1)}, u32[]{:S(2)}) copy-start(bf16[1024,3,256]{2,0,1:T(8,128)(2,1)} %param.15) | copy-start | bytes 4718596
  2.8 8.3 %copy-start.11 = (s32[512]{0:T(512)S(1)}, s32[512]{0:T(512)}, u32[]{:S(2)}) copy-start(s32[512]{0:T(512)} %param.12) | copy-start | bytes 6148
  2.8 23.9 %copy-start.8 = (s32[16]{0:T(128)S(1)}, s32[16]{0:T(128)}, u32[]{:S(2)}) copy-start(s32[16]{0:T(128)} %param.13) | copy-start | bytes 196
  5.4 37.9 %collective-permute-start.8 = (bf16[2,1024,256]{2,1,0:T(8,128)(2,1)S(1)}, bf16[2,1024,256]{2,1,0:T(8,128)(2,1)}, u32[]{:S(2)}, u32[]{:S(2)}) collective-permute-start(bf16[2,1024,256]{2,1,0:T(8,128)(2,1)S(1)} %bitcast.17), channel_id=1, source_target_pairs={{0,1},{1,0},{2,3},{3,2},{4,5},{5,4},{6,7},{7,6},{8,9},{9,8},{10,11... | collective-permute-start | bytes 3145736 | tf_op jit(solution)/shard_map/ppermute | solution.py:477
  5.5 22.8 %collective-permute-start.1 = (bf16[512,384]{1,0:T(8,128)(2,1)S(1)}, bf16[512,384]{1,0:T(8,128)(2,1)S(1)}, u32[]{:S(2)}, u32[]{:S(2)}) collective-permute-start(bf16[512,384]{1,0:T(8,128)(2,1)S(1)} %get-tuple-element.27), channel_id=1, source_target_pairs={{0,2},{2,0},{4,6},{6,4},{8,10},{10,8},{12,14},{14,12},{1,3},{3,1},... | collective-permute-start | bytes 1179656 | tf_op jit(solution)/shard_map/ppermute | solution.py:484
  8.4 28.4 %collective-permute-start.4 = (bf16[256,1024]{1,0:T(8,128)(2,1)}, bf16[256,1024]{1,0:T(8,128)(2,1)S(1)}, u32[]{:S(2)}, u32[]{:S(2)}) collective-permute-start(bf16[256,1024]{1,0:T(8,128)(2,1)} %out_own), channel_id=1, source_target_pairs={{0,1},{1,0},{2,3},{3,2},{4,5},{5,4},{6,7},{7,6},{8,9},{9,8},{10,11... | collective-permute-start | bytes 1572872 | tf_op jit(solution)/shard_map/ppermute | solution.py:477
  8.4 19.8 %collective-permute-start.2 = (bf16[512,256]{1,0:T(8,128)(2,1)S(1)}, bf16[512,256]{1,0:T(8,128)(2,1)S(1)}, u32[]{:S(2)}, u32[]{:S(2)}) collective-permute-start(bf16[512,256]{1,0:T(8,128)(2,1)S(1)} %get-tuple-element.28), channel_id=1, source_target_pairs={{2,6},{4,0},{6,10},{8,4},{10,14},{12,8},{3,7},{5,1},{7,11},{9,5},{... | collective-permute-start | bytes 786440 | tf_op jit(solution)/shard_map/ppermute | solution.py:481
  9.7 27.1 %collective-permute-start.3 = (bf16[512,256]{1,0:T(8,128)(2,1)}, bf16[512,256]{1,0:T(8,128)(2,1)}, u32[]{:S(2)}, u32[]{:S(2)}) collective-permute-start(bf16[512,256]{1,0:T(8,128)(2,1)} %get-tuple-element.30), channel_id=1, source_target_pairs={{2,4},{4,2},{6,8},{8,6},{10,12},{12,10},{3,5},{5,3},{7,9},{9,7},{1... | collective-permute-start | bytes 786440 | tf_op jit(solution)/shard_map/ppermute | solution.py:481
  28.3 15.0 %copy-start.7 = (f32[1024]{0:T(1024)S(1)}, f32[1024]{0:T(1024)}, u32[]{:S(2)}) copy-start(f32[1024]{0:T(1024)} %param.17) | copy-start | bytes 12292
  31.7 5.2 %collective-permute-start.5 = (bf16[512,128]{1,0:T(8,128)(2,1)}, bf16[512,128]{1,0:T(8,128)(2,1)S(1)}, u32[]{:S(2)}, u32[]{:S(2)}) collective-permute-start(bf16[512,128]{1,0:T(8,128)(2,1)} %attend.3), channel_id=1, source_target_pairs={{0,2},{2,0},{4,6},{6,4},{8,10},{10,8},{12,14},{14,12},{1,3},{3,1},... | collective-permute-start | bytes 393224 | tf_op jit(solution)/shard_map/ppermute | solution.py:484
  36.8 6.0 %collective-permute-start.7 = (bf16[512,128]{1,0:T(8,128)(2,1)S(1)}, bf16[512,128]{1,0:T(8,128)(2,1)S(1)}, u32[]{:S(2)}, u32[]{:S(2)}) collective-permute-start(bf16[512,128]{1,0:T(8,128)(2,1)S(1)} %collective-permute-done.5.pair_own), channel_id=1, source_target_pairs={{0,1},{1,0},{2,3},{3,2},{4,5},{5,4},{6,7},{7,6},{8,9},{9,8},{10,11... | collective-permute-start | bytes 393224 | tf_op jit(solution)/shard_map/ppermute | solution.py:477
  37.8 4.5 %copy-start.9 = (bf16[256,1024]{1,0:T(8,128)(2,1)S(1)}, bf16[256,1024]{1,0:T(8,128)(2,1)}, u32[]{:S(2)}) copy-start(bf16[256,1024]{1,0:T(8,128)(2,1)} %w_own.1) | copy-start | bytes 1572868
  37.8 4.6 %copy-start.5 = (f32[32,256]{1,0:T(8,128)S(1)}, f32[32,256]{1,0:T(8,128)}, u32[]{:S(2)}) copy-start(f32[32,256]{1,0:T(8,128)} %pad_maximum_fusion.taps_own) | copy-start | bytes 98308
  41.7 1.6 %collective-permute-start.6 = (bf16[512,128]{1,0:T(8,128)(2,1)S(1)}, bf16[512,128]{1,0:T(8,128)(2,1)S(1)}, u32[]{:S(2)}, u32[]{:S(2)}) collective-permute-start(bf16[512,128]{1,0:T(8,128)(2,1)S(1)} %attend.2.mine_own), channel_id=1, source_target_pairs={{0,1},{1,0},{2,3},{3,2},{4,5},{5,4},{6,7},{7,6},{8,9},{9,8},{10,11... | collective-permute-start | bytes 393224 | tf_op jit(solution)/shard_map/ppermute | solution.py:477
  42.3 12.5 %collective-permute-start.14 = (bf16[256,1024]{1,0:T(8,128)(2,1)S(1)}, bf16[256,1024]{1,0:T(8,128)(2,1)S(1)}, u32[]{:S(2)}, u32[]{:S(2)}) collective-permute-start(bf16[256,1024]{1,0:T(8,128)(2,1)S(1)} %copy-done.9), channel_id=1, source_target_pairs={{0,1},{1,0},{2,3},{3,2},{4,5},{5,4},{6,7},{7,6},{8,9},{9,8},{10,11... | collective-permute-start | bytes 1572872 | tf_op jit(solution)/shard_map/ppermute | solution.py:477
  42.4 4.7 %collective-permute-start.9 = (f32[32,256]{1,0:T(8,128)S(1)}, f32[32,256]{1,0:T(8,128)S(1)}, u32[]{:S(2)}, u32[]{:S(2)}) collective-permute-start(f32[32,256]{1,0:T(8,128)S(1)} %copy-done.5), channel_id=1, source_target_pairs={{0,1},{1,0},{2,3},{3,2},{4,5},{5,4},{6,7},{7,6},{8,9},{9,8},{10,11... | collective-permute-start | bytes 98312 | tf_op jit(solution)/shard_map/ppermute | solution.py:477
  43.3 3.8 %copy-start.4 = (s32[512,128]{1,0:T(8,128)S(1)}, s32[512,128]{1,0:T(8,128)}, u32[]{:S(2)}) copy-start(s32[512,128]{1,0:T(8,128)} %copy-done.2) | copy-start | bytes 786436
  46.4 7.1 %collective-permute-start.11 = (bf16[64,512]{1,0:T(8,128)(2,1)S(1)}, bf16[64,512]{1,0:T(8,128)(2,1)S(1)}, u32[]{:S(2)}, u32[]{:S(2)}) collective-permute-start(bf16[64,512]{1,0:T(8,128)(2,1)S(1)} %get-tuple-element.43), channel_id=1, source_target_pairs={{2,1},{4,3},{6,5},{8,7},{10,9},{12,11},{14,13},{1,2},{3,4},{5,6},{... | collective-permute-start | bytes 196616 | tf_op jit(solution)/shard_map/ppermute | solution.py:532
  50.7 5.0 %collective-permute-start.10 = (bf16[256,512]{1,0:T(8,128)(2,1)S(1)}, bf16[256,512]{1,0:T(8,128)(2,1)S(1)}, u32[]{:S(2)}, u32[]{:S(2)}) collective-permute-start(bf16[256,512]{1,0:T(8,128)(2,1)S(1)} %convolve.1.act_ref), channel_id=1, source_target_pairs={{0,1},{1,0},{2,3},{3,2},{4,5},{5,4},{6,7},{7,6},{8,9},{9,8},{10,11... | collective-permute-start | bytes 786440 | tf_op jit(solution)/shard_map/ppermute | solution.py:477
  53.4 2.4 %collective-permute-start.13 = (bf16[256,512]{1,0:T(8,128)(2,1)S(1)}, bf16[256,512]{1,0:T(8,128)(2,1)S(1)}, u32[]{:S(2)}, u32[]{:S(2)}) collective-permute-start(bf16[256,512]{1,0:T(8,128)(2,1)S(1)} %get-tuple-element.44), channel_id=1, source_target_pairs={{0,1},{1,0},{2,3},{3,2},{4,5},{5,4},{6,7},{7,6},{8,9},{9,8},{10,11... | collective-permute-start | bytes 786440 | tf_op jit(solution)/shard_map/ppermute | solution.py:477
  54.3 1.4 %collective-permute-start.12 = (bf16[16,512]{1,0:T(8,128)(2,1)S(1)}, bf16[16,512]{1,0:T(8,128)(2,1)S(1)}, u32[]{:S(2)}, u32[]{:S(2)}) collective-permute-start(bf16[16,512]{1,0:T(8,128)(2,1)S(1)} %rim.1.rim_ref), channel_id=1, source_target_pairs={{0,1},{1,0},{2,3},{3,2},{4,5},{5,4},{6,7},{7,6},{8,9},{9,8},{10,11... | collective-permute-start | bytes 49160 | tf_op jit(solution)/shard_map/ppermute | solution.py:477
  (4 other events, 5.9 us)
